TPU v7x, 32 devices: a whole 2x2x4 slice. The times are simulated.
32 devices in a mesh: expert: 8 (over z, x), tensor: 4 (over y, core).
Axes of the slice: x: 2, y: 2, z: 4, core: 2. Of those that a mesh axis runs over, the one named last changes fastest.
Arguments:
- tokens: bfloat16 [4096, 2048], P('expert'), may hold values from -6 to 6
- cotangent: bfloat16 [4096, 2048], P('expert'), may hold values from -6 to 6
- attn_gain: bfloat16 [2048], replicated, may hold values from 0.5 to 1.5
- ffn_gain: bfloat16 [2048], replicated, may hold values from 0.5 to 1.5
- query_gain: bfloat16 [2048], P('tensor'), may hold values from 0.5 to 1.5
- key_gain: bfloat16 [2048], P('tensor'), may hold values from 0.5 to 1.5
- query_weight: bfloat16 [2048, 2048], P(None, 'tensor'), may hold values from -0.125 to 0.125
- key_weight: bfloat16 [2048, 2048], P(None, 'tensor'), may hold values from -0.125 to 0.125
- value_weight: bfloat16 [2048, 2048], P(None, 'tensor'), may hold values from -0.125 to 0.125
- output_weight: bfloat16 [2048, 2048], P('tensor'), may hold values from -0.5 to 0.5
- expert_gate: bfloat16 [32, 2048, 1024], P('expert', None, 'tensor'), may hold values from -0.125 to 0.125
- expert_up: bfloat16 [32, 2048, 1024], P('expert', None, 'tensor'), may hold values from -0.125 to 0.125
- expert_down: bfloat16 [32, 1024, 2048], P('expert', 'tensor'), may hold values from -0.5 to 0.5
- adapt_in: bfloat16 [3, 2048, 128], replicated, may hold values from -0.125 to 0.125
- adapt_out: bfloat16 [3, 128, 2048], P(None, None, 'tensor'), may hold values from -1.5 to 1.5
- adapt_in_out: bfloat16 [2048, 128], P('tensor'), may hold values from -0.5 to 0.5
- adapt_out_out: bfloat16 [128, 2048], replicated, may hold values from -1.5 to 1.5
- routes: int32 [4096, 8], P('expert'), may hold values from 0 to 31, all different within a row; in each aligned block of 512 rows (0 to 511, 512 to 1023, ...) at most 160 rows name the same one
- gate_weights: float32 [4096, 8], P('expert'), may hold values from 0.1 to 0.25
- block_parent: int32 [32], P('expert'), may hold values from 0 to 2, as said below
- adapter_pick: int32 [8, 8], P('expert'), may hold values from 0 to 1, as said below
Outputs:
- layer_out: bfloat16 [4096, 2048], P('expert', 'tensor')
- input_grad: float32 [4096, 2048], P('expert')
- grad_adapt_in: float32 [3, 2048, 128], replicated
- grad_adapt_out: float32 [3, 128, 2048], P(None, None, 'tensor')
- grad_adapt_in_out: float32 [2048, 128], P('tensor')
- grad_adapt_out_out: float32 [128, 2048], replicated
Inputs may be any that keep to these rules, and one draw needn't show every extreme that they name: `routes`: in the rows of one tree's 512 tokens no expert is named more than 160 times, a bound that some block reaches. `block_parent`: each entry is the index, within its tree of 4 blocks, of the block directly above it on its path; it is below the block's own index, except for each tree's first block, which names itself; each tree's last block names the block before it. `adapter_pick`: each row holds a single 1.
All inputs are finite; a program needn't handle non-finite values.
Results may differ from a plain program's by a relative error of at most 0.02.
Values may be sent and summed in bfloat16 or wider, within the bound.
No kernel may reach another device: no remote copies, remote signals or barrier semaphores. Data moves between devices by JAX's collectives and lax.ppermute only.
A program may use at most 256 MiB of HBM per device.

v0:
```python
import jax
import jax.numpy as jnp
from jax import lax
from jax.sharding import PartitionSpec as P

HD = 128
TOP = 8
RANK = 16


EPSILON = 1e-05
ROPE_BASE = 10000.0
MASKED_SCORE = -1e30


def ancestry(parents):
    blocks = parents.shape[1]
    places = jnp.arange(blocks, dtype=jnp.int32)
    current = places[None, :]

    def climb(climb_step, climb_state):
        walker, reached = climb_state
        walker = jnp.take_along_axis(parents, walker, axis=1)
        return (walker, reached | (walker[:, :, None] == places[None, None, :]))

    initial = (current, current[:, :, None] == places[None, None, :])
    return lax.fori_loop(0, blocks - 1, climb, initial)[1]


def rope_tables(reached, block_span, head_size):
    depths = jnp.sum(reached.astype(jnp.int32), axis=2) - 1
    offsets = jnp.arange(block_span, dtype=jnp.int32)
    located = (
        (depths[:, :, None] * block_span + offsets[None, None, :]).reshape(-1).astype(jnp.float32)
    )
    halves = head_size // 2
    speeds = ROPE_BASE ** (-2.0 * jnp.arange(halves, dtype=jnp.float32) / head_size)
    angles = located[:, None] * speeds[None, :]
    angles = jnp.concatenate([angles, angles], axis=1)
    return (jnp.cos(angles), jnp.sin(angles))


def rotate(values, cosine_table, sine_table):
    halves = values.shape[-1] // 2
    turned = jnp.concatenate([-values[..., halves:], values[..., :halves]], axis=-1)
    return values * cosine_table[:, None, :] + turned * sine_table[:, None, :]


def unrotate(values, cosine_table, sine_table):
    halves = values.shape[-1] // 2
    sined = values * sine_table[:, None, :]
    return values * cosine_table[:, None, :] + jnp.concatenate(
        [sined[..., halves:], -sined[..., :halves]], axis=-1
    )


def token_mask(reached, total_size):
    blocks = reached.shape[0]
    block_span = total_size // blocks
    widened = jnp.broadcast_to(
        reached[:, None, :, None], (blocks, block_span, blocks, block_span)
    ).reshape(total_size, total_size)
    positions = jnp.arange(total_size, dtype=jnp.int32)
    return widened & (positions[None, :] <= positions[:, None])


def norm_back(scaled_grad, values, inverse, model_width, inner_sum):
    return inverse * scaled_grad - values * inverse**3 * (inner_sum / model_width)


def body(
    tokens,
    cotangent,
    attn_gain,
    ffn_gain,
    query_gain,
    key_gain,
    query_weight,
    key_weight,
    value_weight,
    output_weight,
    expert_gate,
    expert_up,
    expert_down,
    adapt_in,
    adapt_out,
    adapt_in_out,
    adapt_out_out,
    routes,
    gate_weights,
    block_parent,
    adapter_pick,
):
    rows_here, model_width = tokens.shape
    local_width = query_weight.shape[1]
    heads_here = local_width // HD
    tensor_rank = lax.axis_index("tensor")
    tensor_count = lax.axis_size("tensor")
    owners = lax.axis_size("expert")
    experts_here = expert_gate.shape[0]
    experts_all = experts_here * owners
    capacity = 5 * rows_here * TOP // (4 * experts_all)
    column_share = model_width // tensor_count
    float_kind = jnp.float32
    half_kind = jnp.bfloat16
    inputs = tokens.astype(float_kind)
    first_gain = attn_gain.astype(float_kind)
    second_gain = ffn_gain.astype(float_kind)
    first_inverse = lax.rsqrt(jnp.mean(inputs * inputs, axis=1, keepdims=True) + EPSILON)
    normed_in = (inputs * first_inverse * first_gain).astype(half_kind)
    reached = ancestry(block_parent.reshape(1, -1))
    cosine_table, sine_table = rope_tables(reached, rows_here // block_parent.shape[0], HD)
    key_mask = token_mask(reached[0], rows_here)
    select = jnp.repeat(adapter_pick.astype(float_kind), RANK, axis=1)
    select_low = select.astype(half_kind)
    lowrank = (
        jnp.einsum("td,idr->itr", normed_in, adapt_in, preferred_element_type=float_kind)
        * select[None]
    ).astype(half_kind)
    matrices = (query_weight, key_weight, value_weight)
    raw_list = [
        jnp.dot(normed_in, matrices[projection], preferred_element_type=float_kind)
        + jnp.dot(lowrank[projection], adapt_out[projection], preferred_element_type=float_kind)
        for projection in range(3)
    ]
    query_raw, key_raw, value_raw = raw_list
    query_squares, key_squares = lax.psum(
        (jnp.sum(query_raw * query_raw, axis=1), jnp.sum(key_raw * key_raw, axis=1)), "tensor"
    )
    query_inverse = lax.rsqrt(query_squares / model_width + EPSILON)[:, None]
    key_inverse = lax.rsqrt(key_squares / model_width + EPSILON)[:, None]
    query_scale = query_gain.astype(float_kind)
    key_scale = key_gain.astype(float_kind)
    queries = rotate(
        (query_raw * query_inverse * query_scale).reshape(rows_here, heads_here, HD),
        cosine_table,
        sine_table,
    ).astype(half_kind)
    keys = rotate(
        (key_raw * key_inverse * key_scale).reshape(rows_here, heads_here, HD),
        cosine_table,
        sine_table,
    ).astype(half_kind)
    values = value_raw.astype(half_kind).reshape(rows_here, heads_here, HD)
    score_scale = HD ** (-0.5)
    scores = (
        jnp.einsum("qhd,khd->hqk", queries, keys, preferred_element_type=float_kind) * score_scale
    )
    scores = jnp.where(key_mask[None], scores, MASKED_SCORE)
    row_max = jnp.max(scores, axis=2, keepdims=True)
    raised = jnp.exp(scores - row_max)
    row_total = jnp.sum(raised, axis=2, keepdims=True)
    weights_low = (raised / row_total).astype(half_kind)
    log_total = row_max + jnp.log(row_total)
    attended = (
        jnp.einsum("hqk,khd->qhd", weights_low, values, preferred_element_type=float_kind)
        .reshape(rows_here, local_width)
        .astype(half_kind)
    )
    output_part = jnp.dot(attended, output_weight, preferred_element_type=float_kind)
    mixing_part = jnp.dot(attended, adapt_in_out, preferred_element_type=float_kind)
    branch, mixing = lax.psum((output_part, mixing_part), "tensor")
    mixed = (mixing * select).astype(half_kind)
    resid = inputs + branch + jnp.dot(mixed, adapt_out_out, preferred_element_type=float_kind)
    second_inverse = lax.rsqrt(jnp.mean(resid * resid, axis=1, keepdims=True) + EPSILON)
    normed_ffn = (resid * second_inverse * second_gain).astype(half_kind)
    route_list = routes.reshape(-1)
    route_hits = (route_list[:, None] == jnp.arange(experts_all, dtype=jnp.int32)[None, :]).astype(
        jnp.int32
    )
    within = jnp.sum(jnp.cumsum(route_hits, axis=0) * route_hits, axis=1) - 1
    slot_ids = route_list * capacity + within
    slot_owner = (
        jnp.zeros((experts_all * capacity,), jnp.int32)
        .at[slot_ids]
        .set(jnp.arange(rows_here * TOP, dtype=jnp.int32) + 1)
    )
    slot_live = (slot_owner > 0)[:, None]
    source_slot = jnp.maximum(slot_owner - 1, 0)
    source_token = source_slot // TOP
    gate_use, up_use, down_use = (expert_gate, expert_up, expert_down)
    outgoing = jnp.where(slot_live, normed_ffn[source_token], jnp.zeros((), half_kind)).reshape(
        owners, experts_here, capacity, model_width
    )
    arrived = lax.all_to_all(outgoing, "expert", split_axis=0, concat_axis=0, tiled=True)
    kept_states = []
    results = []
    for expert_index in range(experts_here):
        rows_in = arrived[:, expert_index]
        gate_value = jnp.einsum(
            "scd,df->scf", rows_in, gate_use[expert_index], preferred_element_type=float_kind
        )
        up_value = jnp.einsum(
            "scd,df->scf", rows_in, up_use[expert_index], preferred_element_type=float_kind
        )
        hidden = (jax.nn.silu(gate_value) * up_value).astype(half_kind)
        partial_rows = jnp.einsum(
            "scf,fd->scd", hidden, down_use[expert_index], preferred_element_type=float_kind
        )
        results.append(
            lax.psum_scatter(
                partial_rows.astype(jnp.bfloat16), "tensor", scatter_dimension=2, tiled=True
            )
            .astype(jnp.float32)
            .astype(half_kind)
        )
        kept_states.append((gate_value, up_value))
    returned = lax.all_to_all(
        jnp.stack(results, axis=1), "expert", split_axis=0, concat_axis=0, tiled=True
    )
    returned = returned.reshape(experts_all * capacity, column_share)
    picked = returned[slot_ids].reshape(rows_here, TOP, column_share).astype(float_kind)
    mixture = jnp.sum(gate_weights[:, :, None] * picked, axis=1)
    resid_columns = lax.dynamic_slice_in_dim(resid, tensor_rank * column_share, column_share, 1)
    layer_out = (resid_columns + mixture).astype(half_kind)
    grad_out = cotangent.astype(float_kind)
    slot_gates = gate_weights.reshape(-1)[source_slot][:, None]
    grad_slots = jnp.where(
        slot_live, slot_gates * cotangent[source_token].astype(float_kind), 0.0
    ).astype(half_kind)
    grad_slots = grad_slots.reshape(owners, experts_here, capacity, model_width)
    grad_arrived = lax.all_to_all(grad_slots, "expert", split_axis=0, concat_axis=0, tiled=True)
    pieces = []
    for expert_index in range(experts_here):
        gate_value, up_value = kept_states[expert_index]
        hidden_grad = jnp.einsum(
            "scd,fd->scf",
            grad_arrived[:, expert_index],
            down_use[expert_index],
            preferred_element_type=float_kind,
        )
        sigmoid_gate = jax.nn.sigmoid(gate_value)
        gate_grad = (
            hidden_grad * up_value * sigmoid_gate * (1.0 + gate_value * (1.0 - sigmoid_gate))
        ).astype(half_kind)
        up_grad = (hidden_grad * gate_value * sigmoid_gate).astype(half_kind)
        row_grad = jnp.einsum(
            "scf,df->scd", gate_grad, gate_use[expert_index], preferred_element_type=float_kind
        ) + jnp.einsum(
            "scf,df->scd", up_grad, up_use[expert_index], preferred_element_type=float_kind
        )
        pieces.append(
            lax.psum_scatter(row_grad, "tensor", scatter_dimension=2, tiled=True).astype(half_kind)
        )
    came_back = lax.all_to_all(
        jnp.stack(pieces, axis=1), "expert", split_axis=0, concat_axis=0, tiled=True
    )
    came_back = came_back.reshape(experts_all * capacity, column_share)
    ffn_columns_grad = jnp.sum(
        came_back[slot_ids].reshape(rows_here, TOP, column_share).astype(float_kind), axis=1
    )
    ffn_in_grad = lax.all_gather(ffn_columns_grad, "tensor", axis=1, tiled=True)
    second_scaled = ffn_in_grad * second_gain
    resid_grad = grad_out + norm_back(
        second_scaled,
        resid,
        second_inverse,
        model_width,
        jnp.sum(second_scaled * resid, axis=1, keepdims=True),
    )
    branch_grad = resid_grad.astype(half_kind)
    grad_adapt_out_out = jnp.dot(mixed.T, branch_grad, preferred_element_type=float_kind)
    mixed_grad = (
        jnp.dot(branch_grad, adapt_out_out.T, preferred_element_type=float_kind).astype(half_kind)
        * select_low
    )
    grad_adapt_in_out = jnp.dot(attended.T, mixed_grad, preferred_element_type=float_kind)
    attended_grad = (
        jnp.dot(branch_grad, output_weight.T, preferred_element_type=float_kind)
        + jnp.dot(mixed_grad, adapt_in_out.T, preferred_element_type=float_kind)
    ).astype(half_kind)
    attended_grad = attended_grad.reshape(rows_here, heads_here, HD)
    scores = (
        jnp.einsum("qhd,khd->hqk", queries, keys, preferred_element_type=float_kind) * score_scale
    )
    softmax_full = jnp.where(key_mask[None], jnp.exp(scores - log_total), 0.0)
    softmax_low = softmax_full.astype(half_kind)
    value_grad = jnp.einsum(
        "hqk,qhd->khd", softmax_low, attended_grad, preferred_element_type=float_kind
    ).astype(half_kind)
    prob_grad = jnp.einsum("qhd,khd->hqk", attended_grad, values, preferred_element_type=float_kind)
    score_grad = (
        softmax_full * (prob_grad - jnp.sum(softmax_full * prob_grad, axis=2, keepdims=True))
    ).astype(half_kind)
    query_grad = (
        jnp.einsum("hqk,khd->qhd", score_grad, keys, preferred_element_type=float_kind)
        * score_scale
    )
    key_grad = (
        jnp.einsum("hqk,qhd->khd", score_grad, queries, preferred_element_type=float_kind)
        * score_scale
    )
    query_scaled = (
        unrotate(query_grad, cosine_table, sine_table).reshape(rows_here, local_width) * query_scale
    )
    key_scaled = (
        unrotate(key_grad, cosine_table, sine_table).reshape(rows_here, local_width) * key_scale
    )
    query_inner, key_inner = lax.psum(
        (jnp.sum(query_scaled * query_raw, axis=1), jnp.sum(key_scaled * key_raw, axis=1)), "tensor"
    )
    query_raw_grad = norm_back(
        query_scaled, query_raw, query_inverse, model_width, query_inner[:, None]
    ).astype(half_kind)
    key_raw_grad = norm_back(
        key_scaled, key_raw, key_inverse, model_width, key_inner[:, None]
    ).astype(half_kind)
    value_raw_grad = value_grad.reshape(rows_here, local_width)
    raw_grads = (query_raw_grad, key_raw_grad, value_raw_grad)
    normed_part = jnp.dot(query_raw_grad, query_weight.T, preferred_element_type=float_kind)
    normed_part = normed_part + jnp.dot(
        key_raw_grad, key_weight.T, preferred_element_type=float_kind
    )
    normed_part = normed_part + jnp.dot(
        value_raw_grad, value_weight.T, preferred_element_type=float_kind
    )
    lowrank_part = jnp.stack(
        [
            jnp.dot(
                raw_grads[projection], adapt_out[projection].T, preferred_element_type=float_kind
            )
            for projection in range(3)
        ]
    )
    normed_in_grad, lowrank_total = (
        lax.psum(normed_part.astype(jnp.bfloat16), "tensor").astype(jnp.float32),
        lax.psum(lowrank_part.astype(jnp.bfloat16), "tensor").astype(jnp.float32),
    )
    lowrank_grad = lowrank_total.astype(half_kind) * select_low[None]
    grad_adapt_out = jnp.stack(
        [
            jnp.dot(lowrank[projection].T, raw_grads[projection], preferred_element_type=float_kind)
            for projection in range(3)
        ]
    )
    grad_adapt_in = jnp.einsum(
        "td,itr->idr", normed_in, lowrank_grad, preferred_element_type=float_kind
    )
    normed_in_grad = normed_in_grad + jnp.einsum(
        "itr,idr->td", lowrank_grad, adapt_in, preferred_element_type=float_kind
    )
    first_scaled = normed_in_grad * first_gain
    input_grad = resid_grad + norm_back(
        first_scaled,
        inputs,
        first_inverse,
        model_width,
        jnp.sum(first_scaled * inputs, axis=1, keepdims=True),
    )
    summed_grads = (
        lax.psum(grad_adapt_in.astype(jnp.bfloat16), "expert").astype(jnp.float32),
        lax.psum(grad_adapt_out.astype(jnp.bfloat16), "expert").astype(jnp.float32),
        lax.psum(grad_adapt_in_out.astype(jnp.bfloat16), "expert").astype(jnp.float32),
        lax.psum(grad_adapt_out_out.astype(jnp.bfloat16), "expert").astype(jnp.float32),
    )
    return (
        layer_out,
        input_grad,
        summed_grads[0],
        summed_grads[1],
        summed_grads[2],
        summed_grads[3],
    )


def solution(mesh):
    return jax.shard_map(
        body,
        mesh=mesh,
        in_specs=(
            P("expert", None),
            P("expert", None),
            P(),
            P(),
            P("tensor"),
            P("tensor"),
            P(None, "tensor"),
            P(None, "tensor"),
            P(None, "tensor"),
            P("tensor", None),
            P("expert", None, "tensor"),
            P("expert", None, "tensor"),
            P("expert", "tensor", None),
            P(),
            P(None, None, "tensor"),
            P("tensor", None),
            P(),
            P("expert", None),
            P("expert", None),
            P("expert"),
            P("expert", None),
        ),
        out_specs=(
            P("expert", "tensor"),
            P("expert", None),
            P(),
            P(None, None, "tensor"),
            P("tensor", None),
            P(),
        ),
        check_vma=False,
    )
```

profile of v0, /device:TPU:0, one launch (start us, length us, event | category | flops | bytes accessed | tf_op | source)
XLA Modules:
  0.0 1897.2 jit_solution(16502948039855800143)
XLA Ops:
  9.6 9.2 reduce-window.6
  20.4 15.5 scatter_custom_fusion
  36.4 28.7 %gather_fusion.3 = f32[5120]{0:T(1024)S(1)} fusion(f32[4096]{0:T(1024)S(1)} %reshape.427, s32[5120]{0:T(1024)S(1)} %get-tuple-element.100), kind=kCustom, calls=%fused_computation.3 | custom fusion | bytes 61440 | tf_op jit(solution)/shard_map/gather | solution.py:217
  65.2 40.7 %gather_fusion.4 = bf16[5120,2048]{1,0:T(8,128)(2,1)} fusion(bf16[512,2048]{1,0:T(8,128)(2,1)} %param.24, s32[5120]{0:T(1024)S(1)} %get-tuple-element.101), kind=kCustom, calls=%fused_computation.4 | custom fusion | bytes 41963520 | tf_op jit(solution)/shard_map/gather | solution.py:219
  105.9 18.9 fusion.5
  124.8 7.4 all-to-all-start.2
  148.7 8.4 all-reduce.1
  176.0 90.4 %all-reduce.9.cloned.1.call-done = (f32[512,2048]{1,0:T(8,128)}, f32[512,128]{1,0:T(8,128)}) async-done(((f32[512,2048]{1,0:T(8,128)}, f32[512,128]{1,0:T(8,128)}), (f32[512,2048]{1,0:T(8,128)}, f32[512,128]{1,0:T(8,128)})) %all-reduce.9.cloned.1.call-update) | async-done | bytes 4456464 | tf_op jit(solution)/shard_map/psum | solution.py:162
  274.1 40.7 %gather_fusion.1 = bf16[5120,2048]{1,0:T(8,128)(2,1)} fusion(bf16[512,2048]{1,0:T(8,128)(2,1)} %multiply_convert_fusion.1, s32[5120]{0:T(1024)S(1)} %copy-done.75), kind=kCustom, calls=%fused_computation.1 | custom fusion | bytes 41963520 | tf_op jit(solution)/shard_map/gather | solution.py:182
  314.8 17.6 broadcast_select_fusion
  332.4 253.5 %all-to-all-done.2 = bf16[8,4,160,2048]{3,2,1,0:T(8,128)(2,1)} async-done(((bf16[8,4,160,2048]{3,2,1,0:T(8,128)(2,1)}), bf16[8,4,160,2048]{3,2,1,0:T(8,128)(2,1)}, u32[]{:S(2)}, u32[]{:S(2)}) %all-to-all-start.2) | async-done | bytes 20971552 | tf_op jit(solution)/shard_map/all_to_all | solution.py:222
  585.9 6.1 all-to-all-start
  592.2 5.4 fusion.7
  597.6 446.7 %all-to-all-done = bf16[8,4,160,2048]{3,2,1,0:T(8,128)(2,1)} async-done(((bf16[8,4,160,2048]{3,2,1,0:T(8,128)(2,1)}), bf16[8,4,160,2048]{3,2,1,0:T(8,128)(2,1)}, u32[]{:S(2)}, u32[]{:S(2)}) %all-to-all-start) | async-done | bytes 20971552 | tf_op jit(solution)/shard_map/all_to_all | solution.py:185
  1044.3 4.5 fusion.18
  1056.6 5.6 convolution_add_fusion
  1062.5 4.5 fusion.10
  1067.0 5.1 fusion.12
  1072.5 5.8 fusion.11
  1080.2 5.6 convolution_add_fusion.3
  1086.1 5.0 fusion.9
  1091.1 4.2 fusion.14
  1095.4 4.8 fusion.13
  1102.1 5.5 convolution_add_fusion.2
  1108.2 4.5 fusion.8
  1112.7 4.2 fusion.16
  1117.0 4.8 fusion.15
  1123.7 5.6 convolution_add_fusion.1
  1129.4 5.8 convolution_convert_fusion.3
  1135.3 5.9 convolution_convert_fusion.2
  1141.3 6.0 convolution_convert_fusion.1
  1147.5 5.5 convolution_convert_fusion
  1155.7 78.4 %reduce-scatter.17.cloned.1.call-done = f32[8,160,512]{2,1,0:T(8,128)} async-done(((f32[8,160,2048]{2,1,0:T(8,128)}), f32[8,160,512]{2,1,0:T(8,128)}) %reduce-scatter.17.cloned.1.call-update) | async-done | bytes 2621456 | tf_op jit(solution)/shard_map/reduce_scatter | solution.py:243
  1237.1 84.8 %reduce-scatter.19.cloned.1.call-done = f32[8,160,512]{2,1,0:T(8,128)} async-done(((f32[8,160,2048]{2,1,0:T(8,128)}), f32[8,160,512]{2,1,0:T(8,128)}) %reduce-scatter.19.cloned.1.call-update) | async-done | bytes 2621456 | tf_op jit(solution)/shard_map/reduce_scatter | solution.py:243
  1324.9 84.8 %reduce-scatter.21.cloned.1.call-done = f32[8,160,512]{2,1,0:T(8,128)} async-done(((f32[8,160,2048]{2,1,0:T(8,128)}), f32[8,160,512]{2,1,0:T(8,128)}) %reduce-scatter.21.cloned.1.call-update) | async-done | bytes 2621456 | tf_op jit(solution)/shard_map/reduce_scatter | solution.py:243
  1415.9 5.6 all-to-all-start.3
  1421.6 115.7 %all-to-all-done.3 = bf16[8,4,160,512]{3,2,1,0:T(8,128)(2,1)} async-done(((bf16[8,4,160,512]{3,2,1,0:T(8,128)(2,1)}), bf16[8,4,160,512]{3,2,1,0:T(8,128)(2,1)}, u32[]{:S(2)}, u32[]{:S(2)}) %all-to-all-start.3) | async-done | bytes 5242912 | tf_op jit(solution)/shard_map/all_to_all | solution.py:245
  1537.3 20.6 %gather_fusion.5 = bf16[4096,512]{1,0:T(8,128)(2,1)} fusion(bf16[5120,512]{1,0:T(8,128)(2,1)} %bitcast.66, s32[4096]{0:T(1024)S(1)} %broadcast_clamp_fusion), kind=kCustom, calls=%fused_computation.5 | custom fusion | bytes 8404992 | tf_op jit(solution)/shard_map/gather | solution.py:250
  1558.0 5.9 convert_reduce_fusion
  1564.1 7.5 reduce-scatter.13.cloned.1.call-done
  1571.6 54.1 %reduce-scatter.15.cloned.1.call-done = bf16[8,160,512]{2,1,0:T(8,128)(2,1)} async-done(((bf16[8,160,2048]{2,1,0:T(8,128)(2,1)}), bf16[8,160,512]{2,1,0:T(8,128)(2,1)}) %reduce-scatter.15.cloned.1.call-update) | async-done | bytes 1310736 | tf_op jit(solution)/shard_map/reduce_scatter | solution.py:201
  1631.9 5.6 all-to-all-start.1
  1637.8 24.3 %all-gather.2.cloned.1.call-done = f32[512,2048]{1,0:T(8,128)} async-done(((f32[512,512]{1,0:T(8,128)}), f32[512,2048]{1,0:T(8,128)}) %all-gather.2.cloned.1.call-update) | async-done | bytes 4194320 | tf_op jit(solution)/shard_map/all_gather | solution.py:252
  1681.9 6.6 all-reduce
  1709.6 50.0 %all-reduce.13.cloned.1.call-done = (bf16[3,512,128]{2,1,0:T(8,128)(2,1)}, bf16[512,2048]{1,0:T(8,128)(2,1)}) async-done(((bf16[3,512,128]{2,1,0:T(8,128)(2,1)}, bf16[512,2048]{1,0:T(8,128)(2,1)}), (bf16[3,512,128]{2,1,0:T(8,128)(2,1)}, bf16[512,2048]{1,0:T(8,128)(2,1)})) %all-reduce.13.cloned.1.call-update) | async-done | bytes 2490384 | tf_op jit(solution)/shard_map/psum | solution.py:327
  1763.7 20.7 %gather_fusion.2 = bf16[4096,512]{1,0:T(8,128)(2,1)} fusion(bf16[5120,512]{1,0:T(8,128)(2,1)} %bitcast.55, s32[4096]{0:T(1024)S(1)} %broadcast_clamp_fusion), kind=kCustom, calls=%fused_computation.2 | custom fusion | bytes 8404992 | tf_op jit(solution)/shard_map/gather | solution.py:212
  1784.4 4.9 fusion.6
  1796.7 84.4 %all-reduce.11.cloned.1.call-done = (bf16[3,2048,128]{1,2,0:T(8,128)(2,1)}, bf16[3,128,512]{2,1,0:T(8,128)(2,1)}, bf16[512,128]{1,0:T(8,128)(2,1)}, bf16[128,2048]{1,0:T(8,128)(2,1)}) async-done(((bf16[3,2048,128]{1,2,0:T(8,128)(2,1)}, bf16[3,128,512]{2,1,0:T(8,128)(2,1)}, bf16[512,128]{1,0:T(8,128)(2,1)}, bf16[128,2048]{1,0:T(8,128)(2,1)}), (bf16[3,2048,128]{1,2,0:T(8,128)(2,1)}, ...) | async-done | bytes 2621456 | tf_op jit(solution)/shard_map/psum | solution.py:351
  (392 shorter events, 146.6 us)
Async XLA Ops:
  7.2 165.5 %copy-start = (bf16[512,2048]{1,0:T(8,128)(2,1)S(1)}, bf16[512,2048]{1,0:T(8,128)(2,1)}, u32[]{:S(2)}) copy-start(bf16[512,2048]{1,0:T(8,128)(2,1)} %param.32) | copy-start | bytes 6291460
  7.2 28.8 %copy-start.95 = (f32[512,8]{0,1:T(8,128)S(1)}, f32[512,8]{0,1:T(8,128)}, u32[]{:S(2)}) copy-start(f32[512,8]{0,1:T(8,128)} %param.41) | copy-start | bytes 49156
  20.4 15.6 copy-start.80
  36.0 29.2 %copy-start.74 = (s32[5120]{0:T(1024)}, s32[5120]{0:T(1024)S(1)}, u32[]{:S(2)}) copy-start(s32[5120]{0:T(1024)S(1)} %get-tuple-element.101) | copy-start | bytes 61444
  36.2 28.9 %copy-start.45 = (f32[512,8]{1,0:T(8,128)}, f32[512,8]{1,0:T(8,128)S(1)}, u32[]{:S(2)}) copy-start(f32[512,8]{1,0:T(8,128)S(1)} %copy.65) | copy-start | bytes 49156
  124.8 7.5 copy-start.2
  124.8 10.4 copy-start.110
  124.8 11.0 copy-start.111
  124.8 11.5 copy-start.112
  124.8 11.7 copy-start.106
  124.8 461.1 %all-to-all-start.2 = ((bf16[8,4,160,2048]{3,2,1,0:T(8,128)(2,1)}), bf16[8,4,160,2048]{3,2,1,0:T(8,128)(2,1)}, u32[]{:S(2)}, u32[]{:S(2)}) async-start(bf16[8,4,160,2048]{3,2,1,0:T(8,128)(2,1)} %fusion.5), calls=%async_computation.6 | async-start | bytes 41943040 | tf_op jit(solution)/shard_map/all_to_all | solution.py:222
  132.2 134.2 %all-reduce.9.cloned.1.call-start = ((), (), s32[]{:S(2)}) async-start(), calls=%async_computation.21 | async-start | bytes 8912896 | tf_op jit(solution)/shard_map/psum | solution.py:162
  134.6 8.3 copy-start.113
  136.5 27.6 %copy-start.84 = (f32[2048]{0:T(1024)}, f32[2048]{0:T(1024)S(1)}, u32[]{:S(2)}) copy-start(f32[2048]{0:T(1024)S(1)} %convert_element_type.242) | copy-start | bytes 24580
  148.7 15.3 copy-start.12
  162.1 8.0 copy-start.24
  172.7 93.8 %copy-start.50 = (bf16[128,2048]{1,0:T(8,128)(2,1)S(1)}, bf16[128,2048]{1,0:T(8,128)(2,1)}, u32[]{:S(2)}) copy-start(bf16[128,2048]{1,0:T(8,128)(2,1)} %param.39) | copy-start | bytes 1572868
  172.7 93.8 %copy-start.104 = (f32[128]{0:T(128)S(1)}, f32[128]{0:T(128)}, u32[]{:S(2)}) copy-start(f32[128]{0:T(128)} %copy-done.103) | copy-start | bytes 1540
  176.0 95.0 %copy-start.76 = (f32[2048]{0:T(1024)}, f32[2048]{0:T(1024)S(1)}, u32[]{:S(2)}) copy-start(f32[2048]{0:T(1024)S(1)} %convert_element_type.261) | copy-start | bytes 24580
  271.0 43.8 %copy-start.89 = (f32[512]{0:T(512)}, f32[512]{0:T(512)S(1)}, u32[]{:S(2)}) copy-start(f32[512]{0:T(512)S(1)} %get-tuple-element.109) | copy-start | bytes 6148
  585.9 458.4 %all-to-all-start = ((bf16[8,4,160,2048]{3,2,1,0:T(8,128)(2,1)}), bf16[8,4,160,2048]{3,2,1,0:T(8,128)(2,1)}, u32[]{:S(2)}, u32[]{:S(2)}) async-start(bf16[8,4,160,2048]{3,2,1,0:T(8,128)(2,1)} %broadcast_select_fusion), calls=%async_computation | async-start | bytes 41943040 | tf_op jit(solution)/shard_map/all_to_all | solution.py:185
  592.0 561.1 %reduce-scatter.23.cloned.1.call-start = ((), (), s32[]{:S(2)}) async-start(), calls=%async_computation.19 | async-start | bytes 13107200 | tf_op jit(solution)/shard_map/reduce_scatter | solution.py:243
  1062.2 171.9 %reduce-scatter.17.cloned.1.call-start = ((), (), s32[]{:S(2)}) async-start(), calls=%async_computation.16 | async-start | bytes 13107200 | tf_op jit(solution)/shard_map/reduce_scatter | solution.py:243
  1072.5 7.7 copy-start.26
  1085.8 236.1 %reduce-scatter.19.cloned.1.call-start = ((), (), s32[]{:S(2)}) async-start(), calls=%async_computation.17 | async-start | bytes 13107200 | tf_op jit(solution)/shard_map/reduce_scatter | solution.py:243
  1107.6 302.1 %reduce-scatter.21.cloned.1.call-start = ((), (), s32[]{:S(2)}) async-start(), calls=%async_computation.18 | async-start | bytes 13107200 | tf_op jit(solution)/shard_map/reduce_scatter | solution.py:243
  1129.3 434.7 %reduce-scatter.9.cloned.1.call-start = ((), (), s32[]{:S(2)}) async-start(), calls=%async_computation.12 | async-start | bytes 6553600 | tf_op jit(solution)/shard_map/reduce_scatter | solution.py:201
  1135.2 428.8 %reduce-scatter.11.cloned.1.call-start = ((), (), s32[]{:S(2)}) async-start(), calls=%async_computation.13 | async-start | bytes 6553600 | tf_op jit(solution)/shard_map/reduce_scatter | solution.py:201
  1141.2 430.3 %reduce-scatter.13.cloned.1.call-start = ((), (), s32[]{:S(2)}) async-start(), calls=%async_computation.14 | async-start | bytes 6553600 | tf_op jit(solution)/shard_map/reduce_scatter | solution.py:201
  1147.3 478.4 %reduce-scatter.15.cloned.1.call-start = ((), (), s32[]{:S(2)}) async-start(), calls=%async_computation.15 | async-start | bytes 6553600 | tf_op jit(solution)/shard_map/reduce_scatter | solution.py:201
  1415.9 121.4 %all-to-all-start.3 = ((bf16[8,4,160,512]{3,2,1,0:T(8,128)(2,1)}), bf16[8,4,160,512]{3,2,1,0:T(8,128)(2,1)}, u32[]{:S(2)}, u32[]{:S(2)}) async-start(bf16[8,4,160,512]{3,2,1,0:T(8,128)(2,1)} %copy.79), calls=%async_computation.11 | async-start | bytes 10485760 | tf_op jit(solution)/shard_map/all_to_all | solution.py:245
  1421.6 240.6 %all-gather.2.cloned.1.call-start = ((), (), s32[]{:S(2)}) async-start(), calls=%async_computation.20 | async-start | bytes 5242880 | tf_op jit(solution)/shard_map/all_gather | solution.py:252
  1564.0 106.9 %copy-start.108 = (bf16[128]{0:T(256)(128)(2,1)}, bf16[128]{0:T(256)(128)(2,1)S(1)}, u32[]{:S(2)}) copy-start(bf16[128]{0:T(256)(128)(2,1)S(1)} %convert_element_type.294) | copy-start | bytes 772
  1631.9 30.3 %copy-start.77 = (f32[2048]{0:T(1024)S(1)}, f32[2048]{0:T(1024)}, u32[]{:S(2)}) copy-start(f32[2048]{0:T(1024)} %copy-done.76) | copy-start | bytes 24580
  1631.9 131.7 %all-to-all-start.1 = ((bf16[8,4,160,512]{3,2,1,0:T(8,128)(2,1)}), bf16[8,4,160,512]{3,2,1,0:T(8,128)(2,1)}, u32[]{:S(2)}, u32[]{:S(2)}) async-start(bf16[8,4,160,512]{3,2,1,0:T(8,128)(2,1)} %copy.73), calls=%async_computation.5 | async-start | bytes 10485760 | tf_op jit(solution)/shard_map/all_to_all | solution.py:208
  1637.6 28.7 %copy-start.90 = (f32[512]{0:T(512)S(1)}, f32[512]{0:T(512)}, u32[]{:S(2)}) copy-start(f32[512]{0:T(512)} %copy-done.89) | copy-start | bytes 6148
  1637.6 28.7 %copy-start.100 = (f32[512]{0:T(512)S(1)}, f32[512]{0:T(512)}, u32[]{:S(2)}) copy-start(f32[512]{0:T(512)} %get-tuple-element.108) | copy-start | bytes 6148
  1637.6 122.0 %all-reduce.13.cloned.1.call-start = ((), (), s32[]{:S(2)}) async-start(), calls=%async_computation.23 | async-start | bytes 4980736 | tf_op jit(solution)/shard_map/psum | solution.py:327
  1681.9 10.6 copy-start.94
  1681.9 10.6 copy-start.102
  1700.4 180.7 %all-reduce.11.cloned.1.call-start = ((), (), s32[]{:S(2)}) async-start(), calls=%async_computation.22 | async-start | bytes 5242880 | tf_op jit(solution)/shard_map/psum | solution.py:351
  1702.5 57.2 %copy-start.85 = (f32[2048]{0:T(1024)S(1)}, f32[2048]{0:T(1024)}, u32[]{:S(2)}) copy-start(f32[2048]{0:T(1024)} %copy-done.84) | copy-start | bytes 24580
  1702.5 57.1 %copy-start.99 = (f32[512]{0:T(512)S(1)}, f32[512]{0:T(512)}, u32[]{:S(2)}) copy-start(f32[512]{0:T(512)} %copy-done.97) | copy-start | bytes 6148
  1702.5 57.1 %copy-start.109 = (bf16[128]{0:T(256)(128)(2,1)S(1)}, bf16[128]{0:T(256)(128)(2,1)}, u32[]{:S(2)}) copy-start(bf16[128]{0:T(256)(128)(2,1)} %copy-done.108) | copy-start | bytes 772
  1763.7 20.7 %copy-start.46 = (f32[512,8]{1,0:T(8,128)S(1)}, f32[512,8]{1,0:T(8,128)}, u32[]{:S(2)}) copy-start(f32[512,8]{1,0:T(8,128)} %copy-done.45) | copy-start | bytes 49156
  1784.3 7.2 copy-start.11
  1784.3 7.2 copy-start.49
  1784.3 7.2 copy-start.59
  (82 other events, 273.4 us)
Sparse Core Ops, SparseCore 0:
  176.1 90.2 all-reduce.8
  1062.3 83.8 reduce-scatter.22
  1148.8 85.2 reduce-scatter.16
  1236.6 85.2 reduce-scatter.18
  1324.4 85.2 reduce-scatter.20
  1412.1 51.3 reduce-scatter.8
  1466.2 51.3 reduce-scatter.10
  1520.1 51.3 reduce-scatter.12
  1574.3 51.3 reduce-scatter.14
  1627.7 34.4 all-gather.1
  1700.5 59.0 all-reduce.12
  1764.0 117.0 all-reduce.10
where the time goes:
time: 1910 us; the launch traced here: 1900 us
  waiting for transfers between devices  1380 us (72%)
  local copies, waits for them, and re-layouts  190 us (10%)
  matrix products  163 us (9%)
  other arithmetic  110 us (6%)
  starting transfers between devices  27 us (1%)
    all_to_all x1, waiting for transfers between devices, body(): lax.all_to_all(outgoing, 'expert', split_axis=0, concat_axis=0, tiled=True)  447 us
    all_to_all x1, waiting for transfers between devices, body(): lax.all_to_all(grad_slots, 'expert', split_axis=0, concat_axis=0, tiled=T...  253 us
    reduce_scatter x4, waiting for transfers between devices, body(): lax.psum_scatter(row_grad, 'tensor', scatter_dimension=2, tiled=True)  248 us
    all_to_all x1, waiting for transfers between devices, body(): lax.all_to_all(jnp.stack(pieces, axis=1), 'expert', split_axis=0, concat_...  116 us
    psum x1, waiting for transfers between devices, body(): branch, mixing = lax.psum((output_part, mixing_part), 'tensor')  90.4 us
    psum x1, waiting for transfers between devices, body(): lax.psum(grad_adapt_in.astype(jnp.bfloat16), 'expert').astype(jnp.float32)  84.4 us
    reduce_scatter x4, waiting for transfers between devices, body(): lax.psum_scatter(partial_rows.astype(jnp.bfloat16), 'tensor', scatter_dim...  61.7 us
    psum x1, waiting for transfers between devices, body(): lax.psum(lowrank_part.astype(jnp.bfloat16), 'tensor').astype(jnp.float32)  50 us
  transfers between devices with their start and end apart: 16, of which 12 were waited for; matrix products, arithmetic and copies ran while one was open for 16% of the time, Pallas kernels for 0%

commit v1 on v0

v1 whole, which is shorter than its diff:
```python
import jax
import jax.numpy as jnp
from jax import lax
from jax.sharding import PartitionSpec as P

HD = 128
RANK = 16


EPSILON = 1e-05
ROPE_BASE = 10000.0
MASKED_SCORE = -1e30


def ancestry(parents):
    blocks = parents.shape[1]
    places = jnp.arange(blocks, dtype=jnp.int32)
    current = places[None, :]

    def climb(climb_step, climb_state):
        walker, reached = climb_state
        walker = jnp.take_along_axis(parents, walker, axis=1)
        return (walker, reached | (walker[:, :, None] == places[None, None, :]))

    initial = (current, current[:, :, None] == places[None, None, :])
    return lax.fori_loop(0, blocks - 1, climb, initial)[1]


def rope_tables(reached, block_span, head_size):
    depths = jnp.sum(reached.astype(jnp.int32), axis=2) - 1
    offsets = jnp.arange(block_span, dtype=jnp.int32)
    located = (
        (depths[:, :, None] * block_span + offsets[None, None, :]).reshape(-1).astype(jnp.float32)
    )
    halves = head_size // 2
    speeds = ROPE_BASE ** (-2.0 * jnp.arange(halves, dtype=jnp.float32) / head_size)
    angles = located[:, None] * speeds[None, :]
    angles = jnp.concatenate([angles, angles], axis=1)
    return (jnp.cos(angles), jnp.sin(angles))


def rotate(values, cosine_table, sine_table):
    halves = values.shape[-1] // 2
    turned = jnp.concatenate([-values[..., halves:], values[..., :halves]], axis=-1)
    return values * cosine_table[:, None, :] + turned * sine_table[:, None, :]


def unrotate(values, cosine_table, sine_table):
    halves = values.shape[-1] // 2
    sined = values * sine_table[:, None, :]
    return values * cosine_table[:, None, :] + jnp.concatenate(
        [sined[..., halves:], -sined[..., :halves]], axis=-1
    )


def token_mask(reached, total_size):
    blocks = reached.shape[0]
    block_span = total_size // blocks
    widened = jnp.broadcast_to(
        reached[:, None, :, None], (blocks, block_span, blocks, block_span)
    ).reshape(total_size, total_size)
    positions = jnp.arange(total_size, dtype=jnp.int32)
    return widened & (positions[None, :] <= positions[:, None])


def norm_back(scaled_grad, values, inverse, model_width, inner_sum):
    return inverse * scaled_grad - values * inverse**3 * (inner_sum / model_width)


def divide_axes(owners, tensor_count):
    outer = 4
    return {
        "z": ("expert", outer, owners // outer, owners),
        "x": ("expert", owners // outer, 1, owners),
        "y": ("tensor", tensor_count // 2, 2, tensor_count),
        "c": ("tensor", 2, 1, tensor_count),
    }


def turn(array, axes, name, step):
    axis, length, stride, total = axes[name]
    pairs = []
    for index in range(total):
        place = (index // stride) % length
        moved = index + ((place + step) % length - place) * stride
        pairs.append((index, moved))
    return lax.ppermute(array, axis, pairs)


def ring_gather(array, axes, name):
    held = [array]
    for _ in range(axes[name][1] - 1):
        held.append(turn(held[-1], axes, name, 1))
    return jnp.concatenate(held, axis=0)


def add_low(left, right):
    return (left.astype(jnp.float32) + right.astype(jnp.float32)).astype(jnp.bfloat16)


def ring_scatter(array, axes, name):
    length = axes[name][1]
    parts = jnp.split(array, length, axis=0)
    total = parts[-1]
    for index in range(length - 2, -1, -1):
        total = add_low(turn(total, axes, name, -1), parts[index])
    return total


def gather_plane(rows, axes):
    half = rows.shape[0] // 2
    first = ring_gather(ring_gather(rows[:half], axes, "x"), axes, "y")
    second = ring_gather(ring_gather(rows[half:], axes, "y"), axes, "x")
    return ring_gather(jnp.concatenate([first, second], axis=0), axes, "c")


def scatter_plane(rows, axes):
    rows = ring_scatter(rows, axes, "c")
    half = rows.shape[0] // 2
    first = ring_scatter(ring_scatter(rows[:half], axes, "y"), axes, "x")
    second = ring_scatter(ring_scatter(rows[half:], axes, "x"), axes, "y")
    return jnp.concatenate([first, second], axis=0)


def gather_all(rows, axes):
    planes = [rows]
    for _ in range(axes["z"][1] - 1):
        planes.append(turn(planes[-1], axes, "z", 1))
    return [gather_plane(plane, axes) for plane in planes]


def place_tensor(rows, axes, kind):
    rank = lax.axis_index("tensor")
    count = lax.axis_size("tensor")
    size = rows.shape[0]
    span = axes["y"][1]
    held = [rows]
    for _ in range(span - 1):
        held.append(turn(held[-1], axes, "y", 1))
    other = [turn(piece, axes, "c", 1) for piece in held]
    whole = jnp.zeros((count * size, rows.shape[1]), kind)
    core = rank % 2
    for step in range(span):
        level = (rank // 2 + span - step) % span
        whole = lax.dynamic_update_slice_in_dim(
            whole, held[step].astype(kind), (level * 2 + core) * size, 0
        )
        whole = lax.dynamic_update_slice_in_dim(
            whole, other[step].astype(kind), (level * 2 + 1 - core) * size, 0
        )
    return whole


def scatter_tensor(rows, axes):
    rank = lax.axis_index("tensor")
    count = lax.axis_size("tensor")
    size = rows.shape[0] // count
    span = axes["y"][1]
    blocks = rows.reshape(span, 2, size, rows.shape[1])
    core = rank % 2
    mine = lax.dynamic_index_in_dim(blocks, core, 1, keepdims=False)
    theirs = lax.dynamic_index_in_dim(blocks, 1 - core, 1, keepdims=False)
    mine = add_low(mine, turn(theirs, axes, "c", 1))
    total = None
    for step in range(span - 1, -1, -1):
        level = (rank // 2 + span - step) % span
        part = lax.dynamic_index_in_dim(mine, level, 0, keepdims=False)
        total = part if total is None else add_low(turn(total, axes, "y", -1), part)
    return total


def swap_columns(rows, axes):
    rank = lax.axis_index("tensor")
    count = lax.axis_size("tensor")
    size, width = rows.shape
    span = axes["y"][1]
    share = width // count
    level, core = rank // 2, rank % 2
    whole = jnp.zeros((count * size, share), rows.dtype)
    for step in range(span):
        toward = (level + step) % span
        piece = lax.dynamic_slice_in_dim(rows, toward * 2 * share, 2 * share, 1)
        if step:
            piece = turn(piece, axes, "y", step)
        mine = lax.dynamic_slice_in_dim(piece, core * share, share, 1)
        theirs = lax.dynamic_slice_in_dim(piece, (1 - core) * share, share, 1)
        theirs = turn(theirs, axes, "c", 1)
        source = (level + span - step) % span
        whole = lax.dynamic_update_slice_in_dim(whole, mine, (source * 2 + core) * size, 0)
        whole = lax.dynamic_update_slice_in_dim(whole, theirs, (source * 2 + 1 - core) * size, 0)
    return whole


def sum_tensor(array, axes):
    total = add_low(array, turn(array, axes, "c", 1))
    moving = total
    result = total.astype(jnp.float32)
    for _ in range(axes["y"][1] - 1):
        moving = turn(moving, axes, "y", 1)
        result = result + moving.astype(jnp.float32)
    return result


def body(
    tokens,
    cotangent,
    attn_gain,
    ffn_gain,
    query_gain,
    key_gain,
    query_weight,
    key_weight,
    value_weight,
    output_weight,
    expert_gate,
    expert_up,
    expert_down,
    adapt_in,
    adapt_out,
    adapt_in_out,
    adapt_out_out,
    routes,
    gate_weights,
    block_parent,
    adapter_pick,
):
    rows_here, model_width = tokens.shape
    local_width = query_weight.shape[1]
    heads_here = local_width // HD
    tensor_rank = lax.axis_index("tensor")
    tensor_count = lax.axis_size("tensor")
    owners = lax.axis_size("expert")
    owner_rank = lax.axis_index("expert")
    axes = divide_axes(owners, tensor_count)
    experts_here, _, hidden_here = expert_gate.shape
    experts_all = experts_here * owners
    column_share = model_width // tensor_count
    row_share = rows_here // tensor_count
    float_kind = jnp.float32
    half_kind = jnp.bfloat16

    def own_rows(array):
        return lax.dynamic_slice_in_dim(array, tensor_rank * row_share, row_share, 0)

    def matmul(left, right):
        return jnp.dot(left, right, preferred_element_type=float_kind)

    def matmul_t(left, right):
        return lax.dot_general(
            left, right, (((1,), (1,)), ((), ())), preferred_element_type=float_kind
        )

    def t_matmul(left, right):
        return lax.dot_general(
            left, right, (((0,), (0,)), ((), ())), preferred_element_type=float_kind
        )

    cotangent_rows = own_rows(cotangent)
    routes_rows = own_rows(routes)
    weights_rows = own_rows(gate_weights)
    route_weights = jnp.sum(
        jnp.where(
            routes_rows[:, :, None] == jnp.arange(experts_all, dtype=jnp.int32)[None, None, :],
            weights_rows[:, :, None],
            0.0,
        ),
        axis=1,
    )
    weights_high = route_weights.astype(half_kind)
    weights_low = (route_weights - weights_high.astype(float_kind)).astype(half_kind)
    side_width = -(-2 * experts_all // 128) * 128
    side_pad = jnp.zeros((row_share, side_width - 2 * experts_all), half_kind)
    cotangent_sent = jnp.concatenate(
        [cotangent_rows, weights_high, weights_low, side_pad], axis=1
    )
    cotangent_planes = gather_all(cotangent_sent, axes)
    side_index = jnp.arange(side_width, dtype=jnp.int32)
    hidden_owner = owner_rank * experts_here + jnp.arange(
        experts_here * hidden_here, dtype=jnp.int32
    ) // hidden_here
    spread = (
        (side_index[:, None] % experts_all == hidden_owner[None, :])
        & (side_index[:, None] < 2 * experts_all)
    ).astype(half_kind)
    gate_wide = jnp.swapaxes(expert_gate, 0, 1).reshape(model_width, -1)
    up_wide = jnp.swapaxes(expert_up, 0, 1).reshape(model_width, -1)
    down_tall = expert_down.reshape(-1, model_width)

    inputs = tokens.astype(float_kind)
    first_gain = attn_gain.astype(float_kind)
    second_gain = ffn_gain.astype(float_kind)
    first_inverse = lax.rsqrt(jnp.mean(inputs * inputs, axis=1, keepdims=True) + EPSILON)
    normed_in = (inputs * first_inverse * first_gain).astype(half_kind)
    reached = ancestry(block_parent.reshape(1, -1))
    cosine_table, sine_table = rope_tables(reached, rows_here // block_parent.shape[0], HD)
    key_mask = token_mask(reached[0], rows_here)
    picked = jnp.argmax(adapter_pick[0]) * RANK
    adapt_in_used = lax.dynamic_slice_in_dim(adapt_in, picked, RANK, 2)
    adapt_out_used = lax.dynamic_slice_in_dim(adapt_out, picked, RANK, 1)
    mix_in_used = lax.dynamic_slice_in_dim(adapt_in_out, picked, RANK, 1)
    mix_out_used = lax.dynamic_slice_in_dim(adapt_out_out, picked, RANK, 0)
    picks = lax.all_gather(adapter_pick.astype(float_kind), "expert", axis=0, tiled=True)
    lowrank = jnp.einsum(
        "td,idr->itr", normed_in, adapt_in_used, preferred_element_type=float_kind
    ).astype(half_kind)
    matrices = (query_weight, key_weight, value_weight)
    raw_list = [
        matmul(normed_in, matrices[projection])
        + matmul(lowrank[projection], adapt_out_used[projection])
        for projection in range(3)
    ]
    query_raw, key_raw, value_raw = raw_list
    query_squares, key_squares = lax.psum(
        (jnp.sum(query_raw * query_raw, axis=1), jnp.sum(key_raw * key_raw, axis=1)), "tensor"
    )
    query_inverse = lax.rsqrt(query_squares / model_width + EPSILON)[:, None]
    key_inverse = lax.rsqrt(key_squares / model_width + EPSILON)[:, None]
    query_scale = query_gain.astype(float_kind)
    key_scale = key_gain.astype(float_kind)
    queries = rotate(
        (query_raw * query_inverse * query_scale).reshape(rows_here, heads_here, HD),
        cosine_table,
        sine_table,
    ).astype(half_kind)
    keys = rotate(
        (key_raw * key_inverse * key_scale).reshape(rows_here, heads_here, HD),
        cosine_table,
        sine_table,
    ).astype(half_kind)
    values = value_raw.astype(half_kind).reshape(rows_here, heads_here, HD)
    score_scale = HD ** (-0.5)
    scores = (
        jnp.einsum("qhd,khd->hqk", queries, keys, preferred_element_type=float_kind) * score_scale
    )
    scores = jnp.where(key_mask[None], scores, MASKED_SCORE)
    row_max = jnp.max(scores, axis=2, keepdims=True)
    raised = jnp.exp(scores - row_max)
    row_total = jnp.sum(raised, axis=2, keepdims=True)
    weights_half = (raised / row_total).astype(half_kind)
    log_total = row_max + jnp.log(row_total)
    attended = (
        jnp.einsum("hqk,khd->qhd", weights_half, values, preferred_element_type=float_kind)
        .reshape(rows_here, local_width)
        .astype(half_kind)
    )
    output_part = matmul(attended, output_weight).astype(half_kind)
    mixing_part = matmul(attended, mix_in_used).astype(half_kind)
    mixing_pad = jnp.zeros((rows_here, 128 - RANK), half_kind)
    branch_rows = scatter_tensor(
        jnp.concatenate([output_part, mixing_part, mixing_pad], axis=1), axes
    )
    mixed_rows = branch_rows[:, model_width : model_width + RANK]
    resid_rows = (
        own_rows(tokens).astype(float_kind)
        + branch_rows[:, :model_width].astype(float_kind)
        + matmul(mixed_rows, mix_out_used)
    )
    second_inverse = lax.rsqrt(
        jnp.mean(resid_rows * resid_rows, axis=1, keepdims=True) + EPSILON
    )
    normed_rows = (resid_rows * second_inverse * second_gain).astype(half_kind)
    normed_planes = gather_all(normed_rows, axes)

    kept_states = []
    for plane, beside in zip(normed_planes, cotangent_planes):
        gate_value = matmul(plane, gate_wide)
        up_value = matmul(plane, up_wide)
        sigmoid_gate = jax.nn.sigmoid(gate_value)
        weight_wide = matmul(beside[:, model_width:], spread)
        hidden_grad = matmul_t(beside[:, :model_width], down_tall) * weight_wide
        gate_grad = (
            hidden_grad * up_value * sigmoid_gate * (1.0 + gate_value * (1.0 - sigmoid_gate))
        ).astype(half_kind)
        up_grad = (hidden_grad * gate_value * sigmoid_gate).astype(half_kind)
        hidden = (gate_value * sigmoid_gate * up_value * weight_wide).astype(half_kind)
        kept_states.append((gate_grad, up_grad, hidden))
    total = None
    for gate_grad, up_grad, _ in reversed(kept_states):
        part = (matmul_t(gate_grad, gate_wide) + matmul_t(up_grad, up_wide)).astype(half_kind)
        part = scatter_plane(part, axes)
        total = part if total is None else add_low(turn(total, axes, "z", -1), part)
    ffn_rows_grad = total.astype(float_kind)
    total = None
    for _, _, hidden in reversed(kept_states):
        part = scatter_plane(matmul(hidden, down_tall).astype(half_kind), axes)
        total = part if total is None else add_low(turn(total, axes, "z", -1), part)
    layer_rows = (resid_rows + total.astype(float_kind)).astype(half_kind)
    layer_out = swap_columns(layer_rows, axes)

    second_scaled = ffn_rows_grad * second_gain
    resid_grad_rows = cotangent_rows.astype(float_kind) + norm_back(
        second_scaled,
        resid_rows,
        second_inverse,
        model_width,
        jnp.sum(second_scaled * resid_rows, axis=1, keepdims=True),
    )
    branch_sent = jnp.concatenate(
        [resid_grad_rows.astype(half_kind), mixed_rows, jnp.zeros((row_share, 128 - RANK), half_kind)],
        axis=1,
    )
    branch_whole = place_tensor(branch_sent, axes, half_kind)
    branch_grad = branch_whole[:, :model_width]
    mixed = branch_whole[:, model_width : model_width + RANK]
    mixed_grad = matmul_t(branch_grad, mix_out_used).astype(half_kind)
    attended_grad = (
        matmul_t(branch_grad, output_weight) + matmul_t(mixed_grad, mix_in_used)
    ).astype(half_kind)
    attended_grad = attended_grad.reshape(rows_here, heads_here, HD)
    scores = (
        jnp.einsum("qhd,khd->hqk", queries, keys, preferred_element_type=float_kind) * score_scale
    )
    softmax_full = jnp.where(key_mask[None], jnp.exp(scores - log_total), 0.0)
    softmax_half = softmax_full.astype(half_kind)
    value_grad = jnp.einsum(
        "hqk,qhd->khd", softmax_half, attended_grad, preferred_element_type=float_kind
    ).astype(half_kind)
    prob_grad = jnp.einsum("qhd,khd->hqk", attended_grad, values, preferred_element_type=float_kind)
    score_grad = (
        softmax_full * (prob_grad - jnp.sum(softmax_full * prob_grad, axis=2, keepdims=True))
    ).astype(half_kind)
    query_grad = (
        jnp.einsum("hqk,khd->qhd", score_grad, keys, preferred_element_type=float_kind)
        * score_scale
    )
    key_grad = (
        jnp.einsum("hqk,qhd->khd", score_grad, queries, preferred_element_type=float_kind)
        * score_scale
    )
    query_scaled = (
        unrotate(query_grad, cosine_table, sine_table).reshape(rows_here, local_width) * query_scale
    )
    key_scaled = (
        unrotate(key_grad, cosine_table, sine_table).reshape(rows_here, local_width) * key_scale
    )
    query_inner, key_inner = lax.psum(
        (jnp.sum(query_scaled * query_raw, axis=1), jnp.sum(key_scaled * key_raw, axis=1)), "tensor"
    )
    query_raw_grad = norm_back(
        query_scaled, query_raw, query_inverse, model_width, query_inner[:, None]
    ).astype(half_kind)
    key_raw_grad = norm_back(
        key_scaled, key_raw, key_inverse, model_width, key_inner[:, None]
    ).astype(half_kind)
    value_raw_grad = value_grad.reshape(rows_here, local_width)
    raw_grads = (query_raw_grad, key_raw_grad, value_raw_grad)
    lowrank_part = jnp.concatenate(
        [matmul_t(raw_grads[projection], adapt_out_used[projection]) for projection in range(3)],
        axis=1,
    )
    lowrank_grad = sum_tensor(lowrank_part.astype(half_kind), axes).astype(half_kind)
    normed_part = (
        matmul_t(query_raw_grad, query_weight)
        + matmul_t(key_raw_grad, key_weight)
        + matmul_t(value_raw_grad, value_weight)
    )
    normed_grad_rows = scatter_tensor(normed_part.astype(half_kind), axes).astype(float_kind)
    lowrank_rows = own_rows(lowrank_grad)
    for projection in range(3):
        normed_grad_rows = normed_grad_rows + matmul_t(
            lowrank_rows[:, projection * RANK : (projection + 1) * RANK], adapt_in_used[projection]
        )
    first_scaled = normed_grad_rows * first_gain
    inputs_rows = own_rows(inputs)
    input_grad_rows = resid_grad_rows + norm_back(
        first_scaled,
        inputs_rows,
        own_rows(first_inverse),
        model_width,
        jnp.sum(first_scaled * inputs_rows, axis=1, keepdims=True),
    )
    input_grad = place_tensor(input_grad_rows.astype(half_kind), axes, float_kind)

    normed_share = lax.dynamic_slice_in_dim(
        normed_in, tensor_rank * column_share, column_share, 1
    )
    branch_share = lax.dynamic_slice_in_dim(
        branch_grad, tensor_rank * column_share, column_share, 1
    )
    compact = jnp.concatenate(
        [t_matmul(lowrank_grad, normed_share), t_matmul(mixed, branch_share)]
        + [t_matmul(lowrank[projection], raw_grads[projection]) for projection in range(3)]
        + [t_matmul(mixed_grad, attended)],
        axis=0,
    ).astype(half_kind)
    kinds = compact.shape[0] // RANK
    trees = ring_gather(ring_gather(compact, axes, "x"), axes, "z")
    far, near = axes["z"][1], axes["x"][1]
    tree_index = (
        (owner_rank // near + far - jnp.arange(far, dtype=jnp.int32)[:, None]) % far * near
        + (owner_rank % near + near - jnp.arange(near, dtype=jnp.int32)[None, :]) % near
    ).reshape(-1)
    tree_picks = matmul(
        (tree_index[:, None] == jnp.arange(owners, dtype=jnp.int32)[None, :]).astype(float_kind),
        picks,
    ).astype(half_kind)
    trees = trees.reshape(owners, kinds, RANK, column_share)
    grad_adapt_out = jnp.einsum(
        "sa,skrc->karc", tree_picks, trees[:, 4:7], preferred_element_type=float_kind
    ).reshape(3, -1, column_share)
    grad_adapt_in_out = jnp.einsum(
        "sa,src->car", tree_picks, trees[:, 7], preferred_element_type=float_kind
    ).reshape(column_share, -1)
    shared = place_tensor(
        trees[:, :4].reshape(owners * 4 * RANK, column_share), axes, half_kind
    ).reshape(tensor_count, owners, 4, RANK, column_share)
    grad_adapt_in = jnp.einsum(
        "sa,tskrc->ktcar", tree_picks, shared[:, :, :3], preferred_element_type=float_kind
    ).reshape(3, model_width, -1)
    grad_adapt_out_out = jnp.einsum(
        "sa,tsrc->artc", tree_picks, shared[:, :, 3], preferred_element_type=float_kind
    ).reshape(-1, model_width)
    return (
        layer_out,
        input_grad,
        grad_adapt_in,
        grad_adapt_out,
        grad_adapt_in_out,
        grad_adapt_out_out,
    )


def solution(mesh):
    return jax.shard_map(
        body,
        mesh=mesh,
        in_specs=(
            P("expert", None),
            P("expert", None),
            P(),
            P(),
            P("tensor"),
            P("tensor"),
            P(None, "tensor"),
            P(None, "tensor"),
            P(None, "tensor"),
            P("tensor", None),
            P("expert", None, "tensor"),
            P("expert", None, "tensor"),
            P("expert", "tensor", None),
            P(),
            P(None, None, "tensor"),
            P("tensor", None),
            P(),
            P("expert", None),
            P("expert", None),
            P("expert"),
            P("expert", None),
        ),
        out_specs=(
            P("expert", "tensor"),
            P("expert", None),
            P(),
            P(None, None, "tensor"),
            P("tensor", None),
            P(),
        ),
        check_vma=False,
    )
```

time: 1910 us -> 959 us (0.50)
  waiting for transfers between devices: 1380 us -> 352 us
  matrix products: 163 us -> 255 us
  starting transfers between devices: 27 us -> 88.5 us
  other arithmetic: 110 us -> 56.5 us
  local copies, waits for them, and re-layouts: 190 us -> 155 us
  blocking collectives: 15 us -> 39.9 us
    all_to_all x4 -> x0, waiting for transfers between devices: 816 us -> none  [the longest x1 447 us: body(): lax.all_to_all(outgoing, 'expert', split_axis=0, concat_axis=0, tiled=True)]
    ppermute x0 -> x114, waiting for transfers between devices: none -> 352 us  [turn(): return lax.ppermute(array, axis, pairs)]
    reduce_scatter x8 -> x0, waiting for transfers between devices: 310 us -> none  [the longest x4 248 us: body(): lax.psum_scatter(row_grad, 'tensor', scatter_dimension=2, tiled=True)]
    psum x3 -> x0, waiting for transfers between devices: 225 us -> none  [the longest x1 90.4 us: body(): branch, mixing = lax.psum((output_part, mixing_part), 'tensor')]
    gather x5 -> x0, local copies, waits for them, and re-layouts: 151 us -> none  [the longest x1 40.7 us: body(): cotangent[source_token].astype(float_kind)]
    dot_general x52 -> x63, matrix products: 159 us -> 251 us  [the longest x24 130 us: matmul_t(): lax.dot_general(left, right, (((1,), (1,)), ((), ())), preferred_element_...]
    ppermute x0 -> x114, starting transfers between devices: none -> 88.5 us  [turn(): return lax.ppermute(array, axis, pairs)]
    unnamed x231 -> x299, local copies, waits for them, and re-layouts: 12.7 us -> 79.9 us
  transfers between devices with their start and end apart: 16 -> 114, of which waited for: 12 -> 57; matrix products, arithmetic and copies ran while one was open for 16% -> 41% of each run, Pallas kernels for 0% -> 0%
where the time goes in v1:
time: 959 us; the launch traced here: 951 us
  waiting for transfers between devices  352 us (37%)
  matrix products  255 us (27%)
  local copies, waits for them, and re-layouts  155 us (16%)
  starting transfers between devices  88.5 us (9%)
  other arithmetic  56.5 us (6%)
  blocking collectives  39.9 us (4%)
    ppermute x114, waiting for transfers between devices, turn(): return lax.ppermute(array, axis, pairs)  352 us
    dot_general x24, matrix products, matmul_t(): lax.dot_general(left, right, (((1,), (1,)), ((), ())), preferred_element_...  130 us
    dot_general x26, matrix products, matmul(): return jnp.dot(left, right, preferred_element_type=float_kind)  107 us
    ppermute x114, starting transfers between devices, turn(): return lax.ppermute(array, axis, pairs)  88.5 us
    unnamed x299, local copies, waits for them, and re-layouts  79.9 us
    convert_element_type x40, other arithmetic, add_low(): (left.astype(jnp.float32) + right.astype(jnp.float32)).astype(jnp.bfloat16)  25.3 us
    all_gather x1, blocking collectives, body(): lax.all_gather(adapter_pick.astype(float_kind), 'expert', axis=0, tiled=T...  24.7 us
  transfers between devices with their start and end apart: 114, of which 57 were waited for; matrix products, arithmetic and copies ran while one was open for 41% of the time, Pallas kernels for 0%

profile of v1, /device:TPU:0, one launch (start us, length us, event | category | flops | bytes accessed | tf_op | source)
XLA Modules:
  0.0 951.1 jit_solution(8049125755133046176)
XLA Ops:
  29.0 8.5 all-reduce.1
  64.5 24.7 %all-gather = f32[8,1,8]{2,1,0:T(1,128)S(1)} all-gather(f32[1,1,8]{2,1,0:T(1,128)S(1)} %convert_bitcast_fusion), channel_id=1, replica_groups=mesh['expert'=8,'tensor'=4] {'expert'}, dimensions={0}, use_global_device_ids=true | all-gather | bytes 288 | tf_op jit(solution)/shard_map/all_gather | solution.py:302
  96.3 6.3 copy.148
  106.9 8.9 collective-permute-done.62
  130.0 9.7 %collective-permute-done.29 = bf16[64,2176]{1,0:T(8,128)(2,1)S(1)} collective-permute-done((bf16[64,2176]{1,0:T(8,128)(2,1)S(1)}, bf16[64,2176]{1,0:T(8,128)(2,1)S(1)}, u32[]{:S(2)}, u32[]{:S(2)}) %collective-permute-start.29) | collective-permute-done | bytes 278560 | tf_op jit(solution)/shard_map/ppermute | solution.py:87
  144.3 6.6 collective-permute-done.1
  156.1 7.5 collective-permute-done.47
  179.1 17.0 %collective-permute-done.31 = bf16[64,2176]{1,0:T(8,128)(2,1)S(1)} collective-permute-done((bf16[64,2176]{1,0:T(8,128)(2,1)S(1)}, bf16[64,2176]{1,0:T(8,128)(2,1)S(1)}, u32[]{:S(2)}, u32[]{:S(2)}) %collective-permute-start.31) | collective-permute-done | bytes 278560 | tf_op jit(solution)/shard_map/ppermute | solution.py:87
  205.6 6.5 collective-permute-done.58
  215.0 16.6 %collective-permute-done.15 = bf16[64,2176]{1,0:T(8,128)(2,1)S(1)} collective-permute-done((bf16[64,2176]{1,0:T(8,128)(2,1)S(1)}, bf16[64,2176]{1,0:T(8,128)(2,1)S(1)}, u32[]{:S(2)}, u32[]{:S(2)}) %collective-permute-start.15) | collective-permute-done | bytes 278560 | tf_op jit(solution)/shard_map/ppermute | solution.py:87
  235.3 14.5 %collective-permute-done.24 = bf16[64,2048]{1,0:T(8,128)(2,1)S(1)} collective-permute-done((bf16[64,2048]{1,0:T(8,128)(2,1)S(1)}, bf16[64,2048]{1,0:T(8,128)(2,1)S(1)}, u32[]{:S(2)}, u32[]{:S(2)}) %collective-permute-start.24) | collective-permute-done | bytes 262176 | tf_op jit(solution)/shard_map/ppermute | solution.py:87
  254.9 11.5 %collective-permute-done.4 = bf16[128,2048]{1,0:T(8,128)(2,1)S(1)} collective-permute-done((bf16[128,2048]{1,0:T(8,128)(2,1)S(1)}, bf16[128,2048]{1,0:T(8,128)(2,1)S(1)}, u32[]{:S(2)}, u32[]{:S(2)}) %collective-permute-start.4) | collective-permute-done | bytes 524320 | tf_op jit(solution)/shard_map/ppermute | solution.py:87
  276.6 10.6 %collective-permute-done.25 = bf16[128,2048]{1,0:T(8,128)(2,1)S(1)} collective-permute-done((bf16[128,2048]{1,0:T(8,128)(2,1)S(1)}, bf16[128,2048]{1,0:T(8,128)(2,1)S(1)}, u32[]{:S(2)}, u32[]{:S(2)}) %collective-permute-start.25) | collective-permute-done | bytes 524320 | tf_op jit(solution)/shard_map/ppermute | solution.py:87
  292.1 8.7 collective-permute-done.43
  305.7 8.3 fusion.25
  330.2 10.3 %fusion.22 = f32[1024,1024]{1,0:T(8,128)} fusion(f32[1024,1024]{1,0:T(8,128)S(1)} %fusion.84, bf16[1024,2048]{1,0:T(8,128)(2,1)} %bitcast.312, bf16[1024,2176]{1,0:T(8,128)(2,1)S(1)} %constant_dynamic-update-slice_fusion.71), kind=kOutput, calls=%fused_computation.67 | convolution fusion | flops 4296015872 | bytes 16777216 | tf_op jit(solution)/shard_map/dot_general | solution.py:249
  355.3 6.9 fusion.183
  369.0 8.0 fusion.33
  377.0 9.8 %add_convert_fusion = bf16[1024,2048]{1,0:T(8,128)(2,1)S(1)} fusion(f32[1024,2048]{1,0:T(8,128)} %fusion.33, bf16[2048,1024]{0,1:T(8,128)(2,1)S(1)} %bitcast.278, f32[1024,1024]{1,0:T(8,128)} %fusion.25, f32[1024,1024]{1,0:T(8,128)} %copy-done.110), kind=kOutput, calls=%fused_computation.8 | convolution fusion | flops 4305453056 | bytes 25165824 | tf_op jit(solution)/shard_map/dot_general | solution.py:249
  386.7 10.8 %convolution_convert_fusion = bf16[1024,2048]{1,0:T(8,128)(2,1)S(1)} fusion(bf16[1024,2048]{1,0:T(8,128)(2,1)} %bitcast.313, f32[1024,1024]{1,0:T(8,128)S(1)} %fusion.83, f32[1024,1024]{1,0:T(8,128)} %copy-done.111, f32[1024,1024]{1,0:T(8,128)} %copy-done.110), kind=kOutput, calls=%fused_computation.53 | convolution fusion | flops 4304404480 | bytes 20971520 | tf_op jit(solution)/shard_map/dot_general | solution.py:246
  406.7 9.9 %fusion.16 = f32[1024,1024]{1,0:T(8,128)} fusion(f32[1024,1024]{1,0:T(8,128)S(1)} %fusion.86, bf16[1024,2048]{1,0:T(8,128)(2,1)} %bitcast.314, bf16[1024,2176]{1,0:T(8,128)(2,1)S(1)} %copy-done.75), kind=kOutput, calls=%fused_computation.65 | convolution fusion | flops 4296015872 | bytes 16777216 | tf_op jit(solution)/shard_map/dot_general | solution.py:249
  423.1 6.3 fusion.182
  429.5 11.5 %fusion.32 = f32[1024,2048]{1,0:T(8,128)} fusion(bf16[2048,1024]{0,1:T(8,128)(2,1)S(1)} %bitcast.287, f32[1024,1024]{1,0:T(8,128)S(1)} %fusion.181, f32[1024,1024]{1,0:T(8,128)S(1)} %copy-done.104, f32[1024,1024]{1,0:T(8,128)} %fusion.182), kind=kOutput, calls=%fused_computation.72 | convolution fusion | flops 4305453056 | bytes 25165824 | tf_op jit(solution)/shard_map/dot_general | solution.py:249
  440.9 8.8 add_convert_fusion.1
  454.1 9.4 convolution_convert_fusion.1
  479.8 8.2 fusion.31
  488.0 8.4 add_convert_fusion.2
  499.3 9.5 %convolution_convert_fusion.2 = bf16[1024,2048]{1,0:T(8,128)(2,1)S(1)} fusion(bf16[1024,2048]{1,0:T(8,128)(2,1)} %bitcast.316, f32[1024,1024]{1,0:T(8,128)S(1)} %copy-done.39, f32[1024,1024]{1,0:T(8,128)} %copy-done.109, f32[1024,1024]{1,0:T(8,128)} %copy-done.108), kind=kOutput, calls=%fused_computation.55 | convolution fusion | flops 4304404480 | bytes 20971520 | tf_op jit(solution)/shard_map/dot_general | solution.py:246
  525.0 13.1 %fusion.30 = f32[1024,2048]{1,0:T(8,128)} fusion(bf16[2048,1024]{0,1:T(8,128)(2,1)S(1)} %bitcast.291, f32[1024,1024]{1,0:T(8,128)} %fusion.177, f32[1024,1024]{1,0:T(8,128)S(1)} %copy-done.106, f32[1024,1024]{1,0:T(8,128)} %fusion.178), kind=kOutput, calls=%fused_computation.70 | convolution fusion | flops 4305453056 | bytes 25165824 | tf_op jit(solution)/shard_map/dot_general | solution.py:249
  538.1 11.7 %add_convert_fusion.3 = bf16[1024,2048]{1,0:T(8,128)(2,1)S(1)} fusion(f32[1024,2048]{1,0:T(8,128)} %fusion.30, bf16[2048,1024]{0,1:T(8,128)(2,1)} %bitcast.276, f32[1024,1024]{1,0:T(8,128)} %fusion.16, f32[1024,1024]{1,0:T(8,128)} %fusion.177), kind=kOutput, calls=%fused_computation.11 | convolution fusion | flops 4305453056 | bytes 25165824 | tf_op jit(solution)/shard_map/dot_general | solution.py:249
  551.3 10.5 %convolution_convert_fusion.3 = bf16[1024,2048]{1,0:T(8,128)(2,1)S(1)} fusion(bf16[1024,2048]{1,0:T(8,128)(2,1)} %bitcast.317, f32[1024,1024]{1,0:T(8,128)} %copy-done.40, f32[1024,1024]{1,0:T(8,128)} %fusion.178, f32[1024,1024]{1,0:T(8,128)} %fusion.177), kind=kOutput, calls=%fused_computation.56 | convolution fusion | flops 4304404480 | bytes 20971520 | tf_op jit(solution)/shard_map/dot_general | solution.py:246
  570.9 10.5 %collective-permute-done.93 = bf16[128,2048]{1,0:T(8,128)(2,1)S(1)} collective-permute-done((bf16[128,2048]{1,0:T(8,128)(2,1)S(1)}, bf16[128,2048]{1,0:T(8,128)(2,1)S(1)}, u32[]{:S(2)}, u32[]{:S(2)}) %collective-permute-start.93) | collective-permute-done | bytes 524320 | tf_op jit(solution)/shard_map/ppermute | solution.py:87
  590.4 7.9 collective-permute-done.67
  616.9 6.3 collective-permute-done.70
  640.0 7.3 collective-permute-done.51
  651.7 9.8 %collective-permute-done.90 = bf16[64,2048]{1,0:T(8,128)(2,1)S(1)} collective-permute-done((bf16[64,2048]{1,0:T(8,128)(2,1)S(1)}, bf16[64,2048]{1,0:T(8,128)(2,1)S(1)}, u32[]{:S(2)}, u32[]{:S(2)}) %collective-permute-start.90) | collective-permute-done | bytes 262176 | tf_op jit(solution)/shard_map/ppermute | solution.py:87
  668.9 8.2 collective-permute-done.54
  683.3 8.2 collective-permute-done.83
  698.5 13.8 %collective-permute-done.84 = bf16[64,2048]{1,0:T(8,128)(2,1)S(1)} collective-permute-done((bf16[64,2048]{1,0:T(8,128)(2,1)S(1)}, bf16[64,2048]{1,0:T(8,128)(2,1)S(1)}, u32[]{:S(2)}, u32[]{:S(2)}) %collective-permute-start.84) | collective-permute-done | bytes 262176 | tf_op jit(solution)/shard_map/ppermute | solution.py:87
  714.0 6.7 collective-permute-done.82
  732.5 6.7 collective-permute-done.21
  742.5 7.1 collective-permute-done.76
  758.0 8.3 collective-permute-done.79
  770.0 7.5 collective-permute-done.23
  781.3 7.4 collective-permute-done.85
  818.5 9.1 collective-permute-done.98
  842.6 6.7 all-reduce
  916.6 8.7 collective-permute-done.101
  (782 shorter events, 491.9 us)
Async XLA Ops:
  57.5 63.0 %collective-permute-start = (bf16[2,128,2176]{2,1,0:T(8,128)(2,1)}, bf16[2,128,2176]{2,1,0:T(8,128)(2,1)}, u32[]{:S(2)}, u32[]{:S(2)}) collective-permute-start(bf16[2,128,2176]{2,1,0:T(8,128)(2,1)} %dynamic-slice_bitcast_fusion), channel_id=1, source_target_pairs={{0,1},{1,0},{2,3},{3,2},{4,5},{5,4},{6,7},{7,6},{8,9},{9,8},{10,11... | collective-permute-start | bytes 3342344 | tf_op jit(solution)/shard_map/ppermute | solution.py:87
  60.5 45.1 %collective-permute-start.10 = (bf16[128,2176]{1,0:T(8,128)(2,1)S(1)}, bf16[128,2176]{1,0:T(8,128)(2,1)S(1)}, u32[]{:S(2)}, u32[]{:S(2)}) collective-permute-start(bf16[128,2176]{1,0:T(8,128)(2,1)S(1)} %concatenate.193), channel_id=1, source_target_pairs={{0,8},{4,12},{8,16},{12,20},{16,24},{20,28},{24,0},{28,4},{1,9},{5... | collective-permute-start | bytes 1671176 | tf_op jit(solution)/shard_map/ppermute | solution.py:87
  63.0 40.2 %collective-permute-start.61 = (bf16[64,2176]{1,0:T(8,128)(2,1)}, bf16[64,2176]{1,0:T(8,128)(2,1)S(1)}, u32[]{:S(2)}, u32[]{:S(2)}) collective-permute-start(bf16[64,2176]{1,0:T(8,128)(2,1)} %get-tuple-element.137), channel_id=1, source_target_pairs={{0,4},{4,0},{8,12},{12,8},{16,20},{20,16},{24,28},{28,24},{1,5},{5... | collective-permute-start | bytes 835592 | tf_op jit(solution)/shard_map/ppermute | solution.py:87
  106.9 20.8 %collective-permute-start.11 = (bf16[128,2176]{1,0:T(8,128)(2,1)S(1)}, bf16[128,2176]{1,0:T(8,128)(2,1)S(1)}, u32[]{:S(2)}, u32[]{:S(2)}) collective-permute-start(bf16[128,2176]{1,0:T(8,128)(2,1)S(1)} %collective-permute-done.10), channel_id=1, source_target_pairs={{0,8},{4,12},{8,16},{12,20},{16,24},{20,28},{24,0},{28,4},{1,9},{5... | collective-permute-start | bytes 1671176 | tf_op jit(solution)/shard_map/ppermute | solution.py:87
  118.0 22.3 %collective-permute-start.46 = (bf16[128,2176]{1,0:T(8,128)(2,1)S(1)}, bf16[128,2176]{1,0:T(8,128)(2,1)S(1)}, u32[]{:S(2)}, u32[]{:S(2)}) collective-permute-start(bf16[128,2176]{1,0:T(8,128)(2,1)S(1)} %pad_maximum_fusion.4), channel_id=1, source_target_pairs={{0,2},{1,3},{2,0},{3,1},{4,6},{5,7},{6,4},{7,5},{8,10},{9,11},{10,... | collective-permute-start | bytes 1671176 | tf_op jit(solution)/shard_map/ppermute | solution.py:87
  122.1 28.8 %collective-permute-start.1 = (bf16[128,2176]{1,0:T(8,128)(2,1)S(1)}, bf16[128,2176]{1,0:T(8,128)(2,1)S(1)}, u32[]{:S(2)}, u32[]{:S(2)}) collective-permute-start(bf16[128,2176]{1,0:T(8,128)(2,1)S(1)} %dynamic-slice_bitcast_fusion.2), channel_id=1, source_target_pairs={{0,2},{1,3},{2,0},{3,1},{4,6},{5,7},{6,4},{7,5},{8,10},{9,11},{10,... | collective-permute-start | bytes 1671176 | tf_op jit(solution)/shard_map/ppermute | solution.py:87
  127.1 27.4 %collective-permute-start.64 = (bf16[128,2176]{1,0:T(8,128)(2,1)S(1)}, bf16[128,2176]{1,0:T(8,128)(2,1)S(1)}, u32[]{:S(2)}, u32[]{:S(2)}) collective-permute-start(bf16[128,2176]{1,0:T(8,128)(2,1)S(1)} %pad_maximum_fusion.7), channel_id=1, source_target_pairs={{0,4},{4,0},{8,12},{12,8},{16,20},{20,16},{24,28},{28,24},{1,5},{5... | collective-permute-start | bytes 1671176 | tf_op jit(solution)/shard_map/ppermute | solution.py:87
  129.9 25.4 %collective-permute-start.12 = (bf16[128,2176]{1,0:T(8,128)(2,1)S(1)}, bf16[128,2176]{1,0:T(8,128)(2,1)S(1)}, u32[]{:S(2)}, u32[]{:S(2)}) collective-permute-start(bf16[128,2176]{1,0:T(8,128)(2,1)S(1)} %collective-permute-done.11), channel_id=1, source_target_pairs={{0,8},{4,12},{8,16},{12,20},{16,24},{20,28},{24,0},{28,4},{1,9},{5... | collective-permute-start | bytes 1671176 | tf_op jit(solution)/shard_map/ppermute | solution.py:87
  139.7 34.7 %collective-permute-start.30 = (bf16[128,2176]{1,0:T(8,128)(2,1)S(1)}, bf16[128,2176]{1,0:T(8,128)(2,1)S(1)}, u32[]{:S(2)}, u32[]{:S(2)}) collective-permute-start(bf16[128,2176]{1,0:T(8,128)(2,1)S(1)} %pad_maximum_fusion.2), channel_id=1, source_target_pairs={{0,2},{1,3},{2,0},{3,1},{4,6},{5,7},{6,4},{7,5},{8,10},{9,11},{10,... | collective-permute-start | bytes 1671176 | tf_op jit(solution)/shard_map/ppermute | solution.py:87
  141.9 21.8 %collective-permute-start.47 = (bf16[64,2176]{1,0:T(8,128)(2,1)S(1)}, bf16[64,2176]{1,0:T(8,128)(2,1)S(1)}, u32[]{:S(2)}, u32[]{:S(2)}) collective-permute-start(bf16[64,2176]{1,0:T(8,128)(2,1)S(1)} %get-tuple-element.142), channel_id=1, source_target_pairs={{0,2},{1,3},{2,0},{3,1},{4,6},{5,7},{6,4},{7,5},{8,10},{9,11},{10,... | collective-permute-start | bytes 835592 | tf_op jit(solution)/shard_map/ppermute | solution.py:87
  154.3 23.6 %collective-permute-start.2 = (bf16[128,2048]{1,0:T(8,128)(2,1)S(1)}, bf16[128,2048]{1,0:T(8,128)(2,1)S(1)}, u32[]{:S(2)}, u32[]{:S(2)}) collective-permute-start(bf16[128,2048]{1,0:T(8,128)(2,1)S(1)} %multiply_convert_fusion.26), channel_id=1, source_target_pairs={{0,8},{4,12},{8,16},{12,20},{16,24},{20,28},{24,0},{28,4},{1,9},{5... | collective-permute-start | bytes 1572872 | tf_op jit(solution)/shard_map/ppermute | solution.py:87
  155.3 147.9 %collective-permute-start.65 = (bf16[512,2176]{1,0:T(8,128)(2,1)S(1)}, bf16[512,2176]{1,0:T(8,128)(2,1)S(1)}, u32[]{:S(2)}, u32[]{:S(2)}) collective-permute-start(bf16[512,2176]{1,0:T(8,128)(2,1)S(1)} %get-tuple-element.131), channel_id=1, source_target_pairs={{0,1},{1,0},{2,3},{3,2},{4,5},{5,4},{6,7},{7,6},{8,9},{9,8},{10,11... | collective-permute-start | bytes 6684680 | tf_op jit(solution)/shard_map/ppermute | solution.py:87
  165.2 32.5 %collective-permute-start.48 = (bf16[128,2176]{1,0:T(8,128)(2,1)S(1)}, bf16[128,2176]{1,0:T(8,128)(2,1)S(1)}, u32[]{:S(2)}, u32[]{:S(2)}) collective-permute-start(bf16[128,2176]{1,0:T(8,128)(2,1)S(1)} %pad_maximum_fusion.5), channel_id=1, source_target_pairs={{0,4},{4,0},{8,12},{12,8},{16,20},{20,16},{24,28},{28,24},{1,5},{5... | collective-permute-start | bytes 1671176 | tf_op jit(solution)/shard_map/ppermute | solution.py:87
  173.2 25.4 %collective-permute-start.57 = (bf16[128,2048]{1,0:T(8,128)(2,1)S(1)}, bf16[128,2048]{1,0:T(8,128)(2,1)S(1)}, u32[]{:S(2)}, u32[]{:S(2)}) collective-permute-start(bf16[128,2048]{1,0:T(8,128)(2,1)S(1)} %pad_maximum_fusion.15), channel_id=1, source_target_pairs={{0,2},{1,3},{2,0},{3,1},{4,6},{5,7},{6,4},{7,5},{8,10},{9,11},{10,... | collective-permute-start | bytes 1572872 | tf_op jit(solution)/shard_map/ppermute | solution.py:87
  174.5 28.8 %collective-permute-start.14 = (bf16[128,2176]{1,0:T(8,128)(2,1)S(1)}, bf16[128,2176]{1,0:T(8,128)(2,1)S(1)}, u32[]{:S(2)}, u32[]{:S(2)}) collective-permute-start(bf16[128,2176]{1,0:T(8,128)(2,1)S(1)} %pad_maximum_fusion), channel_id=1, source_target_pairs={{0,2},{1,3},{2,0},{3,1},{4,6},{5,7},{6,4},{7,5},{8,10},{9,11},{10,... | collective-permute-start | bytes 1671176 | tf_op jit(solution)/shard_map/ppermute | solution.py:87
  198.6 34.6 %collective-permute-start.32 = (bf16[128,2176]{1,0:T(8,128)(2,1)S(1)}, bf16[128,2176]{1,0:T(8,128)(2,1)S(1)}, u32[]{:S(2)}, u32[]{:S(2)}) collective-permute-start(bf16[128,2176]{1,0:T(8,128)(2,1)S(1)} %pad_maximum_fusion.3), channel_id=1, source_target_pairs={{0,4},{4,0},{8,12},{12,8},{16,20},{20,16},{24,28},{28,24},{1,5},{5... | collective-permute-start | bytes 1671176 | tf_op jit(solution)/shard_map/ppermute | solution.py:87
  202.5 126.1 %collective-permute-start.49 = (bf16[512,2176]{1,0:T(8,128)(2,1)}, bf16[512,2176]{1,0:T(8,128)(2,1)S(1)}, u32[]{:S(2)}, u32[]{:S(2)}) collective-permute-start(bf16[512,2176]{1,0:T(8,128)(2,1)} %get-tuple-element.138), channel_id=1, source_target_pairs={{0,1},{1,0},{2,3},{3,2},{4,5},{5,4},{6,7},{7,6},{8,9},{9,8},{10,11... | collective-permute-start | bytes 6684680 | tf_op jit(solution)/shard_map/ppermute | solution.py:87
  212.1 37.9 %collective-permute-start.41 = (bf16[128,2048]{1,0:T(8,128)(2,1)S(1)}, bf16[128,2048]{1,0:T(8,128)(2,1)S(1)}, u32[]{:S(2)}, u32[]{:S(2)}) collective-permute-start(bf16[128,2048]{1,0:T(8,128)(2,1)S(1)} %pad_maximum_fusion.13), channel_id=1, source_target_pairs={{0,2},{1,3},{2,0},{3,1},{4,6},{5,7},{6,4},{7,5},{8,10},{9,11},{10,... | collective-permute-start | bytes 1572872 | tf_op jit(solution)/shard_map/ppermute | solution.py:87
  231.6 41.2 %collective-permute-start.59 = (bf16[128,2048]{1,0:T(8,128)(2,1)S(1)}, bf16[128,2048]{1,0:T(8,128)(2,1)S(1)}, u32[]{:S(2)}, u32[]{:S(2)}) collective-permute-start(bf16[128,2048]{1,0:T(8,128)(2,1)S(1)} %pad_maximum_fusion.16), channel_id=1, source_target_pairs={{0,4},{4,0},{8,12},{12,8},{16,20},{20,16},{24,28},{28,24},{1,5},{5... | collective-permute-start | bytes 1572872 | tf_op jit(solution)/shard_map/ppermute | solution.py:87
  250.0 25.3 %collective-permute-start.16 = (bf16[128,2176]{1,0:T(8,128)(2,1)S(1)}, bf16[128,2176]{1,0:T(8,128)(2,1)S(1)}, u32[]{:S(2)}, u32[]{:S(2)}) collective-permute-start(bf16[128,2176]{1,0:T(8,128)(2,1)S(1)} %pad_maximum_fusion.1), channel_id=1, source_target_pairs={{0,4},{4,0},{8,12},{12,8},{16,20},{20,16},{24,28},{28,24},{1,5},{5... | collective-permute-start | bytes 1671176 | tf_op jit(solution)/shard_map/ppermute | solution.py:87
  272.8 70.8 %collective-permute-start.33 = (bf16[512,2176]{1,0:T(8,128)(2,1)}, bf16[512,2176]{1,0:T(8,128)(2,1)S(1)}, u32[]{:S(2)}, u32[]{:S(2)}) collective-permute-start(bf16[512,2176]{1,0:T(8,128)(2,1)} %get-tuple-element.145), channel_id=1, source_target_pairs={{0,1},{1,0},{2,3},{3,2},{4,5},{5,4},{6,7},{7,6},{8,9},{9,8},{10,11... | collective-permute-start | bytes 6684680 | tf_op jit(solution)/shard_map/ppermute | solution.py:87
  300.8 51.6 %collective-permute-start.60 = (bf16[512,2048]{1,0:T(8,128)(2,1)}, bf16[512,2048]{1,0:T(8,128)(2,1)S(1)}, u32[]{:S(2)}, u32[]{:S(2)}) collective-permute-start(bf16[512,2048]{1,0:T(8,128)(2,1)} %get-tuple-element.161), channel_id=1, source_target_pairs={{0,1},{1,0},{2,3},{3,2},{4,5},{5,4},{6,7},{7,6},{8,9},{9,8},{10,11... | collective-permute-start | bytes 6291464 | tf_op jit(solution)/shard_map/ppermute | solution.py:87
  303.2 22.8 %collective-permute-start.27 = (bf16[128,2048]{1,0:T(8,128)(2,1)S(1)}, bf16[128,2048]{1,0:T(8,128)(2,1)S(1)}, u32[]{:S(2)}, u32[]{:S(2)}) collective-permute-start(bf16[128,2048]{1,0:T(8,128)(2,1)S(1)} %pad_maximum_fusion.12), channel_id=1, source_target_pairs={{0,4},{4,0},{8,12},{12,8},{16,20},{20,16},{24,28},{28,24},{1,5},{5... | collective-permute-start | bytes 1572872 | tf_op jit(solution)/shard_map/ppermute | solution.py:87
  325.9 75.0 %collective-permute-start.17 = (bf16[512,2176]{1,0:T(8,128)(2,1)}, bf16[512,2176]{1,0:T(8,128)(2,1)}, u32[]{:S(2)}, u32[]{:S(2)}) collective-permute-start(bf16[512,2176]{1,0:T(8,128)(2,1)} %get-tuple-element.152), channel_id=1, source_target_pairs={{0,1},{1,0},{2,3},{3,2},{4,5},{5,4},{6,7},{7,6},{8,9},{9,8},{10,11... | collective-permute-start | bytes 6684680 | tf_op jit(solution)/shard_map/ppermute | solution.py:87
  326.0 90.7 %collective-permute-start.44 = (bf16[512,2048]{1,0:T(8,128)(2,1)}, bf16[512,2048]{1,0:T(8,128)(2,1)}, u32[]{:S(2)}, u32[]{:S(2)}) collective-permute-start(bf16[512,2048]{1,0:T(8,128)(2,1)} %get-tuple-element.168), channel_id=1, source_target_pairs={{0,1},{1,0},{2,3},{3,2},{4,5},{5,4},{6,7},{7,6},{8,9},{9,8},{10,11... | collective-permute-start | bytes 6291464 | tf_op jit(solution)/shard_map/ppermute | solution.py:87
  342.4 122.7 %collective-permute-start.28 = (bf16[512,2048]{1,0:T(8,128)(2,1)}, bf16[512,2048]{1,0:T(8,128)(2,1)}, u32[]{:S(2)}, u32[]{:S(2)}) collective-permute-start(bf16[512,2048]{1,0:T(8,128)(2,1)} %get-tuple-element.175), channel_id=1, source_target_pairs={{0,1},{1,0},{2,3},{3,2},{4,5},{5,4},{6,7},{7,6},{8,9},{9,8},{10,11... | collective-permute-start | bytes 6291464 | tf_op jit(solution)/shard_map/ppermute | solution.py:87
  343.6 166.8 %collective-permute-start.9 = (bf16[512,2048]{1,0:T(8,128)(2,1)}, bf16[512,2048]{1,0:T(8,128)(2,1)}, u32[]{:S(2)}, u32[]{:S(2)}) collective-permute-start(bf16[512,2048]{1,0:T(8,128)(2,1)} %get-tuple-element.182), channel_id=1, source_target_pairs={{0,1},{1,0},{2,3},{3,2},{4,5},{5,4},{6,7},{7,6},{8,9},{9,8},{10,11... | collective-permute-start | bytes 6291464 | tf_op jit(solution)/shard_map/ppermute | solution.py:87
  399.1 164.2 %collective-permute-start.92 = (bf16[512,2048]{1,0:T(8,128)(2,1)}, bf16[512,2048]{1,0:T(8,128)(2,1)}, u32[]{:S(2)}, u32[]{:S(2)}) collective-permute-start(bf16[512,2048]{1,0:T(8,128)(2,1)} %split.390), channel_id=1, source_target_pairs={{0,1},{1,0},{2,3},{3,2},{4,5},{5,4},{6,7},{7,6},{8,9},{9,8},{10,11... | collective-permute-start | bytes 6291464 | tf_op jit(solution)/shard_map/ppermute | solution.py:87
  400.9 167.1 %collective-permute-start.66 = (bf16[512,2048]{1,0:T(8,128)(2,1)}, bf16[512,2048]{1,0:T(8,128)(2,1)}, u32[]{:S(2)}, u32[]{:S(2)}) collective-permute-start(bf16[512,2048]{1,0:T(8,128)(2,1)} %split.350), channel_id=1, source_target_pairs={{0,1},{1,0},{2,3},{3,2},{4,5},{5,4},{6,7},{7,6},{8,9},{9,8},{10,11... | collective-permute-start | bytes 6291464 | tf_op jit(solution)/shard_map/ppermute | solution.py:87
  451.2 132.6 %collective-permute-start.86 = (bf16[512,2048]{1,0:T(8,128)(2,1)}, bf16[512,2048]{1,0:T(8,128)(2,1)}, u32[]{:S(2)}, u32[]{:S(2)}) collective-permute-start(bf16[512,2048]{1,0:T(8,128)(2,1)} %split.380), channel_id=1, source_target_pairs={{0,1},{1,0},{2,3},{3,2},{4,5},{5,4},{6,7},{7,6},{8,9},{9,8},{10,11... | collective-permute-start | bytes 6291464 | tf_op jit(solution)/shard_map/ppermute | solution.py:87
  465.1 122.3 %collective-permute-start.50 = (bf16[512,2048]{1,0:T(8,128)(2,1)}, bf16[512,2048]{1,0:T(8,128)(2,1)}, u32[]{:S(2)}, u32[]{:S(2)}) collective-permute-start(bf16[512,2048]{1,0:T(8,128)(2,1)} %split.340), channel_id=1, source_target_pairs={{0,1},{1,0},{2,3},{3,2},{4,5},{5,4},{6,7},{7,6},{8,9},{9,8},{10,11... | collective-permute-start | bytes 6291464 | tf_op jit(solution)/shard_map/ppermute | solution.py:87
  510.4 113.8 %collective-permute-start.80 = (bf16[512,2048]{1,0:T(8,128)(2,1)}, bf16[512,2048]{1,0:T(8,128)(2,1)}, u32[]{:S(2)}, u32[]{:S(2)}) collective-permute-start(bf16[512,2048]{1,0:T(8,128)(2,1)} %split.370), channel_id=1, source_target_pairs={{0,1},{1,0},{2,3},{3,2},{4,5},{5,4},{6,7},{7,6},{8,9},{9,8},{10,11... | collective-permute-start | bytes 6291464 | tf_op jit(solution)/shard_map/ppermute | solution.py:87
  581.5 45.7 %collective-permute-start.34 = (bf16[512,2048]{1,0:T(8,128)(2,1)}, bf16[512,2048]{1,0:T(8,128)(2,1)}, u32[]{:S(2)}, u32[]{:S(2)}) collective-permute-start(bf16[512,2048]{1,0:T(8,128)(2,1)} %split.330), channel_id=1, source_target_pairs={{0,1},{1,0},{2,3},{3,2},{4,5},{5,4},{6,7},{7,6},{8,9},{9,8},{10,11... | collective-permute-start | bytes 6291464 | tf_op jit(solution)/shard_map/ppermute | solution.py:87
  582.3 95.3 %collective-permute-start.74 = (bf16[512,2048]{1,0:T(8,128)(2,1)}, bf16[512,2048]{1,0:T(8,128)(2,1)S(1)}, u32[]{:S(2)}, u32[]{:S(2)}) collective-permute-start(bf16[512,2048]{1,0:T(8,128)(2,1)} %split.360), channel_id=1, source_target_pairs={{0,1},{1,0},{2,3},{3,2},{4,5},{5,4},{6,7},{7,6},{8,9},{9,8},{10,11... | collective-permute-start | bytes 6291464 | tf_op jit(solution)/shard_map/ppermute | solution.py:87
  598.3 81.2 %collective-permute-start.18 = (bf16[512,2048]{1,0:T(8,128)(2,1)S(1)}, bf16[512,2048]{1,0:T(8,128)(2,1)S(1)}, u32[]{:S(2)}, u32[]{:S(2)}) collective-permute-start(bf16[512,2048]{1,0:T(8,128)(2,1)S(1)} %copy-done.49), channel_id=1, source_target_pairs={{0,1},{1,0},{2,3},{3,2},{4,5},{5,4},{6,7},{7,6},{8,9},{9,8},{10,11... | collective-permute-start | bytes 6291464 | tf_op jit(solution)/shard_map/ppermute | solution.py:87
  627.2 173.1 %collective-permute-start.68 = (bf16[64,2048]{1,0:T(8,128)(2,1)S(1)}, bf16[64,2048]{1,0:T(8,128)(2,1)S(1)}, u32[]{:S(2)}, u32[]{:S(2)}) collective-permute-start(bf16[64,2048]{1,0:T(8,128)(2,1)S(1)} %split.354), channel_id=1, source_target_pairs={{0,4},{4,0},{8,12},{12,8},{16,20},{20,16},{24,28},{28,24},{1,5},{5... | collective-permute-start | bytes 786440 | tf_op jit(solution)/shard_map/ppermute | solution.py:87
  647.3 34.8 %collective-permute-start.81 = (bf16[128,2048]{1,0:T(8,128)(2,1)S(1)}, bf16[128,2048]{1,0:T(8,128)(2,1)S(1)}, u32[]{:S(2)}, u32[]{:S(2)}) collective-permute-start(bf16[128,2048]{1,0:T(8,128)(2,1)S(1)} %get-tuple-element.96), channel_id=1, source_target_pairs={{0,2},{1,3},{2,0},{3,1},{4,6},{5,7},{6,4},{7,5},{8,10},{9,11},{10,... | collective-permute-start | bytes 1572872 | tf_op jit(solution)/shard_map/ppermute | solution.py:87
  682.2 46.8 %collective-permute-start.75 = (bf16[128,2048]{1,0:T(8,128)(2,1)S(1)}, bf16[128,2048]{1,0:T(8,128)(2,1)S(1)}, u32[]{:S(2)}, u32[]{:S(2)}) collective-permute-start(bf16[128,2048]{1,0:T(8,128)(2,1)S(1)} %get-tuple-element.100), channel_id=1, source_target_pairs={{0,2},{1,3},{2,0},{3,1},{4,6},{5,7},{6,4},{7,5},{8,10},{9,11},{10,... | collective-permute-start | bytes 1572872 | tf_op jit(solution)/shard_map/ppermute | solution.py:87
  691.5 37.8 %collective-permute-start.77 = (bf16[128,2048]{1,0:T(8,128)(2,1)S(1)}, bf16[128,2048]{1,0:T(8,128)(2,1)S(1)}, u32[]{:S(2)}, u32[]{:S(2)}) collective-permute-start(bf16[128,2048]{1,0:T(8,128)(2,1)S(1)} %get-tuple-element.101), channel_id=1, source_target_pairs={{0,4},{4,0},{8,12},{12,8},{16,20},{20,16},{24,28},{28,24},{1,5},{5... | collective-permute-start | bytes 1572872 | tf_op jit(solution)/shard_map/ppermute | solution.py:87
  692.5 38.9 %collective-permute-start.19 = (bf16[128,2048]{1,0:T(8,128)(2,1)S(1)}, bf16[128,2048]{1,0:T(8,128)(2,1)S(1)}, u32[]{:S(2)}, u32[]{:S(2)}) collective-permute-start(bf16[128,2048]{1,0:T(8,128)(2,1)S(1)} %get-tuple-element.120), channel_id=1, source_target_pairs={{0,2},{1,3},{2,0},{3,1},{4,6},{5,7},{6,4},{7,5},{8,10},{9,11},{10,... | collective-permute-start | bytes 1572872 | tf_op jit(solution)/shard_map/ppermute | solution.py:87
  728.9 52.3 %collective-permute-start.52 = (bf16[64,2048]{1,0:T(8,128)(2,1)S(1)}, bf16[64,2048]{1,0:T(8,128)(2,1)S(1)}, u32[]{:S(2)}, u32[]{:S(2)}) collective-permute-start(bf16[64,2048]{1,0:T(8,128)(2,1)S(1)} %split.344), channel_id=1, source_target_pairs={{0,4},{4,0},{8,12},{12,8},{16,20},{20,16},{24,28},{28,24},{1,5},{5... | collective-permute-start | bytes 786440 | tf_op jit(solution)/shard_map/ppermute | solution.py:87
  729.3 28.6 %collective-permute-start.36 = (bf16[64,2048]{1,0:T(8,128)(2,1)S(1)}, bf16[64,2048]{1,0:T(8,128)(2,1)S(1)}, u32[]{:S(2)}, u32[]{:S(2)}) collective-permute-start(bf16[64,2048]{1,0:T(8,128)(2,1)S(1)} %split.334), channel_id=1, source_target_pairs={{0,4},{4,0},{8,12},{12,8},{16,20},{20,16},{24,28},{28,24},{1,5},{5... | collective-permute-start | bytes 786440 | tf_op jit(solution)/shard_map/ppermute | solution.py:87
  756.1 21.4 %collective-permute-start.23 = (bf16[128,2048]{1,0:T(8,128)(2,1)S(1)}, bf16[128,2048]{1,0:T(8,128)(2,1)S(1)}, u32[]{:S(2)}, u32[]{:S(2)}) collective-permute-start(bf16[128,2048]{1,0:T(8,128)(2,1)S(1)} %pad_maximum_fusion.10), channel_id=1, source_target_pairs={{0,24},{4,28},{8,0},{12,4},{16,8},{20,12},{24,16},{28,20},{1,25},{... | collective-permute-start | bytes 1572872 | tf_op jit(solution)/shard_map/ppermute | solution.py:87
  766.4 22.3 %collective-permute-start.85 = (bf16[128,2048]{1,0:T(8,128)(2,1)S(1)}, bf16[128,2048]{1,0:T(8,128)(2,1)S(1)}, u32[]{:S(2)}, u32[]{:S(2)}) collective-permute-start(bf16[128,2048]{1,0:T(8,128)(2,1)S(1)} %add_convert_fusion.20), channel_id=1, source_target_pairs={{0,24},{4,28},{8,0},{12,4},{16,8},{20,12},{24,16},{28,20},{1,25},{... | collective-permute-start | bytes 1572872 | tf_op jit(solution)/shard_map/ppermute | solution.py:87
  777.7 18.9 %collective-permute-start.39 = (bf16[128,2048]{1,0:T(8,128)(2,1)S(1)}, bf16[128,2048]{1,0:T(8,128)(2,1)S(1)}, u32[]{:S(2)}, u32[]{:S(2)}) collective-permute-start(bf16[128,2048]{1,0:T(8,128)(2,1)S(1)} %add_convert_fusion.32), channel_id=1, source_target_pairs={{0,24},{4,28},{8,0},{12,4},{16,8},{20,12},{24,16},{28,20},{1,25},{... | collective-permute-start | bytes 1572872 | tf_op jit(solution)/shard_map/ppermute | solution.py:87
  813.8 40.8 %collective-permute-start.72 = (bf16[128,1024]{1,0:T(8,128)(2,1)}, bf16[128,1024]{1,0:T(8,128)(2,1)S(1)}, u32[]{:S(2)}, u32[]{:S(2)}) collective-permute-start(bf16[128,1024]{1,0:T(8,128)(2,1)} %constant_dynamic-slice_fusion.2), channel_id=1, source_target_pairs={{0,2},{1,3},{2,0},{3,1},{4,6},{5,7},{6,4},{7,5},{8,10},{9,11},{10,... | collective-permute-start | bytes 786440 | tf_op jit(solution)/shard_map/ppermute | solution.py:87
  855.3 27.9 %collective-permute-start.73 = (bf16[128,512]{1,0:T(8,128)(2,1)S(1)}, bf16[128,512]{1,0:T(8,128)(2,1)S(1)}, u32[]{:S(2)}, u32[]{:S(2)}) collective-permute-start(bf16[128,512]{1,0:T(8,128)(2,1)S(1)} %get-tuple-element.203), channel_id=1, source_target_pairs={{0,1},{1,0},{2,3},{3,2},{4,5},{5,4},{6,7},{7,6},{8,9},{9,8},{10,11... | collective-permute-start | bytes 393224 | tf_op jit(solution)/shard_map/ppermute | solution.py:87
  875.5 28.6 %collective-permute-start.100 = (bf16[2,128,2048]{2,1,0:T(8,128)(2,1)}, bf16[2,128,2048]{2,1,0:T(8,128)(2,1)}, u32[]{:S(2)}, u32[]{:S(2)}) collective-permute-start(bf16[2,128,2048]{2,1,0:T(8,128)(2,1)} %dynamic-slice_bitcast_fusion.1), channel_id=1, source_target_pairs={{0,1},{1,0},{2,3},{3,2},{4,5},{5,4},{6,7},{7,6},{8,9},{9,8},{10,11... | collective-permute-start | bytes 3145736 | tf_op jit(solution)/shard_map/ppermute | solution.py:87
  (181 other events, 1890.6 us)

commit v2 on v1

v2 whole, which is shorter than its diff:
```python
import functools

import jax
import jax.numpy as jnp
from jax import lax
from jax.experimental import pallas as pl
from jax.experimental.pallas import tpu as pltpu
from jax.sharding import PartitionSpec as P

HD = 128
RANK = 16


EPSILON = 1e-05
ROPE_BASE = 10000.0
MASKED_SCORE = -1e30
VMEM_LIMIT = 52 * 2**20


def ancestry(parents):
    blocks = parents.shape[0]
    places = jnp.arange(blocks, dtype=jnp.int32)
    walker = places
    reached = walker[:, None] == places[None, :]
    for _ in range(blocks - 1):
        hits = (walker[:, None] == places[None, :]).astype(jnp.int32)
        walker = jnp.sum(hits * parents[None, :], axis=1)
        reached = reached | (walker[:, None] == places[None, :])
    return reached[None]


def rope_tables(reached, block_span, head_size):
    depths = jnp.sum(reached.astype(jnp.int32), axis=2) - 1
    offsets = jnp.arange(block_span, dtype=jnp.int32)
    located = (
        (depths[:, :, None] * block_span + offsets[None, None, :]).reshape(-1).astype(jnp.float32)
    )
    halves = head_size // 2
    speeds = ROPE_BASE ** (-2.0 * jnp.arange(halves, dtype=jnp.float32) / head_size)
    angles = located[:, None] * speeds[None, :]
    angles = jnp.concatenate([angles, angles], axis=1)
    return (jnp.cos(angles), jnp.sin(angles))


def rotate(values, cosine_table, sine_table):
    halves = values.shape[-1] // 2
    turned = jnp.concatenate([-values[..., halves:], values[..., :halves]], axis=-1)
    return values * cosine_table[:, None, :] + turned * sine_table[:, None, :]


def unrotate(values, cosine_table, sine_table):
    halves = values.shape[-1] // 2
    sined = values * sine_table[:, None, :]
    return values * cosine_table[:, None, :] + jnp.concatenate(
        [sined[..., halves:], -sined[..., :halves]], axis=-1
    )


def token_mask(reached, total_size):
    blocks = reached.shape[0]
    block_span = total_size // blocks
    widened = jnp.broadcast_to(
        reached[:, None, :, None], (blocks, block_span, blocks, block_span)
    ).reshape(total_size, total_size)
    positions = jnp.arange(total_size, dtype=jnp.int32)
    return widened & (positions[None, :] <= positions[:, None])


def norm_back(scaled_grad, values, inverse, model_width, inner_sum):
    return inverse * scaled_grad - values * inverse**3 * (inner_sum / model_width)


def divide_axes(owners, tensor_count):
    outer = 4
    return {
        "z": ("expert", outer, owners // outer, owners),
        "x": ("expert", owners // outer, 1, owners),
        "y": ("tensor", tensor_count // 2, 2, tensor_count),
        "c": ("tensor", 2, 1, tensor_count),
    }


def turn(array, axes, name, step):
    axis, length, stride, total = axes[name]
    pairs = []
    for index in range(total):
        place = (index // stride) % length
        moved = index + ((place + step) % length - place) * stride
        pairs.append((index, moved))
    return lax.ppermute(array, axis, pairs)


def ring(array, axes, name):
    held = [array]
    for _ in range(axes[name][1] - 1):
        held.append(turn(held[-1], axes, name, 1))
    return held


def wide(array):
    return array.astype(jnp.float32)


def low(array):
    return array.astype(jnp.bfloat16)


def gather_first(rows, axes):
    half = rows.shape[0] // 2
    return (
        jnp.concatenate(ring(rows[:half], axes, "x"), axis=0),
        jnp.concatenate(ring(rows[half:], axes, "y"), axis=0),
    )


def gather_second(pair, axes):
    return ring(pair[0], axes, "y") + ring(pair[1], axes, "x")


def send_sum(parts, axes, name):
    total = parts[-1]
    for part in parts[-2:0:-1]:
        total = low(wide(turn(total, axes, name, -1)) + wide(part))
    return turn(total, axes, name, -1)


def scatter_first(pieces, axes):
    span = axes["y"][1]
    return send_sum(pieces[:span], axes, "y"), send_sum(pieces[span:], axes, "x")


def scatter_second(pieces, came, axes):
    span = axes["y"][1]
    first = wide(pieces[0]) + wide(came[0])
    second = wide(pieces[span]) + wide(came[1])
    first = jnp.split(first, axes["x"][1], axis=0)
    second = jnp.split(second, axes["y"][1], axis=0)
    first_came = send_sum([low(part) for part in first], axes, "x")
    second_came = send_sum([low(part) for part in second], axes, "y")
    return (first[0], second[0]), (first_came, second_came)


def scatter_last(kept, came):
    return jnp.concatenate([kept[0] + wide(came[0]), kept[1] + wide(came[1])], axis=0)


def place_tensor(rows, axes, kind):
    rank = lax.axis_index("tensor")
    count = lax.axis_size("tensor")
    size = rows.shape[0]
    span = axes["y"][1]
    held = ring(rows, axes, "y")
    other = [turn(piece, axes, "c", 1) for piece in held]
    whole = jnp.zeros((count * size, rows.shape[1]), kind)
    core = rank % 2
    for step in range(span):
        level = (rank // 2 + span - step) % span
        whole = lax.dynamic_update_slice_in_dim(
            whole, held[step].astype(kind), (level * 2 + core) * size, 0
        )
        whole = lax.dynamic_update_slice_in_dim(
            whole, other[step].astype(kind), (level * 2 + 1 - core) * size, 0
        )
    return whole


def scatter_tensor(rows, axes):
    rank = lax.axis_index("tensor")
    count = lax.axis_size("tensor")
    size = rows.shape[0] // count
    span = axes["y"][1]
    blocks = rows.reshape(span, 2, size, rows.shape[1])
    core = rank % 2
    mine = lax.dynamic_index_in_dim(blocks, core, 1, keepdims=False)
    theirs = lax.dynamic_index_in_dim(blocks, 1 - core, 1, keepdims=False)
    mine = wide(mine) + wide(turn(theirs, axes, "c", 1))
    total = None
    for step in range(span - 1, -1, -1):
        level = (rank // 2 + span - step) % span
        part = lax.dynamic_index_in_dim(mine, level, 0, keepdims=False)
        total = part if total is None else wide(turn(low(total), axes, "y", -1)) + part
    return total


def swap_columns(rows, axes):
    rank = lax.axis_index("tensor")
    count = lax.axis_size("tensor")
    size, width = rows.shape
    span = axes["y"][1]
    share = width // count
    level, core = rank // 2, rank % 2
    whole = jnp.zeros((count * size, share), rows.dtype)
    for step in range(span):
        toward = (level + step) % span
        piece = lax.dynamic_slice_in_dim(rows, toward * 2 * share, 2 * share, 1)
        if step:
            piece = turn(piece, axes, "y", step)
        mine = lax.dynamic_slice_in_dim(piece, core * share, share, 1)
        theirs = lax.dynamic_slice_in_dim(piece, (1 - core) * share, share, 1)
        theirs = turn(theirs, axes, "c", 1)
        source = (level + span - step) % span
        whole = lax.dynamic_update_slice_in_dim(whole, mine, (source * 2 + core) * size, 0)
        whole = lax.dynamic_update_slice_in_dim(whole, theirs, (source * 2 + 1 - core) * size, 0)
    return whole


def sum_tensor(array, axes):
    total = wide(array) + wide(turn(array, axes, "c", 1))
    moving = low(total)
    result = total
    for _ in range(axes["y"][1] - 1):
        moving = turn(moving, axes, "y", 1)
        result = result + wide(moving)
    return result


def dot(left, right):
    return jnp.dot(left, right, preferred_element_type=jnp.float32)


def dot_t(left, right):
    return lax.dot_general(
        left, right, (((1,), (1,)), ((), ())), preferred_element_type=jnp.float32
    )


def t_dot(left, right):
    return lax.dot_general(
        left, right, (((0,), (0,)), ((), ())), preferred_element_type=jnp.float32
    )


def kernel_call(kernel, grid, ins, outs, operands, flops):
    moved = sum(array.size * array.dtype.itemsize for array in operands)
    return pl.pallas_call(
        kernel,
        grid=(grid,),
        in_specs=[pl.BlockSpec(block, index) for block, index in ins],
        out_specs=[pl.BlockSpec(block, index) for _, _, block, index in outs],
        out_shape=[jax.ShapeDtypeStruct(shape, kind) for shape, kind, _, _ in outs],
        compiler_params=pltpu.CompilerParams(vmem_limit_bytes=VMEM_LIMIT),
        cost_estimate=pl.CostEstimate(flops=flops, bytes_accessed=moved, transcendentals=0),
    )(*operands)


def stack_rows(refs, columns):
    return jnp.concatenate([ref[:, columns] for ref in refs], axis=0)


def hidden_kernel(count, width, *refs):
    pieces, (down_own, down_other, spread), (out, side_out) = (
        refs[:count],
        refs[count : count + 3],
        refs[count + 3 :],
    )
    side = stack_rows(pieces, slice(width, None))
    rows = stack_rows(pieces, slice(0, width))
    weight = dot(side, spread[...])
    out[0] = low(dot_t(rows, down_own[...]) * weight)
    out[1] = low(dot_t(rows, down_other[...]) * weight)
    side_out[...] = side


def hidden_call(pieces, down_own, down_other, spread, experts):
    width = down_own.shape[1]
    rows = sum(piece.shape[0] for piece in pieces)
    hidden = down_own.shape[0]
    part = hidden // experts
    side = spread.shape[0]
    whole = lambda e: (0, 0)
    ins = [(piece.shape, whole) for piece in pieces]
    ins += [((part, width), lambda e: (e, 0))] * 2
    ins += [((side, part), lambda e: (0, e))]
    outs = [
        ((2, rows, hidden), jnp.bfloat16, (2, rows, part), lambda e: (0, 0, e)),
        ((rows, side), jnp.bfloat16, (rows, side), whole),
    ]
    return kernel_call(
        functools.partial(hidden_kernel, len(pieces), width),
        experts,
        ins,
        outs,
        [*pieces, down_own, down_other, spread],
        4 * rows * hidden * width,
    )


def gate_kernel(count, *refs):
    pieces = refs[:count]
    gate_own, gate_other, up_own, up_other, spread, side, back = refs[count : count + 7]
    gate_out, up_out, hidden_out = refs[count + 7 :]
    rows = stack_rows(pieces, slice(None))
    weight = dot(side[...], spread[...])
    for half, (gate, up) in enumerate(((gate_own, up_own), (gate_other, up_other))):
        gate_value = dot(rows, gate[0])
        up_value = dot(rows, up[0])
        sigmoid = jax.nn.sigmoid(gate_value)
        silu = gate_value * sigmoid
        grad = wide(back[half])
        gate_out[half] = low(grad * up_value * (sigmoid + silu * (1.0 - sigmoid)))
        up_out[half] = low(grad * silu)
        hidden_out[half] = low(silu * up_value * weight)


def gate_call(pieces, gates, ups, spread, side, back):
    experts, width, part = gates[0].shape
    rows = side.shape[0]
    whole = lambda e: (0, 0)
    ins = [(piece.shape, whole) for piece in pieces]
    ins += [((1, width, part), lambda e: (e, 0, 0))] * 4
    ins += [((spread.shape[0], part), lambda e: (0, e)), (side.shape, whole)]
    ins += [((2, rows, part), lambda e: (0, 0, e))]
    out = (back.shape, jnp.bfloat16, (2, rows, part), lambda e: (0, 0, e))
    return kernel_call(
        functools.partial(gate_kernel, len(pieces)),
        experts,
        ins,
        [out] * 3,
        [*pieces, *gates, *ups, spread, side, back],
        8 * rows * experts * part * width,
    )


def rows_kernel(gate_grad, up_grad, gate_own, gate_other, up_own, up_other, *outs):
    total = None
    pairs = ((gate_grad, gate_own, gate_other), (up_grad, up_own, up_other))
    for grad, *weights in pairs:
        for half, weight in enumerate(weights):
            joined = jnp.concatenate([weight[e] for e in range(weight.shape[0])], axis=1)
            term = dot_t(grad[half], joined)
            total = term if total is None else total + term
    size = outs[0].shape[0]
    for index, out in enumerate(outs):
        out[...] = low(total[index * size : (index + 1) * size])


def rows_call(gate_grad, up_grad, gates, ups, count):
    experts, width, part = gates[0].shape
    rows = gate_grad.shape[1]
    tile = min(width, 512)
    ins = [(gate_grad.shape, lambda n: (0, 0, 0))] * 2
    ins += [((experts, tile, part), lambda n: (0, n, 0))] * 4
    size = rows // count
    out = ((size, width), jnp.bfloat16, (size, tile), lambda n: (0, n))
    return kernel_call(
        rows_kernel,
        width // tile,
        ins,
        [out] * count,
        [gate_grad, up_grad, *gates, *ups],
        8 * rows * experts * part * width,
    )


def down_kernel(hidden, down_own, down_other, *outs):
    total = dot(hidden[0], down_own[...]) + dot(hidden[1], down_other[...])
    size = outs[0].shape[0]
    for index, out in enumerate(outs):
        out[...] = low(total[index * size : (index + 1) * size])


def down_call(hidden, downs, count):
    _, rows, part = hidden.shape
    width = downs[0].shape[1]
    tile = min(width, 512)
    ins = [(hidden.shape, lambda n: (0, 0, 0))] + [((part, tile), lambda n: (0, n))] * 2
    size = rows // count
    out = ((size, width), jnp.bfloat16, (size, tile), lambda n: (0, n))
    return kernel_call(
        down_kernel,
        width // tile,
        ins,
        [out] * count,
        [hidden, *downs],
        4 * rows * part * width,
    )


def body(
    tokens,
    cotangent,
    attn_gain,
    ffn_gain,
    query_gain,
    key_gain,
    query_weight,
    key_weight,
    value_weight,
    output_weight,
    expert_gate,
    expert_up,
    expert_down,
    adapt_in,
    adapt_out,
    adapt_in_out,
    adapt_out_out,
    routes,
    gate_weights,
    block_parent,
    adapter_pick,
):
    rows_here, model_width = tokens.shape
    local_width = query_weight.shape[1]
    heads_here = local_width // HD
    tensor_rank = lax.axis_index("tensor")
    tensor_count = lax.axis_size("tensor")
    owners = lax.axis_size("expert")
    owner_rank = lax.axis_index("expert")
    axes = divide_axes(owners, tensor_count)
    far, near, span = axes["z"][1], axes["x"][1], axes["y"][1]
    experts_here, _, hidden_here = expert_gate.shape
    experts_all = experts_here * owners
    column_share = model_width // tensor_count
    row_share = rows_here // tensor_count
    float_kind = jnp.float32
    half_kind = jnp.bfloat16
    hold = lax.optimization_barrier

    def own_rows(array):
        return lax.dynamic_slice_in_dim(array, tensor_rank * row_share, row_share, 0)

    cotangent_rows = own_rows(cotangent)
    routes_rows = own_rows(routes)
    weights_rows = own_rows(gate_weights)
    route_weights = jnp.sum(
        jnp.where(
            routes_rows[:, :, None] == jnp.arange(experts_all, dtype=jnp.int32)[None, None, :],
            weights_rows[:, :, None],
            0.0,
        ),
        axis=1,
    )
    weights_high = low(route_weights)
    weights_low = low(route_weights - wide(weights_high))
    side_width = -(-2 * experts_all // 128) * 128
    side_pad = jnp.zeros((row_share, side_width - 2 * experts_all), half_kind)
    cot_plane = jnp.concatenate([cotangent_rows, weights_high, weights_low, side_pad], axis=1)
    side_index = jnp.arange(side_width, dtype=jnp.int32)
    hidden_owner = (
        owner_rank * experts_here
        + jnp.arange(experts_here * hidden_here, dtype=jnp.int32) // hidden_here
    )
    spread = low(
        (side_index[:, None] % experts_all == hidden_owner[None, :])
        & (side_index[:, None] < 2 * experts_all)
    )

    cot_next = turn(cot_plane, axes, "z", 1)
    cot_first = gather_first(cot_plane, axes)
    inputs = wide(tokens)
    first_gain = wide(attn_gain)
    second_gain = wide(ffn_gain)
    first_inverse = lax.rsqrt(jnp.mean(inputs * inputs, axis=1, keepdims=True) + EPSILON)
    normed_in = low(inputs * first_inverse * first_gain)
    reached = ancestry(block_parent)
    cosine_table, sine_table = rope_tables(reached, rows_here // block_parent.shape[0], HD)
    key_mask = token_mask(reached[0], rows_here)
    picked = jnp.argmax(adapter_pick[0]) * RANK
    adapt_in_used = lax.dynamic_slice_in_dim(adapt_in, picked, RANK, 2)
    adapt_out_used = lax.dynamic_slice_in_dim(adapt_out, picked, RANK, 1)
    mix_in_used = lax.dynamic_slice_in_dim(adapt_in_out, picked, RANK, 1)
    mix_out_used = lax.dynamic_slice_in_dim(adapt_out_out, picked, RANK, 0)
    lowrank = low(
        jnp.einsum("td,idr->itr", normed_in, adapt_in_used, preferred_element_type=float_kind)
    )
    matrices = (query_weight, key_weight, value_weight)
    query_raw, key_raw, value_raw = [
        dot(normed_in, matrices[projection]) + dot(lowrank[projection], adapt_out_used[projection])
        for projection in range(3)
    ]

    cot_planes = [None] * far
    cot_next, cot_first, query_raw, key_raw, value_raw = hold(
        (cot_next, cot_first, query_raw, key_raw, value_raw)
    )
    cot_later = turn(cot_next, axes, "z", 1)
    cot_planes[0] = gather_second(cot_first, axes)
    cot_first = gather_first(cot_next, axes)
    query_squares, key_squares = lax.psum(
        (jnp.sum(query_raw * query_raw, axis=1), jnp.sum(key_raw * key_raw, axis=1)), "tensor"
    )
    query_inverse = lax.rsqrt(query_squares / model_width + EPSILON)[:, None]
    key_inverse = lax.rsqrt(key_squares / model_width + EPSILON)[:, None]
    query_scale = wide(query_gain)
    key_scale = wide(key_gain)
    queries = low(
        rotate(
            (query_raw * query_inverse * query_scale).reshape(rows_here, heads_here, HD),
            cosine_table,
            sine_table,
        )
    )
    keys = low(
        rotate(
            (key_raw * key_inverse * key_scale).reshape(rows_here, heads_here, HD),
            cosine_table,
            sine_table,
        )
    )
    values = low(value_raw).reshape(rows_here, heads_here, HD)
    score_scale = HD ** (-0.5)
    scores = (
        jnp.einsum("qhd,khd->hqk", queries, keys, preferred_element_type=float_kind) * score_scale
    )
    scores = jnp.where(key_mask[None], scores, MASKED_SCORE)
    row_max = jnp.max(scores, axis=2, keepdims=True)
    raised = jnp.exp(scores - row_max)
    row_total = jnp.sum(raised, axis=2, keepdims=True)
    weights_half = low(raised / row_total)
    log_total = row_max + jnp.log(row_total)
    attended = low(
        jnp.einsum(
            "hqk,khd->qhd", weights_half, values, preferred_element_type=float_kind
        ).reshape(rows_here, local_width)
    )

    cot_next, cot_first, cot_planes[0], attended = hold(
        (cot_later, cot_first, cot_planes[0], attended)
    )
    cot_later = turn(cot_next, axes, "z", 1)
    cot_planes[1] = gather_second(cot_first, axes)
    cot_first = gather_first(cot_next, axes)
    gates = (expert_gate, turn(expert_gate, axes, "c", 1))
    ups = (expert_up, turn(expert_up, axes, "c", 1))
    down_tall = expert_down.reshape(-1, model_width)
    downs = (down_tall, turn(down_tall, axes, "c", 1))
    picks = lax.all_gather(adapter_pick.astype(float_kind), "expert", axis=0, tiled=True)
    mixing_pad = jnp.zeros((local_width, 128 - RANK), half_kind)
    output_used = jnp.concatenate([output_weight, mix_in_used, mixing_pad], axis=1)
    branch_rows = scatter_tensor(low(dot(attended, output_used)), axes)
    mixed_rows = low(branch_rows[:, model_width : model_width + RANK])
    resid_rows = (
        wide(own_rows(tokens)) + branch_rows[:, :model_width] + dot(mixed_rows, mix_out_used)
    )
    second_inverse = lax.rsqrt(
        jnp.mean(resid_rows * resid_rows, axis=1, keepdims=True) + EPSILON
    )
    norm_plane = low(resid_rows * second_inverse * second_gain)

    cot_next, cot_first, cot_planes[1], norm_plane, gates, ups, downs = hold(
        (cot_later, cot_first, cot_planes[1], norm_plane, gates, ups, downs)
    )
    norm_next = turn(norm_plane, axes, "z", 1)
    norm_first = gather_first(norm_plane, axes)
    cot_planes[2] = gather_second(cot_first, axes)
    cot_first = gather_first(cot_next, axes)
    backs = [None] * far

    def hidden_step(index):
        backs[index] = hidden_call(cot_planes[index], *downs, spread, experts_here)

    hidden_step(0)

    norm_planes = [None] * far
    norm_next, norm_first, cot_planes[2], cot_first, backs[0] = hold(
        (norm_next, norm_first, cot_planes[2], cot_first, backs[0])
    )
    norm_later = turn(norm_next, axes, "z", 1)
    norm_planes[0] = gather_second(norm_first, axes)
    norm_first = gather_first(norm_next, axes)
    cot_planes[3] = gather_second(cot_first, axes)
    hidden_step(1)
    hidden_step(2)

    norm_next, norm_first, norm_planes[0], cot_planes[3], backs[1], backs[2] = hold(
        (norm_later, norm_first, norm_planes[0], cot_planes[3], backs[1], backs[2])
    )
    norm_later = turn(norm_next, axes, "z", 1)
    norm_planes[1] = gather_second(norm_first, axes)
    norm_first = gather_first(norm_next, axes)
    gate_grads, up_grads, hiddens = [None] * far, [None] * far, [None] * far

    def gate_step(index):
        back, side = backs[index]
        gate_grads[index], up_grads[index], hiddens[index] = gate_call(
            norm_planes[index], gates, ups, spread, side, back
        )

    parts = [None] * far

    def rows_step(index):
        parts[index] = rows_call(gate_grads[index], up_grads[index], gates, ups, near + span)

    hidden_step(3)
    gate_step(0)

    norm_next, norm_first, norm_planes[1], backs[3], gate_grads[0] = hold(
        (norm_later, norm_first, norm_planes[1], backs[3], gate_grads[0])
    )
    norm_planes[2] = gather_second(norm_first, axes)
    norm_first = gather_first(norm_next, axes)
    gate_step(1)
    rows_step(1)

    norm_first, norm_planes[2], parts[1] = hold((norm_first, norm_planes[2], parts[1]))
    norm_planes[3] = gather_second(norm_first, axes)
    came = [None] * far
    kept = [None] * far
    sums = [None] * far
    came[1] = scatter_first(parts[1], axes)
    gate_step(2)
    rows_step(2)

    norm_planes[3], came[1], parts[2] = hold((norm_planes[3], came[1], parts[2]))
    kept[1], came[1] = scatter_second(parts[1], came[1], axes)
    came[2] = scatter_first(parts[2], axes)
    gate_step(3)
    rows_step(3)

    kept[1], came[1], came[2], parts[3] = hold((kept[1], came[1], came[2], parts[3]))
    sums[1] = scatter_last(kept[1], came[1])
    ring_sum = turn(low(sums[1]), axes, "z", 1)
    kept[2], came[2] = scatter_second(parts[2], came[2], axes)
    came[3] = scatter_first(parts[3], axes)
    rows_step(0)

    ring_sum, kept[2], came[2], came[3], parts[0] = hold(
        (ring_sum, kept[2], came[2], came[3], parts[0])
    )
    ring_sum = turn(low(wide(ring_sum) + scatter_last(kept[2], came[2])), axes, "z", 1)
    kept[3], came[3] = scatter_second(parts[3], came[3], axes)
    came[0] = scatter_first(parts[0], axes)
    mixes = [None] * far

    def down_step(index):
        mixes[index] = down_call(hiddens[index], downs, near + span)

    down_step(1)
    down_step(2)

    ring_sum, kept[3], came[3], came[0], mixes[1], mixes[2] = hold(
        (ring_sum, kept[3], came[3], came[0], mixes[1], mixes[2])
    )
    ring_sum = turn(low(wide(ring_sum) + scatter_last(kept[3], came[3])), axes, "z", 1)
    kept[0], came[0] = scatter_second(parts[0], came[0], axes)
    mix_came = [None] * far
    mix_kept = [None] * far
    mix_came[1] = scatter_first(mixes[1], axes)
    down_step(3)
    down_step(0)

    ring_sum, kept[0], came[0], mix_came[1], mixes[3], mixes[0] = hold(
        (ring_sum, kept[0], came[0], mix_came[1], mixes[3], mixes[0])
    )
    ffn_rows_grad = wide(ring_sum) + scatter_last(kept[0], came[0])
    second_scaled = ffn_rows_grad * second_gain
    resid_grad_rows = wide(cotangent_rows) + norm_back(
        second_scaled,
        resid_rows,
        second_inverse,
        model_width,
        jnp.sum(second_scaled * resid_rows, axis=1, keepdims=True),
    )
    branch_sent = jnp.concatenate(
        [low(resid_grad_rows), mixed_rows, jnp.zeros((row_share, 128 - RANK), half_kind)], axis=1
    )
    branch_whole = place_tensor(branch_sent, axes, half_kind)
    mix_kept[1], mix_came[1] = scatter_second(mixes[1], mix_came[1], axes)

    branch_whole, mix_kept[1], mix_came[1] = hold((branch_whole, mix_kept[1], mix_came[1]))
    mix_sum = turn(low(scatter_last(mix_kept[1], mix_came[1])), axes, "z", 1)
    mix_came[2] = scatter_first(mixes[2], axes)
    branch_grad = branch_whole[:, :model_width]
    mixed = branch_whole[:, model_width : model_width + RANK]
    mixed_grad = low(dot_t(branch_grad, mix_out_used))
    attended_grad = low(dot_t(branch_grad, output_weight) + dot_t(mixed_grad, mix_in_used))
    attended_grad = attended_grad.reshape(rows_here, heads_here, HD)
    scores = (
        jnp.einsum("qhd,khd->hqk", queries, keys, preferred_element_type=float_kind) * score_scale
    )
    softmax_full = jnp.where(key_mask[None], jnp.exp(scores - log_total), 0.0)
    softmax_half = low(softmax_full)
    value_grad = low(
        jnp.einsum("hqk,qhd->khd", softmax_half, attended_grad, preferred_element_type=float_kind)
    )
    prob_grad = jnp.einsum("qhd,khd->hqk", attended_grad, values, preferred_element_type=float_kind)
    score_grad = low(
        softmax_full * (prob_grad - jnp.sum(softmax_full * prob_grad, axis=2, keepdims=True))
    )
    query_grad = (
        jnp.einsum("hqk,khd->qhd", score_grad, keys, preferred_element_type=float_kind)
        * score_scale
    )
    key_grad = (
        jnp.einsum("hqk,qhd->khd", score_grad, queries, preferred_element_type=float_kind)
        * score_scale
    )
    query_scaled = (
        unrotate(query_grad, cosine_table, sine_table).reshape(rows_here, local_width) * query_scale
    )
    key_scaled = (
        unrotate(key_grad, cosine_table, sine_table).reshape(rows_here, local_width) * key_scale
    )

    query_scaled, key_scaled, value_grad, mix_sum, mix_came[2] = hold(
        (query_scaled, key_scaled, value_grad, mix_sum, mix_came[2])
    )
    mix_kept[2], mix_came[2] = scatter_second(mixes[2], mix_came[2], axes)
    mix_came[3] = scatter_first(mixes[3], axes)
    query_inner, key_inner = lax.psum(
        (jnp.sum(query_scaled * query_raw, axis=1), jnp.sum(key_scaled * key_raw, axis=1)), "tensor"
    )
    query_raw_grad = low(
        norm_back(query_scaled, query_raw, query_inverse, model_width, query_inner[:, None])
    )
    key_raw_grad = low(
        norm_back(key_scaled, key_raw, key_inverse, model_width, key_inner[:, None])
    )
    value_raw_grad = value_grad.reshape(rows_here, local_width)
    raw_grads = (query_raw_grad, key_raw_grad, value_raw_grad)
    lowrank_part = low(
        jnp.concatenate(
            [dot_t(raw_grads[projection], adapt_out_used[projection]) for projection in range(3)],
            axis=1,
        )
    )
    normed_part = low(
        dot_t(query_raw_grad, query_weight)
        + dot_t(key_raw_grad, key_weight)
        + dot_t(value_raw_grad, value_weight)
    )

    normed_part, lowrank_part, mix_kept[2], mix_came[2], mix_came[3] = hold(
        (normed_part, lowrank_part, mix_kept[2], mix_came[2], mix_came[3])
    )
    mix_sum = turn(low(wide(mix_sum) + scatter_last(mix_kept[2], mix_came[2])), axes, "z", 1)
    mix_kept[3], mix_came[3] = scatter_second(mixes[3], mix_came[3], axes)
    mix_came[0] = scatter_first(mixes[0], axes)
    lowrank_grad = low(sum_tensor(lowrank_part, axes))
    normed_grad_rows = scatter_tensor(normed_part, axes)
    lowrank_rows = own_rows(lowrank_grad)
    for projection in range(3):
        normed_grad_rows = normed_grad_rows + dot_t(
            lowrank_rows[:, projection * RANK : (projection + 1) * RANK], adapt_in_used[projection]
        )
    first_scaled = normed_grad_rows * first_gain
    inputs_rows = own_rows(inputs)
    input_grad_rows = resid_grad_rows + norm_back(
        first_scaled,
        inputs_rows,
        own_rows(first_inverse),
        model_width,
        jnp.sum(first_scaled * inputs_rows, axis=1, keepdims=True),
    )
    normed_share = lax.dynamic_slice_in_dim(
        normed_in, tensor_rank * column_share, column_share, 1
    )
    branch_share = lax.dynamic_slice_in_dim(
        branch_grad, tensor_rank * column_share, column_share, 1
    )
    compact = low(
        jnp.concatenate(
            [t_dot(lowrank_grad, normed_share), t_dot(mixed, branch_share)]
            + [t_dot(lowrank[projection], raw_grads[projection]) for projection in range(3)]
            + [t_dot(mixed_grad, attended)],
            axis=0,
        )
    )

    input_grad_rows, compact, mix_sum, mix_kept[3], mix_came[3], mix_came[0] = hold(
        (low(input_grad_rows), compact, mix_sum, mix_kept[3], mix_came[3], mix_came[0])
    )
    input_grad = place_tensor(input_grad_rows, axes, float_kind)
    mix_sum = turn(low(wide(mix_sum) + scatter_last(mix_kept[3], mix_came[3])), axes, "z", 1)
    mix_kept[0], mix_came[0] = scatter_second(mixes[0], mix_came[0], axes)
    layer_rows = low(resid_rows + wide(mix_sum) + scatter_last(mix_kept[0], mix_came[0]))
    layer_out = swap_columns(layer_rows, axes)

    kinds = compact.shape[0] // RANK
    trees = jnp.concatenate(
        ring(jnp.concatenate(ring(compact, axes, "x"), axis=0), axes, "z"), axis=0
    )
    tree_index = (
        (owner_rank // near + far - jnp.arange(far, dtype=jnp.int32)[:, None]) % far * near
        + (owner_rank % near + near - jnp.arange(near, dtype=jnp.int32)[None, :]) % near
    ).reshape(-1)
    tree_picks = low(
        dot(
            (tree_index[:, None] == jnp.arange(owners, dtype=jnp.int32)[None, :]).astype(
                float_kind
            ),
            picks,
        )
    )
    trees = trees.reshape(owners, kinds, RANK, column_share)
    grad_adapt_out = jnp.einsum(
        "sa,skrc->karc", tree_picks, trees[:, 4:7], preferred_element_type=float_kind
    ).reshape(3, -1, column_share)
    grad_adapt_in_out = jnp.einsum(
        "sa,src->car", tree_picks, trees[:, 7], preferred_element_type=float_kind
    ).reshape(column_share, -1)
    shared = place_tensor(
        trees[:, :4].reshape(owners * 4 * RANK, column_share), axes, half_kind
    ).reshape(tensor_count, owners, 4, RANK, column_share)
    grad_adapt_in = jnp.einsum(
        "sa,tskrc->ktcar", tree_picks, shared[:, :, :3], preferred_element_type=float_kind
    ).reshape(3, model_width, -1)
    grad_adapt_out_out = jnp.einsum(
        "sa,tsrc->artc", tree_picks, shared[:, :, 3], preferred_element_type=float_kind
    ).reshape(-1, model_width)
    return (
        layer_out,
        input_grad,
        grad_adapt_in,
        grad_adapt_out,
        grad_adapt_in_out,
        grad_adapt_out_out,
    )


def solution(mesh):
    return jax.shard_map(
        body,
        mesh=mesh,
        in_specs=(
            P("expert", None),
            P("expert", None),
            P(),
            P(),
            P("tensor"),
            P("tensor"),
            P(None, "tensor"),
            P(None, "tensor"),
            P(None, "tensor"),
            P("tensor", None),
            P("expert", None, "tensor"),
            P("expert", None, "tensor"),
            P("expert", "tensor", None),
            P(),
            P(None, None, "tensor"),
            P("tensor", None),
            P(),
            P("expert", None),
            P("expert", None),
            P("expert"),
            P("expert", None),
        ),
        out_specs=(
            P("expert", "tensor"),
            P("expert", None),
            P(),
            P(None, None, "tensor"),
            P("tensor", None),
            P(),
        ),
        check_vma=False,
    )
```

time: 959 us -> 678 us (0.71)
  matrix products: 255 us -> 47.7 us
  waiting for transfers between devices: 352 us -> 165 us
  Pallas kernels: 0 us -> 182 us
  local copies, waits for them, and re-layouts: 155 us -> 75.8 us
  other arithmetic: 56.5 us -> 71.2 us
    dot_general x56 -> x27, matrix products: 243 us -> 35.1 us  [the longest x9 20.4 us: dot(): return jnp.dot(left, right, preferred_element_type=jnp.float32)]
    ppermute x114 -> x101, waiting for transfers between devices: 352 us -> 165 us  [turn(): return lax.ppermute(array, axis, pairs)]
    pallas_call x0 -> x16, Pallas kernels: none -> 182 us  [kernel_call(): pl.pallas_call(kernel, grid=(grid,), in_specs=[pl.BlockSpec(block, index)...]
    unnamed x299 -> x261, local copies, waits for them, and re-layouts: 79.9 us -> 17.4 us
    convert_element_type x54 -> x22, other arithmetic: 39.2 us -> 18.8 us  [the longest x17 16.3 us: low(): return array.astype(jnp.bfloat16)]
    concatenate x20 -> x3, local copies, waits for them, and re-layouts: 26 us -> 6.42 us  [the longest x1 4.57 us: body(): jnp.concatenate([output_weight, mix_in_used, mixing_pad], axis=1)]
    add x0 -> x31, other arithmetic: none -> 19.5 us  [the longest x8 8.77 us: scatter_second(): second = wide(pieces[span]) + wide(came[1])]
    reshape x0 -> x4, local copies, waits for them, and re-layouts: none -> 10.2 us  [the longest x1 2.57 us: body(): (query_raw * query_inverse * query_scale).reshape(rows_here, heads_here, HD)]
  transfers between devices with their start and end apart: 114 -> 101, of which waited for: 57 -> 28; matrix products, arithmetic and copies ran while one was open for 41% -> 23% of each run, Pallas kernels for 0% -> 27%
where the time goes in v2:
time: 678 us; the launch traced here: 669 us
  Pallas kernels  182 us (27%)
  waiting for transfers between devices  165 us (24%)
  starting transfers between devices  89.3 us (13%)
  local copies, waits for them, and re-layouts  75.8 us (11%)
  other arithmetic  71.2 us (11%)
  matrix products  47.7 us (7%)
  blocking collectives  33.2 us (5%)
    pallas_call x16, Pallas kernels, kernel_call(): pl.pallas_call(kernel, grid=(grid,), in_specs=[pl.BlockSpec(block, index)...  182 us
    ppermute x101, waiting for transfers between devices, turn(): return lax.ppermute(array, axis, pairs)  165 us
    ppermute x101, starting transfers between devices, turn(): return lax.ppermute(array, axis, pairs)  89.3 us
    dot_general x9, matrix products, dot(): return jnp.dot(left, right, preferred_element_type=jnp.float32)  20.4 us
    all_gather x1, blocking collectives, body(): lax.all_gather(adapter_pick.astype(float_kind), 'expert', axis=0, tiled=T...  18.5 us
    unnamed x261, local copies, waits for them, and re-layouts  17.4 us
    convert_element_type x17, other arithmetic, low(): return array.astype(jnp.bfloat16)  16.3 us
  transfers between devices with their start and end apart: 101, of which 28 were waited for; matrix products, arithmetic and copies ran while one was open for 23% of the time, Pallas kernels for 27%

profile of v2, /device:TPU:0, one launch (start us, length us, event | category | flops | bytes accessed | tf_op | source)
XLA Modules:
  0.0 668.8 jit_solution(15600576551858658082)
XLA Ops:
  19.6 3.5 multiply_convert_fusion.1
  23.0 4.0 fusion.130
  29.2 4.5 fusion.129
  36.1 3.5 fusion.27
  44.8 4.6 concatenate.129
  49.4 18.5 %all-gather = f32[8,1,8]{2,1,0:T(1,128)S(1)} all-gather(f32[1,1,8]{2,1,0:T(1,128)S(1)} %copy-done.113), channel_id=1, replica_groups=mesh['expert'=8,'tensor'=4] {'expert'}, dimensions={0}, use_global_device_ids=true | all-gather | bytes 288 | tf_op jit(solution)/shard_map/all_gather | solution.py:527
  74.8 5.9 all-reduce.1
  105.7 9.2 %collective-permute-done.6.refs_1_ = bf16[128,2176]{1,0:T(8,128)(2,1)S(1)} collective-permute-done((bf16[128,2176]{1,0:T(8,128)(2,1)S(1)}, bf16[128,2176]{1,0:T(8,128)(2,1)S(1)}, u32[]{:S(2)}, u32[]{:S(2)}) %collective-permute-start.6) | collective-permute-done | bytes 557088 | tf_op jit(solution)/shard_map/ppermute | solution.py:90
  123.0 6.2 collective-permute-done.12
  129.9 13.6 %collective-permute-done.9 = bf16[128,2176]{1,0:T(8,128)(2,1)S(1)} collective-permute-done((bf16[128,2176]{1,0:T(8,128)(2,1)S(1)}, bf16[128,2176]{1,0:T(8,128)(2,1)S(1)}, u32[]{:S(2)}, u32[]{:S(2)}) %collective-permute-start.9) | collective-permute-done | bytes 557088 | tf_op jit(solution)/shard_map/ppermute | solution.py:90
  148.0 8.9 %collective-permute-done.13.refs_1_ = bf16[128,2176]{1,0:T(8,128)(2,1)S(1)} collective-permute-done((bf16[128,2176]{1,0:T(8,128)(2,1)S(1)}, bf16[128,2176]{1,0:T(8,128)(2,1)S(1)}, u32[]{:S(2)}, u32[]{:S(2)}) %collective-permute-start.13) | collective-permute-done | bytes 557088 | tf_op jit(solution)/shard_map/ppermute | solution.py:90
  164.7 8.5 %shard_map.244 = (bf16[2,512,1024]{2,1,0:T(8,128)(2,1)}, bf16[512,128]{1,0:T(8,128)(2,1)S(1)}) custom-call(bf16[128,2176]{1,0:T(8,128)(2,1)S(1)} %pad_maximum_fusion.refs_0_, bf16[128,2176]{1,0:T(8,128)(2,1)S(1)} %collective-permute-done.6.refs_1_, bf16[128,2176]{1,0:T(8,128)(2,1)} %pad_maximum_fusion.1.refs_2_, bf16[128,2176]{1,0:T(8,128)(2,1)} %copy-done.118, ...), custom_call_target="tpu_custom_call" | custom-call | flops 4294967296 | bytes 10878976 | tf_op jit(solution)/shard_map/pallas_call | solution.py:235
  176.7 8.6 %collective-permute-done.21.refs_1_ = bf16[128,2176]{1,0:T(8,128)(2,1)S(1)} collective-permute-done((bf16[128,2176]{1,0:T(8,128)(2,1)S(1)}, bf16[128,2176]{1,0:T(8,128)(2,1)S(1)}, u32[]{:S(2)}, u32[]{:S(2)}) %collective-permute-start.21) | collective-permute-done | bytes 557088 | tf_op jit(solution)/shard_map/ppermute | solution.py:90
  189.2 8.6 %shard_map.245 = (bf16[2,512,1024]{2,1,0:T(8,128)(2,1)}, bf16[512,128]{1,0:T(8,128)(2,1)S(1)}) custom-call(bf16[128,2176]{1,0:T(8,128)(2,1)S(1)} %pad_maximum_fusion.2.refs_0_, bf16[128,2176]{1,0:T(8,128)(2,1)S(1)} %collective-permute-done.13.refs_1_, bf16[128,2176]{1,0:T(8,128)(2,1)} %copy-done.71, bf16[128,2176]{1,0:T(8,128)(2,1)} %copy-done.119, ...), custom_call_target="tpu_custom_call" | custom-call | flops 4294967296 | bytes 10878976 | tf_op jit(solution)/shard_map/pallas_call | solution.py:235
  202.2 8.5 %shard_map.246 = (bf16[2,512,1024]{2,1,0:T(8,128)(2,1)}, bf16[512,128]{1,0:T(8,128)(2,1)S(1)}) custom-call(bf16[128,2176]{1,0:T(8,128)(2,1)S(1)} %pad_maximum_fusion.4.refs_0_, bf16[128,2176]{1,0:T(8,128)(2,1)S(1)} %collective-permute-done.21.refs_1_, bf16[128,2176]{1,0:T(8,128)(2,1)} %copy-done.72, bf16[128,2176]{1,0:T(8,128)(2,1)} %copy-done.121, ...), custom_call_target="tpu_custom_call" | custom-call | flops 4294967296 | bytes 10878976 | tf_op jit(solution)/shard_map/pallas_call | solution.py:235
  210.8 8.1 %collective-permute-done.28.refs_1_ = bf16[128,2048]{1,0:T(8,128)(2,1)S(1)} collective-permute-done((bf16[128,2048]{1,0:T(8,128)(2,1)S(1)}, bf16[128,2048]{1,0:T(8,128)(2,1)S(1)}, u32[]{:S(2)}, u32[]{:S(2)}) %collective-permute-start.28) | collective-permute-done | bytes 524320 | tf_op jit(solution)/shard_map/ppermute | solution.py:90
  222.9 14.4 %shard_map.248 = (bf16[2,512,1024]{2,1,0:T(8,128)(2,1)}, bf16[2,512,1024]{2,1,0:T(8,128)(2,1)}, bf16[2,512,1024]{2,1,0:T(8,128)(2,1)}) custom-call(bf16[128,2048]{1,0:T(8,128)(2,1)S(1)} %pad_maximum_fusion.8.refs_0_, bf16[128,2048]{1,0:T(8,128)(2,1)S(1)} %collective-permute-done.28.refs_1_, bf16[128,2048]{1,0:T(8,128)(2,1)S(1)} %pad_maximum_fusion.9.refs_2_, ...), custom_call_target="tpu_custom_call" | custom-call | flops 8589934592 | bytes 21364736 | tf_op jit(solution)/shard_map/pallas_call | solution.py:235
  237.3 8.5 %shard_map.259 = (bf16[128,2048]{1,0:T(8,128)(2,1)S(1)}, bf16[128,2048]{1,0:T(8,128)(2,1)}, bf16[128,2048]{1,0:T(8,128)(2,1)S(1)}, bf16[128,2048]{1,0:T(8,128)(2,1)}) custom-call(bf16[2,512,1024]{2,1,0:T(8,128)(2,1)} %get-tuple-element.384.hidden, bf16[1024,2048]{1,0:T(8,128)(2,1)} %bitcast.238, bf16[1024,2048]{1,0:T(8,128)(2,1)} %collective-permute-done.17.refs_5_.down_other), custom_call_target="tpu_custom_call" | custom-call | flops 4294967296 | bytes 10485760 | tf_op jit(solution)/shard_map/pallas_call | solution.py:235
  249.9 8.5 %shard_map.247 = (bf16[2,512,1024]{2,1,0:T(8,128)(2,1)}, bf16[512,128]{1,0:T(8,128)(2,1)S(1)}) custom-call(bf16[128,2176]{1,0:T(8,128)(2,1)S(1)} %pad_maximum_fusion.6.refs_0_, bf16[128,2176]{1,0:T(8,128)(2,1)S(1)} %collective-permute-done.30.refs_1_, bf16[128,2176]{1,0:T(8,128)(2,1)} %copy-done.73, bf16[128,2176]{1,0:T(8,128)(2,1)} %copy-done.120, ...), custom_call_target="tpu_custom_call" | custom-call | flops 4294967296 | bytes 10878976 | tf_op jit(solution)/shard_map/pallas_call | solution.py:235
  258.5 4.7 collective-permute-done.35.refs_1_
  267.3 14.4 %shard_map.249 = (bf16[2,512,1024]{2,1,0:T(8,128)(2,1)}, bf16[2,512,1024]{2,1,0:T(8,128)(2,1)}, bf16[2,512,1024]{2,1,0:T(8,128)(2,1)}) custom-call(bf16[128,2048]{1,0:T(8,128)(2,1)S(1)} %pad_maximum_fusion.10.refs_0_, bf16[128,2048]{1,0:T(8,128)(2,1)S(1)} %collective-permute-done.35.refs_1_, bf16[128,2048]{1,0:T(8,128)(2,1)S(1)} %pad_maximum_fusion.11.refs_2_, ...), custom_call_target="tpu_custom_call" | custom-call | flops 8589934592 | bytes 21364736 | tf_op jit(solution)/shard_map/pallas_call | solution.py:235
  281.7 13.9 %shard_map.250 = (bf16[128,2048]{1,0:T(8,128)(2,1)S(1)}, bf16[128,2048]{1,0:T(8,128)(2,1)S(1)}, bf16[128,2048]{1,0:T(8,128)(2,1)S(1)}, bf16[128,2048]{1,0:T(8,128)(2,1)}) custom-call(bf16[2,512,1024]{2,1,0:T(8,128)(2,1)} %get-tuple-element.291.gate_grad, bf16[2,512,1024]{2,1,0:T(8,128)(2,1)} %get-tuple-element.292.up_grad, bf16[4,2048,256]{2,1,0:T(8,128)(2,1)} %gate_own.3, ...), custom_call_target="tpu_custom_call" | custom-call | flops 8589934592 | bytes 20971520 | tf_op jit(solution)/shard_map/pallas_call | solution.py:235
  295.6 13.8 %shard_map.255 = (bf16[128,2048]{1,0:T(8,128)(2,1)S(1)}, bf16[128,2048]{1,0:T(8,128)(2,1)S(1)}, bf16[128,2048]{1,0:T(8,128)(2,1)S(1)}, bf16[128,2048]{1,0:T(8,128)(2,1)}) custom-call(bf16[2,512,1024]{2,1,0:T(8,128)(2,1)} %get-tuple-element.341.gate_grad, bf16[2,512,1024]{2,1,0:T(8,128)(2,1)} %get-tuple-element.342.up_grad, bf16[4,2048,256]{2,1,0:T(8,128)(2,1)} %gate_own.3, ...), custom_call_target="tpu_custom_call" | custom-call | flops 8589934592 | bytes 20971520 | tf_op jit(solution)/shard_map/pallas_call | solution.py:235
  314.4 14.4 %shard_map.251 = (bf16[2,512,1024]{2,1,0:T(8,128)(2,1)}, bf16[2,512,1024]{2,1,0:T(8,128)(2,1)}, bf16[2,512,1024]{2,1,0:T(8,128)(2,1)}) custom-call(bf16[128,2048]{1,0:T(8,128)(2,1)S(1)} %pad_maximum_fusion.12.refs_0_, bf16[128,2048]{1,0:T(8,128)(2,1)S(1)} %collective-permute-done.39.refs_1_, bf16[128,2048]{1,0:T(8,128)(2,1)S(1)} %pad_maximum_fusion.13.refs_2_, ...), custom_call_target="tpu_custom_call" | custom-call | flops 8589934592 | bytes 21364736 | tf_op jit(solution)/shard_map/pallas_call | solution.py:235
  328.8 14.2 %shard_map.252 = (bf16[128,2048]{1,0:T(8,128)(2,1)S(1)}, bf16[128,2048]{1,0:T(8,128)(2,1)S(1)}, bf16[128,2048]{1,0:T(8,128)(2,1)S(1)}, bf16[128,2048]{1,0:T(8,128)(2,1)}) custom-call(bf16[2,512,1024]{2,1,0:T(8,128)(2,1)} %get-tuple-element.308.gate_grad, bf16[2,512,1024]{2,1,0:T(8,128)(2,1)} %get-tuple-element.309.up_grad, bf16[4,2048,256]{2,1,0:T(8,128)(2,1)} %gate_own.3, ...), custom_call_target="tpu_custom_call" | custom-call | flops 8589934592 | bytes 20971520 | tf_op jit(solution)/shard_map/pallas_call | solution.py:235
  350.9 14.4 %shard_map.253 = (bf16[2,512,1024]{2,1,0:T(8,128)(2,1)}, bf16[2,512,1024]{2,1,0:T(8,128)(2,1)}, bf16[2,512,1024]{2,1,0:T(8,128)(2,1)}) custom-call(bf16[128,2048]{1,0:T(8,128)(2,1)S(1)} %pad_maximum_fusion.14.refs_0_, bf16[128,2048]{1,0:T(8,128)(2,1)S(1)} %collective-permute-done.41.refs_1_, bf16[128,2048]{1,0:T(8,128)(2,1)S(1)} %pad_maximum_fusion.15.refs_2_, ...), custom_call_target="tpu_custom_call" | custom-call | flops 8589934592 | bytes 21364736 | tf_op jit(solution)/shard_map/pallas_call | solution.py:235
  365.2 13.9 %shard_map.254 = (bf16[128,2048]{1,0:T(8,128)(2,1)S(1)}, bf16[128,2048]{1,0:T(8,128)(2,1)S(1)}, bf16[128,2048]{1,0:T(8,128)(2,1)S(1)}, bf16[128,2048]{1,0:T(8,128)(2,1)}) custom-call(bf16[2,512,1024]{2,1,0:T(8,128)(2,1)} %get-tuple-element.325.gate_grad, bf16[2,512,1024]{2,1,0:T(8,128)(2,1)} %get-tuple-element.326.up_grad, bf16[4,2048,256]{2,1,0:T(8,128)(2,1)} %gate_own.3, ...), custom_call_target="tpu_custom_call" | custom-call | flops 8589934592 | bytes 20971520 | tf_op jit(solution)/shard_map/pallas_call | solution.py:235
  390.6 8.4 %shard_map.256 = (bf16[128,2048]{1,0:T(8,128)(2,1)S(1)}, bf16[128,2048]{1,0:T(8,128)(2,1)S(1)}, bf16[128,2048]{1,0:T(8,128)(2,1)S(1)}, bf16[128,2048]{1,0:T(8,128)(2,1)}) custom-call(bf16[2,512,1024]{2,1,0:T(8,128)(2,1)} %get-tuple-element.358.hidden, bf16[1024,2048]{1,0:T(8,128)(2,1)} %bitcast.240, bf16[1024,2048]{1,0:T(8,128)(2,1)} %collective-permute-done.17.refs_5_.down_other), custom_call_target="tpu_custom_call" | custom-call | flops 4294967296 | bytes 10485760 | tf_op jit(solution)/shard_map/pallas_call | solution.py:235
  399.1 5.3 collective-permute-done.50
  416.2 8.5 %shard_map.257 = (bf16[128,2048]{1,0:T(8,128)(2,1)S(1)}, bf16[128,2048]{1,0:T(8,128)(2,1)}, bf16[128,2048]{1,0:T(8,128)(2,1)S(1)}, bf16[128,2048]{1,0:T(8,128)(2,1)}) custom-call(bf16[2,512,1024]{2,1,0:T(8,128)(2,1)} %get-tuple-element.363.hidden, bf16[1024,2048]{1,0:T(8,128)(2,1)} %bitcast.241, bf16[1024,2048]{1,0:T(8,128)(2,1)} %collective-permute-done.17.refs_5_.down_other), custom_call_target="tpu_custom_call" | custom-call | flops 4294967296 | bytes 10485760 | tf_op jit(solution)/shard_map/pallas_call | solution.py:235
  424.8 6.9 %collective-permute-done.55 = bf16[64,2048]{1,0:T(8,128)(2,1)} collective-permute-done((bf16[64,2048]{1,0:T(8,128)(2,1)}, bf16[64,2048]{1,0:T(8,128)(2,1)}, u32[]{:S(2)}, u32[]{:S(2)}) %collective-permute-start.55) | collective-permute-done | bytes 262176 | tf_op jit(solution)/shard_map/ppermute | solution.py:90
  442.5 8.7 %shard_map.258 = (bf16[128,2048]{1,0:T(8,128)(2,1)S(1)}, bf16[128,2048]{1,0:T(8,128)(2,1)}, bf16[128,2048]{1,0:T(8,128)(2,1)S(1)}, bf16[128,2048]{1,0:T(8,128)(2,1)}) custom-call(bf16[2,512,1024]{2,1,0:T(8,128)(2,1)} %get-tuple-element.379.hidden, bf16[1024,2048]{1,0:T(8,128)(2,1)} %bitcast.242, bf16[1024,2048]{1,0:T(8,128)(2,1)} %collective-permute-done.17.refs_5_.down_other), custom_call_target="tpu_custom_call" | custom-call | flops 4294967296 | bytes 10485760 | tf_op jit(solution)/shard_map/pallas_call | solution.py:235
  465.6 10.9 %collective-permute-done.65 = bf16[128,2176]{1,0:T(8,128)(2,1)S(1)} collective-permute-done((bf16[128,2176]{1,0:T(8,128)(2,1)}, bf16[128,2176]{1,0:T(8,128)(2,1)S(1)}, u32[]{:S(2)}, u32[]{:S(2)}) %collective-permute-start.65) | collective-permute-done | bytes 557088 | tf_op jit(solution)/shard_map/ppermute | solution.py:90
  482.9 3.2 collective-permute-start.69
  506.8 3.6 slice.170
  518.8 8.8 %all-reduce = (f32[512]{0:T(512)S(1)}, f32[512]{0:T(512)S(1)}) all-reduce(f32[512]{0:T(512)S(1)} %multiply_reduce_fusion.4, f32[512]{0:T(512)S(1)} %multiply_reduce_fusion.3), channel_id=1, replica_groups=mesh['expert'=8,'tensor'=4] {'tensor'}, use_global_device_ids=true, to_apply=%region_17.18 | all-reduce | flops 1024 | bytes 8192 | tf_op jit(solution)/shard_map/psum | solution.py:700
  548.1 3.2 collective-permute-done.79
  557.2 12.4 %collective-permute-done.77 = bf16[128,2048]{1,0:T(8,128)(2,1)S(1)} collective-permute-done((bf16[128,2048]{1,0:T(8,128)(2,1)S(1)}, bf16[128,2048]{1,0:T(8,128)(2,1)S(1)}, u32[]{:S(2)}, u32[]{:S(2)}) %collective-permute-start.77) | collective-permute-done | bytes 524320 | tf_op jit(solution)/shard_map/ppermute | solution.py:90
  571.5 13.4 %collective-permute-done.80 = bf16[128,2048]{1,0:T(8,128)(2,1)S(1)} collective-permute-done((bf16[128,2048]{1,0:T(8,128)(2,1)S(1)}, bf16[128,2048]{1,0:T(8,128)(2,1)S(1)}, u32[]{:S(2)}, u32[]{:S(2)}) %collective-permute-start.80) | collective-permute-done | bytes 524320 | tf_op jit(solution)/shard_map/ppermute | solution.py:90
  592.5 6.2 collective-permute-done.86
  598.8 7.4 %collective-permute-done.87 = bf16[64,2048]{1,0:T(8,128)(2,1)S(1)} collective-permute-done((bf16[64,2048]{1,0:T(8,128)(2,1)S(1)}, bf16[64,2048]{1,0:T(8,128)(2,1)S(1)}, u32[]{:S(2)}, u32[]{:S(2)}) %collective-permute-start.87) | collective-permute-done | bytes 262176 | tf_op jit(solution)/shard_map/ppermute | solution.py:90
  606.3 4.2 collective-permute-done.95
  613.7 6.1 collective-permute-done.96
  620.2 8.2 %collective-permute-done.97 = bf16[256,512]{1,0:T(8,128)(2,1)S(1)} collective-permute-done((bf16[256,512]{1,0:T(8,128)(2,1)S(1)}, bf16[256,512]{1,0:T(8,128)(2,1)S(1)}, u32[]{:S(2)}, u32[]{:S(2)}) %collective-permute-start.97) | collective-permute-done | bytes 262176 | tf_op jit(solution)/shard_map/ppermute | solution.py:90
  635.1 8.0 %collective-permute-done.99 = bf16[512,512]{1,0:T(8,128)(2,1)} collective-permute-done((bf16[512,512]{1,0:T(8,128)(2,1)S(1)}, bf16[512,512]{1,0:T(8,128)(2,1)}, u32[]{:S(2)}, u32[]{:S(2)}) %collective-permute-start.99) | collective-permute-done | bytes 524320 | tf_op jit(solution)/shard_map/ppermute | solution.py:90
  653.4 3.7 copy.186
  657.1 5.3 reshape.547
  662.4 3.5 copy.196
  (702 shorter events, 258.5 us)
Async XLA Ops:
  4.5 68.0 %collective-permute-start = (bf16[128,2176]{1,0:T(8,128)(2,1)}, bf16[128,2176]{1,0:T(8,128)(2,1)}, u32[]{:S(2)}, u32[]{:S(2)}) collective-permute-start(bf16[128,2176]{1,0:T(8,128)(2,1)} %concatenate.121), channel_id=1, source_target_pairs={{0,8},{4,12},{8,16},{12,20},{16,24},{20,28},{24,0},{28,4},{1,9},{5... | collective-permute-start | bytes 1671176 | tf_op jit(solution)/shard_map/ppermute | solution.py:90
  8.7 60.8 %collective-permute-start.2 = (bf16[64,2176]{1,0:T(8,128)(2,1)S(1)}, bf16[64,2176]{1,0:T(8,128)(2,1)}, u32[]{:S(2)}, u32[]{:S(2)}) collective-permute-start(bf16[64,2176]{1,0:T(8,128)(2,1)S(1)} %get-tuple-element.484), channel_id=1, source_target_pairs={{0,2},{1,3},{2,0},{3,1},{4,6},{5,7},{6,4},{7,5},{8,10},{9,11},{10,... | collective-permute-start | bytes 835592 | tf_op jit(solution)/shard_map/ppermute | solution.py:90
  10.2 61.3 %collective-permute-start.1 = (bf16[64,2176]{1,0:T(8,128)(2,1)S(1)}, bf16[64,2176]{1,0:T(8,128)(2,1)}, u32[]{:S(2)}, u32[]{:S(2)}) collective-permute-start(bf16[64,2176]{1,0:T(8,128)(2,1)S(1)} %get-tuple-element.485), channel_id=1, source_target_pairs={{0,4},{4,0},{8,12},{12,8},{16,20},{20,16},{24,28},{28,24},{1,5},{5... | collective-permute-start | bytes 835592 | tf_op jit(solution)/shard_map/ppermute | solution.py:90
  11.7 147.7 %collective-permute-start.17 = (bf16[1024,2048]{1,0:T(8,128)(2,1)}, bf16[1024,2048]{1,0:T(8,128)(2,1)}, u32[]{:S(2)}, u32[]{:S(2)}) collective-permute-start(bf16[1024,2048]{1,0:T(8,128)(2,1)} %bitcast.234), channel_id=1, source_target_pairs={{0,1},{1,0},{2,3},{3,2},{4,5},{5,4},{6,7},{7,6},{8,9},{9,8},{10,11... | collective-permute-start | bytes 12582920 | tf_op jit(solution)/shard_map/ppermute | solution.py:90
  74.5 30.7 %collective-permute-start.3 = (bf16[128,2176]{1,0:T(8,128)(2,1)}, bf16[128,2176]{1,0:T(8,128)(2,1)}, u32[]{:S(2)}, u32[]{:S(2)}) collective-permute-start(bf16[128,2176]{1,0:T(8,128)(2,1)} %collective-permute-done), channel_id=1, source_target_pairs={{0,8},{4,12},{8,16},{12,20},{16,24},{20,28},{24,0},{28,4},{1,9},{5... | collective-permute-start | bytes 1671176 | tf_op jit(solution)/shard_map/ppermute | solution.py:90
  94.6 20.3 %collective-permute-start.6 = (bf16[128,2176]{1,0:T(8,128)(2,1)S(1)}, bf16[128,2176]{1,0:T(8,128)(2,1)S(1)}, u32[]{:S(2)}, u32[]{:S(2)}) collective-permute-start(bf16[128,2176]{1,0:T(8,128)(2,1)S(1)} %pad_maximum_fusion.refs_0_), channel_id=1, source_target_pairs={{0,2},{1,3},{2,0},{3,1},{4,6},{5,7},{6,4},{7,5},{8,10},{9,11},{10,... | collective-permute-start | bytes 1671176 | tf_op jit(solution)/shard_map/ppermute | solution.py:90
  105.0 54.4 %collective-permute-start.15 = (bf16[4,2048,256]{2,1,0:T(8,128)(2,1)S(1)}, bf16[4,2048,256]{2,1,0:T(8,128)(2,1)S(1)}, u32[]{:S(2)}, u32[]{:S(2)}) collective-permute-start(bf16[4,2048,256]{2,1,0:T(8,128)(2,1)S(1)} %copy-done.114), channel_id=1, source_target_pairs={{0,1},{1,0},{2,3},{3,2},{4,5},{5,4},{6,7},{7,6},{8,9},{9,8},{10,11... | collective-permute-start | bytes 12582920 | tf_op jit(solution)/shard_map/ppermute | solution.py:90
  105.4 54.1 %collective-permute-start.16 = (bf16[4,2048,256]{2,1,0:T(8,128)(2,1)S(1)}, bf16[4,2048,256]{2,1,0:T(8,128)(2,1)S(1)}, u32[]{:S(2)}, u32[]{:S(2)}) collective-permute-start(bf16[4,2048,256]{2,1,0:T(8,128)(2,1)S(1)} %copy-done.115), channel_id=1, source_target_pairs={{0,1},{1,0},{2,3},{3,2},{4,5},{5,4},{6,7},{7,6},{8,9},{9,8},{10,11... | collective-permute-start | bytes 12582920 | tf_op jit(solution)/shard_map/ppermute | solution.py:90
  198.1 22.2 %collective-permute-start.30 = (bf16[128,2176]{1,0:T(8,128)(2,1)S(1)}, bf16[128,2176]{1,0:T(8,128)(2,1)S(1)}, u32[]{:S(2)}, u32[]{:S(2)}) collective-permute-start(bf16[128,2176]{1,0:T(8,128)(2,1)S(1)} %pad_maximum_fusion.6.refs_0_), channel_id=1, source_target_pairs={{0,2},{1,3},{2,0},{3,1},{4,6},{5,7},{6,4},{7,5},{8,10},{9,11},{10,... | collective-permute-start | bytes 1671176 | tf_op jit(solution)/shard_map/ppermute | solution.py:90
  199.9 20.5 %collective-permute-start.31 = (bf16[128,2176]{1,0:T(8,128)(2,1)S(1)}, bf16[128,2176]{1,0:T(8,128)(2,1)S(1)}, u32[]{:S(2)}, u32[]{:S(2)}) collective-permute-start(bf16[128,2176]{1,0:T(8,128)(2,1)S(1)} %pad_maximum_fusion.7.refs_2_), channel_id=1, source_target_pairs={{0,4},{4,0},{8,12},{12,8},{16,20},{20,16},{24,28},{28,24},{1,5},{5... | collective-permute-start | bytes 1671176 | tf_op jit(solution)/shard_map/ppermute | solution.py:90
  200.6 18.3 %collective-permute-start.28 = (bf16[128,2048]{1,0:T(8,128)(2,1)S(1)}, bf16[128,2048]{1,0:T(8,128)(2,1)S(1)}, u32[]{:S(2)}, u32[]{:S(2)}) collective-permute-start(bf16[128,2048]{1,0:T(8,128)(2,1)S(1)} %pad_maximum_fusion.8.refs_0_), channel_id=1, source_target_pairs={{0,2},{1,3},{2,0},{3,1},{4,6},{5,7},{6,4},{7,5},{8,10},{9,11},{10,... | collective-permute-start | bytes 1572872 | tf_op jit(solution)/shard_map/ppermute | solution.py:90
  201.0 19.3 %collective-permute-start.29 = (bf16[128,2048]{1,0:T(8,128)(2,1)S(1)}, bf16[128,2048]{1,0:T(8,128)(2,1)}, u32[]{:S(2)}, u32[]{:S(2)}) collective-permute-start(bf16[128,2048]{1,0:T(8,128)(2,1)S(1)} %pad_maximum_fusion.9.refs_2_), channel_id=1, source_target_pairs={{0,4},{4,0},{8,12},{12,8},{16,20},{20,16},{24,28},{28,24},{1,5},{5... | collective-permute-start | bytes 1572872 | tf_op jit(solution)/shard_map/ppermute | solution.py:90
  220.4 38.0 %collective-permute-start.32 = (bf16[128,2048]{1,0:T(8,128)(2,1)S(1)}, bf16[128,2048]{1,0:T(8,128)(2,1)S(1)}, u32[]{:S(2)}, u32[]{:S(2)}) collective-permute-start(bf16[128,2048]{1,0:T(8,128)(2,1)S(1)} %collective-permute-done.25), channel_id=1, source_target_pairs={{0,8},{4,12},{8,16},{12,20},{16,24},{20,28},{24,0},{28,4},{1,9},{5... | collective-permute-start | bytes 1572872 | tf_op jit(solution)/shard_map/ppermute | solution.py:90
  263.2 46.2 %collective-permute-start.38 = (bf16[64,2048]{1,0:T(8,128)(2,1)S(1)}, bf16[64,2048]{1,0:T(8,128)(2,1)S(1)}, u32[]{:S(2)}, u32[]{:S(2)}) collective-permute-start(bf16[64,2048]{1,0:T(8,128)(2,1)S(1)} %get-tuple-element.488), channel_id=1, source_target_pairs={{0,2},{1,3},{2,0},{3,1},{4,6},{5,7},{6,4},{7,5},{8,10},{9,11},{10,... | collective-permute-start | bytes 786440 | tf_op jit(solution)/shard_map/ppermute | solution.py:90
  264.8 44.7 %collective-permute-start.37 = (bf16[64,2048]{1,0:T(8,128)(2,1)S(1)}, bf16[64,2048]{1,0:T(8,128)(2,1)S(1)}, u32[]{:S(2)}, u32[]{:S(2)}) collective-permute-start(bf16[64,2048]{1,0:T(8,128)(2,1)S(1)} %get-tuple-element.489), channel_id=1, source_target_pairs={{0,4},{4,0},{8,12},{12,8},{16,20},{20,16},{24,28},{28,24},{1,5},{5... | collective-permute-start | bytes 786440 | tf_op jit(solution)/shard_map/ppermute | solution.py:90
  265.6 44.0 %collective-permute-start.39 = (bf16[128,2048]{1,0:T(8,128)(2,1)S(1)}, bf16[128,2048]{1,0:T(8,128)(2,1)S(1)}, u32[]{:S(2)}, u32[]{:S(2)}) collective-permute-start(bf16[128,2048]{1,0:T(8,128)(2,1)S(1)} %pad_maximum_fusion.12.refs_0_), channel_id=1, source_target_pairs={{0,2},{1,3},{2,0},{3,1},{4,6},{5,7},{6,4},{7,5},{8,10},{9,11},{10,... | collective-permute-start | bytes 1572872 | tf_op jit(solution)/shard_map/ppermute | solution.py:90
  265.8 43.7 %collective-permute-start.40 = (bf16[128,2048]{1,0:T(8,128)(2,1)S(1)}, bf16[128,2048]{1,0:T(8,128)(2,1)S(1)}, u32[]{:S(2)}, u32[]{:S(2)}) collective-permute-start(bf16[128,2048]{1,0:T(8,128)(2,1)S(1)} %pad_maximum_fusion.13.refs_2_), channel_id=1, source_target_pairs={{0,4},{4,0},{8,12},{12,8},{16,20},{20,16},{24,28},{28,24},{1,5},{5... | collective-permute-start | bytes 1572872 | tf_op jit(solution)/shard_map/ppermute | solution.py:90
  310.4 32.7 %collective-permute-start.41 = (bf16[128,2048]{1,0:T(8,128)(2,1)S(1)}, bf16[128,2048]{1,0:T(8,128)(2,1)S(1)}, u32[]{:S(2)}, u32[]{:S(2)}) collective-permute-start(bf16[128,2048]{1,0:T(8,128)(2,1)S(1)} %pad_maximum_fusion.14.refs_0_), channel_id=1, source_target_pairs={{0,2},{1,3},{2,0},{3,1},{4,6},{5,7},{6,4},{7,5},{8,10},{9,11},{10,... | collective-permute-start | bytes 1572872 | tf_op jit(solution)/shard_map/ppermute | solution.py:90
  311.9 31.1 %collective-permute-start.42 = (bf16[128,2048]{1,0:T(8,128)(2,1)S(1)}, bf16[128,2048]{1,0:T(8,128)(2,1)}, u32[]{:S(2)}, u32[]{:S(2)}) collective-permute-start(bf16[128,2048]{1,0:T(8,128)(2,1)S(1)} %pad_maximum_fusion.15.refs_2_), channel_id=1, source_target_pairs={{0,4},{4,0},{8,12},{12,8},{16,20},{20,16},{24,28},{28,24},{1,5},{5... | collective-permute-start | bytes 1572872 | tf_op jit(solution)/shard_map/ppermute | solution.py:90
  312.7 30.4 %collective-permute-start.43 = (bf16[128,2048]{1,0:T(8,128)(2,1)S(1)}, bf16[128,2048]{1,0:T(8,128)(2,1)S(1)}, u32[]{:S(2)}, u32[]{:S(2)}) collective-permute-start(bf16[128,2048]{1,0:T(8,128)(2,1)S(1)} %get-tuple-element.300), channel_id=1, source_target_pairs={{0,2},{1,3},{2,0},{3,1},{4,6},{5,7},{6,4},{7,5},{8,10},{9,11},{10,... | collective-permute-start | bytes 1572872 | tf_op jit(solution)/shard_map/ppermute | solution.py:90
  313.0 30.1 %collective-permute-start.44 = (bf16[128,2048]{1,0:T(8,128)(2,1)}, bf16[128,2048]{1,0:T(8,128)(2,1)}, u32[]{:S(2)}, u32[]{:S(2)}) collective-permute-start(bf16[128,2048]{1,0:T(8,128)(2,1)} %get-tuple-element.301), channel_id=1, source_target_pairs={{0,4},{4,0},{8,12},{12,8},{16,20},{20,16},{24,28},{28,24},{1,5},{5... | collective-permute-start | bytes 1572872 | tf_op jit(solution)/shard_map/ppermute | solution.py:90
  345.9 33.2 %collective-permute-start.46 = (bf16[64,2048]{1,0:T(8,128)(2,1)}, bf16[64,2048]{1,0:T(8,128)(2,1)}, u32[]{:S(2)}, u32[]{:S(2)}) collective-permute-start(bf16[64,2048]{1,0:T(8,128)(2,1)} %split.208), channel_id=1, source_target_pairs={{0,2},{1,3},{2,0},{3,1},{4,6},{5,7},{6,4},{7,5},{8,10},{9,11},{10,... | collective-permute-start | bytes 786440 | tf_op jit(solution)/shard_map/ppermute | solution.py:90
  348.4 30.8 %collective-permute-start.45 = (bf16[64,2048]{1,0:T(8,128)(2,1)}, bf16[64,2048]{1,0:T(8,128)(2,1)}, u32[]{:S(2)}, u32[]{:S(2)}) collective-permute-start(bf16[64,2048]{1,0:T(8,128)(2,1)} %split.209), channel_id=1, source_target_pairs={{0,4},{4,0},{8,12},{12,8},{16,20},{20,16},{24,28},{28,24},{1,5},{5... | collective-permute-start | bytes 786440 | tf_op jit(solution)/shard_map/ppermute | solution.py:90
  349.1 30.0 %collective-permute-start.47 = (bf16[128,2048]{1,0:T(8,128)(2,1)S(1)}, bf16[128,2048]{1,0:T(8,128)(2,1)S(1)}, u32[]{:S(2)}, u32[]{:S(2)}) collective-permute-start(bf16[128,2048]{1,0:T(8,128)(2,1)S(1)} %get-tuple-element.317), channel_id=1, source_target_pairs={{0,2},{1,3},{2,0},{3,1},{4,6},{5,7},{6,4},{7,5},{8,10},{9,11},{10,... | collective-permute-start | bytes 1572872 | tf_op jit(solution)/shard_map/ppermute | solution.py:90
  349.4 29.7 %collective-permute-start.48 = (bf16[128,2048]{1,0:T(8,128)(2,1)}, bf16[128,2048]{1,0:T(8,128)(2,1)}, u32[]{:S(2)}, u32[]{:S(2)}) collective-permute-start(bf16[128,2048]{1,0:T(8,128)(2,1)} %get-tuple-element.318), channel_id=1, source_target_pairs={{0,4},{4,0},{8,12},{12,8},{16,20},{20,16},{24,28},{28,24},{1,5},{5... | collective-permute-start | bytes 1572872 | tf_op jit(solution)/shard_map/ppermute | solution.py:90
  381.4 17.7 %collective-permute-start.51 = (bf16[64,2048]{1,0:T(8,128)(2,1)}, bf16[64,2048]{1,0:T(8,128)(2,1)S(1)}, u32[]{:S(2)}, u32[]{:S(2)}) collective-permute-start(bf16[64,2048]{1,0:T(8,128)(2,1)} %split.206), channel_id=1, source_target_pairs={{0,2},{1,3},{2,0},{3,1},{4,6},{5,7},{6,4},{7,5},{8,10},{9,11},{10,... | collective-permute-start | bytes 786440 | tf_op jit(solution)/shard_map/ppermute | solution.py:90
  385.0 19.4 %collective-permute-start.49 = (bf16[128,2048]{1,0:T(8,128)(2,1)S(1)}, bf16[128,2048]{1,0:T(8,128)(2,1)}, u32[]{:S(2)}, u32[]{:S(2)}) collective-permute-start(bf16[128,2048]{1,0:T(8,128)(2,1)S(1)} %pad_maximum_fusion.16), channel_id=1, source_target_pairs={{0,8},{4,12},{8,16},{12,20},{16,24},{20,28},{24,0},{28,4},{1,9},{5... | collective-permute-start | bytes 1572872 | tf_op jit(solution)/shard_map/ppermute | solution.py:90
  386.8 17.6 %collective-permute-start.52 = (bf16[128,2048]{1,0:T(8,128)(2,1)S(1)}, bf16[128,2048]{1,0:T(8,128)(2,1)}, u32[]{:S(2)}, u32[]{:S(2)}) collective-permute-start(bf16[128,2048]{1,0:T(8,128)(2,1)S(1)} %get-tuple-element.339), channel_id=1, source_target_pairs={{0,2},{1,3},{2,0},{3,1},{4,6},{5,7},{6,4},{7,5},{8,10},{9,11},{10,... | collective-permute-start | bytes 1572872 | tf_op jit(solution)/shard_map/ppermute | solution.py:90
  387.2 17.1 %collective-permute-start.53 = (bf16[128,2048]{1,0:T(8,128)(2,1)}, bf16[128,2048]{1,0:T(8,128)(2,1)}, u32[]{:S(2)}, u32[]{:S(2)}) collective-permute-start(bf16[128,2048]{1,0:T(8,128)(2,1)} %get-tuple-element.340), channel_id=1, source_target_pairs={{0,4},{4,0},{8,12},{12,8},{16,20},{20,16},{24,28},{28,24},{1,5},{5... | collective-permute-start | bytes 1572872 | tf_op jit(solution)/shard_map/ppermute | solution.py:90
  407.2 17.6 %collective-permute-start.56 = (bf16[64,2048]{1,0:T(8,128)(2,1)}, bf16[64,2048]{1,0:T(8,128)(2,1)S(1)}, u32[]{:S(2)}, u32[]{:S(2)}) collective-permute-start(bf16[64,2048]{1,0:T(8,128)(2,1)} %split.204), channel_id=1, source_target_pairs={{0,2},{1,3},{2,0},{3,1},{4,6},{5,7},{6,4},{7,5},{8,10},{9,11},{10,... | collective-permute-start | bytes 786440 | tf_op jit(solution)/shard_map/ppermute | solution.py:90
  412.2 19.5 %collective-permute-start.54 = (bf16[128,2048]{1,0:T(8,128)(2,1)}, bf16[128,2048]{1,0:T(8,128)(2,1)S(1)}, u32[]{:S(2)}, u32[]{:S(2)}) collective-permute-start(bf16[128,2048]{1,0:T(8,128)(2,1)} %fusion.42), channel_id=1, source_target_pairs={{0,8},{4,12},{8,16},{12,20},{16,24},{20,28},{24,0},{28,4},{1,9},{5... | collective-permute-start | bytes 1572872 | tf_op jit(solution)/shard_map/ppermute | solution.py:90
  412.2 19.5 %collective-permute-start.57 = (bf16[128,2048]{1,0:T(8,128)(2,1)S(1)}, bf16[128,2048]{1,0:T(8,128)(2,1)S(1)}, u32[]{:S(2)}, u32[]{:S(2)}) collective-permute-start(bf16[128,2048]{1,0:T(8,128)(2,1)S(1)} %get-tuple-element.356), channel_id=1, source_target_pairs={{0,2},{1,3},{2,0},{3,1},{4,6},{5,7},{6,4},{7,5},{8,10},{9,11},{10,... | collective-permute-start | bytes 1572872 | tf_op jit(solution)/shard_map/ppermute | solution.py:90
  412.2 19.5 %collective-permute-start.58 = (bf16[128,2048]{1,0:T(8,128)(2,1)}, bf16[128,2048]{1,0:T(8,128)(2,1)S(1)}, u32[]{:S(2)}, u32[]{:S(2)}) collective-permute-start(bf16[128,2048]{1,0:T(8,128)(2,1)} %get-tuple-element.357), channel_id=1, source_target_pairs={{0,4},{4,0},{8,12},{12,8},{16,20},{20,16},{24,28},{28,24},{1,5},{5... | collective-permute-start | bytes 1572872 | tf_op jit(solution)/shard_map/ppermute | solution.py:90
  434.5 16.8 %collective-permute-start.61 = (bf16[64,2048]{1,0:T(8,128)(2,1)}, bf16[64,2048]{1,0:T(8,128)(2,1)S(1)}, u32[]{:S(2)}, u32[]{:S(2)}) collective-permute-start(bf16[64,2048]{1,0:T(8,128)(2,1)} %split.202), channel_id=1, source_target_pairs={{0,2},{1,3},{2,0},{3,1},{4,6},{5,7},{6,4},{7,5},{8,10},{9,11},{10,... | collective-permute-start | bytes 786440 | tf_op jit(solution)/shard_map/ppermute | solution.py:90
  451.3 61.0 %collective-permute-start.70 = (bf16[128,2048]{1,0:T(8,128)(2,1)}, bf16[128,2048]{1,0:T(8,128)(2,1)}, u32[]{:S(2)}, u32[]{:S(2)}) collective-permute-start(bf16[128,2048]{1,0:T(8,128)(2,1)} %get-tuple-element.403), channel_id=1, source_target_pairs={{0,2},{1,3},{2,0},{3,1},{4,6},{5,7},{6,4},{7,5},{8,10},{9,11},{10,... | collective-permute-start | bytes 1572872 | tf_op jit(solution)/shard_map/ppermute | solution.py:90
  453.4 60.1 %collective-permute-start.71 = (bf16[128,2048]{1,0:T(8,128)(2,1)}, bf16[128,2048]{1,0:T(8,128)(2,1)}, u32[]{:S(2)}, u32[]{:S(2)}) collective-permute-start(bf16[128,2048]{1,0:T(8,128)(2,1)} %get-tuple-element.404), channel_id=1, source_target_pairs={{0,4},{4,0},{8,12},{12,8},{16,20},{20,16},{24,28},{28,24},{1,5},{5... | collective-permute-start | bytes 1572872 | tf_op jit(solution)/shard_map/ppermute | solution.py:90
  464.3 17.5 %collective-permute-start.68 = (bf16[64,2048]{1,0:T(8,128)(2,1)S(1)}, bf16[64,2048]{1,0:T(8,128)(2,1)S(1)}, u32[]{:S(2)}, u32[]{:S(2)}) collective-permute-start(bf16[64,2048]{1,0:T(8,128)(2,1)S(1)} %split.200), channel_id=1, source_target_pairs={{0,2},{1,3},{2,0},{3,1},{4,6},{5,7},{6,4},{7,5},{8,10},{9,11},{10,... | collective-permute-start | bytes 786440 | tf_op jit(solution)/shard_map/ppermute | solution.py:90
  478.5 60.9 %collective-permute-start.74 = (bf16[128,2048]{1,0:T(8,128)(2,1)}, bf16[128,2048]{1,0:T(8,128)(2,1)}, u32[]{:S(2)}, u32[]{:S(2)}) collective-permute-start(bf16[128,2048]{1,0:T(8,128)(2,1)} %get-tuple-element.412), channel_id=1, source_target_pairs={{0,2},{1,3},{2,0},{3,1},{4,6},{5,7},{6,4},{7,5},{8,10},{9,11},{10,... | collective-permute-start | bytes 1572872 | tf_op jit(solution)/shard_map/ppermute | solution.py:90
  481.9 58.9 %collective-permute-start.75 = (bf16[128,2048]{1,0:T(8,128)(2,1)}, bf16[128,2048]{1,0:T(8,128)(2,1)}, u32[]{:S(2)}, u32[]{:S(2)}) collective-permute-start(bf16[128,2048]{1,0:T(8,128)(2,1)} %get-tuple-element.413), channel_id=1, source_target_pairs={{0,4},{4,0},{8,12},{12,8},{16,20},{20,16},{24,28},{28,24},{1,5},{5... | collective-permute-start | bytes 1572872 | tf_op jit(solution)/shard_map/ppermute | solution.py:90
  482.9 30.6 %collective-permute-start.69 = (bf16[128,2048]{1,0:T(8,128)(2,1)}, bf16[128,2048]{1,0:T(8,128)(2,1)}, u32[]{:S(2)}, u32[]{:S(2)}) collective-permute-start(bf16[128,2048]{1,0:T(8,128)(2,1)} %pad_maximum_fusion.17), channel_id=1, source_target_pairs={{0,8},{4,12},{8,16},{12,20},{16,24},{20,28},{24,0},{28,4},{1,9},{5... | collective-permute-start | bytes 1572872 | tf_op jit(solution)/shard_map/ppermute | solution.py:90
  512.3 59.1 %collective-permute-start.83 = (bf16[128,2048]{1,0:T(8,128)(2,1)}, bf16[128,2048]{1,0:T(8,128)(2,1)}, u32[]{:S(2)}, u32[]{:S(2)}) collective-permute-start(bf16[128,2048]{1,0:T(8,128)(2,1)} %get-tuple-element.425), channel_id=1, source_target_pairs={{0,2},{1,3},{2,0},{3,1},{4,6},{5,7},{6,4},{7,5},{8,10},{9,11},{10,... | collective-permute-start | bytes 1572872 | tf_op jit(solution)/shard_map/ppermute | solution.py:90
  539.4 32.1 %collective-permute-start.84 = (bf16[128,2048]{1,0:T(8,128)(2,1)S(1)}, bf16[128,2048]{1,0:T(8,128)(2,1)S(1)}, u32[]{:S(2)}, u32[]{:S(2)}) collective-permute-start(bf16[128,2048]{1,0:T(8,128)(2,1)S(1)} %copy-done.122), channel_id=1, source_target_pairs={{0,4},{4,0},{8,12},{12,8},{16,20},{20,16},{24,28},{28,24},{1,5},{5... | collective-permute-start | bytes 1572872 | tf_op jit(solution)/shard_map/ppermute | solution.py:90
  543.6 27.9 %collective-permute-start.82 = (bf16[64,2048]{1,0:T(8,128)(2,1)S(1)}, bf16[64,2048]{1,0:T(8,128)(2,1)S(1)}, u32[]{:S(2)}, u32[]{:S(2)}) collective-permute-start(bf16[64,2048]{1,0:T(8,128)(2,1)S(1)} %split.196), channel_id=1, source_target_pairs={{0,2},{1,3},{2,0},{3,1},{4,6},{5,7},{6,4},{7,5},{8,10},{9,11},{10,... | collective-permute-start | bytes 786440 | tf_op jit(solution)/shard_map/ppermute | solution.py:90
  544.8 26.7 %collective-permute-start.81 = (bf16[64,2048]{1,0:T(8,128)(2,1)S(1)}, bf16[64,2048]{1,0:T(8,128)(2,1)S(1)}, u32[]{:S(2)}, u32[]{:S(2)}) collective-permute-start(bf16[64,2048]{1,0:T(8,128)(2,1)S(1)} %split.197), channel_id=1, source_target_pairs={{0,4},{4,0},{8,12},{12,8},{16,20},{20,16},{24,28},{28,24},{1,5},{5... | collective-permute-start | bytes 786440 | tf_op jit(solution)/shard_map/ppermute | solution.py:90
  586.2 26.2 %collective-permute-start.91 = (bf16[128,2048]{1,0:T(8,128)(2,1)S(1)}, bf16[128,2048]{1,0:T(8,128)(2,1)S(1)}, u32[]{:S(2)}, u32[]{:S(2)}) collective-permute-start(bf16[128,2048]{1,0:T(8,128)(2,1)S(1)} %add_convert_fusion.1), channel_id=1, source_target_pairs={{0,1},{1,0},{2,3},{3,2},{4,5},{5,4},{6,7},{7,6},{8,9},{9,8},{10,11... | collective-permute-start | bytes 1572872 | tf_op jit(solution)/shard_map/ppermute | solution.py:90
  586.3 25.9 %collective-permute-start.92 = (bf16[128,2048]{1,0:T(8,128)(2,1)S(1)}, bf16[128,2048]{1,0:T(8,128)(2,1)}, u32[]{:S(2)}, u32[]{:S(2)}) collective-permute-start(bf16[128,2048]{1,0:T(8,128)(2,1)S(1)} %add_convert_fusion.1), channel_id=1, source_target_pairs={{0,2},{1,3},{2,0},{3,1},{4,6},{5,7},{6,4},{7,5},{8,10},{9,11},{10,... | collective-permute-start | bytes 1572872 | tf_op jit(solution)/shard_map/ppermute | solution.py:90
  589.0 21.5 %collective-permute-start.85 = (bf16[128,2048]{1,0:T(8,128)(2,1)S(1)}, bf16[128,2048]{1,0:T(8,128)(2,1)S(1)}, u32[]{:S(2)}, u32[]{:S(2)}) collective-permute-start(bf16[128,2048]{1,0:T(8,128)(2,1)S(1)} %fusion.46), channel_id=1, source_target_pairs={{0,8},{4,12},{8,16},{12,20},{16,24},{20,28},{24,0},{28,4},{1,9},{5... | collective-permute-start | bytes 1572872 | tf_op jit(solution)/shard_map/ppermute | solution.py:90
  612.2 30.9 %collective-permute-start.93 = (bf16[128,2048]{1,0:T(8,128)(2,1)}, bf16[128,2048]{1,0:T(8,128)(2,1)}, u32[]{:S(2)}, u32[]{:S(2)}) collective-permute-start(bf16[128,2048]{1,0:T(8,128)(2,1)} %collective-permute-done.92), channel_id=1, source_target_pairs={{0,1},{1,0},{2,3},{3,2},{4,5},{5,4},{6,7},{7,6},{8,9},{9,8},{10,11... | collective-permute-start | bytes 1572872 | tf_op jit(solution)/shard_map/ppermute | solution.py:90
  (192 other events, 2042.2 us)

commit v3 on v2

v3 whole, which is shorter than its diff:
```python
import functools

import jax
import jax.numpy as jnp
from jax import lax
from jax.experimental import pallas as pl
from jax.experimental.pallas import tpu as pltpu
from jax.sharding import PartitionSpec as P

HD = 128
RANK = 16


EPSILON = 1e-05
ROPE_BASE = 10000.0
MASKED_SCORE = -1e30
VMEM_LIMIT = 56 * 2**20


def ancestry(parents):
    blocks = parents.shape[0]
    places = jnp.arange(blocks, dtype=jnp.int32)
    walker = places
    reached = walker[:, None] == places[None, :]
    for _ in range(blocks - 1):
        hits = (walker[:, None] == places[None, :]).astype(jnp.int32)
        walker = jnp.sum(hits * parents[None, :], axis=1)
        reached = reached | (walker[:, None] == places[None, :])
    return reached[None]


def rope_tables(reached, block_span, head_size):
    depths = jnp.sum(reached.astype(jnp.int32), axis=2) - 1
    offsets = jnp.arange(block_span, dtype=jnp.int32)
    located = (
        (depths[:, :, None] * block_span + offsets[None, None, :]).reshape(-1).astype(jnp.float32)
    )
    halves = head_size // 2
    speeds = ROPE_BASE ** (-2.0 * jnp.arange(halves, dtype=jnp.float32) / head_size)
    angles = located[:, None] * speeds[None, :]
    angles = jnp.concatenate([angles, angles], axis=1)
    return (jnp.cos(angles), jnp.sin(angles))


def unrotate(values, cosine_table, sine_table):
    halves = values.shape[-1] // 2
    sined = values * sine_table[:, None, :]
    return values * cosine_table[:, None, :] + jnp.concatenate(
        [sined[..., halves:], -sined[..., :halves]], axis=-1
    )


def token_mask(reached, total_size):
    blocks = reached.shape[0]
    block_span = total_size // blocks
    widened = jnp.broadcast_to(
        reached[:, None, :, None], (blocks, block_span, blocks, block_span)
    ).reshape(total_size, total_size)
    positions = jnp.arange(total_size, dtype=jnp.int32)
    return widened & (positions[None, :] <= positions[:, None])


def norm_back(scaled_grad, values, inverse, model_width, inner_sum):
    return inverse * scaled_grad - values * inverse**3 * (inner_sum / model_width)


def divide_axes(owners, tensor_count):
    outer = 4
    return {
        "z": ("expert", outer, owners // outer, owners),
        "x": ("expert", owners // outer, 1, owners),
        "y": ("tensor", tensor_count // 2, 2, tensor_count),
        "c": ("tensor", 2, 1, tensor_count),
    }


def turn(array, axes, name, step):
    axis, length, stride, total = axes[name]
    pairs = []
    for index in range(total):
        place = (index // stride) % length
        moved = index + ((place + step) % length - place) * stride
        pairs.append((index, moved))
    return lax.ppermute(array, axis, pairs)


def ring(array, axes, name):
    held = [array]
    for _ in range(axes[name][1] - 1):
        held.append(turn(held[-1], axes, name, 1))
    return held


def wide(array):
    return array.astype(jnp.float32)


def low(array):
    return array.astype(jnp.bfloat16)


def gather_first(rows, axes):
    half = rows.shape[0] // 2
    return (
        jnp.concatenate(ring(rows[:half], axes, "x"), axis=0),
        jnp.concatenate(ring(rows[half:], axes, "y"), axis=0),
    )


def gather_second(pair, axes):
    return ring(pair[0], axes, "y") + ring(pair[1], axes, "x")


def send_sum(parts, axes, name):
    total = parts[-1]
    for part in parts[-2:0:-1]:
        total = low(wide(turn(total, axes, name, -1)) + wide(part))
    return turn(total, axes, name, -1)


def scatter_first(pieces, axes):
    span = axes["y"][1]
    return send_sum(pieces[:span], axes, "y"), send_sum(pieces[span:], axes, "x")


def scatter_second(pieces, came, axes):
    span = axes["y"][1]
    first = wide(pieces[0]) + wide(came[0])
    second = wide(pieces[span]) + wide(came[1])
    first = jnp.split(first, axes["x"][1], axis=0)
    second = jnp.split(second, axes["y"][1], axis=0)
    first_came = send_sum([low(part) for part in first], axes, "x")
    second_came = send_sum([low(part) for part in second], axes, "y")
    return (first[0], second[0]), (first_came, second_came)


def scatter_last(kept, came):
    return jnp.concatenate([kept[0] + wide(came[0]), kept[1] + wide(came[1])], axis=0)


def place_tensor(rows, axes, kind):
    rank = lax.axis_index("tensor")
    count = lax.axis_size("tensor")
    size = rows.shape[0]
    span = axes["y"][1]
    held = ring(rows, axes, "y")
    other = [turn(piece, axes, "c", 1) for piece in held]
    whole = jnp.zeros((count * size, rows.shape[1]), kind)
    core = rank % 2
    for step in range(span):
        level = (rank // 2 + span - step) % span
        whole = lax.dynamic_update_slice_in_dim(
            whole, held[step].astype(kind), (level * 2 + core) * size, 0
        )
        whole = lax.dynamic_update_slice_in_dim(
            whole, other[step].astype(kind), (level * 2 + 1 - core) * size, 0
        )
    return whole


def scatter_tensor(mine, theirs, axes):
    rank = lax.axis_index("tensor")
    span = axes["y"][1]
    size = mine.shape[0] // span
    came = turn(theirs, axes, "c", 1)
    total = None
    for step in range(span - 1, -1, -1):
        level = (rank // 2 + span - step) % span
        part = wide(lax.dynamic_slice_in_dim(mine, level * size, size, 0)) + wide(
            lax.dynamic_slice_in_dim(came, level * size, size, 0)
        )
        if step:
            total = turn(low(part if total is None else part + wide(total)), axes, "y", -1)
    return part, total


def swap_columns(rows, axes):
    rank = lax.axis_index("tensor")
    count = lax.axis_size("tensor")
    size, width = rows.shape
    span = axes["y"][1]
    share = width // count
    level, core = rank // 2, rank % 2
    whole = jnp.zeros((count * size, share), rows.dtype)
    for step in range(span):
        toward = (level + step) % span
        piece = lax.dynamic_slice_in_dim(rows, toward * 2 * share, 2 * share, 1)
        if step:
            piece = turn(piece, axes, "y", step)
        mine = lax.dynamic_slice_in_dim(piece, core * share, share, 1)
        theirs = lax.dynamic_slice_in_dim(piece, (1 - core) * share, share, 1)
        theirs = turn(theirs, axes, "c", 1)
        source = (level + span - step) % span
        whole = lax.dynamic_update_slice_in_dim(whole, mine, (source * 2 + core) * size, 0)
        whole = lax.dynamic_update_slice_in_dim(whole, theirs, (source * 2 + 1 - core) * size, 0)
    return whole


def sum_tensor(array, axes):
    total = wide(array) + wide(turn(array, axes, "c", 1))
    moving = low(total)
    result = total
    for _ in range(axes["y"][1] - 1):
        moving = turn(moving, axes, "y", 1)
        result = result + wide(moving)
    return result


def dot(left, right):
    return jnp.dot(left, right, preferred_element_type=jnp.float32)


def dot_t(left, right):
    return lax.dot_general(
        left, right, (((1,), (1,)), ((), ())), preferred_element_type=jnp.float32
    )


def t_dot(left, right):
    return lax.dot_general(
        left, right, (((0,), (0,)), ((), ())), preferred_element_type=jnp.float32
    )


ANY = pl.BlockSpec(memory_space=pl.ANY)


def whole(array):
    shape = array.shape
    return pl.BlockSpec(shape, lambda *_: (0,) * len(shape))


def kernel_call(kernel, grid, in_specs, out_specs, out_shape, operands, flops, scratch=(), scalars=0):
    moved = sum(array.size * array.dtype.itemsize for array in operands)
    return pl.pallas_call(
        kernel,
        grid_spec=pltpu.PrefetchScalarGridSpec(
            num_scalar_prefetch=scalars,
            grid=grid,
            in_specs=in_specs,
            out_specs=out_specs,
            scratch_shapes=list(scratch),
        ),
        out_shape=[jax.ShapeDtypeStruct(shape, kind) for shape, kind in out_shape],
        compiler_params=pltpu.CompilerParams(vmem_limit_bytes=VMEM_LIMIT),
        cost_estimate=pl.CostEstimate(flops=flops, bytes_accessed=moved, transcendentals=0),
    )(*operands)


def project_kernel(
    tokens, gain, query_weight, key_weight, value_weight, adapt_in, adapt_out, select,
    normed_out, lowrank_out, query_out, key_out, value_out, squares_out,
    weights, maps, sems,
):
    copies = [pltpu.make_async_copy(adapt_in, maps, sems.at[3])]
    for index, source in enumerate((query_weight, key_weight, value_weight)):
        copies.append(pltpu.make_async_copy(source, weights.at[index], sems.at[index]))
    for copy in copies:
        copy.start()
    inputs = wide(tokens[...])
    inverse = lax.rsqrt(jnp.mean(inputs * inputs, axis=1, keepdims=True) + EPSILON)
    normed_out[...] = low(inputs * inverse * gain[...])
    copies[0].wait()
    for index in range(3):
        lowrank_out[index] = low(dot(normed_out[...], maps[index]) * select[...])
    squares = []
    for index, out in enumerate((query_out, key_out, value_out)):
        copies[index + 1].wait()
        raw = dot(normed_out[...], weights[index]) + dot(lowrank_out[index], adapt_out[index])
        out[...] = raw
        squares.append(jnp.sum(raw * raw, axis=1, keepdims=True))
    lane = lax.broadcasted_iota(jnp.int32, (tokens.shape[0], 128), 1)
    columns = jnp.where(lane == 0, squares[0], jnp.where(lane == 1, squares[1], 0.0))
    squares_out[...] = jnp.transpose(columns)[:8]


def project_call(tokens, gain, weights, adapt_in, adapt_out, select):
    rows, width = tokens.shape
    local = weights[0].shape[1]
    rank = adapt_in.shape[2]
    out_shape = [((rows, width), jnp.bfloat16), ((3, rows, rank), jnp.bfloat16)]
    out_shape += [((rows, local), jnp.float32)] * 3 + [((8, rows), jnp.float32)]
    operands = [tokens, gain, *weights, adapt_in, adapt_out, select]
    return kernel_call(
        project_kernel,
        (1,),
        [whole(tokens), whole(gain), ANY, ANY, ANY, ANY, whole(adapt_out), whole(select)],
        [pl.BlockSpec(shape, lambda *_, size=len(shape): (0,) * size) for shape, _ in out_shape],
        out_shape,
        operands,
        6 * rows * width * local,
        [
            pltpu.VMEM((3, width, local), jnp.bfloat16),
            pltpu.VMEM(adapt_in.shape, jnp.bfloat16),
            pltpu.SemaphoreType.DMA((4,)),
        ],
    )


def spread_columns(rows):
    return jnp.transpose(jnp.concatenate([rows] * (128 // rows.shape[0]), axis=0))


def turned(values):
    half = values.shape[1] // 2
    return jnp.concatenate([values[:, half:], values[:, :half]], axis=1)


def attend_kernel(
    width, size, core, squares, query_raw, key_raw, value_raw, query_gain, key_gain, cosine, sine,
    mask, output_weight, mix_in, queries, keys, values, attended, mine, theirs, held, weight, sem,
):
    head = pl.program_id(0)
    last = pl.num_programs(0) - 1
    copy = pltpu.make_async_copy(output_weight, weight, sem)

    @pl.when(head == 0)
    def _():
        copy.start()

    inverse = lax.rsqrt(spread_columns(squares[...]) / width + EPSILON)
    query = query_raw[...] * inverse[:, 0:1] * query_gain[...]
    key = key_raw[...] * inverse[:, 1:2] * key_gain[...]
    query = low(query * cosine[...] + turned(query) * sine[...])
    key = low(key * cosine[...] + turned(key) * sine[...])
    value = low(value_raw[...])
    queries[...] = query
    keys[...] = key
    values[...] = value
    scores = dot_t(query, key) * HD ** (-0.5) + mask[...]
    raised = jnp.exp(scores - jnp.max(scores, axis=1, keepdims=True))
    weights = low(raised / jnp.sum(raised, axis=1, keepdims=True))
    result = low(dot(weights, value))
    attended[...] = result
    held[head] = result

    @pl.when(head == last)
    def _():
        copy.wait()
        heads = held.shape[0]
        levels = mine.shape[0] // size
        for out, offset in ((mine, core[0]), (theirs, 1 - core[0])):
            taken = []
            for level in range(levels):
                rows = pl.ds(pl.multiple_of((2 * level + offset) * size, size), size)
                taken.append(
                    jnp.concatenate([held[index, rows, :] for index in range(heads)], axis=1)
                )
            taken = jnp.concatenate(taken, axis=0)
            out[:, :width] = dot(taken, weight[...]).astype(out.dtype)
            out[:, width:] = dot(taken, mix_in[...]).astype(out.dtype)


def attend_call(core, squares, raws, gains, tables, mask, output_weight, mix_in, size):
    rows, local = raws[0].shape
    heads = local // HD
    width = output_weight.shape[1]
    wide_width = width + mix_in.shape[1]
    block = pl.BlockSpec((rows, HD), lambda head, *_: (0, head))
    gain_block = pl.BlockSpec((1, HD), lambda head, *_: (0, head))
    fixed = pl.BlockSpec((rows // 2, wide_width), lambda *_: (0, 0))
    operands = [core, squares, *raws, *gains, *tables, mask, output_weight, mix_in]
    return kernel_call(
        functools.partial(attend_kernel, width, size),
        (heads,),
        [whole(squares)] + [block] * 3 + [gain_block] * 2
        + [whole(tables[0]), whole(tables[1]), whole(mask), ANY, whole(mix_in)],
        [block] * 4 + [fixed] * 2,
        [((rows, local), jnp.bfloat16)] * 4
        + [((rows // 2, wide_width), jnp.float32), ((rows // 2, wide_width), jnp.bfloat16)],
        operands,
        4 * rows * rows * local + 2 * rows * local * width,
        [
            pltpu.VMEM((heads, rows, HD), jnp.bfloat16),
            pltpu.VMEM(output_weight.shape, jnp.bfloat16),
            pltpu.SemaphoreType.DMA,
        ],
        1,
    )


def resid_kernel(
    width, kept, came, tokens, mix_out, select, gain, resid_out, norm_out, mixed_out
):
    mixed = low((kept[:, width:] + wide(came[:, width:])) * select[...])
    mixed_out[...] = mixed
    resid = (
        wide(tokens[...])
        + (kept[:, :width] + wide(came[:, :width]))
        + dot(mixed, mix_out[...])
    )
    resid_out[...] = resid
    inverse = lax.rsqrt(jnp.mean(resid * resid, axis=1, keepdims=True) + EPSILON)
    norm_out[...] = low(resid * inverse * gain[...])


def resid_call(kept, came, tokens, mix_out, select, gain):
    rows, width = tokens.shape
    out_shape = [((rows, width), jnp.float32), ((rows, width), jnp.bfloat16)]
    out_shape += [((rows, mix_out.shape[0]), jnp.bfloat16)]
    operands = [kept, came, tokens, mix_out, select, gain]
    return kernel_call(
        functools.partial(resid_kernel, width),
        (1,),
        [whole(array) for array in operands],
        [pl.BlockSpec(shape, lambda *_: (0, 0)) for shape, _ in out_shape],
        out_shape,
        operands,
        2 * rows * width * mix_out.shape[0],
    )


def hidden_kernel(count, width, *refs):
    pieces, (down_own, down_other, spread), (out, side_out), (rows, side) = (
        refs[:count],
        refs[count : count + 3],
        refs[count + 3 : count + 5],
        refs[count + 5 :],
    )
    step = pl.program_id(0)
    size = pieces[0].shape[0]

    @pl.when(step == 0)
    def _():
        for index, piece in enumerate(pieces):
            place = slice(index * size, (index + 1) * size)
            rows[place] = piece[:, :width]
            side[place] = piece[:, width:]
        side_out[...] = side[...]

    def emit(down):
        grad = dot_t(rows[...], down[...]) * dot(side[...], spread[...])
        part = out.shape[2]
        for index in range(out.shape[0]):
            out[index] = low(grad[:, index * part : (index + 1) * part])

    half = pl.num_programs(0) // 2

    @pl.when(step < half)
    def _():
        emit(down_own)

    @pl.when(step >= half)
    def _():
        emit(down_other)


def hidden_call(pieces, downs, spread, experts):
    hidden, width = downs[0].shape
    rows = sum(piece.shape[0] for piece in pieces)
    part = hidden // experts
    side = spread.shape[0]
    pair = 2 * part
    half = experts // 2
    last = half - 1
    return kernel_call(
        functools.partial(hidden_kernel, len(pieces), width),
        (2 * half,),
        [whole(piece) for piece in pieces]
        + [
            pl.BlockSpec((pair, width), lambda n: (jnp.minimum(n, last), 0)),
            pl.BlockSpec((pair, width), lambda n: (jnp.maximum(n - half, 0), 0)),
            pl.BlockSpec((side, pair), lambda n: (0, lax.rem(n, half))),
        ],
        [
            pl.BlockSpec((2, rows, part), lambda n: (n, 0, 0)),
            pl.BlockSpec((rows, side), lambda n: (0, 0)),
        ],
        [((2 * experts, rows, part), jnp.bfloat16), ((rows, side), jnp.bfloat16)],
        [*pieces, *downs, spread],
        4 * rows * hidden * width,
        [pltpu.VMEM((rows, width), jnp.bfloat16), pltpu.VMEM((rows, side), jnp.bfloat16)],
    )


def expert_kernel(count, offset, *refs):
    pieces = refs[:count]
    gate_own, up_own, gate_other, up_other, spread, side, back = refs[count : count + 7]
    outs, hidden_out = refs[count + 7 : 2 * count + 7], refs[2 * count + 7]
    rows, weights, gate_grad, up_grad, hidden, grads, sems, row_sem, back_sem, out_sem = refs[
        2 * count + 8 :
    ]
    step = pl.program_id(0)
    size = pieces[0].shape[0]
    experts, _, part = gate_own.shape
    total_rows = rows.shape[0]
    sources = (gate_own, up_own, gate_other, up_other)

    def load(expert):
        slot = weights.at[expert]
        return [
            pltpu.make_async_copy(
                source.at[expert], slot.at[:, pl.ds(index * part, part)], sems.at[expert]
            )
            for index, source in enumerate(sources)
        ]

    row_copies = [
        pltpu.make_async_copy(piece, rows.at[pl.ds(index * size, size)], row_sem.at[index])
        for index, piece in enumerate(pieces)
    ]
    back_copy = pltpu.make_async_copy(
        back.at[:, pl.ds(offset, total_rows), :], grads, back_sem
    )
    out_copy = pltpu.make_async_copy(hidden, hidden_out, out_sem)

    @pl.when(step == 0)
    def _():
        for copy in row_copies + load(0) + [back_copy] + load(1):
            copy.start()
        for copy in row_copies:
            copy.wait()
        back_copy.wait()

        def work(expert, carry):
            for ahead in range(2, experts):

                @pl.when(expert == ahead - 2)
                def _():
                    for copy in load(ahead):
                        copy.start()

            for copy in load(expert):
                copy.wait()
            values = dot(rows[...], weights[expert])
            weight = dot(side[...], spread[expert])
            for half in range(2):
                gate_value = values[:, 2 * half * part : (2 * half + 1) * part]
                up_value = values[:, (2 * half + 1) * part : (2 * half + 2) * part]
                sigmoid = jax.nn.sigmoid(gate_value)
                silu = gate_value * sigmoid
                place = half * experts + expert
                grad = wide(grads[place])
                gate_grad[place] = low(grad * up_value * (sigmoid + silu * (1.0 - sigmoid)))
                up_grad[place] = low(grad * silu)
                hidden[place] = low(silu * up_value * weight)
            return carry

        lax.fori_loop(0, experts, work, 0)
        out_copy.start()

    tile = outs[0].shape[1]
    columns = pl.ds(pl.multiple_of(step * tile, tile), tile)
    total = None
    for expert in range(experts):
        for half in range(2):
            place = half * experts + expert
            for index, grad in enumerate((gate_grad, up_grad)):
                first = (2 * half + index) * part
                term = dot_t(grad[place], weights[expert, columns, first : first + part])
                total = term if total is None else total + term
    for index, out in enumerate(outs):
        out[...] = low(total[index * size : (index + 1) * size])

    @pl.when(step == pl.num_programs(0) - 1)
    def _():
        out_copy.wait()


def expert_call(pieces, gates, ups, spread, side, back, offset):
    count = len(pieces)
    experts, width, part = gates[0].shape
    size = pieces[0].shape[0]
    rows = size * count
    tile = min(width, 512)
    shape = (2 * experts, rows, part)
    slots = pltpu.VMEM(shape, jnp.bfloat16)
    side_block = pl.BlockSpec((rows, side.shape[1]), lambda n: (offset // rows, 0))
    return kernel_call(
        functools.partial(expert_kernel, count, offset),
        (width // tile,),
        [ANY] * (count + 4) + [whole(spread), side_block, ANY],
        [pl.BlockSpec((size, tile), lambda n: (0, n))] * count + [ANY],
        [((size, width), jnp.bfloat16)] * count + [(shape, jnp.bfloat16)],
        [*pieces, gates[0], ups[0], gates[1], ups[1], spread, side, back],
        16 * rows * experts * part * width,
        [
            pltpu.VMEM((rows, width), jnp.bfloat16),
            pltpu.VMEM((experts, width, 4 * part), jnp.bfloat16),
            slots,
            slots,
            slots,
            slots,
            pltpu.SemaphoreType.DMA((experts,)),
            pltpu.SemaphoreType.DMA((count,)),
            pltpu.SemaphoreType.DMA,
            pltpu.SemaphoreType.DMA,
        ],
    )


def down_kernel(count, *refs):
    hiddens, (down_own, down_other), outs = refs[:count], refs[count : count + 2], refs[count + 2 :]
    places, _, part = hiddens[0].shape
    pieces = len(outs) // count
    size = outs[0].shape[0]
    for index, hidden in enumerate(hiddens):
        total = None
        for place in range(places):
            down = down_own if place < places // 2 else down_other
            first = place % (places // 2) * part
            term = dot(hidden[place], down[first : first + part, :])
            total = term if total is None else total + term
        for piece in range(pieces):
            outs[index * pieces + piece][...] = low(total[piece * size : (piece + 1) * size])


def down_call(hiddens, downs, pieces):
    places, rows, part = hiddens[0].shape
    hidden, width = downs[0].shape
    tile = min(width, 512)
    count = len(hiddens)
    size = rows // pieces
    down_block = pl.BlockSpec((hidden, tile), lambda n: (0, n))
    outs = kernel_call(
        functools.partial(down_kernel, count),
        (width // tile,),
        [whole(array) for array in hiddens] + [down_block] * 2,
        [pl.BlockSpec((size, tile), lambda n: (0, n))] * (count * pieces),
        [((size, width), jnp.bfloat16)] * (count * pieces),
        [*hiddens, *downs],
        4 * count * rows * hidden * width,
    )
    return [outs[index * pieces : (index + 1) * pieces] for index in range(count)]


def body(
    tokens,
    cotangent,
    attn_gain,
    ffn_gain,
    query_gain,
    key_gain,
    query_weight,
    key_weight,
    value_weight,
    output_weight,
    expert_gate,
    expert_up,
    expert_down,
    adapt_in,
    adapt_out,
    adapt_in_out,
    adapt_out_out,
    routes,
    gate_weights,
    block_parent,
    adapter_pick,
):
    rows_here, model_width = tokens.shape
    local_width = query_weight.shape[1]
    heads_here = local_width // HD
    tensor_rank = lax.axis_index("tensor")
    tensor_count = lax.axis_size("tensor")
    owners = lax.axis_size("expert")
    owner_rank = lax.axis_index("expert")
    axes = divide_axes(owners, tensor_count)
    far, near, span = axes["z"][1], axes["x"][1], axes["y"][1]
    experts_here, _, hidden_here = expert_gate.shape
    experts_all = experts_here * owners
    column_share = model_width // tensor_count
    row_share = rows_here // tensor_count
    float_kind = jnp.float32
    half_kind = jnp.bfloat16
    hold = lax.optimization_barrier

    def own_rows(array):
        return lax.dynamic_slice_in_dim(array, tensor_rank * row_share, row_share, 0)

    cotangent_rows = own_rows(cotangent)
    routes_rows = own_rows(routes)
    weights_rows = own_rows(gate_weights)
    route_weights = jnp.sum(
        jnp.where(
            routes_rows[:, :, None] == jnp.arange(experts_all, dtype=jnp.int32)[None, None, :],
            weights_rows[:, :, None],
            0.0,
        ),
        axis=1,
    )
    weights_high = low(route_weights)
    weights_low = low(route_weights - wide(weights_high))
    side_width = -(-2 * experts_all // 128) * 128
    side_pad = jnp.zeros((row_share, side_width - 2 * experts_all), half_kind)
    cot_plane = jnp.concatenate([cotangent_rows, weights_high, weights_low, side_pad], axis=1)
    side_index = jnp.arange(side_width, dtype=jnp.int32)
    hidden_owner = (
        owner_rank * experts_here
        + jnp.arange(experts_here * hidden_here, dtype=jnp.int32) // hidden_here
    )
    spread_flat = low(
        (side_index[:, None] % experts_all == hidden_owner[None, :])
        & (side_index[:, None] < 2 * experts_all)
    )
    spread = jnp.swapaxes(spread_flat.reshape(side_width, experts_here, hidden_here), 0, 1)

    cot_next = turn(cot_plane, axes, "z", 1)
    cot_first = gather_first(cot_plane, axes)
    inputs = wide(tokens)
    first_gain = wide(attn_gain)[None, :]
    second_gain = wide(ffn_gain)[None, :]
    query_scale = wide(query_gain)[None, :]
    key_scale = wide(key_gain)[None, :]
    reached = ancestry(block_parent)
    cosine_table, sine_table = rope_tables(reached, rows_here // block_parent.shape[0], HD)
    signs = jnp.where(jnp.arange(HD) < HD // 2, -1.0, 1.0)[None, :]
    key_mask = token_mask(reached[0], rows_here)
    mask_added = jnp.where(key_mask, 0.0, MASKED_SCORE)
    select = jnp.repeat(wide(adapter_pick), RANK, axis=1)
    core = jnp.reshape(tensor_rank % 2, (1,)).astype(jnp.int32)
    picked = jnp.argmax(adapter_pick[0]) * RANK
    adapt_in_used = lax.dynamic_slice_in_dim(adapt_in, picked, RANK, 2)
    adapt_out_used = lax.dynamic_slice_in_dim(adapt_out, picked, RANK, 1)
    mix_in_used = lax.dynamic_slice_in_dim(adapt_in_out, picked, RANK, 1)
    mix_out_used = lax.dynamic_slice_in_dim(adapt_out_out, picked, RANK, 0)
    normed_in, lowrank, query_raw, key_raw, value_raw, squares = project_call(
        tokens,
        first_gain,
        (query_weight, key_weight, value_weight),
        adapt_in,
        adapt_out,
        select,
    )

    cot_planes = [None] * far
    cot_next, cot_first, squares = hold((cot_next, cot_first, squares))
    squares = lax.psum(squares, "tensor")
    cot_later = turn(cot_next, axes, "z", 1)
    cot_planes[0] = gather_second(cot_first, axes)
    cot_first = gather_first(cot_next, axes)
    queries, keys, values, attended, mine, theirs = attend_call(
        core,
        squares,
        (query_raw, key_raw, value_raw),
        (query_scale, key_scale),
        (cosine_table, sine_table * signs),
        mask_added,
        output_weight,
        adapt_in_out,
        row_share,
    )

    cot_next, cot_first, mine, theirs = hold((cot_later, cot_first, mine, theirs))
    cot_later = turn(cot_next, axes, "z", 1)
    gates = (expert_gate, turn(expert_gate, axes, "c", 1))
    ups = (expert_up, turn(expert_up, axes, "c", 1))
    down_tall = expert_down.reshape(-1, model_width)
    downs = (down_tall, turn(down_tall, axes, "c", 1))
    branch_kept, branch_came = scatter_tensor(mine, theirs, axes)
    branch_came, cot_planes[0] = hold((branch_came, cot_planes[0]))
    cot_planes[1] = gather_second(cot_first, axes)
    cot_first = gather_first(cot_next, axes)
    resid_rows, norm_plane, mixed_rows = resid_call(
        branch_kept, branch_came, own_rows(tokens), adapt_out_out, select, second_gain
    )
    query_squares = squares[0]
    key_squares = squares[1]
    query_inverse = lax.rsqrt(query_squares / model_width + EPSILON)[:, None]
    key_inverse = lax.rsqrt(key_squares / model_width + EPSILON)[:, None]
    second_inverse = lax.rsqrt(
        jnp.mean(resid_rows * resid_rows, axis=1, keepdims=True) + EPSILON
    )
    score_scale = HD ** (-0.5)
    queries = queries.reshape(rows_here, heads_here, HD)
    keys = keys.reshape(rows_here, heads_here, HD)
    values = values.reshape(rows_here, heads_here, HD)

    cot_later, cot_first, cot_planes[1], norm_plane, gates, ups, downs = hold(
        (cot_later, cot_first, cot_planes[1], norm_plane, gates, ups, downs)
    )
    norm_next = turn(norm_plane, axes, "z", 1)
    norm_first = gather_first(norm_plane, axes)
    cot_planes[2] = gather_second(cot_first, axes)
    cot_first = gather_first(cot_later, axes)
    backs, sides = [None] * far, [None] * far

    def hidden_step(first, second):
        pieces = cot_planes[first] + cot_planes[second]
        back, side = hidden_call(pieces, downs, spread_flat, experts_here)
        backs[first], sides[first] = (back, 0), side
        backs[second], sides[second] = (back, side.shape[0] // 2), side
        return back

    back_first = hidden_step(0, 1)

    norm_planes = [None] * far
    norm_next, norm_first, cot_planes[2], cot_first, back_first = hold(
        (norm_next, norm_first, cot_planes[2], cot_first, back_first)
    )
    backs[0], backs[1] = (back_first, backs[0][1]), (back_first, backs[1][1])
    norm_later = turn(norm_next, axes, "z", 1)
    norm_planes[0] = gather_second(norm_first, axes)
    norm_first = gather_first(norm_next, axes)
    cot_planes[3] = gather_second(cot_first, axes)
    parts, hiddens = [None] * far, [None] * far

    def expert_step(index):
        back, offset = backs[index]
        *parts[index], hiddens[index] = expert_call(
            norm_planes[index], gates, ups, spread, sides[index], back, offset
        )

    norm_next, norm_first, norm_planes[0], cot_planes[3] = hold(
        (norm_later, norm_first, norm_planes[0], cot_planes[3])
    )
    norm_later = turn(norm_next, axes, "z", 1)
    norm_planes[1] = gather_second(norm_first, axes)
    norm_first = gather_first(norm_next, axes)
    expert_step(0)
    back_second = hidden_step(2, 3)

    norm_next, norm_first, norm_planes[1], back_second, parts[0] = hold(
        (norm_later, norm_first, norm_planes[1], back_second, parts[0])
    )
    backs[2], backs[3] = (back_second, backs[2][1]), (back_second, backs[3][1])
    norm_planes[2] = gather_second(norm_first, axes)
    norm_first = gather_first(norm_next, axes)
    expert_step(1)

    norm_first, norm_planes[2], parts[1] = hold((norm_first, norm_planes[2], parts[1]))
    norm_planes[3] = gather_second(norm_first, axes)
    came = [None] * far
    kept = [None] * far
    sums = [None] * far
    came[1] = scatter_first(parts[1], axes)
    expert_step(2)

    norm_planes[3], came[1], parts[2] = hold((norm_planes[3], came[1], parts[2]))
    kept[1], came[1] = scatter_second(parts[1], came[1], axes)
    came[2] = scatter_first(parts[2], axes)
    came[0] = scatter_first(parts[0], axes)
    expert_step(3)

    kept[1], came[1], came[2], came[0], parts[3] = hold(
        (kept[1], came[1], came[2], came[0], parts[3])
    )
    sums[1] = scatter_last(kept[1], came[1])
    ring_sum = turn(low(sums[1]), axes, "z", 1)
    kept[2], came[2] = scatter_second(parts[2], came[2], axes)
    came[3] = scatter_first(parts[3], axes)
    kept[0], came[0] = scatter_second(parts[0], came[0], axes)
    mixes = [None] * far
    mixes[1], mixes[2] = down_call([hiddens[1], hiddens[2]], downs, near + span)

    ring_sum, kept[2], came[2], came[3], mixes[1], mixes[2] = hold(
        (ring_sum, kept[2], came[2], came[3], mixes[1], mixes[2])
    )
    ring_sum = turn(low(wide(ring_sum) + scatter_last(kept[2], came[2])), axes, "z", 1)
    kept[3], came[3] = scatter_second(parts[3], came[3], axes)
    mix_came = [None] * far
    mix_kept = [None] * far
    mix_came[1] = scatter_first(mixes[1], axes)
    mixes[3], mixes[0] = down_call([hiddens[3], hiddens[0]], downs, near + span)

    ring_sum, kept[3], came[3], kept[0], came[0], mix_came[1], mixes[3], mixes[0] = hold(
        (ring_sum, kept[3], came[3], kept[0], came[0], mix_came[1], mixes[3], mixes[0])
    )
    ring_sum = turn(low(wide(ring_sum) + scatter_last(kept[3], came[3])), axes, "z", 1)
    mix_kept[1], mix_came[1] = scatter_second(mixes[1], mix_came[1], axes)

    ring_sum, mix_kept[1], mix_came[1] = hold((ring_sum, mix_kept[1], mix_came[1]))
    ffn_rows_grad = wide(ring_sum) + scatter_last(kept[0], came[0])
    second_scaled = ffn_rows_grad * second_gain
    resid_grad_rows = wide(cotangent_rows) + norm_back(
        second_scaled,
        resid_rows,
        second_inverse,
        model_width,
        jnp.sum(second_scaled * resid_rows, axis=1, keepdims=True),
    )
    branch_sent = jnp.concatenate(
        [low(resid_grad_rows), mixed_rows], axis=1
    )
    branch_whole = place_tensor(branch_sent, axes, half_kind)
    mix_sum = turn(low(scatter_last(mix_kept[1], mix_came[1])), axes, "z", 1)
    mix_came[2] = scatter_first(mixes[2], axes)

    branch_whole, mix_came[2] = hold((branch_whole, mix_came[2]))
    branch_grad = branch_whole[:, :model_width]
    mixed = lax.dynamic_slice_in_dim(branch_whole, model_width + picked, RANK, 1)
    mixed_grad = low(dot_t(branch_grad, mix_out_used))
    attended_grad = low(dot_t(branch_grad, output_weight) + dot_t(mixed_grad, mix_in_used))
    attended_grad = attended_grad.reshape(rows_here, heads_here, HD)
    scores = (
        jnp.einsum("qhd,khd->hqk", queries, keys, preferred_element_type=float_kind) * score_scale
    )
    scores = scores + mask_added[None]
    raised = jnp.exp(scores - jnp.max(scores, axis=2, keepdims=True))
    softmax_full = raised / jnp.sum(raised, axis=2, keepdims=True)
    softmax_half = low(softmax_full)
    value_grad = low(
        jnp.einsum("hqk,qhd->khd", softmax_half, attended_grad, preferred_element_type=float_kind)
    )
    prob_grad = jnp.einsum("qhd,khd->hqk", attended_grad, values, preferred_element_type=float_kind)
    score_grad = low(
        softmax_full * (prob_grad - jnp.sum(softmax_full * prob_grad, axis=2, keepdims=True))
    )
    query_grad = (
        jnp.einsum("hqk,khd->qhd", score_grad, keys, preferred_element_type=float_kind)
        * score_scale
    )
    key_grad = (
        jnp.einsum("hqk,qhd->khd", score_grad, queries, preferred_element_type=float_kind)
        * score_scale
    )
    query_scaled = (
        unrotate(query_grad, cosine_table, sine_table).reshape(rows_here, local_width) * query_scale
    )
    key_scaled = (
        unrotate(key_grad, cosine_table, sine_table).reshape(rows_here, local_width) * key_scale
    )

    query_scaled, key_scaled, value_grad, mix_sum, mix_came[2] = hold(
        (query_scaled, key_scaled, value_grad, mix_sum, mix_came[2])
    )
    mix_kept[2], mix_came[2] = scatter_second(mixes[2], mix_came[2], axes)
    mix_came[3] = scatter_first(mixes[3], axes)
    query_inner, key_inner = lax.psum(
        (jnp.sum(query_scaled * query_raw, axis=1), jnp.sum(key_scaled * key_raw, axis=1)), "tensor"
    )
    query_raw_grad = low(
        norm_back(query_scaled, query_raw, query_inverse, model_width, query_inner[:, None])
    )
    key_raw_grad = low(
        norm_back(key_scaled, key_raw, key_inverse, model_width, key_inner[:, None])
    )
    value_raw_grad = value_grad.reshape(rows_here, local_width)
    raw_grads = (query_raw_grad, key_raw_grad, value_raw_grad)
    lowrank_part = low(
        jnp.concatenate(
            [dot_t(raw_grads[projection], adapt_out_used[projection]) for projection in range(3)],
            axis=1,
        )
    )
    normed_part = (
        dot_t(query_raw_grad, query_weight)
        + dot_t(key_raw_grad, key_weight)
        + dot_t(value_raw_grad, value_weight)
    )

    normed_part, lowrank_part, mix_kept[2], mix_came[2], mix_came[3] = hold(
        (normed_part, lowrank_part, mix_kept[2], mix_came[2], mix_came[3])
    )
    mix_sum = turn(low(wide(mix_sum) + scatter_last(mix_kept[2], mix_came[2])), axes, "z", 1)
    mix_kept[3], mix_came[3] = scatter_second(mixes[3], mix_came[3], axes)
    mix_came[0] = scatter_first(mixes[0], axes)
    lowrank_grad = low(sum_tensor(lowrank_part, axes))
    blocks = normed_part.reshape(span, 2, row_share, model_width)
    kept_part, came_part = scatter_tensor(
        lax.dynamic_index_in_dim(blocks, core[0], 1, False).reshape(-1, model_width),
        low(lax.dynamic_index_in_dim(blocks, 1 - core[0], 1, False).reshape(-1, model_width)),
        axes,
    )
    normed_grad_rows = kept_part + wide(came_part)
    lowrank_rows = own_rows(lowrank_grad)
    for projection in range(3):
        normed_grad_rows = normed_grad_rows + dot_t(
            lowrank_rows[:, projection * RANK : (projection + 1) * RANK], adapt_in_used[projection]
        )
    first_scaled = normed_grad_rows * first_gain
    inputs_rows = own_rows(inputs)
    first_inverse = lax.rsqrt(
        jnp.mean(inputs_rows * inputs_rows, axis=1, keepdims=True) + EPSILON
    )
    input_grad_rows = resid_grad_rows + norm_back(
        first_scaled,
        inputs_rows,
        first_inverse,
        model_width,
        jnp.sum(first_scaled * inputs_rows, axis=1, keepdims=True),
    )
    normed_share = lax.dynamic_slice_in_dim(
        normed_in, tensor_rank * column_share, column_share, 1
    )
    branch_share = lax.dynamic_slice_in_dim(
        branch_grad, tensor_rank * column_share, column_share, 1
    )
    compact = low(
        jnp.concatenate(
            [t_dot(lowrank_grad, normed_share), t_dot(mixed, branch_share)]
            + [
                lax.dynamic_slice_in_dim(
                    t_dot(lowrank[projection], raw_grads[projection]), picked, RANK, 0
                )
                for projection in range(3)
            ]
            + [t_dot(mixed_grad, attended)],
            axis=0,
        )
    )

    input_grad_rows, compact, mix_sum, mix_kept[3], mix_came[3], mix_came[0] = hold(
        (low(input_grad_rows), compact, mix_sum, mix_kept[3], mix_came[3], mix_came[0])
    )
    input_grad = place_tensor(input_grad_rows, axes, float_kind)
    mix_sum = turn(low(wide(mix_sum) + scatter_last(mix_kept[3], mix_came[3])), axes, "z", 1)
    mix_kept[0], mix_came[0] = scatter_second(mixes[0], mix_came[0], axes)
    layer_rows = low(resid_rows + wide(mix_sum) + scatter_last(mix_kept[0], mix_came[0]))
    layer_out = swap_columns(layer_rows, axes)

    kinds = compact.shape[0] // RANK
    picks_sent = low(
        jnp.broadcast_to(wide(adapter_pick)[:, :, None], (1, adapter_pick.shape[1], 128))
    ).reshape(-1, 128)
    picks_sent = jnp.concatenate(
        [picks_sent, jnp.zeros((16 - picks_sent.shape[0], 128), half_kind)], axis=0
    )
    picks_sent = jnp.tile(picks_sent, (1, column_share // 128))
    compact = jnp.concatenate([compact, picks_sent], axis=0)
    trees = jnp.concatenate(
        ring(jnp.concatenate(ring(compact, axes, "x"), axis=0), axes, "z"), axis=0
    )
    trees = trees.reshape(owners, kinds + 1, RANK, column_share)
    tree_picks = trees[:, kinds, : adapter_pick.shape[1], 0]
    grad_adapt_out = jnp.einsum(
        "sa,skrc->karc", tree_picks, trees[:, 4:7], preferred_element_type=float_kind
    ).reshape(3, -1, column_share)
    grad_adapt_in_out = jnp.einsum(
        "sa,src->car", tree_picks, trees[:, 7], preferred_element_type=float_kind
    ).reshape(column_share, -1)
    shared = place_tensor(
        trees[:, :4].reshape(owners * 4 * RANK, column_share), axes, half_kind
    ).reshape(tensor_count, owners, 4, RANK, column_share)
    grad_adapt_in = jnp.einsum(
        "sa,tskrc->ktcar", tree_picks, shared[:, :, :3], preferred_element_type=float_kind
    ).reshape(3, model_width, -1)
    grad_adapt_out_out = jnp.einsum(
        "sa,tsrc->artc", tree_picks, shared[:, :, 3], preferred_element_type=float_kind
    ).reshape(-1, model_width)
    return (
        layer_out,
        input_grad,
        grad_adapt_in,
        grad_adapt_out,
        grad_adapt_in_out,
        grad_adapt_out_out,
    )


def solution(mesh):
    return jax.shard_map(
        body,
        mesh=mesh,
        in_specs=(
            P("expert", None),
            P("expert", None),
            P(),
            P(),
            P("tensor"),
            P("tensor"),
            P(None, "tensor"),
            P(None, "tensor"),
            P(None, "tensor"),
            P("tensor", None),
            P("expert", None, "tensor"),
            P("expert", None, "tensor"),
            P("expert", "tensor", None),
            P(),
            P(None, None, "tensor"),
            P("tensor", None),
            P(),
            P("expert", None),
            P("expert", None),
            P("expert"),
            P("expert", None),
        ),
        out_specs=(
            P("expert", "tensor"),
            P("expert", None),
            P(),
            P(None, None, "tensor"),
            P("tensor", None),
            P(),
        ),
        check_vma=False,
    )
```

time: 678 us -> 608 us (0.90)
  other arithmetic: 71.2 us -> 45.1 us
  local copies, waits for them, and re-layouts: 75.8 us -> 51.5 us
  matrix products: 47.7 us -> 26 us
  blocking collectives: 33.2 us -> 18.9 us
  Pallas kernels: 182 us -> 191 us
    dot_general x12 -> x0, matrix products: 26.2 us -> none  [the longest x9 20.4 us: dot(): return jnp.dot(left, right, preferred_element_type=jnp.float32)]
    all_gather x1 -> x0, blocking collectives: 18.5 us -> none  [body(): lax.all_gather(adapter_pick.astype(float_kind), 'expert', axis=0, tiled=T...]
    pallas_call x16 -> x11, Pallas kernels: 182 us -> 191 us  [kernel_call(): pl.pallas_call(kernel, grid_spec=pltpu.PrefetchScalarGridSpec(num_scalar_...]
    unnamed x261 -> x248, local copies, waits for them, and re-layouts: 17.4 us -> 18.4 us
  transfers between devices with their start and end apart: 101 -> 101, of which waited for: 28 -> 35; matrix products, arithmetic and copies ran while one was open for 23% -> 16% of each run, Pallas kernels for 27% -> 32%
where the time goes in v3:
time: 608 us; the launch traced here: 599 us
  Pallas kernels  191 us (31%)
  waiting for transfers between devices  169 us (28%)
  starting transfers between devices  93.5 us (15%)
  local copies, waits for them, and re-layouts  51.5 us (8%)
  other arithmetic  45.1 us (7%)
  matrix products  26 us (4%)
  blocking collectives  18.9 us (3%)
    pallas_call x11, Pallas kernels, kernel_call(): pl.pallas_call(kernel, grid_spec=pltpu.PrefetchScalarGridSpec(num_scalar_...  191 us
    ppermute x101, waiting for transfers between devices, turn(): return lax.ppermute(array, axis, pairs)  169 us
    ppermute x101, starting transfers between devices, turn(): return lax.ppermute(array, axis, pairs)  93.5 us
    unnamed x248, local copies, waits for them, and re-layouts  18.4 us
  transfers between devices with their start and end apart: 101, of which 35 were waited for; matrix products, arithmetic and copies ran while one was open for 16% of the time, Pallas kernels for 32%

profile of v3, /device:TPU:0, one launch (start us, length us, event | category | flops | bytes accessed | tf_op | source)
XLA Modules:
  0.0 599.3 jit_solution(14651633461970708926)
XLA Ops:
  3.7 3.1 collective-permute-start
  20.9 14.9 %shard_map.244 = (bf16[512,2048]{1,0:T(8,128)(2,1)}, bf16[3,512,128]{2,1,0:T(8,128)(2,1)}, f32[512,512]{1,0:T(8,128)}, f32[512,512]{1,0:T(8,128)}, f32[512,512]{1,0:T(8,128)}, /*index=5*/f32[8,512]{1,0:T(8,128)}) custom-call(bf16[512,2048]{1,0:T(8,128)(2,1)} %tokens.1, f32[1,2048]{1,0:T(1,128)} %bitcast.178, bf16[2048,512]{1,0:T(8,128)(2,1)} %query_weight.1, ...), custom_call_target="tpu_custom_call" | custom-call | flops 3221225472 | bytes 10363392 | tf_op jit(solution)/shard_map/pallas_call | solution.py:235
  42.9 12.0 %psum.21.squares = f32[8,512]{1,0:T(8,128)} all-reduce(f32[8,512]{1,0:T(8,128)S(1)} %copy-done.83), channel_id=1, replica_groups=mesh['expert'=8,'tensor'=4] {'tensor'}, use_global_device_ids=true, to_apply=%region_1.2 | all-reduce | flops 4096 | bytes 32768 | tf_op jit(solution)/shard_map/psum | solution.py:727
  54.8 11.0 %shard_map.245 = (bf16[512,512]{1,0:T(8,128)(2,1)}, bf16[512,512]{1,0:T(8,128)(2,1)}, bf16[512,512]{1,0:T(8,128)(2,1)}, bf16[512,512]{1,0:T(8,128)(2,1)}, f32[25...) custom-call(s32[1]{0:T(128)} %bitcast.2.core, f32[8,512]{1,0:T(8,128)} %psum.21.squares, ...), custom_call_target="tpu_custom_call" | custom-call | flops 1610612736 | bytes 6967300 | tf_op jit(solution)/shard_map/pallas_call | solution.py:235
  68.3 5.6 collective-permute-done.5
  78.0 8.8 %collective-permute-done.8.refs_1_ = bf16[128,2176]{1,0:T(8,128)(2,1)S(1)} collective-permute-done((bf16[128,2176]{1,0:T(8,128)(2,1)S(1)}, bf16[128,2176]{1,0:T(8,128)(2,1)S(1)}, u32[]{:S(2)}, u32[]{:S(2)}) %collective-permute-start.8) | collective-permute-done | bytes 557088 | tf_op jit(solution)/shard_map/ppermute | solution.py:84
  89.4 10.2 %collective-permute-done.9.refs_3_ = bf16[128,2176]{1,0:T(8,128)(2,1)S(1)} collective-permute-done((bf16[128,2176]{1,0:T(8,128)(2,1)S(1)}, bf16[128,2176]{1,0:T(8,128)(2,1)S(1)}, u32[]{:S(2)}, u32[]{:S(2)}) %collective-permute-start.9) | collective-permute-done | bytes 557088 | tf_op jit(solution)/shard_map/ppermute | solution.py:84
  102.8 3.3 collective-permute-done.11
  112.3 3.5 fusion.107
  115.8 2.5 collective-permute-done.10
  118.4 5.3 collective-permute-done.7.came
  124.9 3.4 shard_map.246
  128.3 3.3 collective-permute-done.13.refs_5_
  131.6 3.2 collective-permute-done.14.refs_7_
  134.8 8.3 %collective-permute-start.18 = (bf16[128,2048]{1,0:T(8,128)(2,1)}, bf16[128,2048]{1,0:T(8,128)(2,1)S(1)}, u32[]{:S(2)}, u32[]{:S(2)}) collective-permute-start(bf16[128,2048]{1,0:T(8,128)(2,1)} %get-tuple-element.238), channel_id=1, source_target_pairs={{0,8},{4,12},{8,16},{12,20},{16,24},{20,28},{24,0},{28,4},{1,9},{5... | collective-permute-start | bytes 1572872 | tf_op jit(solution)/shard_map/ppermute | solution.py:84
  148.3 15.7 %shard_map.247 = (bf16[8,1024,256]{2,1,0:T(8,128)(2,1)}, bf16[1024,128]{1,0:T(8,128)(2,1)}) custom-call(bf16[128,2176]{1,0:T(8,128)(2,1)} %pad_maximum_fusion.refs_0_, bf16[128,2176]{1,0:T(8,128)(2,1)} %copy-done.92, bf16[128,2176]{1,0:T(8,128)(2,1)} %pad_maximum_fusion.1.refs_2_, bf16[128,2176]{1,0:T(8,128)(2,1)} %copy-done.93, ...), custom_call_target="tpu_custom_call" | custom-call | flops 8589934592 | bytes 13107200 | tf_op jit(solution)/shard_map/pallas_call | solution.py:235
  165.8 9.0 %collective-permute-done.23 = bf16[64,2176]{1,0:T(8,128)(2,1)S(1)} collective-permute-done((bf16[64,2176]{1,0:T(8,128)(2,1)S(1)}, bf16[64,2176]{1,0:T(8,128)(2,1)S(1)}, u32[]{:S(2)}, u32[]{:S(2)}) %collective-permute-start.23) | collective-permute-done | bytes 278560 | tf_op jit(solution)/shard_map/ppermute | solution.py:84
  184.1 10.1 %collective-permute-done.25 = bf16[128,2048]{1,0:T(8,128)(2,1)S(1)} collective-permute-done((bf16[128,2048]{1,0:T(8,128)(2,1)S(1)}, bf16[128,2048]{1,0:T(8,128)(2,1)S(1)}, u32[]{:S(2)}, u32[]{:S(2)}) %collective-permute-start.25) | collective-permute-done | bytes 524320 | tf_op jit(solution)/shard_map/ppermute | solution.py:84
  195.0 8.6 %collective-permute-done.30.refs_5_ = bf16[128,2176]{1,0:T(8,128)(2,1)S(1)} collective-permute-done((bf16[128,2176]{1,0:T(8,128)(2,1)S(1)}, bf16[128,2176]{1,0:T(8,128)(2,1)S(1)}, u32[]{:S(2)}, u32[]{:S(2)}) %collective-permute-start.30) | collective-permute-done | bytes 557088 | tf_op jit(solution)/shard_map/ppermute | solution.py:84
  208.3 25.8 %shard_map.249 = (bf16[128,2048]{1,0:T(8,128)(2,1)}, bf16[128,2048]{1,0:T(8,128)(2,1)}, bf16[128,2048]{1,0:T(8,128)(2,1)}, bf16[128,2048]{1,0:T(8,128)(2,1)}, bf16[8,512,256]{2,1,0:T(8,128)(2,1)}) custom-call(bf16[128,2048]{1,0:T(8,128)(2,1)} %copy-done.45, bf16[128,2048]{1,0:T(8,128)(2,1)} %copy-done.110, bf16[128,2048]{1,0:T(8,128)(2,1)} %copy-done.46, ...), custom_call_target="tpu_custom_call" | custom-call | flops 17179869184 | bytes 23592960 | tf_op jit(solution)/shard_map/pallas_call | solution.py:235
  234.1 15.7 %shard_map.248 = (bf16[8,1024,256]{2,1,0:T(8,128)(2,1)}, bf16[1024,128]{1,0:T(8,128)(2,1)}) custom-call(bf16[128,2176]{1,0:T(8,128)(2,1)} %copy-done.36, bf16[128,2176]{1,0:T(8,128)(2,1)} %copy-done.90, bf16[128,2176]{1,0:T(8,128)(2,1)} %copy-done.37, bf16[128,2176]{1,0:T(8,128)(2,1)} %copy-done.91, bf16[128,2176]{1,0:T(8,128)(2,1)} %copy-done.40, ...), custom_call_target="tpu_custom_call" | custom-call | flops 8589934592 | bytes 13107200 | tf_op jit(solution)/shard_map/pallas_call | solution.py:235
  254.5 26.0 %shard_map.250 = (bf16[128,2048]{1,0:T(8,128)(2,1)}, bf16[128,2048]{1,0:T(8,128)(2,1)}, bf16[128,2048]{1,0:T(8,128)(2,1)}, bf16[128,2048]{1,0:T(8,128)(2,1)}, bf16[8,512,256]{2,1,0:T(8,128)(2,1)}) custom-call(bf16[128,2048]{1,0:T(8,128)(2,1)} %copy-done.47, bf16[128,2048]{1,0:T(8,128)(2,1)} %copy-done.107, bf16[128,2048]{1,0:T(8,128)(2,1)} %copy-done.48, ...), custom_call_target="tpu_custom_call" | custom-call | flops 17179869184 | bytes 23592960 | tf_op jit(solution)/shard_map/pallas_call | solution.py:235
  284.8 25.7 %shard_map.251 = (bf16[128,2048]{1,0:T(8,128)(2,1)}, bf16[128,2048]{1,0:T(8,128)(2,1)}, bf16[128,2048]{1,0:T(8,128)(2,1)}, bf16[128,2048]{1,0:T(8,128)(2,1)}, bf16[8,512,256]{2,1,0:T(8,128)(2,1)}) custom-call(bf16[128,2048]{1,0:T(8,128)(2,1)} %copy-done.51, bf16[128,2048]{1,0:T(8,128)(2,1)} %copy-done.112, bf16[128,2048]{1,0:T(8,128)(2,1)} %copy-done.53, ...), custom_call_target="tpu_custom_call" | custom-call | flops 17179869184 | bytes 23592960 | tf_op jit(solution)/shard_map/pallas_call | solution.py:235
  310.6 13.2 %shard_map.253 = (bf16[128,2048]{1,0:T(8,128)(2,1)}, bf16[128,2048]{1,0:T(8,128)(2,1)}, bf16[128,2048]{1,0:T(8,128)(2,1)}, bf16[128,2048]{1,0:T(8,128)(2,1)}, bf...) custom-call(bf16[8,512,256]{2,1,0:T(8,128)(2,1)} %get-tuple-element., ...), custom_call_target="tpu_custom_call" | custom-call | flops 8589934592 | bytes 12582912 | tf_op jit(solution)/shard_map/pallas_call | solution.py:235
  329.5 26.1 %shard_map.252 = (bf16[128,2048]{1,0:T(8,128)(2,1)}, bf16[128,2048]{1,0:T(8,128)(2,1)}, bf16[128,2048]{1,0:T(8,128)(2,1)}, bf16[128,2048]{1,0:T(8,128)(2,1)}, bf16[8,512,256]{2,1,0:T(8,128)(2,1)}) custom-call(bf16[128,2048]{1,0:T(8,128)(2,1)} %copy-done.49, bf16[128,2048]{1,0:T(8,128)(2,1)} %collective-permute-done.41.refs_1_, bf16[128,2048]{1,0:T(8,128)(2,1)} %copy-done.50, ...), custom_call_target="tpu_custom_call" | custom-call | flops 17179869184 | bytes 23592960 | tf_op jit(solution)/shard_map/pallas_call | solution.py:235
  363.5 2.2 collective-permute-done.52
  369.9 3.3 collective-permute-done.54
  373.5 5.5 collective-permute-start.56
  384.8 13.1 %shard_map.254 = (bf16[128,2048]{1,0:T(8,128)(2,1)}, bf16[128,2048]{1,0:T(8,128)(2,1)}, bf16[128,2048]{1,0:T(8,128)(2,1)}, bf16[128,2048]{1,0:T(8,128)(2,1)}, bf...) custom-call(bf16[8,512,256]{2,1,0:T(8,128)(2,1)} %get-tuple-element., ...), custom_call_target="tpu_custom_call" | custom-call | flops 8589934592 | bytes 12582912 | tf_op jit(solution)/shard_map/pallas_call | solution.py:235
  408.5 3.4 collective-permute-done.64
  415.5 2.5 fusion.96
  422.1 11.9 %collective-permute-done.67 = bf16[128,2176]{1,0:T(8,128)(2,1)S(1)} collective-permute-done((bf16[128,2176]{1,0:T(8,128)(2,1)S(1)}, bf16[128,2176]{1,0:T(8,128)(2,1)S(1)}, u32[]{:S(2)}, u32[]{:S(2)}) %collective-permute-start.67) | collective-permute-done | bytes 557088 | tf_op jit(solution)/shard_map/ppermute | solution.py:84
  449.3 2.3 broadcast_multiply_fusion.1
  453.1 4.3 fusion.11
  458.7 6.9 %all-reduce.1 = (f32[512]{0:T(512)S(1)}, f32[512]{0:T(512)S(1)}) all-reduce(f32[512]{0:T(512)S(1)} %multiply_reduce_fusion.2, f32[512]{0:T(512)S(1)} %multiply_reduce_fusion.1), channel_id=1, replica_groups=mesh['expert'=8,'tensor'=4] {'tensor'}, use_global_device_ids=true, to_apply=%region_14.15 | all-reduce | flops 1024 | bytes 8192 | tf_op jit(solution)/shard_map/psum | solution.py:918
  465.7 2.2 subtract_convert_fusion
  487.9 2.3 collective-permute-done.79
  495.2 11.1 %collective-permute-done.77 = bf16[128,2048]{1,0:T(8,128)(2,1)S(1)} collective-permute-done((bf16[128,2048]{1,0:T(8,128)(2,1)S(1)}, bf16[128,2048]{1,0:T(8,128)(2,1)S(1)}, u32[]{:S(2)}, u32[]{:S(2)}) %collective-permute-start.77) | collective-permute-done | bytes 524320 | tf_op jit(solution)/shard_map/ppermute | solution.py:84
  508.7 4.2 collective-permute-done.82
  517.6 2.5 broadcast_in_dim.70
  522.7 5.2 collective-permute-done.94
  528.1 4.8 collective-permute-done.87
  533.3 15.7 %collective-permute-done.95 = bf16[288,512]{1,0:T(8,128)(2,1)S(1)} collective-permute-done((bf16[288,512]{1,0:T(8,128)(2,1)S(1)}, bf16[288,512]{1,0:T(8,128)(2,1)S(1)}, u32[]{:S(2)}, u32[]{:S(2)}) %collective-permute-start.95) | collective-permute-done | bytes 294944 | tf_op jit(solution)/shard_map/ppermute | solution.py:84
  552.2 5.7 collective-permute-done.96
  559.6 7.0 %collective-permute-done.97 = bf16[288,512]{1,0:T(8,128)(2,1)S(1)} collective-permute-done((bf16[288,512]{1,0:T(8,128)(2,1)S(1)}, bf16[288,512]{1,0:T(8,128)(2,1)S(1)}, u32[]{:S(2)}, u32[]{:S(2)}) %collective-permute-start.97) | collective-permute-done | bytes 294944 | tf_op jit(solution)/shard_map/ppermute | solution.py:84
  571.1 10.1 %collective-permute-done.99 = bf16[512,512]{1,0:T(8,128)(2,1)} collective-permute-done((bf16[512,512]{1,0:T(8,128)(2,1)S(1)}, bf16[512,512]{1,0:T(8,128)(2,1)}, u32[]{:S(2)}, u32[]{:S(2)}) %collective-permute-start.99) | collective-permute-done | bytes 524320 | tf_op jit(solution)/shard_map/ppermute | solution.py:84
  589.6 3.4 reshape.538
  593.0 3.6 copy.150
  (660 shorter events, 187.4 us)
Async XLA Ops:
  3.7 35.9 %collective-permute-start = (bf16[128,2176]{1,0:T(8,128)(2,1)S(1)}, bf16[128,2176]{1,0:T(8,128)(2,1)}, u32[]{:S(2)}, u32[]{:S(2)}) collective-permute-start(bf16[128,2176]{1,0:T(8,128)(2,1)S(1)} %concatenate.119), channel_id=1, source_target_pairs={{0,8},{4,12},{8,16},{12,20},{16,24},{20,28},{24,0},{28,4},{1,9},{5... | collective-permute-start | bytes 1671176 | tf_op jit(solution)/shard_map/ppermute | solution.py:84
  6.8 29.0 %collective-permute-start.1 = (bf16[64,2176]{1,0:T(8,128)(2,1)S(1)}, bf16[64,2176]{1,0:T(8,128)(2,1)}, u32[]{:S(2)}, u32[]{:S(2)}) collective-permute-start(bf16[64,2176]{1,0:T(8,128)(2,1)S(1)} %get-tuple-element.475), channel_id=1, source_target_pairs={{0,4},{4,0},{8,12},{12,8},{16,20},{20,16},{24,28},{28,24},{1,5},{5... | collective-permute-start | bytes 835592 | tf_op jit(solution)/shard_map/ppermute | solution.py:84
  8.4 29.4 %collective-permute-start.2 = (bf16[64,2176]{1,0:T(8,128)(2,1)S(1)}, bf16[64,2176]{1,0:T(8,128)(2,1)}, u32[]{:S(2)}, u32[]{:S(2)}) collective-permute-start(bf16[64,2176]{1,0:T(8,128)(2,1)S(1)} %get-tuple-element.474), channel_id=1, source_target_pairs={{0,2},{1,3},{2,0},{3,1},{4,6},{5,7},{6,4},{7,5},{8,10},{9,11},{10,... | collective-permute-start | bytes 835592 | tf_op jit(solution)/shard_map/ppermute | solution.py:84
  9.9 124.9 %collective-permute-start.15 = (bf16[4,2048,256]{2,1,0:T(8,128)(2,1)}, bf16[4,2048,256]{2,1,0:T(8,128)(2,1)}, u32[]{:S(2)}, u32[]{:S(2)}) collective-permute-start(bf16[4,2048,256]{2,1,0:T(8,128)(2,1)} %refs_4_.3), channel_id=1, source_target_pairs={{0,1},{1,0},{2,3},{3,2},{4,5},{5,4},{6,7},{7,6},{8,9},{9,8},{10,11... | collective-permute-start | bytes 12582920 | tf_op jit(solution)/shard_map/ppermute | solution.py:84
  9.9 124.9 %collective-permute-start.16 = (bf16[4,2048,256]{2,1,0:T(8,128)(2,1)}, bf16[4,2048,256]{2,1,0:T(8,128)(2,1)}, u32[]{:S(2)}, u32[]{:S(2)}) collective-permute-start(bf16[4,2048,256]{2,1,0:T(8,128)(2,1)} %refs_5_.3), channel_id=1, source_target_pairs={{0,1},{1,0},{2,3},{3,2},{4,5},{5,4},{6,7},{7,6},{8,9},{9,8},{10,11... | collective-permute-start | bytes 12582920 | tf_op jit(solution)/shard_map/ppermute | solution.py:84
  35.8 99.0 %collective-permute-start.17 = (bf16[1024,2048]{1,0:T(8,128)(2,1)}, bf16[1024,2048]{1,0:T(8,128)(2,1)}, u32[]{:S(2)}, u32[]{:S(2)}) collective-permute-start(bf16[1024,2048]{1,0:T(8,128)(2,1)} %bitcast.8.refs_8_.refs_2_), channel_id=1, source_target_pairs={{0,1},{1,0},{2,3},{3,2},{4,5},{5,4},{6,7},{7,6},{8,9},{9,8},{10,11... | collective-permute-start | bytes 12582920 | tf_op jit(solution)/shard_map/ppermute | solution.py:84
  40.7 25.2 %collective-permute-start.4 = (bf16[64,2176]{1,0:T(8,128)(2,1)S(1)}, bf16[64,2176]{1,0:T(8,128)(2,1)S(1)}, u32[]{:S(2)}, u32[]{:S(2)}) collective-permute-start(bf16[64,2176]{1,0:T(8,128)(2,1)S(1)} %get-tuple-element.473), channel_id=1, source_target_pairs={{0,4},{4,0},{8,12},{12,8},{16,20},{20,16},{24,28},{28,24},{1,5},{5... | collective-permute-start | bytes 835592 | tf_op jit(solution)/shard_map/ppermute | solution.py:84
  41.3 33.9 %collective-permute-start.3 = (bf16[128,2176]{1,0:T(8,128)(2,1)}, bf16[128,2176]{1,0:T(8,128)(2,1)}, u32[]{:S(2)}, u32[]{:S(2)}) collective-permute-start(bf16[128,2176]{1,0:T(8,128)(2,1)} %collective-permute-done), channel_id=1, source_target_pairs={{0,8},{4,12},{8,16},{12,20},{16,24},{20,28},{24,0},{28,4},{1,9},{5... | collective-permute-start | bytes 1671176 | tf_op jit(solution)/shard_map/ppermute | solution.py:84
  75.2 25.9 %collective-permute-start.6 = (bf16[256,2176]{1,0:T(8,128)(2,1)S(1)}, bf16[256,2176]{1,0:T(8,128)(2,1)S(1)}, u32[]{:S(2)}, u32[]{:S(2)}) collective-permute-start(bf16[256,2176]{1,0:T(8,128)(2,1)S(1)} %copy-done.89), channel_id=1, source_target_pairs={{0,1},{1,0},{2,3},{3,2},{4,5},{5,4},{6,7},{7,6},{8,9},{9,8},{10,11... | collective-permute-start | bytes 3342344 | tf_op jit(solution)/shard_map/ppermute | solution.py:84
  134.8 40.3 %collective-permute-start.18 = (bf16[128,2048]{1,0:T(8,128)(2,1)}, bf16[128,2048]{1,0:T(8,128)(2,1)S(1)}, u32[]{:S(2)}, u32[]{:S(2)}) collective-permute-start(bf16[128,2048]{1,0:T(8,128)(2,1)} %get-tuple-element.238), channel_id=1, source_target_pairs={{0,8},{4,12},{8,16},{12,20},{16,24},{20,28},{24,0},{28,4},{1,9},{5... | collective-permute-start | bytes 1572872 | tf_op jit(solution)/shard_map/ppermute | solution.py:84
  144.2 21.0 %collective-permute-start.19 = (bf16[64,2048]{1,0:T(8,128)(2,1)S(1)}, bf16[64,2048]{1,0:T(8,128)(2,1)S(1)}, u32[]{:S(2)}, u32[]{:S(2)}) collective-permute-start(bf16[64,2048]{1,0:T(8,128)(2,1)S(1)} %get-tuple-element.485), channel_id=1, source_target_pairs={{0,4},{4,0},{8,12},{12,8},{16,20},{20,16},{24,28},{28,24},{1,5},{5... | collective-permute-start | bytes 786440 | tf_op jit(solution)/shard_map/ppermute | solution.py:84
  144.3 21.1 %collective-permute-start.20 = (bf16[64,2048]{1,0:T(8,128)(2,1)S(1)}, bf16[64,2048]{1,0:T(8,128)(2,1)S(1)}, u32[]{:S(2)}, u32[]{:S(2)}) collective-permute-start(bf16[64,2048]{1,0:T(8,128)(2,1)S(1)} %get-tuple-element.484), channel_id=1, source_target_pairs={{0,2},{1,3},{2,0},{3,1},{4,6},{5,7},{6,4},{7,5},{8,10},{9,11},{10,... | collective-permute-start | bytes 786440 | tf_op jit(solution)/shard_map/ppermute | solution.py:84
  144.6 30.5 %collective-permute-start.21 = (bf16[128,2176]{1,0:T(8,128)(2,1)S(1)}, bf16[128,2176]{1,0:T(8,128)(2,1)S(1)}, u32[]{:S(2)}, u32[]{:S(2)}) collective-permute-start(bf16[128,2176]{1,0:T(8,128)(2,1)S(1)} %pad_maximum_fusion.4.refs_0_), channel_id=1, source_target_pairs={{0,2},{1,3},{2,0},{3,1},{4,6},{5,7},{6,4},{7,5},{8,10},{9,11},{10,... | collective-permute-start | bytes 1671176 | tf_op jit(solution)/shard_map/ppermute | solution.py:84
  146.4 28.8 %collective-permute-start.22 = (bf16[128,2176]{1,0:T(8,128)(2,1)S(1)}, bf16[128,2176]{1,0:T(8,128)(2,1)S(1)}, u32[]{:S(2)}, u32[]{:S(2)}) collective-permute-start(bf16[128,2176]{1,0:T(8,128)(2,1)S(1)} %pad_maximum_fusion.5.refs_2_), channel_id=1, source_target_pairs={{0,4},{4,0},{8,12},{12,8},{16,20},{20,16},{24,28},{28,24},{1,5},{5... | collective-permute-start | bytes 1671176 | tf_op jit(solution)/shard_map/ppermute | solution.py:84
  182.2 21.4 %collective-permute-start.30 = (bf16[128,2176]{1,0:T(8,128)(2,1)S(1)}, bf16[128,2176]{1,0:T(8,128)(2,1)S(1)}, u32[]{:S(2)}, u32[]{:S(2)}) collective-permute-start(bf16[128,2176]{1,0:T(8,128)(2,1)S(1)} %pad_maximum_fusion.6.refs_4_), channel_id=1, source_target_pairs={{0,2},{1,3},{2,0},{3,1},{4,6},{5,7},{6,4},{7,5},{8,10},{9,11},{10,... | collective-permute-start | bytes 1671176 | tf_op jit(solution)/shard_map/ppermute | solution.py:84
  183.6 20.0 %collective-permute-start.31 = (bf16[128,2176]{1,0:T(8,128)(2,1)S(1)}, bf16[128,2176]{1,0:T(8,128)(2,1)S(1)}, u32[]{:S(2)}, u32[]{:S(2)}) collective-permute-start(bf16[128,2176]{1,0:T(8,128)(2,1)S(1)} %pad_maximum_fusion.7.refs_6_), channel_id=1, source_target_pairs={{0,4},{4,0},{8,12},{12,8},{16,20},{20,16},{24,28},{28,24},{1,5},{5... | collective-permute-start | bytes 1671176 | tf_op jit(solution)/shard_map/ppermute | solution.py:84
  203.6 46.4 %collective-permute-start.32 = (bf16[128,2048]{1,0:T(8,128)(2,1)S(1)}, bf16[128,2048]{1,0:T(8,128)(2,1)S(1)}, u32[]{:S(2)}, u32[]{:S(2)}) collective-permute-start(bf16[128,2048]{1,0:T(8,128)(2,1)S(1)} %collective-permute-done.25), channel_id=1, source_target_pairs={{0,8},{4,12},{8,16},{12,20},{16,24},{20,28},{24,0},{28,4},{1,9},{5... | collective-permute-start | bytes 1572872 | tf_op jit(solution)/shard_map/ppermute | solution.py:84
  204.2 45.7 %collective-permute-start.33 = (bf16[64,2048]{1,0:T(8,128)(2,1)S(1)}, bf16[64,2048]{1,0:T(8,128)(2,1)S(1)}, u32[]{:S(2)}, u32[]{:S(2)}) collective-permute-start(bf16[64,2048]{1,0:T(8,128)(2,1)S(1)} %get-tuple-element.481), channel_id=1, source_target_pairs={{0,4},{4,0},{8,12},{12,8},{16,20},{20,16},{24,28},{28,24},{1,5},{5... | collective-permute-start | bytes 786440 | tf_op jit(solution)/shard_map/ppermute | solution.py:84
  204.4 45.5 %collective-permute-start.34 = (bf16[64,2048]{1,0:T(8,128)(2,1)S(1)}, bf16[64,2048]{1,0:T(8,128)(2,1)S(1)}, u32[]{:S(2)}, u32[]{:S(2)}) collective-permute-start(bf16[64,2048]{1,0:T(8,128)(2,1)S(1)} %get-tuple-element.480), channel_id=1, source_target_pairs={{0,2},{1,3},{2,0},{3,1},{4,6},{5,7},{6,4},{7,5},{8,10},{9,11},{10,... | collective-permute-start | bytes 786440 | tf_op jit(solution)/shard_map/ppermute | solution.py:84
  204.7 45.2 %collective-permute-start.35 = (bf16[128,2048]{1,0:T(8,128)(2,1)S(1)}, bf16[128,2048]{1,0:T(8,128)(2,1)S(1)}, u32[]{:S(2)}, u32[]{:S(2)}) collective-permute-start(bf16[128,2048]{1,0:T(8,128)(2,1)S(1)} %pad_maximum_fusion.11.refs_0_), channel_id=1, source_target_pairs={{0,2},{1,3},{2,0},{3,1},{4,6},{5,7},{6,4},{7,5},{8,10},{9,11},{10,... | collective-permute-start | bytes 1572872 | tf_op jit(solution)/shard_map/ppermute | solution.py:84
  206.5 43.5 %collective-permute-start.36 = (bf16[128,2048]{1,0:T(8,128)(2,1)S(1)}, bf16[128,2048]{1,0:T(8,128)(2,1)S(1)}, u32[]{:S(2)}, u32[]{:S(2)}) collective-permute-start(bf16[128,2048]{1,0:T(8,128)(2,1)S(1)} %pad_maximum_fusion.12.refs_2_), channel_id=1, source_target_pairs={{0,4},{4,0},{8,12},{12,8},{16,20},{20,16},{24,28},{28,24},{1,5},{5... | collective-permute-start | bytes 1572872 | tf_op jit(solution)/shard_map/ppermute | solution.py:84
  250.1 30.4 %collective-permute-start.37 = (bf16[64,2048]{1,0:T(8,128)(2,1)S(1)}, bf16[64,2048]{1,0:T(8,128)(2,1)S(1)}, u32[]{:S(2)}, u32[]{:S(2)}) collective-permute-start(bf16[64,2048]{1,0:T(8,128)(2,1)S(1)} %get-tuple-element.479), channel_id=1, source_target_pairs={{0,4},{4,0},{8,12},{12,8},{16,20},{20,16},{24,28},{28,24},{1,5},{5... | collective-permute-start | bytes 786440 | tf_op jit(solution)/shard_map/ppermute | solution.py:84
  250.3 30.2 %collective-permute-start.38 = (bf16[64,2048]{1,0:T(8,128)(2,1)S(1)}, bf16[64,2048]{1,0:T(8,128)(2,1)S(1)}, u32[]{:S(2)}, u32[]{:S(2)}) collective-permute-start(bf16[64,2048]{1,0:T(8,128)(2,1)S(1)} %get-tuple-element.478), channel_id=1, source_target_pairs={{0,2},{1,3},{2,0},{3,1},{4,6},{5,7},{6,4},{7,5},{8,10},{9,11},{10,... | collective-permute-start | bytes 786440 | tf_op jit(solution)/shard_map/ppermute | solution.py:84
  250.6 30.0 %collective-permute-start.39 = (bf16[128,2048]{1,0:T(8,128)(2,1)S(1)}, bf16[128,2048]{1,0:T(8,128)(2,1)S(1)}, u32[]{:S(2)}, u32[]{:S(2)}) collective-permute-start(bf16[128,2048]{1,0:T(8,128)(2,1)S(1)} %pad_maximum_fusion.13.refs_0_), channel_id=1, source_target_pairs={{0,2},{1,3},{2,0},{3,1},{4,6},{5,7},{6,4},{7,5},{8,10},{9,11},{10,... | collective-permute-start | bytes 1572872 | tf_op jit(solution)/shard_map/ppermute | solution.py:84
  252.4 28.3 %collective-permute-start.40 = (bf16[128,2048]{1,0:T(8,128)(2,1)S(1)}, bf16[128,2048]{1,0:T(8,128)(2,1)S(1)}, u32[]{:S(2)}, u32[]{:S(2)}) collective-permute-start(bf16[128,2048]{1,0:T(8,128)(2,1)S(1)} %pad_maximum_fusion.14.refs_2_), channel_id=1, source_target_pairs={{0,4},{4,0},{8,12},{12,8},{16,20},{20,16},{24,28},{28,24},{1,5},{5... | collective-permute-start | bytes 1572872 | tf_op jit(solution)/shard_map/ppermute | solution.py:84
  254.2 75.1 %collective-permute-start.49 = (bf16[128,2048]{1,0:T(8,128)(2,1)S(1)}, bf16[128,2048]{1,0:T(8,128)(2,1)S(1)}, u32[]{:S(2)}, u32[]{:S(2)}) collective-permute-start(bf16[128,2048]{1,0:T(8,128)(2,1)S(1)} %copy-done.103), channel_id=1, source_target_pairs={{0,2},{1,3},{2,0},{3,1},{4,6},{5,7},{6,4},{7,5},{8,10},{9,11},{10,... | collective-permute-start | bytes 1572872 | tf_op jit(solution)/shard_map/ppermute | solution.py:84
  280.7 43.1 %collective-permute-start.41 = (bf16[128,2048]{1,0:T(8,128)(2,1)S(1)}, bf16[128,2048]{1,0:T(8,128)(2,1)}, u32[]{:S(2)}, u32[]{:S(2)}) collective-permute-start(bf16[128,2048]{1,0:T(8,128)(2,1)S(1)} %pad_maximum_fusion.15.refs_0_), channel_id=1, source_target_pairs={{0,2},{1,3},{2,0},{3,1},{4,6},{5,7},{6,4},{7,5},{8,10},{9,11},{10,... | collective-permute-start | bytes 1572872 | tf_op jit(solution)/shard_map/ppermute | solution.py:84
  282.5 41.6 %collective-permute-start.42 = (bf16[128,2048]{1,0:T(8,128)(2,1)S(1)}, bf16[128,2048]{1,0:T(8,128)(2,1)S(1)}, u32[]{:S(2)}, u32[]{:S(2)}) collective-permute-start(bf16[128,2048]{1,0:T(8,128)(2,1)S(1)} %pad_maximum_fusion.16.refs_2_), channel_id=1, source_target_pairs={{0,4},{4,0},{8,12},{12,8},{16,20},{20,16},{24,28},{28,24},{1,5},{5... | collective-permute-start | bytes 1572872 | tf_op jit(solution)/shard_map/ppermute | solution.py:84
  282.7 41.4 %collective-permute-start.43 = (bf16[128,2048]{1,0:T(8,128)(2,1)}, bf16[128,2048]{1,0:T(8,128)(2,1)S(1)}, u32[]{:S(2)}, u32[]{:S(2)}) collective-permute-start(bf16[128,2048]{1,0:T(8,128)(2,1)} %get-tuple-element.298), channel_id=1, source_target_pairs={{0,2},{1,3},{2,0},{3,1},{4,6},{5,7},{6,4},{7,5},{8,10},{9,11},{10,... | collective-permute-start | bytes 1572872 | tf_op jit(solution)/shard_map/ppermute | solution.py:84
  283.0 41.1 %collective-permute-start.44 = (bf16[128,2048]{1,0:T(8,128)(2,1)S(1)}, bf16[128,2048]{1,0:T(8,128)(2,1)S(1)}, u32[]{:S(2)}, u32[]{:S(2)}) collective-permute-start(bf16[128,2048]{1,0:T(8,128)(2,1)S(1)} %copy-done.109), channel_id=1, source_target_pairs={{0,4},{4,0},{8,12},{12,8},{16,20},{20,16},{24,28},{28,24},{1,5},{5... | collective-permute-start | bytes 1572872 | tf_op jit(solution)/shard_map/ppermute | solution.py:84
  323.8 31.9 %collective-permute-start.50 = (bf16[128,2048]{1,0:T(8,128)(2,1)S(1)}, bf16[128,2048]{1,0:T(8,128)(2,1)S(1)}, u32[]{:S(2)}, u32[]{:S(2)}) collective-permute-start(bf16[128,2048]{1,0:T(8,128)(2,1)S(1)} %copy-done.102), channel_id=1, source_target_pairs={{0,4},{4,0},{8,12},{12,8},{16,20},{20,16},{24,28},{28,24},{1,5},{5... | collective-permute-start | bytes 1572872 | tf_op jit(solution)/shard_map/ppermute | solution.py:84
  325.2 30.5 %collective-permute-start.45 = (bf16[64,2048]{1,0:T(8,128)(2,1)S(1)}, bf16[64,2048]{1,0:T(8,128)(2,1)S(1)}, u32[]{:S(2)}, u32[]{:S(2)}) collective-permute-start(bf16[64,2048]{1,0:T(8,128)(2,1)S(1)} %split.209), channel_id=1, source_target_pairs={{0,4},{4,0},{8,12},{12,8},{16,20},{20,16},{24,28},{28,24},{1,5},{5... | collective-permute-start | bytes 786440 | tf_op jit(solution)/shard_map/ppermute | solution.py:84
  327.2 28.5 %collective-permute-start.46 = (bf16[64,2048]{1,0:T(8,128)(2,1)S(1)}, bf16[64,2048]{1,0:T(8,128)(2,1)S(1)}, u32[]{:S(2)}, u32[]{:S(2)}) collective-permute-start(bf16[64,2048]{1,0:T(8,128)(2,1)S(1)} %split.208), channel_id=1, source_target_pairs={{0,2},{1,3},{2,0},{3,1},{4,6},{5,7},{6,4},{7,5},{8,10},{9,11},{10,... | collective-permute-start | bytes 786440 | tf_op jit(solution)/shard_map/ppermute | solution.py:84
  329.0 26.7 %collective-permute-start.47 = (bf16[128,2048]{1,0:T(8,128)(2,1)}, bf16[128,2048]{1,0:T(8,128)(2,1)S(1)}, u32[]{:S(2)}, u32[]{:S(2)}) collective-permute-start(bf16[128,2048]{1,0:T(8,128)(2,1)} %get-tuple-element.313), channel_id=1, source_target_pairs={{0,2},{1,3},{2,0},{3,1},{4,6},{5,7},{6,4},{7,5},{8,10},{9,11},{10,... | collective-permute-start | bytes 1572872 | tf_op jit(solution)/shard_map/ppermute | solution.py:84
  329.3 26.4 %collective-permute-start.48 = (bf16[128,2048]{1,0:T(8,128)(2,1)}, bf16[128,2048]{1,0:T(8,128)(2,1)S(1)}, u32[]{:S(2)}, u32[]{:S(2)}) collective-permute-start(bf16[128,2048]{1,0:T(8,128)(2,1)} %get-tuple-element.314), channel_id=1, source_target_pairs={{0,4},{4,0},{8,12},{12,8},{16,20},{20,16},{24,28},{28,24},{1,5},{5... | collective-permute-start | bytes 1572872 | tf_op jit(solution)/shard_map/ppermute | solution.py:84
  373.5 27.6 %collective-permute-start.56 = (bf16[128,2048]{1,0:T(8,128)(2,1)S(1)}, bf16[128,2048]{1,0:T(8,128)(2,1)S(1)}, u32[]{:S(2)}, u32[]{:S(2)}) collective-permute-start(bf16[128,2048]{1,0:T(8,128)(2,1)S(1)} %fusion.23), channel_id=1, source_target_pairs={{0,8},{4,12},{8,16},{12,20},{16,24},{20,28},{24,0},{28,4},{1,9},{5... | collective-permute-start | bytes 1572872 | tf_op jit(solution)/shard_map/ppermute | solution.py:84
  399.0 37.4 %collective-permute-start.69 = (bf16[128,2048]{1,0:T(8,128)(2,1)S(1)}, bf16[128,2048]{1,0:T(8,128)(2,1)S(1)}, u32[]{:S(2)}, u32[]{:S(2)}) collective-permute-start(bf16[128,2048]{1,0:T(8,128)(2,1)S(1)} %copy-done.101), channel_id=1, source_target_pairs={{0,2},{1,3},{2,0},{3,1},{4,6},{5,7},{6,4},{7,5},{8,10},{9,11},{10,... | collective-permute-start | bytes 1572872 | tf_op jit(solution)/shard_map/ppermute | solution.py:84
  399.9 37.8 %collective-permute-start.70 = (bf16[128,2048]{1,0:T(8,128)(2,1)S(1)}, bf16[128,2048]{1,0:T(8,128)(2,1)S(1)}, u32[]{:S(2)}, u32[]{:S(2)}) collective-permute-start(bf16[128,2048]{1,0:T(8,128)(2,1)S(1)} %copy-done.100), channel_id=1, source_target_pairs={{0,4},{4,0},{8,12},{12,8},{16,20},{20,16},{24,28},{28,24},{1,5},{5... | collective-permute-start | bytes 1572872 | tf_op jit(solution)/shard_map/ppermute | solution.py:84
  411.9 67.2 %collective-permute-start.74 = (bf16[128,2048]{1,0:T(8,128)(2,1)}, bf16[128,2048]{1,0:T(8,128)(2,1)}, u32[]{:S(2)}, u32[]{:S(2)}) collective-permute-start(bf16[128,2048]{1,0:T(8,128)(2,1)} %get-tuple-element.405), channel_id=1, source_target_pairs={{0,2},{1,3},{2,0},{3,1},{4,6},{5,7},{6,4},{7,5},{8,10},{9,11},{10,... | collective-permute-start | bytes 1572872 | tf_op jit(solution)/shard_map/ppermute | solution.py:84
  420.9 59.0 %collective-permute-start.75 = (bf16[128,2048]{1,0:T(8,128)(2,1)}, bf16[128,2048]{1,0:T(8,128)(2,1)}, u32[]{:S(2)}, u32[]{:S(2)}) collective-permute-start(bf16[128,2048]{1,0:T(8,128)(2,1)} %get-tuple-element.406), channel_id=1, source_target_pairs={{0,4},{4,0},{8,12},{12,8},{16,20},{20,16},{24,28},{28,24},{1,5},{5... | collective-permute-start | bytes 1572872 | tf_op jit(solution)/shard_map/ppermute | solution.py:84
  435.9 72.8 %collective-permute-start.83 = (bf16[128,2048]{1,0:T(8,128)(2,1)}, bf16[128,2048]{1,0:T(8,128)(2,1)}, u32[]{:S(2)}, u32[]{:S(2)}) collective-permute-start(bf16[128,2048]{1,0:T(8,128)(2,1)} %get-tuple-element.421), channel_id=1, source_target_pairs={{0,2},{1,3},{2,0},{3,1},{4,6},{5,7},{6,4},{7,5},{8,10},{9,11},{10,... | collective-permute-start | bytes 1572872 | tf_op jit(solution)/shard_map/ppermute | solution.py:84
  436.4 20.9 %collective-permute-start.71 = (bf16[128,2048]{1,0:T(8,128)(2,1)}, bf16[128,2048]{1,0:T(8,128)(2,1)}, u32[]{:S(2)}, u32[]{:S(2)}) collective-permute-start(bf16[128,2048]{1,0:T(8,128)(2,1)} %pad_maximum_fusion.18), channel_id=1, source_target_pairs={{0,8},{4,12},{8,16},{12,20},{16,24},{20,28},{24,0},{28,4},{1,9},{5... | collective-permute-start | bytes 1572872 | tf_op jit(solution)/shard_map/ppermute | solution.py:84
  479.5 29.2 %collective-permute-start.84 = (bf16[128,2048]{1,0:T(8,128)(2,1)S(1)}, bf16[128,2048]{1,0:T(8,128)(2,1)S(1)}, u32[]{:S(2)}, u32[]{:S(2)}) collective-permute-start(bf16[128,2048]{1,0:T(8,128)(2,1)S(1)} %copy-done.99), channel_id=1, source_target_pairs={{0,4},{4,0},{8,12},{12,8},{16,20},{20,16},{24,28},{28,24},{1,5},{5... | collective-permute-start | bytes 1572872 | tf_op jit(solution)/shard_map/ppermute | solution.py:84
  487.4 25.6 %collective-permute-start.80 = (bf16[128,2048]{1,0:T(8,128)(2,1)S(1)}, bf16[128,2048]{1,0:T(8,128)(2,1)S(1)}, u32[]{:S(2)}, u32[]{:S(2)}) collective-permute-start(bf16[128,2048]{1,0:T(8,128)(2,1)S(1)} %fusion.26), channel_id=1, source_target_pairs={{0,8},{4,12},{8,16},{12,20},{16,24},{20,28},{24,0},{28,4},{1,9},{5... | collective-permute-start | bytes 1572872 | tf_op jit(solution)/shard_map/ppermute | solution.py:84
  513.0 38.2 %collective-permute-start.91 = (bf16[128,2048]{1,0:T(8,128)(2,1)S(1)}, bf16[128,2048]{1,0:T(8,128)(2,1)S(1)}, u32[]{:S(2)}, u32[]{:S(2)}) collective-permute-start(bf16[128,2048]{1,0:T(8,128)(2,1)S(1)} %fusion.22), channel_id=1, source_target_pairs={{0,1},{1,0},{2,3},{3,2},{4,5},{5,4},{6,7},{7,6},{8,9},{9,8},{10,11... | collective-permute-start | bytes 1572872 | tf_op jit(solution)/shard_map/ppermute | solution.py:84
  513.0 37.7 %collective-permute-start.92 = (bf16[128,2048]{1,0:T(8,128)(2,1)S(1)}, bf16[128,2048]{1,0:T(8,128)(2,1)S(1)}, u32[]{:S(2)}, u32[]{:S(2)}) collective-permute-start(bf16[128,2048]{1,0:T(8,128)(2,1)S(1)} %fusion.22), channel_id=1, source_target_pairs={{0,2},{1,3},{2,0},{3,1},{4,6},{5,7},{6,4},{7,5},{8,10},{9,11},{10,... | collective-permute-start | bytes 1572872 | tf_op jit(solution)/shard_map/ppermute | solution.py:84
  527.8 21.1 %collective-permute-start.85 = (bf16[128,2048]{1,0:T(8,128)(2,1)S(1)}, bf16[128,2048]{1,0:T(8,128)(2,1)S(1)}, u32[]{:S(2)}, u32[]{:S(2)}) collective-permute-start(bf16[128,2048]{1,0:T(8,128)(2,1)S(1)} %fusion.27), channel_id=1, source_target_pairs={{0,8},{4,12},{8,16},{12,20},{16,24},{20,28},{24,0},{28,4},{1,9},{5... | collective-permute-start | bytes 1572872 | tf_op jit(solution)/shard_map/ppermute | solution.py:84
  550.6 30.6 %collective-permute-start.93 = (bf16[128,2048]{1,0:T(8,128)(2,1)S(1)}, bf16[128,2048]{1,0:T(8,128)(2,1)}, u32[]{:S(2)}, u32[]{:S(2)}) collective-permute-start(bf16[128,2048]{1,0:T(8,128)(2,1)S(1)} %collective-permute-done.92), channel_id=1, source_target_pairs={{0,1},{1,0},{2,3},{3,2},{4,5},{5,4},{6,7},{7,6},{8,9},{9,8},{10,11... | collective-permute-start | bytes 1572872 | tf_op jit(solution)/shard_map/ppermute | solution.py:84
  (184 other events, 1723.1 us)

commit v4 on v3

--- a/solution.py
+++ b/solution.py
@@ -42,14 +42,6 @@
     return (jnp.cos(angles), jnp.sin(angles))
 
 
-def unrotate(values, cosine_table, sine_table):
-    halves = values.shape[-1] // 2
-    sined = values * sine_table[:, None, :]
-    return values * cosine_table[:, None, :] + jnp.concatenate(
-        [sined[..., halves:], -sined[..., :halves]], axis=-1
-    )
-
-
 def token_mask(reached, total_size):
     blocks = reached.shape[0]
     block_span = total_size // blocks
@@ -138,24 +130,9 @@
     return jnp.concatenate([kept[0] + wide(came[0]), kept[1] + wide(came[1])], axis=0)
 
 
-def place_tensor(rows, axes, kind):
-    rank = lax.axis_index("tensor")
-    count = lax.axis_size("tensor")
-    size = rows.shape[0]
-    span = axes["y"][1]
+def gather_tensor(rows, axes):
     held = ring(rows, axes, "y")
-    other = [turn(piece, axes, "c", 1) for piece in held]
-    whole = jnp.zeros((count * size, rows.shape[1]), kind)
-    core = rank % 2
-    for step in range(span):
-        level = (rank // 2 + span - step) % span
-        whole = lax.dynamic_update_slice_in_dim(
-            whole, held[step].astype(kind), (level * 2 + core) * size, 0
-        )
-        whole = lax.dynamic_update_slice_in_dim(
-            whole, other[step].astype(kind), (level * 2 + 1 - core) * size, 0
-        )
-    return whole
+    return held + [turn(piece, axes, "c", 1) for piece in held]
 
 
 def scatter_tensor(mine, theirs, axes):
@@ -259,7 +236,7 @@
         copy.start()
     inputs = wide(tokens[...])
     inverse = lax.rsqrt(jnp.mean(inputs * inputs, axis=1, keepdims=True) + EPSILON)
-    normed_out[...] = low(inputs * inverse * gain[...])
+    normed_out[...] = low(inputs * inverse * wide(gain[...]))
     copies[0].wait()
     for index in range(3):
         lowrank_out[index] = low(dot(normed_out[...], maps[index]) * select[...])
@@ -319,8 +296,8 @@
         copy.start()
 
     inverse = lax.rsqrt(spread_columns(squares[...]) / width + EPSILON)
-    query = query_raw[...] * inverse[:, 0:1] * query_gain[...]
-    key = key_raw[...] * inverse[:, 1:2] * key_gain[...]
+    query = query_raw[...] * inverse[:, 0:1] * wide(query_gain[...])
+    key = key_raw[...] * inverse[:, 1:2] * wide(key_gain[...])
     query = low(query * cosine[...] + turned(query) * sine[...])
     key = low(key * cosine[...] + turned(key) * sine[...])
     value = low(value_raw[...])
@@ -391,7 +368,7 @@
     )
     resid_out[...] = resid
     inverse = lax.rsqrt(jnp.mean(resid * resid, axis=1, keepdims=True) + EPSILON)
-    norm_out[...] = low(resid * inverse * gain[...])
+    norm_out[...] = low(resid * inverse * wide(gain[...]))
 
 
 def resid_call(kept, came, tokens, mix_out, select, gain):
@@ -410,22 +387,38 @@
     )
 
 
-def hidden_kernel(count, width, *refs):
+def plane_order(near, span, size):
+    half = size // 2
+    places = []
+    for down in range(span):
+        for across in range(near):
+            places.append((across, down, down * size, (down * near + across) * half))
+    for across in range(near):
+        for down in range(span):
+            first = (span * near + across * span + down) * half
+            places.append((across, down, down * size + half, first))
+    return places
+
+
+def hidden_kernel(count, near, size, width, *refs):
     pieces, (down_own, down_other, spread), (out, side_out), (rows, side) = (
-        refs[:count],
-        refs[count : count + 3],
-        refs[count + 3 : count + 5],
-        refs[count + 5 :],
+        refs[: count * near],
+        refs[count * near : count * near + 3],
+        refs[count * near + 3 : count * near + 5],
+        refs[count * near + 5 :],
     )
     step = pl.program_id(0)
-    size = pieces[0].shape[0]
+    span = pieces[0].shape[0] // size
+    plane = near * span * size
 
     @pl.when(step == 0)
     def _():
-        for index, piece in enumerate(pieces):
-            place = slice(index * size, (index + 1) * size)
-            rows[place] = piece[:, :width]
-            side[place] = piece[:, width:]
+        for index in range(count):
+            for across, _, source, first in plane_order(near, span, size):
+                piece = pieces[index * near + across]
+                place = slice(index * plane + first, index * plane + first + size // 2)
+                rows[place] = piece[source : source + size // 2, :width]
+                side[place] = piece[source : source + size // 2, width:]
         side_out[...] = side[...]
 
     def emit(down):
@@ -445,8 +438,10 @@
         emit(down_other)
 
 
-def hidden_call(pieces, downs, spread, experts):
+def hidden_call(planes, downs, spread, experts, size):
     hidden, width = downs[0].shape
+    near = len(planes[0])
+    pieces = [piece for plane in planes for piece in plane]
     rows = sum(piece.shape[0] for piece in pieces)
     part = hidden // experts
     side = spread.shape[0]
@@ -454,7 +449,7 @@
     half = experts // 2
     last = half - 1
     return kernel_call(
-        functools.partial(hidden_kernel, len(pieces), width),
+        functools.partial(hidden_kernel, len(planes), near, size, width),
         (2 * half,),
         [whole(piece) for piece in pieces]
         + [
@@ -589,11 +584,11 @@
     )
 
 
-def down_kernel(count, *refs):
+def down_kernel(count, span, *refs):
     hiddens, (down_own, down_other), outs = refs[:count], refs[count : count + 2], refs[count + 2 :]
     places, _, part = hiddens[0].shape
-    pieces = len(outs) // count
-    size = outs[0].shape[0]
+    near = len(outs) // count
+    size = outs[0].shape[0] // span
     for index, hidden in enumerate(hiddens):
         total = None
         for place in range(places):
@@ -601,27 +596,352 @@
             first = place % (places // 2) * part
             term = dot(hidden[place], down[first : first + part, :])
             total = term if total is None else total + term
-        for piece in range(pieces):
-            outs[index * pieces + piece][...] = low(total[piece * size : (piece + 1) * size])
-
-
-def down_call(hiddens, downs, pieces):
+        for across, _, target, first in plane_order(near, span, size):
+            outs[index * near + across][target : target + size // 2] = low(
+                total[first : first + size // 2]
+            )
+
+
+def down_call(hiddens, downs, near, span, size):
     places, rows, part = hiddens[0].shape
     hidden, width = downs[0].shape
     tile = min(width, 512)
     count = len(hiddens)
-    size = rows // pieces
     down_block = pl.BlockSpec((hidden, tile), lambda n: (0, n))
     outs = kernel_call(
-        functools.partial(down_kernel, count),
+        functools.partial(down_kernel, count, span),
         (width // tile,),
         [whole(array) for array in hiddens] + [down_block] * 2,
-        [pl.BlockSpec((size, tile), lambda n: (0, n))] * (count * pieces),
-        [((size, width), jnp.bfloat16)] * (count * pieces),
+        [pl.BlockSpec((span * size, tile), lambda n: (0, n))] * (count * near),
+        [((span * size, width), jnp.bfloat16)] * (count * near),
         [*hiddens, *downs],
         4 * count * rows * hidden * width,
     )
-    return [outs[index * pieces : (index + 1) * pieces] for index in range(count)]
+    return [outs[index * near : (index + 1) * near] for index in range(count)]
+
+
+def backward_kernel(width, share, count, scalars, *refs):
+    pieces = refs[:count]
+    (output_weight, mix_in, mix_out, select, queries, keys, values, attended, query_raw, key_raw,
+     query_gain, key_gain, cosine, sine, mask) = refs[count : count + 15]
+    (query_out, key_out, value_out, inner_out, mix_in_grad, mix_out_grad) = refs[
+        count + 15 : count + 21
+    ]
+    branch, mixed_grad, grads, inner, sems = refs[count + 21 :]
+    head = pl.program_id(0)
+    heads = grads.shape[0]
+    size = pieces[0].shape[0]
+    rows = branch.shape[0]
+
+    @pl.when(head == 0)
+    def _():
+        copies = []
+        for index, piece in enumerate(pieces):
+            place = pl.ds(pl.multiple_of(scalars[index] * size, size), size)
+            copies.append(pltpu.make_async_copy(piece, branch.at[place], sems.at[index]))
+        for copy in copies:
+            copy.start()
+        for copy in copies:
+            copy.wait()
+        mixed_grad[...] = low(
+            wide(low(dot_t(branch[:, :width], mix_out[...]))) * select[...]
+        )
+        for index in range(heads):
+            part = slice(index * HD, (index + 1) * HD)
+            grads[index] = low(
+                dot_t(branch[:, :width], output_weight[part, :])
+                + dot_t(mixed_grad[...], mix_in[part, :])
+            )
+        columns = pl.ds(pl.multiple_of(scalars[count] * share, share), share)
+        whole_grad = t_dot(branch[:, width:], branch[:, columns])
+        mix_out_grad[...] = sliced(whole_grad)
+        inner[...] = jnp.zeros_like(inner)
+
+    scale = HD ** (-0.5)
+    query, key, value = queries[...], keys[...], values[...]
+    grad = grads[head]
+    scores = dot_t(query, key) * scale + mask[...]
+    raised = jnp.exp(scores - jnp.max(scores, axis=1, keepdims=True))
+    weights = raised / jnp.sum(raised, axis=1, keepdims=True)
+    value_out[...] = low(t_dot(low(weights), grad))
+    weight_grad = dot_t(grad, value)
+    center = jnp.sum(weights * weight_grad, axis=1, keepdims=True)
+    score_grad = low(weights * (weight_grad - center))
+    query_grad = dot(score_grad, key) * scale
+    key_grad = t_dot(score_grad, query) * scale
+    query_grad = (query_grad * cosine[...] - turned(query_grad) * sine[...]) * wide(query_gain[...])
+    key_grad = (key_grad * cosine[...] - turned(key_grad) * sine[...]) * wide(key_gain[...])
+    query_out[...] = query_grad
+    key_out[...] = key_grad
+    query_inner = jnp.sum(query_grad * query_raw[...], axis=1, keepdims=True)
+    key_inner = jnp.sum(key_grad * key_raw[...], axis=1, keepdims=True)
+    lane = lax.broadcasted_iota(jnp.int32, (rows, 128), 1)
+    inner[...] += jnp.where(lane == 0, query_inner, jnp.where(lane == 1, key_inner, 0.0))
+    mix_in_grad[...] = sliced(t_dot(mixed_grad[...], attended[...]))
+
+    @pl.when(head == heads - 1)
+    def _():
+        inner_out[...] = jnp.transpose(inner[...])[:8]
+
+
+def sliced(values):
+    total = values[:RANK]
+    for index in range(1, values.shape[0] // RANK):
+        total = total + values[index * RANK : (index + 1) * RANK]
+    return low(total)
+
+
+def backward_call(
+    scalars, pieces, output_weight, mix_in, mix_out, select, states, raws, gains, tables, mask, share
+):
+    rows, local = raws[0].shape
+    heads = local // HD
+    width = output_weight.shape[1]
+    block = pl.BlockSpec((rows, HD), lambda head, *_: (0, head))
+    gain_block = pl.BlockSpec((1, HD), lambda head, *_: (0, head))
+    adapter_block = pl.BlockSpec((RANK, HD), lambda head, *_: (0, head))
+    operands = [
+        scalars, *pieces, output_weight, mix_in, mix_out, select, *states, *raws, *gains, *tables, mask,
+    ]
+    wide_out = ((rows, local), jnp.float32)
+    return kernel_call(
+        functools.partial(backward_kernel, width, share, len(pieces)),
+        (heads,),
+        [ANY] * len(pieces)
+        + [whole(output_weight), whole(mix_in), whole(mix_out), whole(select)]
+        + [block] * 6
+        + [gain_block] * 2
+        + [whole(tables[0]), whole(tables[1]), whole(mask)],
+        [block] * 3
+        + [
+            pl.BlockSpec((8, rows), lambda *_: (0, 0)),
+            adapter_block,
+            pl.BlockSpec((RANK, share), lambda *_: (0, 0)),
+        ],
+        [wide_out, wide_out, ((rows, local), jnp.bfloat16), ((8, rows), jnp.float32)]
+        + [((RANK, local), jnp.bfloat16), ((RANK, share), jnp.bfloat16)],
+        operands,
+        14 * rows * rows * local + 2 * rows * local * width,
+        [
+            pltpu.VMEM((rows, pieces[0].shape[1]), jnp.bfloat16),
+            pltpu.VMEM((rows, mix_out.shape[0]), jnp.bfloat16),
+            pltpu.VMEM((heads, rows, HD), jnp.bfloat16),
+            pltpu.VMEM((rows, 128), jnp.float32),
+            pltpu.SemaphoreType.DMA((len(pieces),)),
+        ],
+        1,
+    )
+
+
+def weight_kernel(
+    width, size, scalars, inner, squares, query_grad, key_grad, value_grad, query_raw, key_raw,
+    query_weight, key_weight, value_weight, lowrank, adapt_out,
+    mine, theirs, lowrank_out, adapt_grad, weights, raw, maps, sems,
+):
+    copies = []
+    for index, source in enumerate((query_weight, key_weight, value_weight)):
+        copies.append(pltpu.make_async_copy(source, weights.at[index], sems.at[index]))
+    for copy in copies:
+        copy.start()
+    inverse = lax.rsqrt(spread_columns(squares[...]) / width + EPSILON)
+    totals = spread_columns(inner[...]) / width
+    for index, (grad, value) in enumerate(((query_grad, query_raw), (key_grad, key_raw))):
+        scale = inverse[:, index : index + 1]
+        raw[index] = low(
+            scale * grad[...]
+            - value[...] * scale**3 * totals[:, index : index + 1]
+        )
+    raw[2] = value_grad[...]
+    picked = pl.ds(pl.multiple_of(scalars[1], RANK), RANK)
+    maps[...] = jnp.zeros_like(maps)
+    lowrank_part = None
+    for index in range(3):
+        maps[index, index * RANK : (index + 1) * RANK, :] = adapt_out[index, picked, :]
+        term = dot_t(raw[index], maps[index])
+        lowrank_part = term if lowrank_part is None else lowrank_part + term
+        adapt_grad[index * RANK : (index + 1) * RANK, :] = sliced(
+            t_dot(lowrank[index], raw[index])
+        )
+    lowrank_out[...] = low(lowrank_part)
+    for copy in copies:
+        copy.wait()
+    levels = mine.shape[0] // size
+    for out, offset in ((theirs, 1 - scalars[0]), (mine, scalars[0])):
+        total = None
+        for index in range(3):
+            taken = [
+                raw[index, pl.ds(pl.multiple_of((2 * level + offset) * size, size), size), :]
+                for level in range(levels)
+            ]
+            term = dot_t(jnp.concatenate(taken, axis=0), weights[index])
+            total = term if total is None else total + term
+        out[...] = total.astype(out.dtype)
+
+
+def weight_call(scalars, inner, squares, grads, raws, weights, lowrank, adapt_out, size):
+    rows, local = raws[0].shape
+    width = weights[0].shape[0]
+    operands = [scalars, inner, squares, *grads, *raws, *weights, lowrank, adapt_out]
+    out_shape = [((rows // 2, width), jnp.float32), ((rows // 2, width), jnp.bfloat16)]
+    out_shape += [((rows, 128), jnp.bfloat16), ((3 * RANK, local), jnp.bfloat16)]
+    return kernel_call(
+        functools.partial(weight_kernel, width, size),
+        (1,),
+        [whole(array) for array in operands[1:8]] + [ANY] * 3 + [whole(lowrank), whole(adapt_out)],
+        [pl.BlockSpec(shape, lambda *_: (0, 0)) for shape, _ in out_shape],
+        out_shape,
+        operands,
+        6 * rows * local * width,
+        [
+            pltpu.VMEM((3, width, local), jnp.bfloat16),
+            pltpu.VMEM((3, rows, local), jnp.bfloat16),
+            pltpu.VMEM((3, 128, local), jnp.bfloat16),
+            pltpu.SemaphoreType.DMA((3,)),
+        ],
+        1,
+    )
+
+
+def input_kernel(
+    kept, came, lowrank, maps, tokens, gain, resid_grad, out
+):
+    grad = kept[...] + wide(came[...]) + dot_t(lowrank[...], maps[...])
+    scaled = grad * wide(gain[...])
+    inputs = wide(tokens[...])
+    width = inputs.shape[1]
+    inverse = lax.rsqrt(jnp.mean(inputs * inputs, axis=1, keepdims=True) + EPSILON)
+    inner = jnp.sum(scaled * inputs, axis=1, keepdims=True)
+    out[...] = low(
+        resid_grad[...] + norm_back(scaled, inputs, inverse, width, inner)
+    )
+
+
+def input_call(kept, came, lowrank, maps, tokens, gain, resid_grad):
+    operands = [kept, came, lowrank, maps, tokens, gain, resid_grad]
+    rows, width = tokens.shape
+    return kernel_call(
+        input_kernel,
+        (1,),
+        [whole(array) for array in operands],
+        [pl.BlockSpec((rows, width), lambda *_: (0, 0))],
+        [((rows, width), jnp.bfloat16)],
+        operands,
+        2 * rows * width * 128,
+    )[0]
+
+
+def compact_kernel(
+    scalars, lowrank_grad, normed, mix_out_grad, adapt_grad, mix_in_grad, select, out, held, sem
+):
+    share = out.shape[1]
+    columns = pl.ds(pl.multiple_of(scalars[0] * share, share), share)
+    copy = pltpu.make_async_copy(normed.at[:, columns], held, sem)
+    copy.start()
+    copy.wait()
+    first = low(t_dot(lowrank_grad[...], held[...]))[: 3 * RANK]
+    out[: 3 * RANK] = first
+    out[3 * RANK : 4 * RANK] = mix_out_grad[...]
+    out[4 * RANK : 7 * RANK] = adapt_grad[...]
+    out[7 * RANK : 8 * RANK] = mix_in_grad[...]
+    chosen = low(jnp.broadcast_to(select[...], (RANK, 128)))
+    out[8 * RANK :] = jnp.concatenate([chosen] * (share // 128), axis=1)
+
+
+def compact_call(scalars, lowrank_grad, normed, mix_out_grad, adapt_grad, mix_in_grad, select):
+    rows = normed.shape[0]
+    share = adapt_grad.shape[1]
+    operands = [scalars, lowrank_grad, normed, mix_out_grad, adapt_grad, mix_in_grad, select]
+    return kernel_call(
+        compact_kernel,
+        (1,),
+        [whole(lowrank_grad), ANY] + [whole(array) for array in operands[3:]],
+        [pl.BlockSpec((9 * RANK, share), lambda *_: (0, 0))],
+        [((9 * RANK, share), jnp.bfloat16)],
+        operands,
+        2 * rows * share * 128,
+        [pltpu.VMEM((rows, share), jnp.bfloat16), pltpu.SemaphoreType.DMA],
+        1,
+    )[0]
+
+
+def spread_kernel(order, *refs):
+    pieces, out = refs[:-1], refs[-1]
+    step = pl.program_id(0)
+    for index, piece in enumerate(pieces):
+
+        @pl.when(step == index)
+        def _():
+            out[...] = wide(piece[...])
+
+
+def spread_call(order, pieces):
+    size, width = pieces[0].shape
+    count = len(pieces)
+    return kernel_call(
+        spread_kernel,
+        (count,),
+        [whole(piece) for piece in pieces],
+        [pl.BlockSpec((size, width), lambda step, order: (order[step], 0))],
+        [((count * size, width), jnp.float32)],
+        [order, *pieces],
+        size * width,
+        (),
+        1,
+    )[0]
+
+
+def assemble_kernel(trees, order, *refs):
+    count = len(refs) - 5
+    own, pieces = refs[0], refs[1:count]
+    in_grad, out_grad, mix_in_grad, mix_out_grad = refs[count : count + 4]
+    (choice,) = refs[count + 4 :]
+    share = own.shape[1]
+    block = own.shape[0] // trees
+    row = lax.broadcasted_iota(jnp.int32, (RANK, 128), 0)
+    lane = lax.broadcasted_iota(jnp.int32, (RANK, 128), 1)
+    same = lax.rem(lane, RANK) == row
+    for tree in range(trees):
+        chosen = own[tree * block + 8 * RANK : tree * block + 9 * RANK, :128]
+        choice[tree * RANK : (tree + 1) * RANK] = low(jnp.where(same, wide(chosen), 0.0))
+
+    def kind(source, stride, index):
+        return jnp.concatenate(
+            [
+                source[tree * stride + index * RANK : tree * stride + (index + 1) * RANK, :]
+                for tree in range(trees)
+            ],
+            axis=0,
+        )
+
+    for index in range(3):
+        out_grad[index] = t_dot(choice[...], kind(own, block, 4 + index))
+    mix_in_grad[...] = t_dot(kind(own, block, 7), choice[...])
+    for place, source in enumerate((own, *pieces)):
+        stride = block if place == 0 else 4 * RANK
+        start = pl.ds(pl.multiple_of(order[place] * share, share), share)
+        for index in range(3):
+            in_grad[index, start, :] = t_dot(kind(source, stride, index), choice[...])
+        mix_out_grad[:, start] = t_dot(choice[...], kind(source, stride, 3))
+
+
+def assemble_call(order, own, pieces, trees):
+    share = own.shape[1]
+    count = 1 + len(pieces)
+    width = count * share
+    out_shape = [((3, width, 128), jnp.float32), ((3, 128, share), jnp.float32)]
+    out_shape += [((share, 128), jnp.float32), ((128, width), jnp.float32)]
+    operands = [order, own, *pieces]
+    return kernel_call(
+        functools.partial(assemble_kernel, trees),
+        (1,),
+        [whole(array) for array in operands[1:]],
+        [pl.BlockSpec(shape, lambda *_, size=len(shape): (0,) * size) for shape, _ in out_shape],
+        out_shape,
+        operands,
+        2 * trees * RANK * 128 * width * 4,
+        [pltpu.VMEM((trees * RANK, 128), jnp.bfloat16)],
+        1,
+    )
 
 
 def body(
@@ -648,8 +968,6 @@
     adapter_pick,
 ):
     rows_here, model_width = tokens.shape
-    local_width = query_weight.shape[1]
-    heads_here = local_width // HD
     tensor_rank = lax.axis_index("tensor")
     tensor_count = lax.axis_size("tensor")
     owners = lax.axis_size("expert")
@@ -660,29 +978,40 @@
     experts_all = experts_here * owners
     column_share = model_width // tensor_count
     row_share = rows_here // tensor_count
-    float_kind = jnp.float32
-    half_kind = jnp.bfloat16
     hold = lax.optimization_barrier
+    level, core = tensor_rank // 2, tensor_rank % 2
 
     def own_rows(array):
         return lax.dynamic_slice_in_dim(array, tensor_rank * row_share, row_share, 0)
 
-    cotangent_rows = own_rows(cotangent)
-    routes_rows = own_rows(routes)
-    weights_rows = own_rows(gate_weights)
+    routes_wide = jnp.swapaxes(routes, 0, 1)
+    weights_wide = jnp.swapaxes(gate_weights, 0, 1)
     route_weights = jnp.sum(
         jnp.where(
-            routes_rows[:, :, None] == jnp.arange(experts_all, dtype=jnp.int32)[None, None, :],
-            weights_rows[:, :, None],
+            routes_wide[:, :, None] == jnp.arange(experts_all, dtype=jnp.int32)[None, None, :],
+            weights_wide[:, :, None],
             0.0,
         ),
-        axis=1,
+        axis=0,
     )
     weights_high = low(route_weights)
     weights_low = low(route_weights - wide(weights_high))
     side_width = -(-2 * experts_all // 128) * 128
-    side_pad = jnp.zeros((row_share, side_width - 2 * experts_all), half_kind)
-    cot_plane = jnp.concatenate([cotangent_rows, weights_high, weights_low, side_pad], axis=1)
+    side_pad = jnp.zeros((rows_here, side_width - 2 * experts_all), jnp.bfloat16)
+    side_rows = jnp.concatenate([weights_high, weights_low, side_pad], axis=1)
+    cot_queue = []
+    for step in range(span):
+        place = ((level + span - step) % span * 2 + core) * row_share
+        cot_queue.append(
+            jnp.concatenate(
+                [
+                    lax.dynamic_slice_in_dim(cotangent, place, row_share, 0),
+                    lax.dynamic_slice_in_dim(side_rows, place, row_share, 0),
+                ],
+                axis=1,
+            )
+        )
+    cot_queue = [jnp.concatenate(cot_queue, axis=0)]
     side_index = jnp.arange(side_width, dtype=jnp.int32)
     hidden_owner = (
         owner_rank * experts_here
@@ -694,104 +1023,74 @@
     )
     spread = jnp.swapaxes(spread_flat.reshape(side_width, experts_here, hidden_here), 0, 1)
 
-    cot_next = turn(cot_plane, axes, "z", 1)
-    cot_first = gather_first(cot_plane, axes)
-    inputs = wide(tokens)
-    first_gain = wide(attn_gain)[None, :]
-    second_gain = wide(ffn_gain)[None, :]
-    query_scale = wide(query_gain)[None, :]
-    key_scale = wide(key_gain)[None, :]
+    cot_planes = [None] * far
+    cot_queue.append(turn(cot_queue[0], axes, "z", 1))
+    cot_planes[0] = ring(cot_queue[0], axes, "x")
+    first_gain, second_gain = attn_gain[None, :], ffn_gain[None, :]
+    gains = (query_gain[None, :], key_gain[None, :])
     reached = ancestry(block_parent)
     cosine_table, sine_table = rope_tables(reached, rows_here // block_parent.shape[0], HD)
     signs = jnp.where(jnp.arange(HD) < HD // 2, -1.0, 1.0)[None, :]
-    key_mask = token_mask(reached[0], rows_here)
-    mask_added = jnp.where(key_mask, 0.0, MASKED_SCORE)
+    tables = (cosine_table, sine_table * signs)
+    mask = jnp.where(token_mask(reached[0], rows_here), 0.0, MASKED_SCORE)
     select = jnp.repeat(wide(adapter_pick), RANK, axis=1)
-    core = jnp.reshape(tensor_rank % 2, (1,)).astype(jnp.int32)
-    picked = jnp.argmax(adapter_pick[0]) * RANK
-    adapt_in_used = lax.dynamic_slice_in_dim(adapt_in, picked, RANK, 2)
-    adapt_out_used = lax.dynamic_slice_in_dim(adapt_out, picked, RANK, 1)
-    mix_in_used = lax.dynamic_slice_in_dim(adapt_in_out, picked, RANK, 1)
-    mix_out_used = lax.dynamic_slice_in_dim(adapt_out_out, picked, RANK, 0)
-    normed_in, lowrank, query_raw, key_raw, value_raw, squares = project_call(
-        tokens,
-        first_gain,
-        (query_weight, key_weight, value_weight),
-        adapt_in,
-        adapt_out,
-        select,
-    )
-
-    cot_planes = [None] * far
-    cot_next, cot_first, squares = hold((cot_next, cot_first, squares))
+    picked = jnp.argmax(adapter_pick[0]).astype(jnp.int32) * RANK
+    weights = (query_weight, key_weight, value_weight)
+    normed_in, lowrank, *raws, squares = project_call(
+        tokens, first_gain, weights, adapt_in, adapt_out, select
+    )
+
     squares = lax.psum(squares, "tensor")
-    cot_later = turn(cot_next, axes, "z", 1)
-    cot_planes[0] = gather_second(cot_first, axes)
-    cot_first = gather_first(cot_next, axes)
-    queries, keys, values, attended, mine, theirs = attend_call(
-        core,
+    squares, cot_queue[1], cot_planes[0] = hold((squares, cot_queue[1], cot_planes[0]))
+    cot_queue.append(turn(cot_queue[1], axes, "z", 1))
+    cot_planes[1] = ring(cot_queue[1], axes, "x")
+    *states, mine, theirs = attend_call(
+        jnp.reshape(core, (1,)).astype(jnp.int32),
         squares,
-        (query_raw, key_raw, value_raw),
-        (query_scale, key_scale),
-        (cosine_table, sine_table * signs),
-        mask_added,
+        raws,
+        gains,
+        tables,
+        mask,
         output_weight,
         adapt_in_out,
         row_share,
     )
 
-    cot_next, cot_first, mine, theirs = hold((cot_later, cot_first, mine, theirs))
-    cot_later = turn(cot_next, axes, "z", 1)
+    branch_kept, branch_came = scatter_tensor(mine, theirs, axes)
+    branch_came, cot_queue[2], cot_planes[1] = hold((branch_came, cot_queue[2], cot_planes[1]))
+    cot_queue.append(turn(cot_queue[2], axes, "z", 1))
+    cot_planes[2] = ring(cot_queue[2], axes, "x")
+    resid_rows, norm_plane, mixed_rows = resid_call(
+        branch_kept, branch_came, own_rows(tokens), adapt_out_out, select, second_gain
+    )
     gates = (expert_gate, turn(expert_gate, axes, "c", 1))
     ups = (expert_up, turn(expert_up, axes, "c", 1))
     down_tall = expert_down.reshape(-1, model_width)
     downs = (down_tall, turn(down_tall, axes, "c", 1))
-    branch_kept, branch_came = scatter_tensor(mine, theirs, axes)
-    branch_came, cot_planes[0] = hold((branch_came, cot_planes[0]))
-    cot_planes[1] = gather_second(cot_first, axes)
-    cot_first = gather_first(cot_next, axes)
-    resid_rows, norm_plane, mixed_rows = resid_call(
-        branch_kept, branch_came, own_rows(tokens), adapt_out_out, select, second_gain
-    )
-    query_squares = squares[0]
-    key_squares = squares[1]
-    query_inverse = lax.rsqrt(query_squares / model_width + EPSILON)[:, None]
-    key_inverse = lax.rsqrt(key_squares / model_width + EPSILON)[:, None]
-    second_inverse = lax.rsqrt(
-        jnp.mean(resid_rows * resid_rows, axis=1, keepdims=True) + EPSILON
-    )
-    score_scale = HD ** (-0.5)
-    queries = queries.reshape(rows_here, heads_here, HD)
-    keys = keys.reshape(rows_here, heads_here, HD)
-    values = values.reshape(rows_here, heads_here, HD)
-
-    cot_later, cot_first, cot_planes[1], norm_plane, gates, ups, downs = hold(
-        (cot_later, cot_first, cot_planes[1], norm_plane, gates, ups, downs)
-    )
+
     norm_next = turn(norm_plane, axes, "z", 1)
     norm_first = gather_first(norm_plane, axes)
-    cot_planes[2] = gather_second(cot_first, axes)
-    cot_first = gather_first(cot_later, axes)
     backs, sides = [None] * far, [None] * far
 
-    def hidden_step(first, second):
-        pieces = cot_planes[first] + cot_planes[second]
-        back, side = hidden_call(pieces, downs, spread_flat, experts_here)
-        backs[first], sides[first] = (back, 0), side
-        backs[second], sides[second] = (back, side.shape[0] // 2), side
+    def hidden_step(*indices):
+        back, side = hidden_call(
+            [cot_planes[index] for index in indices], downs, spread_flat, experts_here, row_share
+        )
+        for order, index in enumerate(indices):
+            backs[index], sides[index] = (back, order * side.shape[0] // len(indices)), side
         return back
 
     back_first = hidden_step(0, 1)
 
     norm_planes = [None] * far
-    norm_next, norm_first, cot_planes[2], cot_first, back_first = hold(
-        (norm_next, norm_first, cot_planes[2], cot_first, back_first)
+    norm_next, norm_first, cot_queue[3], cot_planes[2], back_first = hold(
+        (norm_next, norm_first, cot_queue[3], cot_planes[2], back_first)
     )
     backs[0], backs[1] = (back_first, backs[0][1]), (back_first, backs[1][1])
     norm_later = turn(norm_next, axes, "z", 1)
     norm_planes[0] = gather_second(norm_first, axes)
     norm_first = gather_first(norm_next, axes)
-    cot_planes[3] = gather_second(cot_first, axes)
+    cot_planes[3] = ring(cot_queue[3], axes, "x")
     parts, hiddens = [None] * far, [None] * far
 
     def expert_step(index):
@@ -800,19 +1099,20 @@
             norm_planes[index], gates, ups, spread, sides[index], back, offset
         )
 
-    norm_next, norm_first, norm_planes[0], cot_planes[3] = hold(
-        (norm_later, norm_first, norm_planes[0], cot_planes[3])
-    )
+    back_second = hidden_step(2)
+
+    norm_next, norm_first, norm_planes[0], cot_planes[3], back_second = hold(
+        (norm_later, norm_first, norm_planes[0], cot_planes[3], back_second)
+    )
+    backs[2] = (back_second, 0)
     norm_later = turn(norm_next, axes, "z", 1)
     norm_planes[1] = gather_second(norm_first, axes)
     norm_first = gather_first(norm_next, axes)
     expert_step(0)
-    back_second = hidden_step(2, 3)
-
-    norm_next, norm_first, norm_planes[1], back_second, parts[0] = hold(
-        (norm_later, norm_first, norm_planes[1], back_second, parts[0])
-    )
-    backs[2], backs[3] = (back_second, backs[2][1]), (back_second, backs[3][1])
+
+    norm_next, norm_first, norm_planes[1], parts[0] = hold(
+        (norm_later, norm_first, norm_planes[1], parts[0])
+    )
     norm_planes[2] = gather_second(norm_first, axes)
     norm_first = gather_first(norm_next, axes)
     expert_step(1)
@@ -821,9 +1121,9 @@
     norm_planes[3] = gather_second(norm_first, axes)
     came = [None] * far
     kept = [None] * far
-    sums = [None] * far
     came[1] = scatter_first(parts[1], axes)
     expert_step(2)
+    hidden_step(3)
 
     norm_planes[3], came[1], parts[2] = hold((norm_planes[3], came[1], parts[2]))
     kept[1], came[1] = scatter_second(parts[1], came[1], axes)
@@ -834,199 +1134,133 @@
     kept[1], came[1], came[2], came[0], parts[3] = hold(
         (kept[1], came[1], came[2], came[0], parts[3])
     )
-    sums[1] = scatter_last(kept[1], came[1])
-    ring_sum = turn(low(sums[1]), axes, "z", 1)
+    ring_sum = turn(low(scatter_last(kept[1], came[1])), axes, "z", 1)
     kept[2], came[2] = scatter_second(parts[2], came[2], axes)
     came[3] = scatter_first(parts[3], axes)
     kept[0], came[0] = scatter_second(parts[0], came[0], axes)
-    mixes = [None] * far
-    mixes[1], mixes[2] = down_call([hiddens[1], hiddens[2]], downs, near + span)
+    mixes, mix_came = [None] * far, [None] * far
+
+    def down_step(first, second):
+        mixes[first], mixes[second] = down_call(
+            [hiddens[first], hiddens[second]], downs, near, span, row_share
+        )
+
+    down_step(1, 2)
 
     ring_sum, kept[2], came[2], came[3], mixes[1], mixes[2] = hold(
         (ring_sum, kept[2], came[2], came[3], mixes[1], mixes[2])
     )
     ring_sum = turn(low(wide(ring_sum) + scatter_last(kept[2], came[2])), axes, "z", 1)
     kept[3], came[3] = scatter_second(parts[3], came[3], axes)
-    mix_came = [None] * far
-    mix_kept = [None] * far
-    mix_came[1] = scatter_first(mixes[1], axes)
-    mixes[3], mixes[0] = down_call([hiddens[3], hiddens[0]], downs, near + span)
-
-    ring_sum, kept[3], came[3], kept[0], came[0], mix_came[1], mixes[3], mixes[0] = hold(
-        (ring_sum, kept[3], came[3], kept[0], came[0], mix_came[1], mixes[3], mixes[0])
+    mix_came[1] = send_sum(mixes[1], axes, "x")
+    down_step(3, 0)
+
+    ring_sum, kept[3], came[3], kept[0], came[0], mixes[3], mixes[0] = hold(
+        (ring_sum, kept[3], came[3], kept[0], came[0], mixes[3], mixes[0])
     )
     ring_sum = turn(low(wide(ring_sum) + scatter_last(kept[3], came[3])), axes, "z", 1)
-    mix_kept[1], mix_came[1] = scatter_second(mixes[1], mix_came[1], axes)
-
-    ring_sum, mix_kept[1], mix_came[1] = hold((ring_sum, mix_kept[1], mix_came[1]))
+    ring_sum, mix_came[1] = hold((ring_sum, mix_came[1]))
+
+    mix_sum = turn(low(wide(mixes[1][0]) + wide(mix_came[1])), axes, "z", 1)
+    mix_came[2] = send_sum(mixes[2], axes, "x")
     ffn_rows_grad = wide(ring_sum) + scatter_last(kept[0], came[0])
-    second_scaled = ffn_rows_grad * second_gain
-    resid_grad_rows = wide(cotangent_rows) + norm_back(
+    second_scaled = ffn_rows_grad * wide(second_gain)
+    second_inverse = lax.rsqrt(
+        jnp.mean(resid_rows * resid_rows, axis=1, keepdims=True) + EPSILON
+    )
+    resid_grad_rows = wide(own_rows(cotangent)) + norm_back(
         second_scaled,
         resid_rows,
         second_inverse,
         model_width,
         jnp.sum(second_scaled * resid_rows, axis=1, keepdims=True),
     )
-    branch_sent = jnp.concatenate(
-        [low(resid_grad_rows), mixed_rows], axis=1
-    )
-    branch_whole = place_tensor(branch_sent, axes, half_kind)
-    mix_sum = turn(low(scatter_last(mix_kept[1], mix_came[1])), axes, "z", 1)
-    mix_came[2] = scatter_first(mixes[2], axes)
-
-    branch_whole, mix_came[2] = hold((branch_whole, mix_came[2]))
-    branch_grad = branch_whole[:, :model_width]
-    mixed = lax.dynamic_slice_in_dim(branch_whole, model_width + picked, RANK, 1)
-    mixed_grad = low(dot_t(branch_grad, mix_out_used))
-    attended_grad = low(dot_t(branch_grad, output_weight) + dot_t(mixed_grad, mix_in_used))
-    attended_grad = attended_grad.reshape(rows_here, heads_here, HD)
-    scores = (
-        jnp.einsum("qhd,khd->hqk", queries, keys, preferred_element_type=float_kind) * score_scale
-    )
-    scores = scores + mask_added[None]
-    raised = jnp.exp(scores - jnp.max(scores, axis=2, keepdims=True))
-    softmax_full = raised / jnp.sum(raised, axis=2, keepdims=True)
-    softmax_half = low(softmax_full)
-    value_grad = low(
-        jnp.einsum("hqk,qhd->khd", softmax_half, attended_grad, preferred_element_type=float_kind)
-    )
-    prob_grad = jnp.einsum("qhd,khd->hqk", attended_grad, values, preferred_element_type=float_kind)
-    score_grad = low(
-        softmax_full * (prob_grad - jnp.sum(softmax_full * prob_grad, axis=2, keepdims=True))
-    )
-    query_grad = (
-        jnp.einsum("hqk,khd->qhd", score_grad, keys, preferred_element_type=float_kind)
-        * score_scale
-    )
-    key_grad = (
-        jnp.einsum("hqk,qhd->khd", score_grad, queries, preferred_element_type=float_kind)
-        * score_scale
-    )
-    query_scaled = (
-        unrotate(query_grad, cosine_table, sine_table).reshape(rows_here, local_width) * query_scale
-    )
-    key_scaled = (
-        unrotate(key_grad, cosine_table, sine_table).reshape(rows_here, local_width) * key_scale
-    )
-
-    query_scaled, key_scaled, value_grad, mix_sum, mix_came[2] = hold(
-        (query_scaled, key_scaled, value_grad, mix_sum, mix_came[2])
-    )
-    mix_kept[2], mix_came[2] = scatter_second(mixes[2], mix_came[2], axes)
-    mix_came[3] = scatter_first(mixes[3], axes)
-    query_inner, key_inner = lax.psum(
-        (jnp.sum(query_scaled * query_raw, axis=1), jnp.sum(key_scaled * key_raw, axis=1)), "tensor"
-    )
-    query_raw_grad = low(
-        norm_back(query_scaled, query_raw, query_inverse, model_width, query_inner[:, None])
-    )
-    key_raw_grad = low(
-        norm_back(key_scaled, key_raw, key_inverse, model_width, key_inner[:, None])
-    )
-    value_raw_grad = value_grad.reshape(rows_here, local_width)
-    raw_grads = (query_raw_grad, key_raw_grad, value_raw_grad)
-    lowrank_part = low(
-        jnp.concatenate(
-            [dot_t(raw_grads[projection], adapt_out_used[projection]) for projection in range(3)],
-            axis=1,
-        )
-    )
-    normed_part = (
-        dot_t(query_raw_grad, query_weight)
-        + dot_t(key_raw_grad, key_weight)
-        + dot_t(value_raw_grad, value_weight)
-    )
-
-    normed_part, lowrank_part, mix_kept[2], mix_came[2], mix_came[3] = hold(
-        (normed_part, lowrank_part, mix_kept[2], mix_came[2], mix_came[3])
-    )
-    mix_sum = turn(low(wide(mix_sum) + scatter_last(mix_kept[2], mix_came[2])), axes, "z", 1)
-    mix_kept[3], mix_came[3] = scatter_second(mixes[3], mix_came[3], axes)
-    mix_came[0] = scatter_first(mixes[0], axes)
+    branch_sent = jnp.concatenate([low(resid_grad_rows), mixed_rows], axis=1)
+    branch_pieces = gather_tensor(branch_sent, axes)
+    order = jnp.stack(
+        [
+            (level + span - step) % span * 2 + side
+            for side in (core, 1 - core)
+            for step in range(span)
+        ]
+    ).astype(jnp.int32)
+
+    branch_pieces, mix_sum, mix_came[2] = hold((branch_pieces, mix_sum, mix_came[2]))
+    mix_sum = turn(
+        low(wide(mix_sum) + (wide(mixes[2][0]) + wide(mix_came[2]))), axes, "z", 1
+    )
+    mix_came[3] = send_sum(mixes[3], axes, "x")
+    rank_list = jnp.reshape(tensor_rank, (1,)).astype(jnp.int32)
+    query_grad, key_grad, value_grad, inner, mix_in_grad, mix_out_grad = backward_call(
+        jnp.concatenate([order, rank_list]),
+        branch_pieces,
+        output_weight,
+        adapt_in_out,
+        adapt_out_out,
+        select,
+        states,
+        raws[:2],
+        gains,
+        tables,
+        mask,
+        column_share,
+    )
+    inner = lax.psum(inner, "tensor")
+    normed_mine, normed_theirs, lowrank_part, adapt_grad = weight_call(
+        jnp.stack([core, picked]).astype(jnp.int32),
+        inner,
+        squares,
+        (query_grad, key_grad, value_grad),
+        raws[:2],
+        weights,
+        lowrank,
+        adapt_out,
+        row_share,
+    )
+
+    normed_mine, normed_theirs, lowrank_part, mix_sum, mix_came[3] = hold(
+        (normed_mine, normed_theirs, lowrank_part, mix_sum, mix_came[3])
+    )
+    mix_sum = turn(
+        low(wide(mix_sum) + (wide(mixes[3][0]) + wide(mix_came[3]))), axes, "z", 1
+    )
+    mix_came[0] = send_sum(mixes[0], axes, "x")
     lowrank_grad = low(sum_tensor(lowrank_part, axes))
-    blocks = normed_part.reshape(span, 2, row_share, model_width)
-    kept_part, came_part = scatter_tensor(
-        lax.dynamic_index_in_dim(blocks, core[0], 1, False).reshape(-1, model_width),
-        low(lax.dynamic_index_in_dim(blocks, 1 - core[0], 1, False).reshape(-1, model_width)),
-        axes,
-    )
-    normed_grad_rows = kept_part + wide(came_part)
-    lowrank_rows = own_rows(lowrank_grad)
-    for projection in range(3):
-        normed_grad_rows = normed_grad_rows + dot_t(
-            lowrank_rows[:, projection * RANK : (projection + 1) * RANK], adapt_in_used[projection]
-        )
-    first_scaled = normed_grad_rows * first_gain
-    inputs_rows = own_rows(inputs)
-    first_inverse = lax.rsqrt(
-        jnp.mean(inputs_rows * inputs_rows, axis=1, keepdims=True) + EPSILON
-    )
-    input_grad_rows = resid_grad_rows + norm_back(
-        first_scaled,
-        inputs_rows,
-        first_inverse,
-        model_width,
-        jnp.sum(first_scaled * inputs_rows, axis=1, keepdims=True),
-    )
-    normed_share = lax.dynamic_slice_in_dim(
-        normed_in, tensor_rank * column_share, column_share, 1
-    )
-    branch_share = lax.dynamic_slice_in_dim(
-        branch_grad, tensor_rank * column_share, column_share, 1
-    )
-    compact = low(
-        jnp.concatenate(
-            [t_dot(lowrank_grad, normed_share), t_dot(mixed, branch_share)]
-            + [
-                lax.dynamic_slice_in_dim(
-                    t_dot(lowrank[projection], raw_grads[projection]), picked, RANK, 0
-                )
-                for projection in range(3)
-            ]
-            + [t_dot(mixed_grad, attended)],
-            axis=0,
-        )
-    )
-
-    input_grad_rows, compact, mix_sum, mix_kept[3], mix_came[3], mix_came[0] = hold(
-        (low(input_grad_rows), compact, mix_sum, mix_kept[3], mix_came[3], mix_came[0])
-    )
-    input_grad = place_tensor(input_grad_rows, axes, float_kind)
-    mix_sum = turn(low(wide(mix_sum) + scatter_last(mix_kept[3], mix_came[3])), axes, "z", 1)
-    mix_kept[0], mix_came[0] = scatter_second(mixes[0], mix_came[0], axes)
-    layer_rows = low(resid_rows + wide(mix_sum) + scatter_last(mix_kept[0], mix_came[0]))
+    normed_kept, normed_came = scatter_tensor(normed_mine, normed_theirs, axes)
+    maps = jnp.swapaxes(lax.dynamic_slice_in_dim(adapt_in, picked, RANK, 2), 0, 1)
+    maps = maps.reshape(model_width, 3 * RANK)
+    maps = jnp.concatenate(
+        [maps, jnp.zeros((model_width, 128 - 3 * RANK), jnp.bfloat16)], axis=1
+    )
+    input_rows = input_call(
+        normed_kept,
+        normed_came,
+        own_rows(lowrank_grad),
+        maps,
+        own_rows(tokens),
+        first_gain,
+        resid_grad_rows,
+    )
+    compact = compact_call(
+        rank_list, lowrank_grad, normed_in, mix_out_grad, adapt_grad, mix_in_grad, select
+    )
+    trees = jnp.concatenate(ring(compact, axes, "x"), axis=0)
+
+    input_rows, trees, mix_sum, mix_came[0] = hold((input_rows, trees, mix_sum, mix_came[0]))
+    input_grad = spread_call(order, gather_tensor(input_rows, axes))
+    mix_total = wide(mix_sum) + (wide(mixes[0][0]) + wide(mix_came[0]))
+    mix_total = jnp.split(mix_total, span, axis=0)
+    mix_last = send_sum([low(part) for part in mix_total], axes, "y")
+    trees = jnp.concatenate(ring(trees, axes, "z"), axis=0)
+
+    trees, mix_last = hold((trees, mix_last))
+    shared = trees.reshape(owners, -1, column_share)[:, : 4 * RANK]
+    shared = gather_tensor(shared.reshape(-1, column_share), axes)
+    grad_adapt_in, grad_adapt_out, grad_adapt_in_out, grad_adapt_out_out = assemble_call(
+        order, trees, shared[1:], owners
+    )
+    layer_rows = low(resid_rows + mix_total[0] + wide(mix_last))
     layer_out = swap_columns(layer_rows, axes)
-
-    kinds = compact.shape[0] // RANK
-    picks_sent = low(
-        jnp.broadcast_to(wide(adapter_pick)[:, :, None], (1, adapter_pick.shape[1], 128))
-    ).reshape(-1, 128)
-    picks_sent = jnp.concatenate(
-        [picks_sent, jnp.zeros((16 - picks_sent.shape[0], 128), half_kind)], axis=0
-    )
-    picks_sent = jnp.tile(picks_sent, (1, column_share // 128))
-    compact = jnp.concatenate([compact, picks_sent], axis=0)
-    trees = jnp.concatenate(
-        ring(jnp.concatenate(ring(compact, axes, "x"), axis=0), axes, "z"), axis=0
-    )
-    trees = trees.reshape(owners, kinds + 1, RANK, column_share)
-    tree_picks = trees[:, kinds, : adapter_pick.shape[1], 0]
-    grad_adapt_out = jnp.einsum(
-        "sa,skrc->karc", tree_picks, trees[:, 4:7], preferred_element_type=float_kind
-    ).reshape(3, -1, column_share)
-    grad_adapt_in_out = jnp.einsum(
-        "sa,src->car", tree_picks, trees[:, 7], preferred_element_type=float_kind
-    ).reshape(column_share, -1)
-    shared = place_tensor(
-        trees[:, :4].reshape(owners * 4 * RANK, column_share), axes, half_kind
-    ).reshape(tensor_count, owners, 4, RANK, column_share)
-    grad_adapt_in = jnp.einsum(
-        "sa,tskrc->ktcar", tree_picks, shared[:, :, :3], preferred_element_type=float_kind
-    ).reshape(3, model_width, -1)
-    grad_adapt_out_out = jnp.einsum(
-        "sa,tsrc->artc", tree_picks, shared[:, :, 3], preferred_element_type=float_kind
-    ).reshape(-1, model_width)
     return (
         layer_out,
         input_grad,

time: 608 us -> 570 us (0.938)
  Pallas kernels: 191 us -> 242 us
  local copies, waits for them, and re-layouts: 51.5 us -> 22.8 us
  matrix products: 26 us -> 0 us
  starting transfers between devices: 93.5 us -> 69.2 us
  other arithmetic: 45.1 us -> 27.9 us
    pallas_call x11 -> x18, Pallas kernels: 191 us -> 242 us  [kernel_call(): pl.pallas_call(kernel, grid_spec=pltpu.PrefetchScalarGridSpec(num_scalar_...]
    ppermute x101 -> x78, starting transfers between devices: 93.5 us -> 69.2 us  [turn(): return lax.ppermute(array, axis, pairs)]
    dot_general x26 -> x0, matrix products: 22.5 us -> none  [the longest x12 11.7 us: dot_t(): lax.dot_general(left, right, (((1,), (1,)), ((), ())), preferred_element_...]
    unnamed x248 -> x149, local copies, waits for them, and re-layouts: 18.4 us -> 9.35 us
    reshape x5 -> x1, local copies, waits for them, and re-layouts: 6.53 us -> 0.28 us  [body(): maps = maps.reshape(model_width, 3 * RANK)]
    convert_element_type x17 -> x15, other arithmetic: 11.6 us -> 15.8 us  [low(): return array.astype(jnp.bfloat16)]
    ppermute x101 -> x78, waiting for transfers between devices: 169 us -> 171 us  [turn(): return lax.ppermute(array, axis, pairs)]
  transfers between devices with their start and end apart: 101 -> 78, of which waited for: 35 -> 19; matrix products, arithmetic and copies ran while one was open for 16% -> 7% of each run, Pallas kernels for 32% -> 42%
where the time goes in v4:
time: 570 us; the launch traced here: 561 us
  Pallas kernels  242 us (42%)
  waiting for transfers between devices  171 us (30%)
  starting transfers between devices  69.2 us (12%)
  other arithmetic  27.9 us (5%)
  blocking collectives  24.8 us (4%)
  local copies, waits for them, and re-layouts  22.8 us (4%)
    pallas_call x18, Pallas kernels, kernel_call(): pl.pallas_call(kernel, grid_spec=pltpu.PrefetchScalarGridSpec(num_scalar_...  242 us
    ppermute x78, waiting for transfers between devices, turn(): return lax.ppermute(array, axis, pairs)  171 us
    ppermute x78, starting transfers between devices, turn(): return lax.ppermute(array, axis, pairs)  69.2 us
    convert_element_type x15, other arithmetic, low(): return array.astype(jnp.bfloat16)  15.8 us
    psum x1, blocking collectives, body(): squares = lax.psum(squares, 'tensor')  13.2 us
    psum x1, blocking collectives, body(): inner = lax.psum(inner, 'tensor')  11.6 us
  transfers between devices with their start and end apart: 78, of which 19 were waited for; matrix products, arithmetic and copies ran while one was open for 7% of the time, Pallas kernels for 42%

profile of v4, /device:TPU:0, one launch (start us, length us, event | category | flops | bytes accessed | tf_op | source)
XLA Modules:
  0.0 561.2 jit_solution(1654580284896817158)
XLA Ops:
  3.5 3.1 collective-permute-start
  10.2 14.9 %shard_map.244 = (bf16[512,2048]{1,0:T(8,128)(2,1)}, bf16[3,512,128]{2,1,0:T(8,128)(2,1)}, f32[512,512]{1,0:T(8,128)}, f32[512,512]{1,0:T(8,128)}, f32[512,512]{1,0:T(8,128)}, /*index=5*/f32[8,512]{1,0:T(8,128)}) custom-call(bf16[512,2048]{1,0:T(8,128)(2,1)} %tokens.1, bf16[1,2048]{1,0:T(2,128)(2,1)} %broadcast_in_dim.43.gain, ...), custom_call_target="tpu_custom_call" | custom-call | flops 3221225472 | bytes 10359296 | tf_op jit(solution)/shard_map/pallas_call | solution.py:212
  26.3 13.2 %psum.14.squares = f32[8,512]{1,0:T(8,128)} all-reduce(f32[8,512]{1,0:T(8,128)} %get-tuple-element.181), channel_id=1, replica_groups=mesh['expert'=8,'tensor'=4] {'tensor'}, use_global_device_ids=true, to_apply=%region_0.1 | all-reduce | flops 4096 | bytes 32768 | tf_op jit(solution)/shard_map/psum | solution.py:1043
  42.9 11.3 %shard_map.245 = (bf16[512,512]{1,0:T(8,128)(2,1)}, bf16[512,512]{1,0:T(8,128)(2,1)}, bf16[512,512]{1,0:T(8,128)(2,1)}, bf16[512,512]{1,0:T(8,128)(2,1)}, f32[25...) custom-call(s32[1]{0:T(128)} %bitcast.core, f32[8,512]{1,0:T(8,128)} %psum.14.squares, ...), custom_call_target="tpu_custom_call" | custom-call | flops 1610612736 | bytes 6965252 | tf_op jit(solution)/shard_map/pallas_call | solution.py:212
  57.3 2.8 add_convert_fusion.3
  61.2 1.9 constant_dynamic-slice_fusion.5.tokens
  63.1 20.3 %collective-permute-done.4.refs_0_ = bf16[256,2176]{1,0:T(8,128)(2,1)} collective-permute-done((bf16[256,2176]{1,0:T(8,128)(2,1)S(1)}, bf16[256,2176]{1,0:T(8,128)(2,1)}, u32[]{:S(2)}, u32[]{:S(2)}) %collective-permute-start.4) | collective-permute-done | bytes 1114144 | tf_op jit(solution)/shard_map/ppermute | solution.py:76
  84.2 3.2 shard_map.246
  90.5 6.8 %collective-permute-done.8 = bf16[64,2048]{1,0:T(8,128)(2,1)S(1)} collective-permute-done((bf16[64,2048]{1,0:T(8,128)(2,1)S(1)}, bf16[64,2048]{1,0:T(8,128)(2,1)S(1)}, u32[]{:S(2)}, u32[]{:S(2)}) %collective-permute-start.8) | collective-permute-done | bytes 262176 | tf_op jit(solution)/shard_map/ppermute | solution.py:76
  99.4 15.7 %shard_map.247 = (bf16[8,1024,256]{2,1,0:T(8,128)(2,1)}, bf16[1024,128]{1,0:T(8,128)(2,1)}) custom-call(bf16[256,2176]{1,0:T(8,128)(2,1)} %copy-done.12, bf16[256,2176]{1,0:T(8,128)(2,1)} %collective-permute-done.1.refs_1_, bf16[256,2176]{1,0:T(8,128)(2,1)} %copy-done.47, bf16[256,2176]{1,0:T(8,128)(2,1)} %collective-permute-done.5.refs_3_, ...), custom_call_target="tpu_custom_call" | custom-call | flops 8589934592 | bytes 13107200 | tf_op jit(solution)/shard_map/pallas_call | solution.py:212
  115.1 21.9 %collective-permute-done.6 = bf16[128,2048]{1,0:T(8,128)(2,1)S(1)} collective-permute-done((bf16[128,2048]{1,0:T(8,128)(2,1)S(1)}, bf16[128,2048]{1,0:T(8,128)(2,1)S(1)}, u32[]{:S(2)}, u32[]{:S(2)}) %collective-permute-start.6) | collective-permute-done | bytes 524320 | tf_op jit(solution)/shard_map/ppermute | solution.py:76
  139.1 4.7 collective-permute-done.14
  146.8 5.4 collective-permute-done.12
  153.0 10.0 %shard_map.248 = (bf16[8,512,256]{2,1,0:T(8,128)(2,1)}, bf16[512,128]{1,0:T(8,128)(2,1)}) custom-call(bf16[256,2176]{1,0:T(8,128)(2,1)} %collective-permute-done.4.refs_0_, bf16[256,2176]{1,0:T(8,128)(2,1)} %copy-done.50, bf16[1024,2048]{1,0:T(8,128)(2,1)} %bitcast.13.refs_4_.refs_2_, bf16[1024,2048]{1,0:T(8,128)(2,1)} %collective-permute-done.11.refs_5_.refs_3_, ...), custom_call_target="tpu_custom_call" | custom-call | flops 4294967296 | bytes 10878976 | tf_op jit(solution)/shard_map/pallas_call | solution.py:212
  163.2 16.6 %collective-permute-done.16.refs_3_ = bf16[128,2048]{1,0:T(8,128)(2,1)S(1)} collective-permute-done((bf16[128,2048]{1,0:T(8,128)(2,1)S(1)}, bf16[128,2048]{1,0:T(8,128)(2,1)S(1)}, u32[]{:S(2)}, u32[]{:S(2)}) %collective-permute-start.16) | collective-permute-done | bytes 524320 | tf_op jit(solution)/shard_map/ppermute | solution.py:76
  185.2 25.7 %shard_map.249 = (bf16[128,2048]{1,0:T(8,128)(2,1)}, bf16[128,2048]{1,0:T(8,128)(2,1)}, bf16[128,2048]{1,0:T(8,128)(2,1)}, bf16[128,2048]{1,0:T(8,128)(2,1)}, bf16[8,512,256]{2,1,0:T(8,128)(2,1)}) custom-call(bf16[128,2048]{1,0:T(8,128)(2,1)} %copy-done.23, bf16[128,2048]{1,0:T(8,128)(2,1)} %copy-done.68, bf16[128,2048]{1,0:T(8,128)(2,1)} %copy-done.22, ...), custom_call_target="tpu_custom_call" | custom-call | flops 17179869184 | bytes 23592960 | tf_op jit(solution)/shard_map/pallas_call | solution.py:212
  211.0 10.0 %shard_map.252 = (bf16[8,512,256]{2,1,0:T(8,128)(2,1)}, bf16[512,128]{1,0:T(8,128)(2,1)}) custom-call(bf16[256,2176]{1,0:T(8,128)(2,1)} %copy-done.48, bf16[256,2176]{1,0:T(8,128)(2,1)} %copy-done.49, bf16[1024,2048]{1,0:T(8,128)(2,1)} %bitcast.13.refs_4_.refs_2_, bf16[1024,2048]{1,0:T(8,128)(2,1)} %collective-permute-done.11.refs_5_.refs_3_, ...), custom_call_target="tpu_custom_call" | custom-call | flops 4294967296 | bytes 10878976 | tf_op jit(solution)/shard_map/pallas_call | solution.py:212
  226.3 25.8 %shard_map.250 = (bf16[128,2048]{1,0:T(8,128)(2,1)}, bf16[128,2048]{1,0:T(8,128)(2,1)}, bf16[128,2048]{1,0:T(8,128)(2,1)}, bf16[128,2048]{1,0:T(8,128)(2,1)}, bf16[8,512,256]{2,1,0:T(8,128)(2,1)}) custom-call(bf16[128,2048]{1,0:T(8,128)(2,1)} %copy-done.25, bf16[128,2048]{1,0:T(8,128)(2,1)} %copy-done.64, bf16[128,2048]{1,0:T(8,128)(2,1)} %copy-done.24, ...), custom_call_target="tpu_custom_call" | custom-call | flops 17179869184 | bytes 23592960 | tf_op jit(solution)/shard_map/pallas_call | solution.py:212
  256.4 26.0 %shard_map.251 = (bf16[128,2048]{1,0:T(8,128)(2,1)}, bf16[128,2048]{1,0:T(8,128)(2,1)}, bf16[128,2048]{1,0:T(8,128)(2,1)}, bf16[128,2048]{1,0:T(8,128)(2,1)}, bf16[8,512,256]{2,1,0:T(8,128)(2,1)}) custom-call(bf16[128,2048]{1,0:T(8,128)(2,1)} %copy-done.29, bf16[128,2048]{1,0:T(8,128)(2,1)} %copy-done.69, bf16[128,2048]{1,0:T(8,128)(2,1)} %copy-done.28, ...), custom_call_target="tpu_custom_call" | custom-call | flops 17179869184 | bytes 21364736 | tf_op jit(solution)/shard_map/pallas_call | solution.py:212
  282.5 13.2 %shard_map.254 = (bf16[256,2048]{1,0:T(8,128)(2,1)}, bf16[256,2048]{1,0:T(8,128)(2,1)}, bf16[256,2048]{1,0:T(8,128)(2,1)}, bf16[256,2048]{1,0:T(8,128)(2,1)}) custom-call(bf16[8,512,256]{2,1,0:T(8,128)(2,1)} %get-tuple-element.274.refs_0_, bf16[8,512,256]{2,1,0:T(8,128)(2,1)} %get-tuple-element.275.refs_1_, bf16[1024,2048]{1,0:T(8,128)(2,1)} %bitcast.13.refs_4_.refs_2_, ...), custom_call_target="tpu_custom_call" | custom-call | flops 8589934592 | bytes 12582912 | tf_op jit(solution)/shard_map/pallas_call | solution.py:212
  302.7 25.7 %shard_map.253 = (bf16[128,2048]{1,0:T(8,128)(2,1)}, bf16[128,2048]{1,0:T(8,128)(2,1)}, bf16[128,2048]{1,0:T(8,128)(2,1)}, bf16[128,2048]{1,0:T(8,128)(2,1)}, bf16[8,512,256]{2,1,0:T(8,128)(2,1)}) custom-call(bf16[128,2048]{1,0:T(8,128)(2,1)} %copy-done.27, bf16[128,2048]{1,0:T(8,128)(2,1)} %copy-done.62, bf16[128,2048]{1,0:T(8,128)(2,1)} %copy-done.26, ...), custom_call_target="tpu_custom_call" | custom-call | flops 17179869184 | bytes 21364736 | tf_op jit(solution)/shard_map/pallas_call | solution.py:212
  335.3 11.9 %collective-permute-done.41 = bf16[64,2048]{1,0:T(8,128)(2,1)S(1)} collective-permute-done((bf16[64,2048]{1,0:T(8,128)(2,1)S(1)}, bf16[64,2048]{1,0:T(8,128)(2,1)S(1)}, u32[]{:S(2)}, u32[]{:S(2)}) %collective-permute-start.41) | collective-permute-done | bytes 262176 | tf_op jit(solution)/shard_map/ppermute | solution.py:76
  352.0 3.9 collective-permute-start.44
  355.9 13.3 %shard_map.255 = (bf16[256,2048]{1,0:T(8,128)(2,1)}, bf16[256,2048]{1,0:T(8,128)(2,1)}, bf16[256,2048]{1,0:T(8,128)(2,1)}, bf16[256,2048]{1,0:T(8,128)(2,1)}) custom-call(bf16[8,512,256]{2,1,0:T(8,128)(2,1)} %get-tuple-element.293.refs_0_, bf16[8,512,256]{2,1,0:T(8,128)(2,1)} %get-tuple-element.294.refs_1_, bf16[1024,2048]{1,0:T(8,128)(2,1)} %bitcast.13.refs_4_.refs_2_, ...), custom_call_target="tpu_custom_call" | custom-call | flops 8589934592 | bytes 12582912 | tf_op jit(solution)/shard_map/pallas_call | solution.py:212
  373.8 16.7 %collective-permute-done.50 = bf16[256,2048]{1,0:T(8,128)(2,1)S(1)} collective-permute-done((bf16[256,2048]{1,0:T(8,128)(2,1)S(1)}, bf16[256,2048]{1,0:T(8,128)(2,1)S(1)}, u32[]{:S(2)}, u32[]{:S(2)}) %collective-permute-start.50) | collective-permute-done | bytes 1048608 | tf_op jit(solution)/shard_map/ppermute | solution.py:76
  390.9 2.6 fusion.22
  395.6 3.9 collective-permute-start.54
  399.5 3.6 collective-permute-done.51.refs_1_
  404.5 8.2 %collective-permute-done.54 = bf16[256,2048]{1,0:T(8,128)(2,1)S(1)} collective-permute-done((bf16[256,2048]{1,0:T(8,128)(2,1)S(1)}, bf16[256,2048]{1,0:T(8,128)(2,1)S(1)}, u32[]{:S(2)}, u32[]{:S(2)}) %collective-permute-start.54) | collective-permute-done | bytes 1048608 | tf_op jit(solution)/shard_map/ppermute | solution.py:76
  414.3 2.3 collective-permute-start.56
  419.0 19.2 %shard_map.256 = (f32[512,512]{1,0:T(8,128)}, f32[512,512]{1,0:T(8,128)}, bf16[512,512]{1,0:T(8,128)(2,1)}, f32[8,512]{1,0:T(8,128)}, bf16[16,512]{1,0:T(8,128)(2,1)}, /*index=5*/bf16[16,512]{1,0:T(8,128)(2,1)}) custom-call(s32[5]{0:T(128)} %concatenate.73.scalars, bf16[128,2176]{1,0:T(8,128)(2,1)} %copy-done.19, bf16[128,2176]{1,0:T(8,128)(2,1)} %copy-done.53, ...), custom_call_target="tpu_custom_call" | custom-call | flops 2952790016 | bytes 10750484 | tf_op jit(solution)/shard_map/pallas_call | solution.py:212
  438.2 11.6 %psum.15.inner = f32[8,512]{1,0:T(8,128)} all-reduce(f32[8,512]{1,0:T(8,128)} %get-tuple-element.322), channel_id=1, replica_groups=mesh['expert'=8,'tensor'=4] {'tensor'}, use_global_device_ids=true, to_apply=%region_9.10 | all-reduce | flops 4096 | bytes 32768 | tf_op jit(solution)/shard_map/psum | solution.py:1208
  449.7 11.6 %shard_map.257 = (f32[256,2048]{1,0:T(8,128)}, bf16[256,2048]{1,0:T(8,128)(2,1)}, bf16[512,128]{1,0:T(8,128)(2,1)}, bf16[48,512]{1,0:T(8,128)(2,1)}) custom-call(s32[2]{0:T(128)} %pad_add_fusion.scalars, f32[8,512]{1,0:T(8,128)} %psum.15.inner, f32[8,512]{1,0:T(8,128)} %psum.14.squares, f32[512,512]{1,0:T(8,128)} %get-tuple-element.323.query_grad, ...), custom_call_target="tpu_custom_call" | custom-call | flops 3221225472 | bytes 11829256 | tf_op jit(solution)/shard_map/pallas_call | solution.py:212
  462.8 3.2 add_convert_fusion
  470.3 2.1 collective-permute-done.61
  473.2 2.9 shard_map.259
  476.0 2.4 collective-permute-start.62
  482.1 9.1 %collective-permute-done.62 = bf16[144,512]{1,0:T(8,128)(2,1)S(1)} collective-permute-done((bf16[144,512]{1,0:T(8,128)(2,1)}, bf16[144,512]{1,0:T(8,128)(2,1)S(1)}, u32[]{:S(2)}, u32[]{:S(2)}) %collective-permute-start.62) | collective-permute-done | bytes 147488 | tf_op jit(solution)/shard_map/ppermute | solution.py:76
  491.3 3.6 shard_map.258.refs_0_
  495.6 9.9 %collective-permute-done.65 = bf16[288,512]{1,0:T(8,128)(2,1)S(1)} collective-permute-done((bf16[288,512]{1,0:T(8,128)(2,1)S(1)}, bf16[288,512]{1,0:T(8,128)(2,1)S(1)}, u32[]{:S(2)}, u32[]{:S(2)}) %collective-permute-start.65) | collective-permute-done | bytes 294944 | tf_op jit(solution)/shard_map/ppermute | solution.py:76
  505.5 9.8 %collective-permute-done.66 = bf16[288,512]{1,0:T(8,128)(2,1)} collective-permute-done((bf16[288,512]{1,0:T(8,128)(2,1)S(1)}, bf16[288,512]{1,0:T(8,128)(2,1)}, u32[]{:S(2)}, u32[]{:S(2)}) %collective-permute-start.66) | collective-permute-done | bytes 294944 | tf_op jit(solution)/shard_map/ppermute | solution.py:76
  515.2 2.0 add_add_fusion
  520.1 4.2 collective-permute-done.67
  525.4 6.2 %collective-permute-done.68 = bf16[128,2048]{1,0:T(8,128)(2,1)} collective-permute-done((bf16[128,2048]{1,0:T(8,128)(2,1)}, bf16[128,2048]{1,0:T(8,128)(2,1)}, u32[]{:S(2)}, u32[]{:S(2)}) %collective-permute-start.68) | collective-permute-done | bytes 524320 | tf_op jit(solution)/shard_map/ppermute | solution.py:76
  535.6 10.1 %collective-permute-done.75.refs_1_ = bf16[512,512]{1,0:T(8,128)(2,1)} collective-permute-done((bf16[512,512]{1,0:T(8,128)(2,1)S(1)}, bf16[512,512]{1,0:T(8,128)(2,1)}, u32[]{:S(2)}, u32[]{:S(2)}) %collective-permute-start.75) | collective-permute-done | bytes 524320 | tf_op jit(solution)/shard_map/ppermute | solution.py:76
  545.7 2.7 collective-permute-done.70
  549.1 4.6 shard_map.260
  555.4 5.3 shard_map.261
  (400 shorter events, 92.5 us)
Async XLA Ops:
  3.5 39.4 %collective-permute-start = (bf16[256,2176]{1,0:T(8,128)(2,1)S(1)}, bf16[256,2176]{1,0:T(8,128)(2,1)S(1)}, u32[]{:S(2)}, u32[]{:S(2)}) collective-permute-start(bf16[256,2176]{1,0:T(8,128)(2,1)S(1)} %maximum_maximum_fusion.refs_0_), channel_id=1, source_target_pairs={{0,8},{4,12},{8,16},{12,20},{16,24},{20,28},{24,0},{28,4},{1,9},{5... | collective-permute-start | bytes 3342344 | tf_op jit(solution)/shard_map/ppermute | solution.py:76
  6.6 36.3 %collective-permute-start.1 = (bf16[256,2176]{1,0:T(8,128)(2,1)S(1)}, bf16[256,2176]{1,0:T(8,128)(2,1)}, u32[]{:S(2)}, u32[]{:S(2)}) collective-permute-start(bf16[256,2176]{1,0:T(8,128)(2,1)S(1)} %maximum_maximum_fusion.refs_0_), channel_id=1, source_target_pairs={{0,4},{4,0},{8,12},{12,8},{16,20},{20,16},{24,28},{28,24},{1,5},{5... | collective-permute-start | bytes 3342344 | tf_op jit(solution)/shard_map/ppermute | solution.py:76
  8.1 89.9 %collective-permute-start.11 = (bf16[1024,2048]{1,0:T(8,128)(2,1)}, bf16[1024,2048]{1,0:T(8,128)(2,1)}, u32[]{:S(2)}, u32[]{:S(2)}) collective-permute-start(bf16[1024,2048]{1,0:T(8,128)(2,1)} %bitcast.13.refs_4_.refs_2_), channel_id=1, source_target_pairs={{0,1},{1,0},{2,3},{3,2},{4,5},{5,4},{6,7},{7,6},{8,9},{9,8},{10,11... | collective-permute-start | bytes 12582920 | tf_op jit(solution)/shard_map/ppermute | solution.py:76
  54.3 29.1 %collective-permute-start.4 = (bf16[256,2176]{1,0:T(8,128)(2,1)S(1)}, bf16[256,2176]{1,0:T(8,128)(2,1)}, u32[]{:S(2)}, u32[]{:S(2)}) collective-permute-start(bf16[256,2176]{1,0:T(8,128)(2,1)S(1)} %collective-permute-done.refs_2_), channel_id=1, source_target_pairs={{0,8},{4,12},{8,16},{12,20},{16,24},{20,28},{24,0},{28,4},{1,9},{5... | collective-permute-start | bytes 3342344 | tf_op jit(solution)/shard_map/ppermute | solution.py:76
  56.2 27.2 %collective-permute-start.5 = (bf16[256,2176]{1,0:T(8,128)(2,1)S(1)}, bf16[256,2176]{1,0:T(8,128)(2,1)}, u32[]{:S(2)}, u32[]{:S(2)}) collective-permute-start(bf16[256,2176]{1,0:T(8,128)(2,1)S(1)} %collective-permute-done.refs_2_), channel_id=1, source_target_pairs={{0,4},{4,0},{8,12},{12,8},{16,20},{20,16},{24,28},{28,24},{1,5},{5... | collective-permute-start | bytes 3342344 | tf_op jit(solution)/shard_map/ppermute | solution.py:76
  60.0 23.4 %collective-permute-start.3 = (bf16[128,2176]{1,0:T(8,128)(2,1)S(1)}, bf16[128,2176]{1,0:T(8,128)(2,1)S(1)}, u32[]{:S(2)}, u32[]{:S(2)}) collective-permute-start(bf16[128,2176]{1,0:T(8,128)(2,1)S(1)} %get-tuple-element.360), channel_id=1, source_target_pairs={{0,2},{1,3},{2,0},{3,1},{4,6},{5,7},{6,4},{7,5},{8,10},{9,11},{10,... | collective-permute-start | bytes 1671176 | tf_op jit(solution)/shard_map/ppermute | solution.py:76
  60.5 123.0 %collective-permute-start.23 = (bf16[4,2048,256]{2,1,0:T(8,128)(2,1)}, bf16[4,2048,256]{2,1,0:T(8,128)(2,1)}, u32[]{:S(2)}, u32[]{:S(2)}) collective-permute-start(bf16[4,2048,256]{2,1,0:T(8,128)(2,1)} %refs_4_.8), channel_id=1, source_target_pairs={{0,1},{1,0},{2,3},{3,2},{4,5},{5,4},{6,7},{7,6},{8,9},{9,8},{10,11... | collective-permute-start | bytes 12582920 | tf_op jit(solution)/shard_map/ppermute | solution.py:76
  83.4 100.7 %collective-permute-start.24 = (bf16[4,2048,256]{2,1,0:T(8,128)(2,1)}, bf16[4,2048,256]{2,1,0:T(8,128)(2,1)}, u32[]{:S(2)}, u32[]{:S(2)}) collective-permute-start(bf16[4,2048,256]{2,1,0:T(8,128)(2,1)} %refs_5_.8), channel_id=1, source_target_pairs={{0,1},{1,0},{2,3},{3,2},{4,5},{5,4},{6,7},{7,6},{8,9},{9,8},{10,11... | collective-permute-start | bytes 12582920 | tf_op jit(solution)/shard_map/ppermute | solution.py:76
  97.3 39.7 %collective-permute-start.10 = (bf16[256,2176]{1,0:T(8,128)(2,1)}, bf16[256,2176]{1,0:T(8,128)(2,1)S(1)}, u32[]{:S(2)}, u32[]{:S(2)}) collective-permute-start(bf16[256,2176]{1,0:T(8,128)(2,1)} %collective-permute-done.4.refs_0_), channel_id=1, source_target_pairs={{0,4},{4,0},{8,12},{12,8},{16,20},{20,16},{24,28},{28,24},{1,5},{5... | collective-permute-start | bytes 3342344 | tf_op jit(solution)/shard_map/ppermute | solution.py:76
  97.9 39.2 %collective-permute-start.9 = (bf16[256,2176]{1,0:T(8,128)(2,1)}, bf16[256,2176]{1,0:T(8,128)(2,1)S(1)}, u32[]{:S(2)}, u32[]{:S(2)}) collective-permute-start(bf16[256,2176]{1,0:T(8,128)(2,1)} %collective-permute-done.4.refs_0_), channel_id=1, source_target_pairs={{0,8},{4,12},{8,16},{12,20},{16,24},{20,28},{24,0},{28,4},{1,9},{5... | collective-permute-start | bytes 3342344 | tf_op jit(solution)/shard_map/ppermute | solution.py:76
  98.0 39.0 %collective-permute-start.6 = (bf16[128,2048]{1,0:T(8,128)(2,1)S(1)}, bf16[128,2048]{1,0:T(8,128)(2,1)S(1)}, u32[]{:S(2)}, u32[]{:S(2)}) collective-permute-start(bf16[128,2048]{1,0:T(8,128)(2,1)S(1)} %copy-done.30), channel_id=1, source_target_pairs={{0,8},{4,12},{8,16},{12,20},{16,24},{20,28},{24,0},{28,4},{1,9},{5... | collective-permute-start | bytes 1572872 | tf_op jit(solution)/shard_map/ppermute | solution.py:76
  143.9 36.0 %collective-permute-start.17 = (bf16[256,2176]{1,0:T(8,128)(2,1)S(1)}, bf16[256,2176]{1,0:T(8,128)(2,1)S(1)}, u32[]{:S(2)}, u32[]{:S(2)}) collective-permute-start(bf16[256,2176]{1,0:T(8,128)(2,1)S(1)} %collective-permute-done.9.refs_0_), channel_id=1, source_target_pairs={{0,4},{4,0},{8,12},{12,8},{16,20},{20,16},{24,28},{28,24},{1,5},{5... | collective-permute-start | bytes 3342344 | tf_op jit(solution)/shard_map/ppermute | solution.py:76
  152.1 27.7 %collective-permute-start.16 = (bf16[128,2048]{1,0:T(8,128)(2,1)S(1)}, bf16[128,2048]{1,0:T(8,128)(2,1)S(1)}, u32[]{:S(2)}, u32[]{:S(2)}) collective-permute-start(bf16[128,2048]{1,0:T(8,128)(2,1)S(1)} %pad_maximum_fusion.3.refs_2_), channel_id=1, source_target_pairs={{0,4},{4,0},{8,12},{12,8},{16,20},{20,16},{24,28},{28,24},{1,5},{5... | collective-permute-start | bytes 1572872 | tf_op jit(solution)/shard_map/ppermute | solution.py:76
  180.7 40.5 %collective-permute-start.18 = (bf16[128,2048]{1,0:T(8,128)(2,1)S(1)}, bf16[128,2048]{1,0:T(8,128)(2,1)S(1)}, u32[]{:S(2)}, u32[]{:S(2)}) collective-permute-start(bf16[128,2048]{1,0:T(8,128)(2,1)S(1)} %collective-permute-done.12), channel_id=1, source_target_pairs={{0,8},{4,12},{8,16},{12,20},{16,24},{20,28},{24,0},{28,4},{1,9},{5... | collective-permute-start | bytes 1572872 | tf_op jit(solution)/shard_map/ppermute | solution.py:76
  181.1 39.9 %collective-permute-start.20 = (bf16[64,2048]{1,0:T(8,128)(2,1)S(1)}, bf16[64,2048]{1,0:T(8,128)(2,1)S(1)}, u32[]{:S(2)}, u32[]{:S(2)}) collective-permute-start(bf16[64,2048]{1,0:T(8,128)(2,1)S(1)} %get-tuple-element.370), channel_id=1, source_target_pairs={{0,2},{1,3},{2,0},{3,1},{4,6},{5,7},{6,4},{7,5},{8,10},{9,11},{10,... | collective-permute-start | bytes 786440 | tf_op jit(solution)/shard_map/ppermute | solution.py:76
  182.1 39.0 %collective-permute-start.19 = (bf16[64,2048]{1,0:T(8,128)(2,1)S(1)}, bf16[64,2048]{1,0:T(8,128)(2,1)S(1)}, u32[]{:S(2)}, u32[]{:S(2)}) collective-permute-start(bf16[64,2048]{1,0:T(8,128)(2,1)S(1)} %get-tuple-element.371), channel_id=1, source_target_pairs={{0,4},{4,0},{8,12},{12,8},{16,20},{20,16},{24,28},{28,24},{1,5},{5... | collective-permute-start | bytes 786440 | tf_op jit(solution)/shard_map/ppermute | solution.py:76
  183.6 37.6 %collective-permute-start.21 = (bf16[128,2048]{1,0:T(8,128)(2,1)S(1)}, bf16[128,2048]{1,0:T(8,128)(2,1)S(1)}, u32[]{:S(2)}, u32[]{:S(2)}) collective-permute-start(bf16[128,2048]{1,0:T(8,128)(2,1)S(1)} %pad_maximum_fusion.4.refs_0_), channel_id=1, source_target_pairs={{0,2},{1,3},{2,0},{3,1},{4,6},{5,7},{6,4},{7,5},{8,10},{9,11},{10,... | collective-permute-start | bytes 1572872 | tf_op jit(solution)/shard_map/ppermute | solution.py:76
  184.1 37.1 %collective-permute-start.22 = (bf16[128,2048]{1,0:T(8,128)(2,1)S(1)}, bf16[128,2048]{1,0:T(8,128)(2,1)S(1)}, u32[]{:S(2)}, u32[]{:S(2)}) collective-permute-start(bf16[128,2048]{1,0:T(8,128)(2,1)S(1)} %pad_maximum_fusion.5.refs_2_), channel_id=1, source_target_pairs={{0,4},{4,0},{8,12},{12,8},{16,20},{20,16},{24,28},{28,24},{1,5},{5... | collective-permute-start | bytes 1572872 | tf_op jit(solution)/shard_map/ppermute | solution.py:76
  221.3 30.9 %collective-permute-start.26 = (bf16[64,2048]{1,0:T(8,128)(2,1)S(1)}, bf16[64,2048]{1,0:T(8,128)(2,1)S(1)}, u32[]{:S(2)}, u32[]{:S(2)}) collective-permute-start(bf16[64,2048]{1,0:T(8,128)(2,1)S(1)} %get-tuple-element.368), channel_id=1, source_target_pairs={{0,2},{1,3},{2,0},{3,1},{4,6},{5,7},{6,4},{7,5},{8,10},{9,11},{10,... | collective-permute-start | bytes 786440 | tf_op jit(solution)/shard_map/ppermute | solution.py:76
  222.2 30.0 %collective-permute-start.25 = (bf16[64,2048]{1,0:T(8,128)(2,1)S(1)}, bf16[64,2048]{1,0:T(8,128)(2,1)S(1)}, u32[]{:S(2)}, u32[]{:S(2)}) collective-permute-start(bf16[64,2048]{1,0:T(8,128)(2,1)S(1)} %get-tuple-element.369), channel_id=1, source_target_pairs={{0,4},{4,0},{8,12},{12,8},{16,20},{20,16},{24,28},{28,24},{1,5},{5... | collective-permute-start | bytes 786440 | tf_op jit(solution)/shard_map/ppermute | solution.py:76
  223.7 28.6 %collective-permute-start.27 = (bf16[128,2048]{1,0:T(8,128)(2,1)S(1)}, bf16[128,2048]{1,0:T(8,128)(2,1)S(1)}, u32[]{:S(2)}, u32[]{:S(2)}) collective-permute-start(bf16[128,2048]{1,0:T(8,128)(2,1)S(1)} %pad_maximum_fusion.6.refs_0_), channel_id=1, source_target_pairs={{0,2},{1,3},{2,0},{3,1},{4,6},{5,7},{6,4},{7,5},{8,10},{9,11},{10,... | collective-permute-start | bytes 1572872 | tf_op jit(solution)/shard_map/ppermute | solution.py:76
  224.2 28.1 %collective-permute-start.28 = (bf16[128,2048]{1,0:T(8,128)(2,1)S(1)}, bf16[128,2048]{1,0:T(8,128)(2,1)S(1)}, u32[]{:S(2)}, u32[]{:S(2)}) collective-permute-start(bf16[128,2048]{1,0:T(8,128)(2,1)S(1)} %pad_maximum_fusion.7.refs_2_), channel_id=1, source_target_pairs={{0,4},{4,0},{8,12},{12,8},{16,20},{20,16},{24,28},{28,24},{1,5},{5... | collective-permute-start | bytes 1572872 | tf_op jit(solution)/shard_map/ppermute | solution.py:76
  225.4 75.8 %collective-permute-start.37 = (bf16[128,2048]{1,0:T(8,128)(2,1)S(1)}, bf16[128,2048]{1,0:T(8,128)(2,1)S(1)}, u32[]{:S(2)}, u32[]{:S(2)}) collective-permute-start(bf16[128,2048]{1,0:T(8,128)(2,1)S(1)} %copy-done.57), channel_id=1, source_target_pairs={{0,2},{1,3},{2,0},{3,1},{4,6},{5,7},{6,4},{7,5},{8,10},{9,11},{10,... | collective-permute-start | bytes 1572872 | tf_op jit(solution)/shard_map/ppermute | solution.py:76
  252.3 43.4 %collective-permute-start.29 = (bf16[128,2048]{1,0:T(8,128)(2,1)S(1)}, bf16[128,2048]{1,0:T(8,128)(2,1)S(1)}, u32[]{:S(2)}, u32[]{:S(2)}) collective-permute-start(bf16[128,2048]{1,0:T(8,128)(2,1)S(1)} %pad_maximum_fusion.8.refs_0_), channel_id=1, source_target_pairs={{0,2},{1,3},{2,0},{3,1},{4,6},{5,7},{6,4},{7,5},{8,10},{9,11},{10,... | collective-permute-start | bytes 1572872 | tf_op jit(solution)/shard_map/ppermute | solution.py:76
  253.5 43.8 %collective-permute-start.30 = (bf16[128,2048]{1,0:T(8,128)(2,1)S(1)}, bf16[128,2048]{1,0:T(8,128)(2,1)S(1)}, u32[]{:S(2)}, u32[]{:S(2)}) collective-permute-start(bf16[128,2048]{1,0:T(8,128)(2,1)S(1)} %pad_maximum_fusion.9.refs_2_), channel_id=1, source_target_pairs={{0,4},{4,0},{8,12},{12,8},{16,20},{20,16},{24,28},{28,24},{1,5},{5... | collective-permute-start | bytes 1572872 | tf_op jit(solution)/shard_map/ppermute | solution.py:76
  254.4 42.9 %collective-permute-start.31 = (bf16[128,2048]{1,0:T(8,128)(2,1)S(1)}, bf16[128,2048]{1,0:T(8,128)(2,1)S(1)}, u32[]{:S(2)}, u32[]{:S(2)}) collective-permute-start(bf16[128,2048]{1,0:T(8,128)(2,1)S(1)} %copy-done.67), channel_id=1, source_target_pairs={{0,2},{1,3},{2,0},{3,1},{4,6},{5,7},{6,4},{7,5},{8,10},{9,11},{10,... | collective-permute-start | bytes 1572872 | tf_op jit(solution)/shard_map/ppermute | solution.py:76
  255.9 41.4 %collective-permute-start.32 = (bf16[128,2048]{1,0:T(8,128)(2,1)S(1)}, bf16[128,2048]{1,0:T(8,128)(2,1)S(1)}, u32[]{:S(2)}, u32[]{:S(2)}) collective-permute-start(bf16[128,2048]{1,0:T(8,128)(2,1)S(1)} %copy-done.65), channel_id=1, source_target_pairs={{0,4},{4,0},{8,12},{12,8},{16,20},{20,16},{24,28},{28,24},{1,5},{5... | collective-permute-start | bytes 1572872 | tf_op jit(solution)/shard_map/ppermute | solution.py:76
  295.7 32.8 %collective-permute-start.38 = (bf16[128,2048]{1,0:T(8,128)(2,1)S(1)}, bf16[128,2048]{1,0:T(8,128)(2,1)S(1)}, u32[]{:S(2)}, u32[]{:S(2)}) collective-permute-start(bf16[128,2048]{1,0:T(8,128)(2,1)S(1)} %copy-done.56), channel_id=1, source_target_pairs={{0,4},{4,0},{8,12},{12,8},{16,20},{20,16},{24,28},{28,24},{1,5},{5... | collective-permute-start | bytes 1572872 | tf_op jit(solution)/shard_map/ppermute | solution.py:76
  298.3 30.2 %collective-permute-start.34 = (bf16[64,2048]{1,0:T(8,128)(2,1)S(1)}, bf16[64,2048]{1,0:T(8,128)(2,1)S(1)}, u32[]{:S(2)}, u32[]{:S(2)}) collective-permute-start(bf16[64,2048]{1,0:T(8,128)(2,1)S(1)} %split.120), channel_id=1, source_target_pairs={{0,2},{1,3},{2,0},{3,1},{4,6},{5,7},{6,4},{7,5},{8,10},{9,11},{10,... | collective-permute-start | bytes 786440 | tf_op jit(solution)/shard_map/ppermute | solution.py:76
  299.0 29.5 %collective-permute-start.33 = (bf16[64,2048]{1,0:T(8,128)(2,1)S(1)}, bf16[64,2048]{1,0:T(8,128)(2,1)S(1)}, u32[]{:S(2)}, u32[]{:S(2)}) collective-permute-start(bf16[64,2048]{1,0:T(8,128)(2,1)S(1)} %split.121), channel_id=1, source_target_pairs={{0,4},{4,0},{8,12},{12,8},{16,20},{20,16},{24,28},{28,24},{1,5},{5... | collective-permute-start | bytes 786440 | tf_op jit(solution)/shard_map/ppermute | solution.py:76
  300.3 28.2 %collective-permute-start.35 = (bf16[128,2048]{1,0:T(8,128)(2,1)S(1)}, bf16[128,2048]{1,0:T(8,128)(2,1)S(1)}, u32[]{:S(2)}, u32[]{:S(2)}) collective-permute-start(bf16[128,2048]{1,0:T(8,128)(2,1)S(1)} %copy-done.61), channel_id=1, source_target_pairs={{0,2},{1,3},{2,0},{3,1},{4,6},{5,7},{6,4},{7,5},{8,10},{9,11},{10,... | collective-permute-start | bytes 1572872 | tf_op jit(solution)/shard_map/ppermute | solution.py:76
  301.2 27.3 %collective-permute-start.36 = (bf16[128,2048]{1,0:T(8,128)(2,1)S(1)}, bf16[128,2048]{1,0:T(8,128)(2,1)S(1)}, u32[]{:S(2)}, u32[]{:S(2)}) collective-permute-start(bf16[128,2048]{1,0:T(8,128)(2,1)S(1)} %copy-done.60), channel_id=1, source_target_pairs={{0,4},{4,0},{8,12},{12,8},{16,20},{20,16},{24,28},{28,24},{1,5},{5... | collective-permute-start | bytes 1572872 | tf_op jit(solution)/shard_map/ppermute | solution.py:76
  328.7 20.0 %collective-permute-start.39 = (bf16[128,2048]{1,0:T(8,128)(2,1)S(1)}, bf16[128,2048]{1,0:T(8,128)(2,1)S(1)}, u32[]{:S(2)}, u32[]{:S(2)}) collective-permute-start(bf16[128,2048]{1,0:T(8,128)(2,1)S(1)} %pad_maximum_fusion.10), channel_id=1, source_target_pairs={{0,8},{4,12},{8,16},{12,20},{16,24},{20,28},{24,0},{28,4},{1,9},{5... | collective-permute-start | bytes 1572872 | tf_op jit(solution)/shard_map/ppermute | solution.py:76
  329.4 19.3 %collective-permute-start.42 = (bf16[128,2048]{1,0:T(8,128)(2,1)S(1)}, bf16[128,2048]{1,0:T(8,128)(2,1)S(1)}, u32[]{:S(2)}, u32[]{:S(2)}) collective-permute-start(bf16[128,2048]{1,0:T(8,128)(2,1)S(1)} %copy-done.59), channel_id=1, source_target_pairs={{0,2},{1,3},{2,0},{3,1},{4,6},{5,7},{6,4},{7,5},{8,10},{9,11},{10,... | collective-permute-start | bytes 1572872 | tf_op jit(solution)/shard_map/ppermute | solution.py:76
  347.2 22.2 %collective-permute-start.48 = (bf16[64,2048]{1,0:T(8,128)(2,1)S(1)}, bf16[64,2048]{1,0:T(8,128)(2,1)S(1)}, u32[]{:S(2)}, u32[]{:S(2)}) collective-permute-start(bf16[64,2048]{1,0:T(8,128)(2,1)S(1)} %split.114), channel_id=1, source_target_pairs={{0,2},{1,3},{2,0},{3,1},{4,6},{5,7},{6,4},{7,5},{8,10},{9,11},{10,... | collective-permute-start | bytes 786440 | tf_op jit(solution)/shard_map/ppermute | solution.py:76
  347.6 23.4 %collective-permute-start.47 = (bf16[64,2048]{1,0:T(8,128)(2,1)S(1)}, bf16[64,2048]{1,0:T(8,128)(2,1)S(1)}, u32[]{:S(2)}, u32[]{:S(2)}) collective-permute-start(bf16[64,2048]{1,0:T(8,128)(2,1)S(1)} %split.115), channel_id=1, source_target_pairs={{0,4},{4,0},{8,12},{12,8},{16,20},{20,16},{24,28},{28,24},{1,5},{5... | collective-permute-start | bytes 786440 | tf_op jit(solution)/shard_map/ppermute | solution.py:76
  349.0 23.5 %collective-permute-start.46 = (bf16[64,2048]{1,0:T(8,128)(2,1)S(1)}, bf16[64,2048]{1,0:T(8,128)(2,1)S(1)}, u32[]{:S(2)}, u32[]{:S(2)}) collective-permute-start(bf16[64,2048]{1,0:T(8,128)(2,1)S(1)} %split.116), channel_id=1, source_target_pairs={{0,2},{1,3},{2,0},{3,1},{4,6},{5,7},{6,4},{7,5},{8,10},{9,11},{10,... | collective-permute-start | bytes 786440 | tf_op jit(solution)/shard_map/ppermute | solution.py:76
  350.1 22.4 %collective-permute-start.45 = (bf16[64,2048]{1,0:T(8,128)(2,1)S(1)}, bf16[64,2048]{1,0:T(8,128)(2,1)S(1)}, u32[]{:S(2)}, u32[]{:S(2)}) collective-permute-start(bf16[64,2048]{1,0:T(8,128)(2,1)S(1)} %split.117), channel_id=1, source_target_pairs={{0,4},{4,0},{8,12},{12,8},{16,20},{20,16},{24,28},{28,24},{1,5},{5... | collective-permute-start | bytes 786440 | tf_op jit(solution)/shard_map/ppermute | solution.py:76
  352.0 20.5 %collective-permute-start.44 = (bf16[128,2048]{1,0:T(8,128)(2,1)S(1)}, bf16[128,2048]{1,0:T(8,128)(2,1)S(1)}, u32[]{:S(2)}, u32[]{:S(2)}) collective-permute-start(bf16[128,2048]{1,0:T(8,128)(2,1)S(1)} %fusion.2), channel_id=1, source_target_pairs={{0,8},{4,12},{8,16},{12,20},{16,24},{20,28},{24,0},{28,4},{1,9},{5... | collective-permute-start | bytes 1572872 | tf_op jit(solution)/shard_map/ppermute | solution.py:76
  370.4 20.0 %collective-permute-start.50 = (bf16[256,2048]{1,0:T(8,128)(2,1)S(1)}, bf16[256,2048]{1,0:T(8,128)(2,1)S(1)}, u32[]{:S(2)}, u32[]{:S(2)}) collective-permute-start(bf16[256,2048]{1,0:T(8,128)(2,1)S(1)} %copy-done.52), channel_id=1, source_target_pairs={{0,4},{4,0},{8,12},{12,8},{16,20},{20,16},{24,28},{28,24},{1,5},{5... | collective-permute-start | bytes 3145736 | tf_op jit(solution)/shard_map/ppermute | solution.py:76
  371.0 33.5 %collective-permute-start.55 = (bf16[256,2048]{1,0:T(8,128)(2,1)S(1)}, bf16[256,2048]{1,0:T(8,128)(2,1)S(1)}, u32[]{:S(2)}, u32[]{:S(2)}) collective-permute-start(bf16[256,2048]{1,0:T(8,128)(2,1)S(1)} %copy-done.51), channel_id=1, source_target_pairs={{0,4},{4,0},{8,12},{12,8},{16,20},{20,16},{24,28},{28,24},{1,5},{5... | collective-permute-start | bytes 3145736 | tf_op jit(solution)/shard_map/ppermute | solution.py:76
  403.1 58.2 %collective-permute-start.57 = (bf16[256,2048]{1,0:T(8,128)(2,1)}, bf16[256,2048]{1,0:T(8,128)(2,1)S(1)}, u32[]{:S(2)}, u32[]{:S(2)}) collective-permute-start(bf16[256,2048]{1,0:T(8,128)(2,1)} %get-tuple-element.333), channel_id=1, source_target_pairs={{0,4},{4,0},{8,12},{12,8},{16,20},{20,16},{24,28},{28,24},{1,5},{5... | collective-permute-start | bytes 3145736 | tf_op jit(solution)/shard_map/ppermute | solution.py:76
  414.3 47.1 %collective-permute-start.56 = (bf16[256,2048]{1,0:T(8,128)(2,1)}, bf16[256,2048]{1,0:T(8,128)(2,1)}, u32[]{:S(2)}, u32[]{:S(2)}) collective-permute-start(bf16[256,2048]{1,0:T(8,128)(2,1)} %add_convert_fusion.1), channel_id=1, source_target_pairs={{0,8},{4,12},{8,16},{12,20},{16,24},{20,28},{24,0},{28,4},{1,9},{5... | collective-permute-start | bytes 3145736 | tf_op jit(solution)/shard_map/ppermute | solution.py:76
  462.3 32.6 %collective-permute-start.64 = (bf16[256,2048]{1,0:T(8,128)(2,1)}, bf16[256,2048]{1,0:T(8,128)(2,1)}, u32[]{:S(2)}, u32[]{:S(2)}) collective-permute-start(bf16[256,2048]{1,0:T(8,128)(2,1)} %get-tuple-element.344), channel_id=1, source_target_pairs={{0,4},{4,0},{8,12},{12,8},{16,20},{20,16},{24,28},{28,24},{1,5},{5... | collective-permute-start | bytes 3145736 | tf_op jit(solution)/shard_map/ppermute | solution.py:76
  466.0 28.8 %collective-permute-start.63 = (bf16[256,2048]{1,0:T(8,128)(2,1)}, bf16[256,2048]{1,0:T(8,128)(2,1)}, u32[]{:S(2)}, u32[]{:S(2)}) collective-permute-start(bf16[256,2048]{1,0:T(8,128)(2,1)} %add_convert_fusion), channel_id=1, source_target_pairs={{0,8},{4,12},{8,16},{12,20},{16,24},{20,28},{24,0},{28,4},{1,9},{5... | collective-permute-start | bytes 3145736 | tf_op jit(solution)/shard_map/ppermute | solution.py:76
  469.0 22.2 %collective-permute-start.59 = (bf16[128,2048]{1,0:T(8,128)(2,1)}, bf16[128,2048]{1,0:T(8,128)(2,1)}, u32[]{:S(2)}, u32[]{:S(2)}) collective-permute-start(bf16[128,2048]{1,0:T(8,128)(2,1)} %get-tuple-element.362), channel_id=1, source_target_pairs={{0,2},{1,3},{2,0},{3,1},{4,6},{5,7},{6,4},{7,5},{8,10},{9,11},{10,... | collective-permute-start | bytes 1572872 | tf_op jit(solution)/shard_map/ppermute | solution.py:76
  519.5 29.6 %collective-permute-start.73 = (bf16[128,2048]{1,0:T(8,128)(2,1)S(1)}, bf16[128,2048]{1,0:T(8,128)(2,1)}, u32[]{:S(2)}, u32[]{:S(2)}) collective-permute-start(bf16[128,2048]{1,0:T(8,128)(2,1)S(1)} %copy-done.10), channel_id=1, source_target_pairs={{0,1},{1,0},{2,3},{3,2},{4,5},{5,4},{6,7},{7,6},{8,9},{9,8},{10,11... | collective-permute-start | bytes 1572872 | tf_op jit(solution)/shard_map/ppermute | solution.py:76
  519.6 29.6 %collective-permute-start.74 = (bf16[128,2048]{1,0:T(8,128)(2,1)}, bf16[128,2048]{1,0:T(8,128)(2,1)}, u32[]{:S(2)}, u32[]{:S(2)}) collective-permute-start(bf16[128,2048]{1,0:T(8,128)(2,1)} %collective-permute-done.72.refs_1_), channel_id=1, source_target_pairs={{0,1},{1,0},{2,3},{3,2},{4,5},{5,4},{6,7},{7,6},{8,9},{9,8},{10,11... | collective-permute-start | bytes 1572872 | tf_op jit(solution)/shard_map/ppermute | solution.py:76
  (109 other events, 1261.1 us)

commit v5 on v4

--- a/solution.py
+++ b/solution.py
@@ -91,18 +91,6 @@
     return array.astype(jnp.bfloat16)
 
 
-def gather_first(rows, axes):
-    half = rows.shape[0] // 2
-    return (
-        jnp.concatenate(ring(rows[:half], axes, "x"), axis=0),
-        jnp.concatenate(ring(rows[half:], axes, "y"), axis=0),
-    )
-
-
-def gather_second(pair, axes):
-    return ring(pair[0], axes, "y") + ring(pair[1], axes, "x")
-
-
 def send_sum(parts, axes, name):
     total = parts[-1]
     for part in parts[-2:0:-1]:
@@ -135,20 +123,23 @@
     return held + [turn(piece, axes, "c", 1) for piece in held]
 
 
-def scatter_tensor(mine, theirs, axes):
+def scatter_core(mine, came, axes):
     rank = lax.axis_index("tensor")
     span = axes["y"][1]
     size = mine.shape[0] // span
-    came = turn(theirs, axes, "c", 1)
     total = None
     for step in range(span - 1, -1, -1):
         level = (rank // 2 + span - step) % span
         part = wide(lax.dynamic_slice_in_dim(mine, level * size, size, 0)) + wide(
             lax.dynamic_slice_in_dim(came, level * size, size, 0)
         )
-        if step:
-            total = turn(low(part if total is None else part + wide(total)), axes, "y", -1)
-    return part, total
+        if step == 0:
+            return part, total
+        total = low(part if total is None else part + wide(turn(total, axes, "y", -1)))
+
+
+def gather_x(rows, axes):
+    return jnp.concatenate(ring(rows, axes, "x"), axis=0)
 
 
 def swap_columns(rows, axes):
@@ -175,7 +166,7 @@
 
 def sum_tensor(array, axes):
     total = wide(array) + wide(turn(array, axes, "c", 1))
-    moving = low(total)
+    moving = total.astype(array.dtype)
     result = total
     for _ in range(axes["y"][1] - 1):
         moving = turn(moving, axes, "y", 1)
@@ -388,37 +379,46 @@
 
 
 def plane_order(near, span, size):
-    half = size // 2
-    places = []
-    for down in range(span):
-        for across in range(near):
-            places.append((across, down, down * size, (down * near + across) * half))
-    for across in range(near):
-        for down in range(span):
-            first = (span * near + across * span + down) * half
-            places.append((across, down, down * size + half, first))
-    return places
-
-
-def hidden_kernel(count, near, size, width, *refs):
-    pieces, (down_own, down_other, spread), (out, side_out), (rows, side) = (
-        refs[: count * near],
-        refs[count * near : count * near + 3],
-        refs[count * near + 3 : count * near + 5],
-        refs[count * near + 5 :],
+    return [
+        (across, down * size, (down * near + across) * size)
+        for down in range(span)
+        for across in range(near)
+    ]
+
+
+def hidden_kernel(places, *refs):
+    count = len(places)
+    pieces, (down_own, down_other, spread), (out, side_out), (rows, side, row_sems, side_sems) = (
+        refs[:count],
+        refs[count : count + 3],
+        refs[count + 3 : count + 5],
+        refs[count + 5 :],
     )
     step = pl.program_id(0)
-    span = pieces[0].shape[0] // size
-    plane = near * span * size
+    width = rows.shape[1]
 
     @pl.when(step == 0)
     def _():
-        for index in range(count):
-            for across, _, source, first in plane_order(near, span, size):
-                piece = pieces[index * near + across]
-                place = slice(index * plane + first, index * plane + first + size // 2)
-                rows[place] = piece[source : source + size // 2, :width]
-                side[place] = piece[source : source + size // 2, width:]
+        copies = []
+        for index, (piece, targets) in enumerate(zip(pieces, places)):
+            for source, target, size in targets:
+                taken = piece.at[pl.ds(source, size)]
+                place = pl.ds(target, size)
+                slot = len(copies) // 2
+                copies.append(
+                    pltpu.make_async_copy(
+                        taken.at[:, pl.ds(0, width)], rows.at[place], row_sems.at[slot]
+                    )
+                )
+                copies.append(
+                    pltpu.make_async_copy(
+                        taken.at[:, pl.ds(width, side.shape[1])], side.at[place], side_sems.at[slot]
+                    )
+                )
+        for copy in copies:
+            copy.start()
+        for copy in copies:
+            copy.wait()
         side_out[...] = side[...]
 
     def emit(down):
@@ -441,17 +441,28 @@
 def hidden_call(planes, downs, spread, experts, size):
     hidden, width = downs[0].shape
     near = len(planes[0])
-    pieces = [piece for plane in planes for piece in plane]
-    rows = sum(piece.shape[0] for piece in pieces)
+    pieces, places, rows = [], [], 0
+    for plane in planes:
+        for across, column in enumerate(plane):
+            down = 0
+            for piece in column:
+                targets = []
+                for source in range(0, piece.shape[0], size):
+                    targets.append((source, rows + (down * near + across) * size, size))
+                    down += 1
+                pieces.append(piece)
+                places.append(targets)
+        rows += near * down * size
+    blocks = rows // size
     part = hidden // experts
     side = spread.shape[0]
     pair = 2 * part
     half = experts // 2
     last = half - 1
     return kernel_call(
-        functools.partial(hidden_kernel, len(planes), near, size, width),
+        functools.partial(hidden_kernel, places),
         (2 * half,),
-        [whole(piece) for piece in pieces]
+        [ANY] * len(pieces)
         + [
             pl.BlockSpec((pair, width), lambda n: (jnp.minimum(n, last), 0)),
             pl.BlockSpec((pair, width), lambda n: (jnp.maximum(n - half, 0), 0)),
@@ -464,16 +475,21 @@
         [((2 * experts, rows, part), jnp.bfloat16), ((rows, side), jnp.bfloat16)],
         [*pieces, *downs, spread],
         4 * rows * hidden * width,
-        [pltpu.VMEM((rows, width), jnp.bfloat16), pltpu.VMEM((rows, side), jnp.bfloat16)],
-    )
-
-
-def expert_kernel(count, offset, *refs):
+        [
+            pltpu.VMEM((rows, width), jnp.bfloat16),
+            pltpu.VMEM((rows, side), jnp.bfloat16),
+            pltpu.SemaphoreType.DMA((blocks,)),
+            pltpu.SemaphoreType.DMA((blocks,)),
+        ],
+    )
+
+
+def expert_kernel(count, near, span, offset, *refs):
     pieces = refs[:count]
     gate_own, up_own, gate_other, up_other, spread, side, back = refs[count : count + 7]
-    outs, hidden_out = refs[count + 7 : 2 * count + 7], refs[2 * count + 7]
+    outs, hidden_out = refs[count + 7 : count + 7 + near + span], refs[count + 7 + near + span]
     rows, weights, gate_grad, up_grad, hidden, grads, sems, row_sem, back_sem, out_sem = refs[
-        2 * count + 8 :
+        count + 8 + near + span :
     ]
     step = pl.program_id(0)
     size = pieces[0].shape[0]
@@ -544,15 +560,21 @@
                 first = (2 * half + index) * part
                 term = dot_t(grad[place], weights[expert, columns, first : first + part])
                 total = term if total is None else total + term
-    for index, out in enumerate(outs):
-        out[...] = low(total[index * size : (index + 1) * size])
+    half = total_rows // (2 * near * span)
+    for down in range(span):
+        for across in range(near):
+            first = 2 * (down * near + across) * half
+            outs[down][across * half : (across + 1) * half] = low(total[first : first + half])
+            outs[span + across][down * half : (down + 1) * half] = low(
+                total[first + half : first + 2 * half]
+            )
 
     @pl.when(step == pl.num_programs(0) - 1)
     def _():
         out_copy.wait()
 
 
-def expert_call(pieces, gates, ups, spread, side, back, offset):
+def expert_call(pieces, gates, ups, spread, side, back, offset, near, span):
     count = len(pieces)
     experts, width, part = gates[0].shape
     size = pieces[0].shape[0]
@@ -562,11 +584,15 @@
     slots = pltpu.VMEM(shape, jnp.bfloat16)
     side_block = pl.BlockSpec((rows, side.shape[1]), lambda n: (offset // rows, 0))
     return kernel_call(
-        functools.partial(expert_kernel, count, offset),
+        functools.partial(expert_kernel, count, near, span, offset),
         (width // tile,),
         [ANY] * (count + 4) + [whole(spread), side_block, ANY],
-        [pl.BlockSpec((size, tile), lambda n: (0, n))] * count + [ANY],
-        [((size, width), jnp.bfloat16)] * count + [(shape, jnp.bfloat16)],
+        [pl.BlockSpec((rows // (2 * span), tile), lambda n: (0, n))] * span
+        + [pl.BlockSpec((rows // (2 * near), tile), lambda n: (0, n))] * near
+        + [ANY],
+        [((rows // (2 * span), width), jnp.bfloat16)] * span
+        + [((rows // (2 * near), width), jnp.bfloat16)] * near
+        + [(shape, jnp.bfloat16)],
         [*pieces, gates[0], ups[0], gates[1], ups[1], spread, side, back],
         16 * rows * experts * part * width,
         [
@@ -596,10 +622,8 @@
             first = place % (places // 2) * part
             term = dot(hidden[place], down[first : first + part, :])
             total = term if total is None else total + term
-        for across, _, target, first in plane_order(near, span, size):
-            outs[index * near + across][target : target + size // 2] = low(
-                total[first : first + size // 2]
-            )
+        for across, target, first in plane_order(near, span, size):
+            outs[index * near + across][target : target + size] = low(total[first : first + size])
 
 
 def down_call(hiddens, downs, near, span, size):
@@ -733,16 +757,10 @@
     )
 
 
-def weight_kernel(
-    width, size, scalars, inner, squares, query_grad, key_grad, value_grad, query_raw, key_raw,
-    query_weight, key_weight, value_weight, lowrank, adapt_out,
-    mine, theirs, lowrank_out, adapt_grad, weights, raw, maps, sems,
+def raw_kernel(
+    width, scalars, inner, squares, query_grad, key_grad, value_grad, query_raw, key_raw, lowrank,
+    adapt_out, raw, lowrank_out, adapt_grad, maps,
 ):
-    copies = []
-    for index, source in enumerate((query_weight, key_weight, value_weight)):
-        copies.append(pltpu.make_async_copy(source, weights.at[index], sems.at[index]))
-    for copy in copies:
-        copy.start()
     inverse = lax.rsqrt(spread_columns(squares[...]) / width + EPSILON)
     totals = spread_columns(inner[...]) / width
     for index, (grad, value) in enumerate(((query_grad, query_raw), (key_grad, key_raw))):
@@ -752,7 +770,7 @@
             - value[...] * scale**3 * totals[:, index : index + 1]
         )
     raw[2] = value_grad[...]
-    picked = pl.ds(pl.multiple_of(scalars[1], RANK), RANK)
+    picked = pl.ds(pl.multiple_of(scalars[0], RANK), RANK)
     maps[...] = jnp.zeros_like(maps)
     lowrank_part = None
     for index in range(3):
@@ -763,6 +781,34 @@
             t_dot(lowrank[index], raw[index])
         )
     lowrank_out[...] = low(lowrank_part)
+
+
+def raw_call(scalars, width, inner, squares, grads, raws, lowrank, adapt_out):
+    rows, local = raws[0].shape
+    operands = [scalars, inner, squares, *grads, *raws, lowrank, adapt_out]
+    out_shape = [((3, rows, local), jnp.bfloat16), ((rows, 128), jnp.bfloat16)]
+    out_shape += [((3 * RANK, local), jnp.bfloat16)]
+    return kernel_call(
+        functools.partial(raw_kernel, width),
+        (1,),
+        [whole(array) for array in operands[1:]],
+        [pl.BlockSpec(shape, lambda *_, size=len(shape): (0,) * size) for shape, _ in out_shape],
+        out_shape,
+        operands,
+        6 * rows * local * 256,
+        [pltpu.VMEM((3, 128, local), jnp.bfloat16)],
+        1,
+    )
+
+
+def weight_kernel(
+    size, scalars, raw, query_weight, key_weight, value_weight, mine, theirs, weights, sems
+):
+    copies = []
+    for index, source in enumerate((query_weight, key_weight, value_weight)):
+        copies.append(pltpu.make_async_copy(source, weights.at[index], sems.at[index]))
+    for copy in copies:
+        copy.start()
     for copy in copies:
         copy.wait()
     levels = mine.shape[0] // size
@@ -778,26 +824,20 @@
         out[...] = total.astype(out.dtype)
 
 
-def weight_call(scalars, inner, squares, grads, raws, weights, lowrank, adapt_out, size):
-    rows, local = raws[0].shape
+def weight_call(scalars, raw, weights, size):
+    _, rows, local = raw.shape
     width = weights[0].shape[0]
-    operands = [scalars, inner, squares, *grads, *raws, *weights, lowrank, adapt_out]
+    operands = [scalars, raw, *weights]
     out_shape = [((rows // 2, width), jnp.float32), ((rows // 2, width), jnp.bfloat16)]
-    out_shape += [((rows, 128), jnp.bfloat16), ((3 * RANK, local), jnp.bfloat16)]
     return kernel_call(
-        functools.partial(weight_kernel, width, size),
+        functools.partial(weight_kernel, size),
         (1,),
-        [whole(array) for array in operands[1:8]] + [ANY] * 3 + [whole(lowrank), whole(adapt_out)],
+        [whole(raw)] + [ANY] * 3,
         [pl.BlockSpec(shape, lambda *_: (0, 0)) for shape, _ in out_shape],
         out_shape,
         operands,
         6 * rows * local * width,
-        [
-            pltpu.VMEM((3, width, local), jnp.bfloat16),
-            pltpu.VMEM((3, rows, local), jnp.bfloat16),
-            pltpu.VMEM((3, 128, local), jnp.bfloat16),
-            pltpu.SemaphoreType.DMA((3,)),
-        ],
+        [pltpu.VMEM((3, width, local), jnp.bfloat16), pltpu.SemaphoreType.DMA((3,))],
         1,
     )
 
@@ -1040,10 +1080,19 @@
         tokens, first_gain, weights, adapt_in, adapt_out, select
     )
 
-    squares = lax.psum(squares, "tensor")
-    squares, cot_queue[1], cot_planes[0] = hold((squares, cot_queue[1], cot_planes[0]))
-    cot_queue.append(turn(cot_queue[1], axes, "z", 1))
-    cot_planes[1] = ring(cot_queue[1], axes, "x")
+    def halves(rows):
+        return [rows[: rows.shape[0] // 2], rows[rows.shape[0] // 2 :]]
+
+    squares = sum_tensor(squares, axes)
+    tokens_rows = own_rows(tokens)
+    held = (squares, cot_queue[1], cot_planes[0], expert_gate, expert_up, tables, mask, tokens_rows)
+    held = hold(held)
+    squares, cot_queue[1], cot_planes[0], expert_gate, expert_up, tables, mask, tokens_rows = held
+    gates = (expert_gate, turn(expert_gate, axes, "c", 1))
+    ups = (expert_up, turn(expert_up, axes, "c", 1))
+    cot_queue[1] = halves(cot_queue[1])
+    cot_later = turn(cot_queue[1][0], axes, "z", 1)
+    cot_across = ring(cot_queue[1][0], axes, "x")[1:]
     *states, mine, theirs = attend_call(
         jnp.reshape(core, (1,)).astype(jnp.int32),
         squares,
@@ -1055,22 +1104,33 @@
         adapt_in_out,
         row_share,
     )
-
-    branch_kept, branch_came = scatter_tensor(mine, theirs, axes)
-    branch_came, cot_queue[2], cot_planes[1] = hold((branch_came, cot_queue[2], cot_planes[1]))
-    cot_queue.append(turn(cot_queue[2], axes, "z", 1))
-    cot_planes[2] = ring(cot_queue[2], axes, "x")
+    cot_later, cot_across, mine, theirs = hold((cot_later, cot_across, mine, theirs))
+
+    theirs = turn(theirs, axes, "c", 1)
+    branch_kept, branch_sent = scatter_core(mine, theirs, axes)
+    branch_sent, cot_queue[1] = hold((branch_sent, cot_queue[1]))
+    down_tall = expert_down.reshape(-1, model_width)
+    branch_came = turn(branch_sent, axes, "y", -1)
+    cot_later = [cot_later, turn(cot_queue[1][1], axes, "z", 1)]
+    cot_second = ring(cot_queue[1][1], axes, "x")[1:]
+    held = (branch_came, cot_later, cot_second, gates, ups, down_tall)
+    branch_came, cot_later, cot_second, gates, ups, down_tall = hold(held)
+    downs = (down_tall, turn(down_tall, axes, "c", 1))
+    cot_queue.append(cot_later)
+    cot_planes[1] = [cot_queue[1]] + [list(pair) for pair in zip(cot_across, cot_second)]
+    cot_planes[0] = [[piece] for piece in cot_planes[0]]
     resid_rows, norm_plane, mixed_rows = resid_call(
-        branch_kept, branch_came, own_rows(tokens), adapt_out_out, select, second_gain
-    )
-    gates = (expert_gate, turn(expert_gate, axes, "c", 1))
-    ups = (expert_up, turn(expert_up, axes, "c", 1))
-    down_tall = expert_down.reshape(-1, model_width)
-    downs = (down_tall, turn(down_tall, axes, "c", 1))
-
-    norm_next = turn(norm_plane, axes, "z", 1)
-    norm_first = gather_first(norm_plane, axes)
+        branch_kept, branch_came, tokens_rows, adapt_out_out, select, second_gain
+    )
+
+    norm_queue = [norm_plane, turn(norm_plane, axes, "z", 1)]
+    norm_pairs = [ring(norm_plane, axes, "x")]
     backs, sides = [None] * far, [None] * far
+    maps = jnp.swapaxes(lax.dynamic_slice_in_dim(adapt_in, picked, RANK, 2), 0, 1)
+    maps = maps.reshape(model_width, 3 * RANK)
+    maps = jnp.concatenate(
+        [maps, jnp.zeros((model_width, 128 - 3 * RANK), jnp.bfloat16)], axis=1
+    )
 
     def hidden_step(*indices):
         back, side = hidden_call(
@@ -1080,64 +1140,58 @@
             backs[index], sides[index] = (back, order * side.shape[0] // len(indices)), side
         return back
 
+    def set_back(back, *indices):
+        for index in indices:
+            backs[index] = (back, backs[index][1])
+
+    norm_planes = [None] * far
+    held = (norm_queue[1], norm_pairs[0], maps, downs)
+    norm_queue[1], norm_pairs[0], maps, downs = hold(held)
+    norm_planes[0] = ring(jnp.concatenate(norm_pairs[0], axis=0), axes, "y")
+    norm_queue.append(turn(norm_queue[1], axes, "z", 1))
+    norm_pairs.append(ring(norm_queue[1], axes, "x"))
+    cot_third = [turn(cot_queue[2][0], axes, "z", 1)]
+    cot_across = ring(cot_queue[2][0], axes, "x")[1:]
     back_first = hidden_step(0, 1)
-
-    norm_planes = [None] * far
-    norm_next, norm_first, cot_queue[3], cot_planes[2], back_first = hold(
-        (norm_next, norm_first, cot_queue[3], cot_planes[2], back_first)
-    )
-    backs[0], backs[1] = (back_first, backs[0][1]), (back_first, backs[1][1])
-    norm_later = turn(norm_next, axes, "z", 1)
-    norm_planes[0] = gather_second(norm_first, axes)
-    norm_first = gather_first(norm_next, axes)
-    cot_planes[3] = ring(cot_queue[3], axes, "x")
+    held = (norm_planes[0], norm_queue[2], norm_pairs[1], cot_third, cot_across, cot_queue[2])
+    held, back_first = hold((held, back_first))
+    norm_planes[0], norm_queue[2], norm_pairs[1], cot_third, cot_across, cot_queue[2] = held
+    set_back(back_first, 0, 1)
     parts, hiddens = [None] * far, [None] * far
 
     def expert_step(index):
         back, offset = backs[index]
         *parts[index], hiddens[index] = expert_call(
-            norm_planes[index], gates, ups, spread, sides[index], back, offset
+            norm_planes[index], gates, ups, spread, sides[index], back, offset, near, span
         )
 
-    back_second = hidden_step(2)
-
-    norm_next, norm_first, norm_planes[0], cot_planes[3], back_second = hold(
-        (norm_later, norm_first, norm_planes[0], cot_planes[3], back_second)
-    )
-    backs[2] = (back_second, 0)
-    norm_later = turn(norm_next, axes, "z", 1)
-    norm_planes[1] = gather_second(norm_first, axes)
-    norm_first = gather_first(norm_next, axes)
+    norm_planes[1] = ring(jnp.concatenate(norm_pairs[1], axis=0), axes, "y")
+    norm_queue.append(turn(norm_queue[2], axes, "z", 1))
+    norm_pairs.append(ring(norm_queue[2], axes, "x"))
+    cot_third.append(turn(cot_queue[2][1], axes, "z", 1))
+    cot_second = ring(cot_queue[2][1], axes, "x")[1:]
     expert_step(0)
 
-    norm_next, norm_first, norm_planes[1], parts[0] = hold(
-        (norm_later, norm_first, norm_planes[1], parts[0])
-    )
-    norm_planes[2] = gather_second(norm_first, axes)
-    norm_first = gather_first(norm_next, axes)
+    held = (norm_planes[1], norm_queue[3], norm_pairs[2], cot_third, cot_second, parts[0])
+    norm_planes[1], norm_queue[3], norm_pairs[2], cot_third, cot_second, parts[0] = hold(held)
+    cot_planes[2] = [cot_queue[2]] + [list(pair) for pair in zip(cot_across, cot_second)]
+    cot_queue.append(cot_third)
+    norm_planes[2] = ring(jnp.concatenate(norm_pairs[2], axis=0), axes, "y")
+    norm_pairs.append(ring(norm_queue[3], axes, "x"))
+    cot_across = [ring(rows, axes, "x")[1:] for rows in cot_queue[3]]
     expert_step(1)
 
-    norm_first, norm_planes[2], parts[1] = hold((norm_first, norm_planes[2], parts[1]))
-    norm_planes[3] = gather_second(norm_first, axes)
+    norm_planes[2], norm_pairs[3], parts[1] = hold((norm_planes[2], norm_pairs[3], parts[1]))
+    norm_planes[3] = ring(jnp.concatenate(norm_pairs[3], axis=0), axes, "y")
     came = [None] * far
     kept = [None] * far
     came[1] = scatter_first(parts[1], axes)
+    back_next = hidden_step(2)
+    cot_across, back_next, norm_planes[2] = hold((cot_across, back_next, norm_planes[2]))
+    set_back(back_next, 2)
+    came[0] = scatter_first(parts[0], axes)
+    cot_planes[3] = [cot_queue[3]] + [list(pair) for pair in zip(*cot_across)]
     expert_step(2)
-    hidden_step(3)
-
-    norm_planes[3], came[1], parts[2] = hold((norm_planes[3], came[1], parts[2]))
-    kept[1], came[1] = scatter_second(parts[1], came[1], axes)
-    came[2] = scatter_first(parts[2], axes)
-    came[0] = scatter_first(parts[0], axes)
-    expert_step(3)
-
-    kept[1], came[1], came[2], came[0], parts[3] = hold(
-        (kept[1], came[1], came[2], came[0], parts[3])
-    )
-    ring_sum = turn(low(scatter_last(kept[1], came[1])), axes, "z", 1)
-    kept[2], came[2] = scatter_second(parts[2], came[2], axes)
-    came[3] = scatter_first(parts[3], axes)
-    kept[0], came[0] = scatter_second(parts[0], came[0], axes)
     mixes, mix_came = [None] * far, [None] * far
 
     def down_step(first, second):
@@ -1145,24 +1199,47 @@
             [hiddens[first], hiddens[second]], downs, near, span, row_share
         )
 
+    held = (norm_planes[3], came[1], came[0], parts[2], hiddens[1], hiddens[2])
+    norm_planes[3], came[1], came[0], parts[2], hiddens[1], hiddens[2] = hold(held)
+    kept[1], came[1] = scatter_second(parts[1], came[1], axes)
+    came[2] = scatter_first(parts[2], axes)
     down_step(1, 2)
-
-    ring_sum, kept[2], came[2], came[3], mixes[1], mixes[2] = hold(
-        (ring_sum, kept[2], came[2], came[3], mixes[1], mixes[2])
-    )
+    held = (kept[1], came[1], came[2], mixes[1], mixes[2], cot_planes[3])
+    kept[1], came[1], came[2], mixes[1], mixes[2], cot_planes[3] = hold(held)
+    kept[2], came[2] = scatter_second(parts[2], came[2], axes)
+    ring_sum = turn(low(scatter_last(kept[1], came[1])), axes, "z", 1)
+    mix_came[1] = send_sum(mixes[1], axes, "x")
+    back_last = hidden_step(3)
+    kept[2], came[2], back_last, norm_planes[3] = hold(
+        (kept[2], came[2], back_last, norm_planes[3])
+    )
+    set_back(back_last, 3)
+    kept[0], came[0] = scatter_second(parts[0], came[0], axes)
+    expert_step(3)
+
+    held = (ring_sum, kept[0], came[0], parts[3], hiddens[3], mix_came[1])
+    ring_sum, kept[0], came[0], parts[3], hiddens[3], mix_came[1] = hold(held)
+    came[3] = scatter_first(parts[3], axes)
     ring_sum = turn(low(wide(ring_sum) + scatter_last(kept[2], came[2])), axes, "z", 1)
+    down_step(3, 0)
+
+    ring_sum, came[3], mixes[3], mixes[0] = hold((ring_sum, came[3], mixes[3], mixes[0]))
     kept[3], came[3] = scatter_second(parts[3], came[3], axes)
-    mix_came[1] = send_sum(mixes[1], axes, "x")
-    down_step(3, 0)
-
-    ring_sum, kept[3], came[3], kept[0], came[0], mixes[3], mixes[0] = hold(
-        (ring_sum, kept[3], came[3], kept[0], came[0], mixes[3], mixes[0])
-    )
+
+    ring_sum, kept[3], came[3], mixes = hold((ring_sum, kept[3], came[3], mixes))
     ring_sum = turn(low(wide(ring_sum) + scatter_last(kept[3], came[3])), axes, "z", 1)
-    ring_sum, mix_came[1] = hold((ring_sum, mix_came[1]))
-
-    mix_sum = turn(low(wide(mixes[1][0]) + wide(mix_came[1])), axes, "z", 1)
     mix_came[2] = send_sum(mixes[2], axes, "x")
+
+    def mix_down(index):
+        total = wide(mixes[index][0]) + wide(mix_came[index])
+        total = jnp.split(total, span, axis=0)
+        return total[0], send_sum([low(part) for part in total], axes, "y")
+
+    mix_parts = [None] * far
+    mix_parts[1] = mix_down(1)
+
+    ring_sum, mix_parts[1] = hold((ring_sum, mix_parts[1]))
+    mix_sum = turn(low(mix_parts[1][0] + wide(mix_parts[1][1])), axes, "z", 1)
     ffn_rows_grad = wide(ring_sum) + scatter_last(kept[0], came[0])
     second_scaled = ffn_rows_grad * wide(second_gain)
     second_inverse = lax.rsqrt(
@@ -1176,7 +1253,8 @@
         jnp.sum(second_scaled * resid_rows, axis=1, keepdims=True),
     )
     branch_sent = jnp.concatenate([low(resid_grad_rows), mixed_rows], axis=1)
-    branch_pieces = gather_tensor(branch_sent, axes)
+    branch_pieces = ring(branch_sent, axes, "y")
+    branch_other = turn(branch_pieces[0], axes, "c", 1)
     order = jnp.stack(
         [
             (level + span - step) % span * 2 + side
@@ -1185,10 +1263,12 @@
         ]
     ).astype(jnp.int32)
 
-    branch_pieces, mix_sum, mix_came[2] = hold((branch_pieces, mix_sum, mix_came[2]))
-    mix_sum = turn(
-        low(wide(mix_sum) + (wide(mixes[2][0]) + wide(mix_came[2]))), axes, "z", 1
-    )
+    branch_pieces = hold(branch_pieces)
+    branch_others = [turn(piece, axes, "c", 1) for piece in branch_pieces[1:]]
+    held = (branch_others, branch_other, mix_sum, mix_came[2], mixes)
+    branch_others, branch_other, mix_sum, mix_came[2], mixes = hold(held)
+    branch_pieces = branch_pieces + [branch_other] + branch_others
+    mix_parts[2] = mix_down(2)
     mix_came[3] = send_sum(mixes[3], axes, "x")
     rank_list = jnp.reshape(tensor_rank, (1,)).astype(jnp.int32)
     query_grad, key_grad, value_grad, inner, mix_in_grad, mix_out_grad = backward_call(
@@ -1205,62 +1285,76 @@
         mask,
         column_share,
     )
-    inner = lax.psum(inner, "tensor")
-    normed_mine, normed_theirs, lowrank_part, adapt_grad = weight_call(
-        jnp.stack([core, picked]).astype(jnp.int32),
+
+    inner = sum_tensor(hold(inner), axes)
+    held = (inner, mix_sum, mix_parts[2], mix_came[3], mixes)
+    inner, mix_sum, mix_parts[2], mix_came[3], mixes = hold(held)
+    mix_came[0] = send_sum(mixes[0], axes, "x")
+    mix_sum = turn(
+        low(wide(mix_sum) + mix_parts[2][0] + wide(mix_parts[2][1])), axes, "z", 1
+    )
+    mix_parts[3] = mix_down(3)
+    raw_grads, lowrank_part, adapt_grad = raw_call(
+        jnp.reshape(picked, (1,)),
+        model_width,
         inner,
         squares,
         (query_grad, key_grad, value_grad),
         raws[:2],
-        weights,
         lowrank,
         adapt_out,
-        row_share,
-    )
-
-    normed_mine, normed_theirs, lowrank_part, mix_sum, mix_came[3] = hold(
-        (normed_mine, normed_theirs, lowrank_part, mix_sum, mix_came[3])
-    )
+    )
+    lowrank_came = turn(lowrank_part, axes, "c", 1)
+    normed_mine, normed_theirs = weight_call(
+        jnp.reshape(core, (1,)).astype(jnp.int32), raw_grads, weights, row_share
+    )
+
+    lowrank_part, lowrank_came = hold((lowrank_part, lowrank_came))
+    lowrank_part = low(wide(lowrank_part) + wide(lowrank_came))
+    lowrank_parts = ring(lowrank_part, axes, "y")
+
+    held = (normed_mine, normed_theirs, lowrank_parts, mix_sum, mix_parts[3], mix_came[0])
+    normed_mine, normed_theirs, lowrank_parts, mix_sum, mix_parts[3], mix_came[0] = hold(held)
+    normed_theirs = turn(normed_theirs, axes, "c", 1)
+    lowrank_grad = low(sum(wide(part) for part in lowrank_parts))
+    compact = compact_call(
+        rank_list, lowrank_grad, normed_in, mix_out_grad, adapt_grad, mix_in_grad, select
+    )
+    mix_parts[0] = mix_down(0)
+    normed_theirs, compact = hold((normed_theirs, compact))
+    trees = ring(compact, axes, "x")
+    normed_kept, normed_sent = scatter_core(normed_mine, normed_theirs, axes)
+    normed_came = turn(normed_sent, axes, "y", -1)
     mix_sum = turn(
-        low(wide(mix_sum) + (wide(mixes[3][0]) + wide(mix_came[3]))), axes, "z", 1
-    )
-    mix_came[0] = send_sum(mixes[0], axes, "x")
-    lowrank_grad = low(sum_tensor(lowrank_part, axes))
-    normed_kept, normed_came = scatter_tensor(normed_mine, normed_theirs, axes)
-    maps = jnp.swapaxes(lax.dynamic_slice_in_dim(adapt_in, picked, RANK, 2), 0, 1)
-    maps = maps.reshape(model_width, 3 * RANK)
-    maps = jnp.concatenate(
-        [maps, jnp.zeros((model_width, 128 - 3 * RANK), jnp.bfloat16)], axis=1
-    )
+        low(wide(mix_sum) + mix_parts[3][0] + wide(mix_parts[3][1])), axes, "z", 1
+    )
+    trees = jnp.concatenate(hold(trees), axis=0)
+    tree_queue = [trees] + [turn(trees, axes, "z", step) for step in range(1, far)]
+    normed_came, mix_parts[0], mix_sum = hold((normed_came, mix_parts[0], mix_sum))
+
     input_rows = input_call(
         normed_kept,
         normed_came,
         own_rows(lowrank_grad),
         maps,
-        own_rows(tokens),
+        tokens_rows,
         first_gain,
         resid_grad_rows,
     )
-    compact = compact_call(
-        rank_list, lowrank_grad, normed_in, mix_out_grad, adapt_grad, mix_in_grad, select
-    )
-    trees = jnp.concatenate(ring(compact, axes, "x"), axis=0)
-
-    input_rows, trees, mix_sum, mix_came[0] = hold((input_rows, trees, mix_sum, mix_came[0]))
-    input_grad = spread_call(order, gather_tensor(input_rows, axes))
-    mix_total = wide(mix_sum) + (wide(mixes[0][0]) + wide(mix_came[0]))
-    mix_total = jnp.split(mix_total, span, axis=0)
-    mix_last = send_sum([low(part) for part in mix_total], axes, "y")
-    trees = jnp.concatenate(ring(trees, axes, "z"), axis=0)
-
-    trees, mix_last = hold((trees, mix_last))
+    input_held = ring(input_rows, axes, "y")
+    layer_rows = low(resid_rows + wide(mix_sum) + mix_parts[0][0] + wide(mix_parts[0][1]))
+
+    input_held, layer_rows, tree_queue = hold((input_held, layer_rows, tree_queue))
+    input_pieces = input_held + [turn(piece, axes, "c", 1) for piece in input_held]
+    layer_out = swap_columns(layer_rows, axes)
+
+    trees = jnp.concatenate(tree_queue, axis=0)
     shared = trees.reshape(owners, -1, column_share)[:, : 4 * RANK]
     shared = gather_tensor(shared.reshape(-1, column_share), axes)
+    input_grad = spread_call(order, input_pieces)
     grad_adapt_in, grad_adapt_out, grad_adapt_in_out, grad_adapt_out_out = assemble_call(
         order, trees, shared[1:], owners
     )
-    layer_rows = low(resid_rows + mix_total[0] + wide(mix_last))
-    layer_out = swap_columns(layer_rows, axes)
     return (
         layer_out,
         input_grad,

time: 570 us -> 532 us (0.933)
  waiting for transfers between devices: 171 us -> 146 us
  blocking collectives: 24.8 us -> 0 us
  local copies, waits for them, and re-layouts: 22.8 us -> 32.2 us
  Pallas kernels: 242 us -> 248 us
    ppermute x78 -> x82, waiting for transfers between devices: 171 us -> 146 us  [turn(): return lax.ppermute(array, axis, pairs)]
    psum x2 -> x0, blocking collectives: 24.8 us -> none  [the longest x1 13.2 us: body(): squares = lax.psum(squares, 'tensor')]
    pallas_call x18 -> x19, Pallas kernels: 242 us -> 248 us  [kernel_call(): pl.pallas_call(kernel, grid_spec=pltpu.PrefetchScalarGridSpec(num_scalar_...]
    unnamed x149 -> x161, local copies, waits for them, and re-layouts: 9.35 us -> 12.2 us
    ppermute x78 -> x82, starting transfers between devices: 69.2 us -> 68.4 us  [turn(): return lax.ppermute(array, axis, pairs)]
  transfers between devices with their start and end apart: 78 -> 82, of which waited for: 19 -> 32; matrix products, arithmetic and copies ran while one was open for 7% -> 8% of each run, Pallas kernels for 42% -> 45%
where the time goes in v5:
time: 532 us; the launch traced here: 524 us
  Pallas kernels  248 us (47%)
  waiting for transfers between devices  146 us (27%)
  starting transfers between devices  68.4 us (13%)
  local copies, waits for them, and re-layouts  32.2 us (6%)
  other arithmetic  26.7 us (5%)
    pallas_call x19, Pallas kernels, kernel_call(): pl.pallas_call(kernel, grid_spec=pltpu.PrefetchScalarGridSpec(num_scalar_...  248 us
    ppermute x82, waiting for transfers between devices, turn(): return lax.ppermute(array, axis, pairs)  146 us
    ppermute x82, starting transfers between devices, turn(): return lax.ppermute(array, axis, pairs)  68.4 us
    convert_element_type x15, other arithmetic, low(): return array.astype(jnp.bfloat16)  14 us
    unnamed x161, local copies, waits for them, and re-layouts  12.2 us
  transfers between devices with their start and end apart: 82, of which 32 were waited for; matrix products, arithmetic and copies ran while one was open for 8% of the time, Pallas kernels for 45%

profile of v5, /device:TPU:0, one launch (start us, length us, event | category | flops | bytes accessed | tf_op | source)
XLA Modules:
  0.0 524.4 jit_solution(1623146536525986825)
XLA Ops:
  3.5 3.0 collective-permute-start.3
  9.4 14.9 %shard_map.244 = (bf16[512,2048]{1,0:T(8,128)(2,1)}, bf16[3,512,128]{2,1,0:T(8,128)(2,1)}, f32[512,512]{1,0:T(8,128)}, f32[512,512]{1,0:T(8,128)}, f32[512,512]{1,0:T(8,128)}, /*index=5*/f32[8,512]{1,0:T(8,128)}) custom-call(bf16[512,2048]{1,0:T(8,128)(2,1)} %tokens.1, bf16[1,2048]{1,0:T(2,128)(2,1)} %broadcast_in_dim.43.gain, ...), custom_call_target="tpu_custom_call" | custom-call | flops 3221225472 | bytes 10359296 | tf_op jit(solution)/shard_map/pallas_call | solution.py:203
  38.1 10.9 %shard_map.245 = (bf16[512,512]{1,0:T(8,128)(2,1)}, bf16[512,512]{1,0:T(8,128)(2,1)}, bf16[512,512]{1,0:T(8,128)(2,1)}, bf16[512,512]{1,0:T(8,128)(2,1)}, f32[25...) custom-call(s32[1]{0:T(128)} %bitcast.core.scalars, f32[8,512]{1,0:T(8,128)} %add.341.squares, ...), custom_call_target="tpu_custom_call" | custom-call | flops 1610612736 | bytes 6965252 | tf_op jit(solution)/shard_map/pallas_call | solution.py:203
  50.4 2.2 collective-permute-done.4.refs_0_
  53.4 2.9 collective-permute-done.6
  56.4 2.7 add_convert_fusion
  62.1 11.7 %collective-permute-done.7.came = bf16[128,2176]{1,0:T(8,128)(2,1)S(1)} collective-permute-done((bf16[128,2176]{1,0:T(8,128)(2,1)S(1)}, bf16[128,2176]{1,0:T(8,128)(2,1)S(1)}, u32[]{:S(2)}, u32[]{:S(2)}) %collective-permute-start.7) | collective-permute-done | bytes 557088 | tf_op jit(solution)/shard_map/ppermute | solution.py:76
  75.0 3.0 collective-permute-done.8.refs_1_
  83.2 3.2 shard_map.246
  87.8 13.2 %collective-permute-done.13 = bf16[128,2048]{1,0:T(8,128)(2,1)S(1)} collective-permute-done((bf16[128,2048]{1,0:T(8,128)(2,1)}, bf16[128,2048]{1,0:T(8,128)(2,1)S(1)}, u32[]{:S(2)}, u32[]{:S(2)}) %collective-permute-start.13) | collective-permute-done | bytes 524320 | tf_op jit(solution)/shard_map/ppermute | solution.py:76
  107.6 16.6 %shard_map.247 = (bf16[8,1024,256]{2,1,0:T(8,128)(2,1)}, bf16[1024,128]{1,0:T(8,128)(2,1)}) custom-call(bf16[256,2176]{1,0:T(8,128)(2,1)} %copy-done.14, bf16[256,2176]{1,0:T(8,128)(2,1)} %copy-done.52, bf16[128,2176]{1,0:T(8,128)(2,1)} %copy-done.21, bf16[128,2176]{1,0:T(8,128)(2,1)} %get-tuple-element.264.refs_3_, bf16[128,2176]{1,0:T(8,128)(2,1)} %copy-done.64, ...), custom_call_target="tpu_custom_call" | custom-call | flops 8589934592 | bytes 13107200 | tf_op jit(solution)/shard_map/pallas_call | solution.py:203
  124.5 6.0 %collective-permute-done.17 = bf16[128,2048]{1,0:T(8,128)(2,1)S(1)} collective-permute-done((bf16[128,2048]{1,0:T(8,128)(2,1)S(1)}, bf16[128,2048]{1,0:T(8,128)(2,1)S(1)}, u32[]{:S(2)}, u32[]{:S(2)}) %collective-permute-start.17) | collective-permute-done | bytes 524320 | tf_op jit(solution)/shard_map/ppermute | solution.py:76
  130.5 3.0 collective-permute-done.16
  137.7 25.7 %shard_map.248 = (bf16[128,2048]{1,0:T(8,128)(2,1)}, bf16[128,2048]{1,0:T(8,128)(2,1)}, bf16[128,2048]{1,0:T(8,128)(2,1)}, bf16[128,2048]{1,0:T(8,128)(2,1)}, bf16[8,512,256]{2,1,0:T(8,128)(2,1)}) custom-call(bf16[256,2048]{1,0:T(8,128)(2,1)} %copy-done.41, bf16[256,2048]{1,0:T(8,128)(2,1)} %copy-done.56, bf16[4,2048,256]{2,1,0:T(8,128)(2,1)} %refs_2_.3, ...), custom_call_target="tpu_custom_call" | custom-call | flops 17179869184 | bytes 23592960 | tf_op jit(solution)/shard_map/pallas_call | solution.py:203
  168.3 25.8 %shard_map.249 = (bf16[128,2048]{1,0:T(8,128)(2,1)}, bf16[128,2048]{1,0:T(8,128)(2,1)}, bf16[128,2048]{1,0:T(8,128)(2,1)}, bf16[128,2048]{1,0:T(8,128)(2,1)}, bf16[8,512,256]{2,1,0:T(8,128)(2,1)}) custom-call(bf16[256,2048]{1,0:T(8,128)(2,1)} %copy-done.42, bf16[256,2048]{1,0:T(8,128)(2,1)} %copy-done.57, bf16[4,2048,256]{2,1,0:T(8,128)(2,1)} %refs_2_.3, ...), custom_call_target="tpu_custom_call" | custom-call | flops 17179869184 | bytes 23592960 | tf_op jit(solution)/shard_map/pallas_call | solution.py:203
  194.1 11.0 %shard_map.250 = (bf16[8,512,256]{2,1,0:T(8,128)(2,1)}, bf16[512,128]{1,0:T(8,128)(2,1)}) custom-call(bf16[128,2176]{1,0:T(8,128)(2,1)} %copy-done.60, bf16[128,2176]{1,0:T(8,128)(2,1)} %copy-done.62, bf16[128,2176]{1,0:T(8,128)(2,1)} %copy-done.66, bf16[128,2176]{1,0:T(8,128)(2,1)} %collective-permute-done.24.refs_3_, bf16[1024,2048]{1,0:T(8,128)(2,1)} %bitcast.36, ...), custom_call_target="tpu_custom_call" | custom-call | flops 4294967296 | bytes 10878976 | tf_op jit(solution)/shard_map/pallas_call | solution.py:203
  209.5 26.3 %shard_map.251 = (bf16[128,2048]{1,0:T(8,128)(2,1)}, bf16[128,2048]{1,0:T(8,128)(2,1)}, bf16[128,2048]{1,0:T(8,128)(2,1)}, bf16[128,2048]{1,0:T(8,128)(2,1)}, bf16[8,512,256]{2,1,0:T(8,128)(2,1)}) custom-call(bf16[256,2048]{1,0:T(8,128)(2,1)} %copy-done.40, bf16[256,2048]{1,0:T(8,128)(2,1)} %copy-done.58, bf16[4,2048,256]{2,1,0:T(8,128)(2,1)} %refs_2_.3, ...), custom_call_target="tpu_custom_call" | custom-call | flops 17179869184 | bytes 21364736 | tf_op jit(solution)/shard_map/pallas_call | solution.py:203
  235.8 2.9 collective-permute-done.27.refs_1_
  246.2 13.1 %shard_map.252 = (bf16[256,2048]{1,0:T(8,128)(2,1)}, bf16[256,2048]{1,0:T(8,128)(2,1)}, bf16[256,2048]{1,0:T(8,128)(2,1)}, bf16[256,2048]{1,0:T(8,128)(2,1)}) custom-call(bf16[8,512,256]{2,1,0:T(8,128)(2,1)} %get-tuple-element.341.refs_0_, bf16[8,512,256]{2,1,0:T(8,128)(2,1)} %get-tuple-element.342.refs_1_, bf16[1024,2048]{1,0:T(8,128)(2,1)} %bitcast.37, ...), custom_call_target="tpu_custom_call" | custom-call | flops 8589934592 | bytes 12582912 | tf_op jit(solution)/shard_map/pallas_call | solution.py:203
  260.0 3.9 collective-permute-done.37
  266.3 11.2 %shard_map.253 = (bf16[8,512,256]{2,1,0:T(8,128)(2,1)}, bf16[512,128]{1,0:T(8,128)(2,1)}) custom-call(bf16[128,2176]{1,0:T(8,128)(2,1)} %copy-done.59, bf16[128,2176]{1,0:T(8,128)(2,1)} %collective-permute-done.23.refs_1_, bf16[128,2176]{1,0:T(8,128)(2,1)} %collective-permute-done.32.refs_2_, bf16[128,2176]{1,0:T(8,128)(2,1)} %collective-permute-done.33.refs_3_, ...), custom_call_target="tpu_custom_call" | custom-call | flops 4294967296 | bytes 10878976 | tf_op jit(solution)/shard_map/pallas_call | solution.py:203
  279.2 26.1 %shard_map.254 = (bf16[128,2048]{1,0:T(8,128)(2,1)}, bf16[128,2048]{1,0:T(8,128)(2,1)}, bf16[128,2048]{1,0:T(8,128)(2,1)}, bf16[128,2048]{1,0:T(8,128)(2,1)}, bf16[8,512,256]{2,1,0:T(8,128)(2,1)}) custom-call(bf16[256,2048]{1,0:T(8,128)(2,1)} %copy-done.43, bf16[256,2048]{1,0:T(8,128)(2,1)} %copy-done.54, bf16[4,2048,256]{2,1,0:T(8,128)(2,1)} %refs_2_.3, ...), custom_call_target="tpu_custom_call" | custom-call | flops 17179869184 | bytes 21364736 | tf_op jit(solution)/shard_map/pallas_call | solution.py:203
  308.4 3.9 collective-permute-start.44
  312.3 13.2 %shard_map.255 = (bf16[256,2048]{1,0:T(8,128)(2,1)}, bf16[256,2048]{1,0:T(8,128)(2,1)}, bf16[256,2048]{1,0:T(8,128)(2,1)}, bf16[256,2048]{1,0:T(8,128)(2,1)}) custom-call(bf16[8,512,256]{2,1,0:T(8,128)(2,1)} %get-tuple-element.385.refs_0_, bf16[8,512,256]{2,1,0:T(8,128)(2,1)} %get-tuple-element.386.refs_1_, bf16[1024,2048]{1,0:T(8,128)(2,1)} %bitcast.39, ...), custom_call_target="tpu_custom_call" | custom-call | flops 8589934592 | bytes 12582912 | tf_op jit(solution)/shard_map/pallas_call | solution.py:203
  328.4 3.8 collective-permute-done.47
  332.1 2.6 collective-permute-done.48
  337.8 8.3 %collective-permute-done.49 = bf16[128,2048]{1,0:T(8,128)(2,1)S(1)} collective-permute-done((bf16[128,2048]{1,0:T(8,128)(2,1)S(1)}, bf16[128,2048]{1,0:T(8,128)(2,1)S(1)}, u32[]{:S(2)}, u32[]{:S(2)}) %collective-permute-start.49) | collective-permute-done | bytes 524320 | tf_op jit(solution)/shard_map/ppermute | solution.py:76
  346.1 4.1 collective-permute-done.50
  350.6 2.6 fusion.19
  355.0 7.9 %collective-permute-done.51.refs_1_ = bf16[128,2176]{1,0:T(8,128)(2,1)S(1)} collective-permute-done((bf16[128,2176]{1,0:T(8,128)(2,1)S(1)}, bf16[128,2176]{1,0:T(8,128)(2,1)S(1)}, u32[]{:S(2)}, u32[]{:S(2)}) %collective-permute-start.51) | collective-permute-done | bytes 557088 | tf_op jit(solution)/shard_map/ppermute | solution.py:76
  364.2 15.0 %collective-permute-done.54 = bf16[128,2048]{1,0:T(8,128)(2,1)S(1)} collective-permute-done((bf16[128,2048]{1,0:T(8,128)(2,1)S(1)}, bf16[128,2048]{1,0:T(8,128)(2,1)S(1)}, u32[]{:S(2)}, u32[]{:S(2)}) %collective-permute-start.54) | collective-permute-done | bytes 524320 | tf_op jit(solution)/shard_map/ppermute | solution.py:76
  384.5 19.3 %shard_map.256 = (f32[512,512]{1,0:T(8,128)}, f32[512,512]{1,0:T(8,128)}, bf16[512,512]{1,0:T(8,128)(2,1)}, f32[8,512]{1,0:T(8,128)}, bf16[16,512]{1,0:T(8,128)(2,1)}, /*index=5*/bf16[16,512]{1,0:T(8,128)(2,1)}) custom-call(s32[5]{0:T(128)} %concatenate.56.scalars, bf16[128,2176]{1,0:T(8,128)(2,1)} %copy-done.22, bf16[128,2176]{1,0:T(8,128)(2,1)} %copy-done.67, ...), custom_call_target="tpu_custom_call" | custom-call | flops 2952790016 | bytes 10750484 | tf_op jit(solution)/shard_map/pallas_call | solution.py:203
  407.2 2.6 collective-permute-done.57
  410.4 4.9 shard_map.257
  423.5 9.1 %shard_map.258 = (f32[256,2048]{1,0:T(8,128)}, bf16[256,2048]{1,0:T(8,128)(2,1)}) custom-call(s32[1]{0:T(128)} %bitcast.core.scalars, bf16[3,512,512]{2,1,0:T(8,128)(2,1)} %get-tuple-element.445.raw, bf16[2048,512]{1,0:T(8,128)(2,1)} %query_weight.3, bf16[2048,512]{1,0:T(8,128)(2,1)} %key_weight.3, bf16[2048,512]{1,0:T(8,128)(2,1)} %value_weight.3), custom_call_target="tpu_custom_call" | custom-call | flops 3221225472 | bytes 7864324 | tf_op jit(solution)/shard_map/pallas_call | solution.py:203
  432.6 5.7 %collective-permute-done.61 = bf16[512,128]{1,0:T(8,128)(2,1)S(1)} collective-permute-done((bf16[512,128]{1,0:T(8,128)(2,1)S(1)}, bf16[512,128]{1,0:T(8,128)(2,1)S(1)}, u32[]{:S(2)}, u32[]{:S(2)}) %collective-permute-start.61) | collective-permute-done | bytes 131104 | tf_op jit(solution)/shard_map/ppermute | solution.py:76
  438.3 4.5 collective-permute-done.64
  447.6 2.9 shard_map.259
  456.1 2.6 collective-permute-done.70
  458.7 3.6 collective-permute-start.73
  462.6 2.2 collective-permute-start.71
  464.8 7.0 %collective-permute-done.66.came = bf16[128,2048]{1,0:T(8,128)(2,1)S(1)} collective-permute-done((bf16[128,2048]{1,0:T(8,128)(2,1)S(1)}, bf16[128,2048]{1,0:T(8,128)(2,1)S(1)}, u32[]{:S(2)}, u32[]{:S(2)}) %collective-permute-start.66) | collective-permute-done | bytes 524320 | tf_op jit(solution)/shard_map/ppermute | solution.py:76
  472.6 3.6 shard_map.260.refs_0_
  478.3 9.0 %collective-permute-done.72 = bf16[288,512]{1,0:T(8,128)(2,1)S(1)} collective-permute-done((bf16[288,512]{1,0:T(8,128)(2,1)S(1)}, bf16[288,512]{1,0:T(8,128)(2,1)S(1)}, u32[]{:S(2)}, u32[]{:S(2)}) %collective-permute-start.72) | collective-permute-done | bytes 294944 | tf_op jit(solution)/shard_map/ppermute | solution.py:76
  487.4 2.5 collective-permute-done.69.refs_1_
  495.4 10.7 %collective-permute-done.79.refs_1_ = bf16[512,512]{1,0:T(8,128)(2,1)} collective-permute-done((bf16[512,512]{1,0:T(8,128)(2,1)}, bf16[512,512]{1,0:T(8,128)(2,1)}, u32[]{:S(2)}, u32[]{:S(2)}) %collective-permute-start.79) | collective-permute-done | bytes 524320 | tf_op jit(solution)/shard_map/ppermute | solution.py:76
  514.0 4.6 shard_map.261
  518.6 5.3 %shard_map.262 = (f32[3,2048,128]{2,1,0:T(8,128)}, f32[3,128,512]{2,1,0:T(8,128)}, f32[512,128]{1,0:T(8,128)}, f32[128,2048]{1,0:T(8,128)}) custom-call(s32[4]{0:T(128)} %pad_add_fusion.order, bf16[1152,512]{1,0:T(8,128)(2,1)} %copy-done.4, bf16[512,512]{1,0:T(8,128)(2,1)} %collective-permute-done.79.refs_1_, ...), custom_call_target="tpu_custom_call" | custom-call | flops 268435456 | bytes 2752528 | tf_op jit(solution)/shard_map/pallas_call | solution.py:203
  (428 shorter events, 119.8 us)
Async XLA Ops:
  3.5 29.6 %collective-permute-start.3 = (bf16[256,2176]{1,0:T(8,128)(2,1)S(1)}, bf16[256,2176]{1,0:T(8,128)(2,1)S(1)}, u32[]{:S(2)}, u32[]{:S(2)}) collective-permute-start(bf16[256,2176]{1,0:T(8,128)(2,1)S(1)} %maximum_maximum_fusion.refs_0_), channel_id=1, source_target_pairs={{0,4},{4,0},{8,12},{12,8},{16,20},{20,16},{24,28},{28,24},{1,5},{5... | collective-permute-start | bytes 3342344 | tf_op jit(solution)/shard_map/ppermute | solution.py:76
  6.5 27.9 %collective-permute-start.2 = (bf16[256,2176]{1,0:T(8,128)(2,1)S(1)}, bf16[256,2176]{1,0:T(8,128)(2,1)S(1)}, u32[]{:S(2)}, u32[]{:S(2)}) collective-permute-start(bf16[256,2176]{1,0:T(8,128)(2,1)S(1)} %maximum_maximum_fusion.refs_0_), channel_id=1, source_target_pairs={{0,8},{4,12},{8,16},{12,20},{16,24},{20,28},{24,0},{28,4},{1,9},{5... | collective-permute-start | bytes 3342344 | tf_op jit(solution)/shard_map/ppermute | solution.py:76
  34.4 43.7 %collective-permute-start.10 = (bf16[4,2048,256]{2,1,0:T(8,128)(2,1)}, bf16[4,2048,256]{2,1,0:T(8,128)(2,1)}, u32[]{:S(2)}, u32[]{:S(2)}) collective-permute-start(bf16[4,2048,256]{2,1,0:T(8,128)(2,1)} %refs_2_.3), channel_id=1, source_target_pairs={{0,1},{1,0},{2,3},{3,2},{4,5},{5,4},{6,7},{7,6},{8,9},{9,8},{10,11... | collective-permute-start | bytes 12582920 | tf_op jit(solution)/shard_map/ppermute | solution.py:76
  34.4 44.5 %collective-permute-start.11 = (bf16[4,2048,256]{2,1,0:T(8,128)(2,1)}, bf16[4,2048,256]{2,1,0:T(8,128)(2,1)}, u32[]{:S(2)}, u32[]{:S(2)}) collective-permute-start(bf16[4,2048,256]{2,1,0:T(8,128)(2,1)} %refs_3_.3), channel_id=1, source_target_pairs={{0,1},{1,0},{2,3},{3,2},{4,5},{5,4},{6,7},{7,6},{8,9},{9,8},{10,11... | collective-permute-start | bytes 12582920 | tf_op jit(solution)/shard_map/ppermute | solution.py:76
  78.9 24.2 %collective-permute-start.14 = (bf16[1024,2048]{1,0:T(8,128)(2,1)}, bf16[1024,2048]{1,0:T(8,128)(2,1)}, u32[]{:S(2)}, u32[]{:S(2)}) collective-permute-start(bf16[1024,2048]{1,0:T(8,128)(2,1)} %bitcast.34), channel_id=1, source_target_pairs={{0,1},{1,0},{2,3},{3,2},{4,5},{5,4},{6,7},{7,6},{8,9},{9,8},{10,11... | collective-permute-start | bytes 12582920 | tf_op jit(solution)/shard_map/ppermute | solution.py:76
  104.2 29.3 %collective-permute-start.15 = (bf16[256,2048]{1,0:T(8,128)(2,1)S(1)}, bf16[256,2048]{1,0:T(8,128)(2,1)S(1)}, u32[]{:S(2)}, u32[]{:S(2)}) collective-permute-start(bf16[256,2048]{1,0:T(8,128)(2,1)S(1)} %constant_dynamic-update-slice_fusion.refs_0_), channel_id=1, source_target_pairs={{0,2},{1,3},{2,0},{3,1},{4,6},{5,7},{6,4},{7,5},{8,10},{9,11},{10,... | collective-permute-start | bytes 3145736 | tf_op jit(solution)/shard_map/ppermute | solution.py:76
  105.6 18.6 %collective-permute-start.19 = (bf16[128,2176]{1,0:T(8,128)(2,1)S(1)}, bf16[128,2176]{1,0:T(8,128)(2,1)S(1)}, u32[]{:S(2)}, u32[]{:S(2)}) collective-permute-start(bf16[128,2176]{1,0:T(8,128)(2,1)S(1)} %copy-done.61), channel_id=1, source_target_pairs={{0,4},{4,0},{8,12},{12,8},{16,20},{20,16},{24,28},{28,24},{1,5},{5... | collective-permute-start | bytes 1671176 | tf_op jit(solution)/shard_map/ppermute | solution.py:76
  107.1 17.4 %collective-permute-start.18 = (bf16[128,2176]{1,0:T(8,128)(2,1)S(1)}, bf16[128,2176]{1,0:T(8,128)(2,1)S(1)}, u32[]{:S(2)}, u32[]{:S(2)}) collective-permute-start(bf16[128,2176]{1,0:T(8,128)(2,1)S(1)} %copy-done.61), channel_id=1, source_target_pairs={{0,8},{4,12},{8,16},{12,20},{16,24},{20,28},{24,0},{28,4},{1,9},{5... | collective-permute-start | bytes 1671176 | tf_op jit(solution)/shard_map/ppermute | solution.py:76
  107.1 23.4 %collective-permute-start.17 = (bf16[128,2048]{1,0:T(8,128)(2,1)S(1)}, bf16[128,2048]{1,0:T(8,128)(2,1)S(1)}, u32[]{:S(2)}, u32[]{:S(2)}) collective-permute-start(bf16[128,2048]{1,0:T(8,128)(2,1)S(1)} %collective-permute-done.12), channel_id=1, source_target_pairs={{0,4},{4,0},{8,12},{12,8},{16,20},{20,16},{24,28},{28,24},{1,5},{5... | collective-permute-start | bytes 1572872 | tf_op jit(solution)/shard_map/ppermute | solution.py:76
  107.6 25.9 %collective-permute-start.16 = (bf16[128,2048]{1,0:T(8,128)(2,1)S(1)}, bf16[128,2048]{1,0:T(8,128)(2,1)S(1)}, u32[]{:S(2)}, u32[]{:S(2)}) collective-permute-start(bf16[128,2048]{1,0:T(8,128)(2,1)S(1)} %collective-permute-done.12), channel_id=1, source_target_pairs={{0,8},{4,12},{8,16},{12,20},{16,24},{20,28},{24,0},{28,4},{1,9},{5... | collective-permute-start | bytes 1572872 | tf_op jit(solution)/shard_map/ppermute | solution.py:76
  133.5 29.9 %collective-permute-start.22 = (bf16[128,2048]{1,0:T(8,128)(2,1)S(1)}, bf16[128,2048]{1,0:T(8,128)(2,1)S(1)}, u32[]{:S(2)}, u32[]{:S(2)}) collective-permute-start(bf16[128,2048]{1,0:T(8,128)(2,1)S(1)} %collective-permute-done.16), channel_id=1, source_target_pairs={{0,4},{4,0},{8,12},{12,8},{16,20},{20,16},{24,28},{28,24},{1,5},{5... | collective-permute-start | bytes 1572872 | tf_op jit(solution)/shard_map/ppermute | solution.py:76
  134.0 29.4 %collective-permute-start.21 = (bf16[128,2048]{1,0:T(8,128)(2,1)S(1)}, bf16[128,2048]{1,0:T(8,128)(2,1)S(1)}, u32[]{:S(2)}, u32[]{:S(2)}) collective-permute-start(bf16[128,2048]{1,0:T(8,128)(2,1)S(1)} %collective-permute-done.16), channel_id=1, source_target_pairs={{0,8},{4,12},{8,16},{12,20},{16,24},{20,28},{24,0},{28,4},{1,9},{5... | collective-permute-start | bytes 1572872 | tf_op jit(solution)/shard_map/ppermute | solution.py:76
  134.1 29.4 %collective-permute-start.24 = (bf16[128,2176]{1,0:T(8,128)(2,1)S(1)}, bf16[128,2176]{1,0:T(8,128)(2,1)}, u32[]{:S(2)}, u32[]{:S(2)}) collective-permute-start(bf16[128,2176]{1,0:T(8,128)(2,1)S(1)} %copy-done.63), channel_id=1, source_target_pairs={{0,4},{4,0},{8,12},{12,8},{16,20},{20,16},{24,28},{28,24},{1,5},{5... | collective-permute-start | bytes 1671176 | tf_op jit(solution)/shard_map/ppermute | solution.py:76
  135.5 27.9 %collective-permute-start.23 = (bf16[128,2176]{1,0:T(8,128)(2,1)S(1)}, bf16[128,2176]{1,0:T(8,128)(2,1)}, u32[]{:S(2)}, u32[]{:S(2)}) collective-permute-start(bf16[128,2176]{1,0:T(8,128)(2,1)S(1)} %copy-done.63), channel_id=1, source_target_pairs={{0,8},{4,12},{8,16},{12,20},{16,24},{20,28},{24,0},{28,4},{1,9},{5... | collective-permute-start | bytes 1671176 | tf_op jit(solution)/shard_map/ppermute | solution.py:76
  136.1 27.4 %collective-permute-start.20 = (bf16[256,2048]{1,0:T(8,128)(2,1)S(1)}, bf16[256,2048]{1,0:T(8,128)(2,1)S(1)}, u32[]{:S(2)}, u32[]{:S(2)}) collective-permute-start(bf16[256,2048]{1,0:T(8,128)(2,1)S(1)} %constant_dynamic-update-slice_fusion.2.refs_0_), channel_id=1, source_target_pairs={{0,2},{1,3},{2,0},{3,1},{4,6},{5,7},{6,4},{7,5},{8,10},{9,11},{10,... | collective-permute-start | bytes 3145736 | tf_op jit(solution)/shard_map/ppermute | solution.py:76
  163.5 72.3 %collective-permute-start.30 = (bf16[128,2048]{1,0:T(8,128)(2,1)}, bf16[128,2048]{1,0:T(8,128)(2,1)S(1)}, u32[]{:S(2)}, u32[]{:S(2)}) collective-permute-start(bf16[128,2048]{1,0:T(8,128)(2,1)} %get-tuple-element.316), channel_id=1, source_target_pairs={{0,2},{1,3},{2,0},{3,1},{4,6},{5,7},{6,4},{7,5},{8,10},{9,11},{10,... | collective-permute-start | bytes 1572872 | tf_op jit(solution)/shard_map/ppermute | solution.py:76
  164.1 41.0 %collective-permute-start.26 = (bf16[128,2048]{1,0:T(8,128)(2,1)S(1)}, bf16[128,2048]{1,0:T(8,128)(2,1)S(1)}, u32[]{:S(2)}, u32[]{:S(2)}) collective-permute-start(bf16[128,2048]{1,0:T(8,128)(2,1)S(1)} %collective-permute-done.21), channel_id=1, source_target_pairs={{0,4},{4,0},{8,12},{12,8},{16,20},{20,16},{24,28},{28,24},{1,5},{5... | collective-permute-start | bytes 1572872 | tf_op jit(solution)/shard_map/ppermute | solution.py:76
  164.6 42.1 %collective-permute-start.32 = (bf16[128,2176]{1,0:T(8,128)(2,1)S(1)}, bf16[128,2176]{1,0:T(8,128)(2,1)}, u32[]{:S(2)}, u32[]{:S(2)}) collective-permute-start(bf16[128,2176]{1,0:T(8,128)(2,1)S(1)} %collective-permute-done.18.refs_0_), channel_id=1, source_target_pairs={{0,4},{4,0},{8,12},{12,8},{16,20},{20,16},{24,28},{28,24},{1,5},{5... | collective-permute-start | bytes 1671176 | tf_op jit(solution)/shard_map/ppermute | solution.py:76
  166.1 40.6 %collective-permute-start.33 = (bf16[128,2176]{1,0:T(8,128)(2,1)}, bf16[128,2176]{1,0:T(8,128)(2,1)}, u32[]{:S(2)}, u32[]{:S(2)}) collective-permute-start(bf16[128,2176]{1,0:T(8,128)(2,1)} %collective-permute-done.23.refs_1_), channel_id=1, source_target_pairs={{0,4},{4,0},{8,12},{12,8},{16,20},{20,16},{24,28},{28,24},{1,5},{5... | collective-permute-start | bytes 1671176 | tf_op jit(solution)/shard_map/ppermute | solution.py:76
  166.7 40.0 %collective-permute-start.25 = (bf16[256,2048]{1,0:T(8,128)(2,1)S(1)}, bf16[256,2048]{1,0:T(8,128)(2,1)S(1)}, u32[]{:S(2)}, u32[]{:S(2)}) collective-permute-start(bf16[256,2048]{1,0:T(8,128)(2,1)S(1)} %constant_dynamic-update-slice_fusion.4.refs_0_), channel_id=1, source_target_pairs={{0,2},{1,3},{2,0},{3,1},{4,6},{5,7},{6,4},{7,5},{8,10},{9,11},{10,... | collective-permute-start | bytes 3145736 | tf_op jit(solution)/shard_map/ppermute | solution.py:76
  205.1 30.7 %collective-permute-start.31 = (bf16[128,2048]{1,0:T(8,128)(2,1)}, bf16[128,2048]{1,0:T(8,128)(2,1)S(1)}, u32[]{:S(2)}, u32[]{:S(2)}) collective-permute-start(bf16[128,2048]{1,0:T(8,128)(2,1)} %get-tuple-element.317), channel_id=1, source_target_pairs={{0,4},{4,0},{8,12},{12,8},{16,20},{20,16},{24,28},{28,24},{1,5},{5... | collective-permute-start | bytes 1572872 | tf_op jit(solution)/shard_map/ppermute | solution.py:76
  206.7 29.1 %collective-permute-start.28 = (bf16[128,2048]{1,0:T(8,128)(2,1)}, bf16[128,2048]{1,0:T(8,128)(2,1)S(1)}, u32[]{:S(2)}, u32[]{:S(2)}) collective-permute-start(bf16[128,2048]{1,0:T(8,128)(2,1)} %get-tuple-element.314), channel_id=1, source_target_pairs={{0,2},{1,3},{2,0},{3,1},{4,6},{5,7},{6,4},{7,5},{8,10},{9,11},{10,... | collective-permute-start | bytes 1572872 | tf_op jit(solution)/shard_map/ppermute | solution.py:76
  207.3 28.6 %collective-permute-start.29 = (bf16[128,2048]{1,0:T(8,128)(2,1)}, bf16[128,2048]{1,0:T(8,128)(2,1)S(1)}, u32[]{:S(2)}, u32[]{:S(2)}) collective-permute-start(bf16[128,2048]{1,0:T(8,128)(2,1)} %get-tuple-element.315), channel_id=1, source_target_pairs={{0,4},{4,0},{8,12},{12,8},{16,20},{20,16},{24,28},{28,24},{1,5},{5... | collective-permute-start | bytes 1572872 | tf_op jit(solution)/shard_map/ppermute | solution.py:76
  207.9 30.8 %collective-permute-start.27 = (bf16[256,2048]{1,0:T(8,128)(2,1)S(1)}, bf16[256,2048]{1,0:T(8,128)(2,1)S(1)}, u32[]{:S(2)}, u32[]{:S(2)}) collective-permute-start(bf16[256,2048]{1,0:T(8,128)(2,1)S(1)} %constant_dynamic-update-slice_fusion.6.refs_0_), channel_id=1, source_target_pairs={{0,2},{1,3},{2,0},{3,1},{4,6},{5,7},{6,4},{7,5},{8,10},{9,11},{10,... | collective-permute-start | bytes 3145736 | tf_op jit(solution)/shard_map/ppermute | solution.py:76
  241.6 17.7 %collective-permute-start.34 = (bf16[64,2048]{1,0:T(8,128)(2,1)S(1)}, bf16[64,2048]{1,0:T(8,128)(2,1)S(1)}, u32[]{:S(2)}, u32[]{:S(2)}) collective-permute-start(bf16[64,2048]{1,0:T(8,128)(2,1)S(1)} %split.155), channel_id=1, source_target_pairs={{0,4},{4,0},{8,12},{12,8},{16,20},{20,16},{24,28},{28,24},{1,5},{5... | collective-permute-start | bytes 786440 | tf_op jit(solution)/shard_map/ppermute | solution.py:76
  242.1 17.9 %collective-permute-start.35 = (bf16[64,2048]{1,0:T(8,128)(2,1)S(1)}, bf16[64,2048]{1,0:T(8,128)(2,1)S(1)}, u32[]{:S(2)}, u32[]{:S(2)}) collective-permute-start(bf16[64,2048]{1,0:T(8,128)(2,1)S(1)} %split.154), channel_id=1, source_target_pairs={{0,2},{1,3},{2,0},{3,1},{4,6},{5,7},{6,4},{7,5},{8,10},{9,11},{10,... | collective-permute-start | bytes 786440 | tf_op jit(solution)/shard_map/ppermute | solution.py:76
  242.7 62.8 %collective-permute-start.39 = (bf16[64,2048]{1,0:T(8,128)(2,1)S(1)}, bf16[64,2048]{1,0:T(8,128)(2,1)S(1)}, u32[]{:S(2)}, u32[]{:S(2)}) collective-permute-start(bf16[64,2048]{1,0:T(8,128)(2,1)S(1)} %split.153), channel_id=1, source_target_pairs={{0,4},{4,0},{8,12},{12,8},{16,20},{20,16},{24,28},{28,24},{1,5},{5... | collective-permute-start | bytes 786440 | tf_op jit(solution)/shard_map/ppermute | solution.py:76
  245.7 18.1 %collective-permute-start.37 = (bf16[128,2048]{1,0:T(8,128)(2,1)S(1)}, bf16[128,2048]{1,0:T(8,128)(2,1)S(1)}, u32[]{:S(2)}, u32[]{:S(2)}) collective-permute-start(bf16[128,2048]{1,0:T(8,128)(2,1)S(1)} %copy-done.70), channel_id=1, source_target_pairs={{0,4},{4,0},{8,12},{12,8},{16,20},{20,16},{24,28},{28,24},{1,5},{5... | collective-permute-start | bytes 1572872 | tf_op jit(solution)/shard_map/ppermute | solution.py:76
  259.4 46.1 %collective-permute-start.40 = (bf16[64,2048]{1,0:T(8,128)(2,1)S(1)}, bf16[64,2048]{1,0:T(8,128)(2,1)S(1)}, u32[]{:S(2)}, u32[]{:S(2)}) collective-permute-start(bf16[64,2048]{1,0:T(8,128)(2,1)S(1)} %split.152), channel_id=1, source_target_pairs={{0,2},{1,3},{2,0},{3,1},{4,6},{5,7},{6,4},{7,5},{8,10},{9,11},{10,... | collective-permute-start | bytes 786440 | tf_op jit(solution)/shard_map/ppermute | solution.py:76
  266.2 39.3 %collective-permute-start.38 = (bf16[128,2048]{1,0:T(8,128)(2,1)S(1)}, bf16[128,2048]{1,0:T(8,128)(2,1)S(1)}, u32[]{:S(2)}, u32[]{:S(2)}) collective-permute-start(bf16[128,2048]{1,0:T(8,128)(2,1)S(1)} %pad_maximum_fusion.1), channel_id=1, source_target_pairs={{0,8},{4,12},{8,16},{12,20},{16,24},{20,28},{24,0},{28,4},{1,9},{5... | collective-permute-start | bytes 1572872 | tf_op jit(solution)/shard_map/ppermute | solution.py:76
  277.5 28.0 %collective-permute-start.43 = (bf16[256,2048]{1,0:T(8,128)(2,1)S(1)}, bf16[256,2048]{1,0:T(8,128)(2,1)S(1)}, u32[]{:S(2)}, u32[]{:S(2)}) collective-permute-start(bf16[256,2048]{1,0:T(8,128)(2,1)S(1)} %copy-done.55), channel_id=1, source_target_pairs={{0,4},{4,0},{8,12},{12,8},{16,20},{20,16},{24,28},{28,24},{1,5},{5... | collective-permute-start | bytes 3145736 | tf_op jit(solution)/shard_map/ppermute | solution.py:76
  306.4 19.1 %collective-permute-start.45 = (bf16[128,2048]{1,0:T(8,128)(2,1)S(1)}, bf16[128,2048]{1,0:T(8,128)(2,1)S(1)}, u32[]{:S(2)}, u32[]{:S(2)}) collective-permute-start(bf16[128,2048]{1,0:T(8,128)(2,1)S(1)} %copy-done.73), channel_id=1, source_target_pairs={{0,2},{1,3},{2,0},{3,1},{4,6},{5,7},{6,4},{7,5},{8,10},{9,11},{10,... | collective-permute-start | bytes 1572872 | tf_op jit(solution)/shard_map/ppermute | solution.py:76
  307.8 17.7 %collective-permute-start.46 = (bf16[128,2048]{1,0:T(8,128)(2,1)S(1)}, bf16[128,2048]{1,0:T(8,128)(2,1)S(1)}, u32[]{:S(2)}, u32[]{:S(2)}) collective-permute-start(bf16[128,2048]{1,0:T(8,128)(2,1)S(1)} %copy-done.72), channel_id=1, source_target_pairs={{0,4},{4,0},{8,12},{12,8},{16,20},{20,16},{24,28},{28,24},{1,5},{5... | collective-permute-start | bytes 1572872 | tf_op jit(solution)/shard_map/ppermute | solution.py:76
  355.0 24.2 %collective-permute-start.55 = (bf16[256,2048]{1,0:T(8,128)(2,1)S(1)}, bf16[256,2048]{1,0:T(8,128)(2,1)S(1)}, u32[]{:S(2)}, u32[]{:S(2)}) collective-permute-start(bf16[256,2048]{1,0:T(8,128)(2,1)S(1)} %copy-done.53), channel_id=1, source_target_pairs={{0,4},{4,0},{8,12},{12,8},{16,20},{20,16},{24,28},{28,24},{1,5},{5... | collective-permute-start | bytes 3145736 | tf_op jit(solution)/shard_map/ppermute | solution.py:76
  355.0 24.2 %collective-permute-start.53 = (bf16[128,2176]{1,0:T(8,128)(2,1)S(1)}, bf16[128,2176]{1,0:T(8,128)(2,1)S(1)}, u32[]{:S(2)}, u32[]{:S(2)}) collective-permute-start(bf16[128,2176]{1,0:T(8,128)(2,1)S(1)} %pad_maximum_fusion.refs_0_), channel_id=1, source_target_pairs={{0,1},{1,0},{2,3},{3,2},{4,5},{5,4},{6,7},{7,6},{8,9},{9,8},{10,11... | collective-permute-start | bytes 1671176 | tf_op jit(solution)/shard_map/ppermute | solution.py:76
  380.9 29.5 %collective-permute-start.59 = (bf16[256,2048]{1,0:T(8,128)(2,1)}, bf16[256,2048]{1,0:T(8,128)(2,1)}, u32[]{:S(2)}, u32[]{:S(2)}) collective-permute-start(bf16[256,2048]{1,0:T(8,128)(2,1)} %get-tuple-element.436), channel_id=1, source_target_pairs={{0,4},{4,0},{8,12},{12,8},{16,20},{20,16},{24,28},{28,24},{1,5},{5... | collective-permute-start | bytes 3145736 | tf_op jit(solution)/shard_map/ppermute | solution.py:76
  383.0 27.4 %collective-permute-start.58 = (bf16[128,2048]{1,0:T(8,128)(2,1)}, bf16[128,2048]{1,0:T(8,128)(2,1)}, u32[]{:S(2)}, u32[]{:S(2)}) collective-permute-start(bf16[128,2048]{1,0:T(8,128)(2,1)} %split.146), channel_id=1, source_target_pairs={{0,2},{1,3},{2,0},{3,1},{4,6},{5,7},{6,4},{7,5},{8,10},{9,11},{10,... | collective-permute-start | bytes 1572872 | tf_op jit(solution)/shard_map/ppermute | solution.py:76
  416.7 21.6 %collective-permute-start.62 = (bf16[128,2048]{1,0:T(8,128)(2,1)S(1)}, bf16[128,2048]{1,0:T(8,128)(2,1)S(1)}, u32[]{:S(2)}, u32[]{:S(2)}) collective-permute-start(bf16[128,2048]{1,0:T(8,128)(2,1)S(1)} %add_convert_fusion.4), channel_id=1, source_target_pairs={{0,8},{4,12},{8,16},{12,20},{16,24},{20,28},{24,0},{28,4},{1,9},{5... | collective-permute-start | bytes 1572872 | tf_op jit(solution)/shard_map/ppermute | solution.py:76
  416.7 26.0 %collective-permute-start.64 = (bf16[256,2048]{1,0:T(8,128)(2,1)}, bf16[256,2048]{1,0:T(8,128)(2,1)S(1)}, u32[]{:S(2)}, u32[]{:S(2)}) collective-permute-start(bf16[256,2048]{1,0:T(8,128)(2,1)} %get-tuple-element.456), channel_id=1, source_target_pairs={{0,4},{4,0},{8,12},{12,8},{16,20},{20,16},{24,28},{28,24},{1,5},{5... | collective-permute-start | bytes 3145736 | tf_op jit(solution)/shard_map/ppermute | solution.py:76
  444.8 17.8 %collective-permute-start.68 = (bf16[128,2048]{1,0:T(8,128)(2,1)}, bf16[128,2048]{1,0:T(8,128)(2,1)}, u32[]{:S(2)}, u32[]{:S(2)}) collective-permute-start(bf16[128,2048]{1,0:T(8,128)(2,1)} %add_convert_fusion.2), channel_id=1, source_target_pairs={{0,8},{4,12},{8,16},{12,20},{16,24},{20,28},{24,0},{28,4},{1,9},{5... | collective-permute-start | bytes 1572872 | tf_op jit(solution)/shard_map/ppermute | solution.py:76
  446.0 18.7 %collective-permute-start.67 = (bf16[128,2048]{1,0:T(8,128)(2,1)}, bf16[128,2048]{1,0:T(8,128)(2,1)S(1)}, u32[]{:S(2)}, u32[]{:S(2)}) collective-permute-start(bf16[128,2048]{1,0:T(8,128)(2,1)} %split.144), channel_id=1, source_target_pairs={{0,2},{1,3},{2,0},{3,1},{4,6},{5,7},{6,4},{7,5},{8,10},{9,11},{10,... | collective-permute-start | bytes 1572872 | tf_op jit(solution)/shard_map/ppermute | solution.py:76
  451.8 20.1 %collective-permute-start.66 = (bf16[128,2048]{1,0:T(8,128)(2,1)S(1)}, bf16[128,2048]{1,0:T(8,128)(2,1)S(1)}, u32[]{:S(2)}, u32[]{:S(2)}) collective-permute-start(bf16[128,2048]{1,0:T(8,128)(2,1)S(1)} %get-tuple-element.496), channel_id=1, source_target_pairs={{0,2},{1,3},{2,0},{3,1},{4,6},{5,7},{6,4},{7,5},{8,10},{9,11},{10,... | collective-permute-start | bytes 1572872 | tf_op jit(solution)/shard_map/ppermute | solution.py:76
  458.7 19.6 %collective-permute-start.73 = (bf16[288,512]{1,0:T(8,128)(2,1)S(1)}, bf16[288,512]{1,0:T(8,128)(2,1)S(1)}, u32[]{:S(2)}, u32[]{:S(2)}) collective-permute-start(bf16[288,512]{1,0:T(8,128)(2,1)S(1)} %constant_dynamic-update-slice_fusion.8), channel_id=1, source_target_pairs={{0,24},{4,28},{8,0},{12,4},{16,8},{20,12},{24,16},{28,20},{1,25},{... | collective-permute-start | bytes 884744 | tf_op jit(solution)/shard_map/ppermute | solution.py:76
  462.3 25.1 %collective-permute-start.72 = (bf16[288,512]{1,0:T(8,128)(2,1)S(1)}, bf16[288,512]{1,0:T(8,128)(2,1)S(1)}, u32[]{:S(2)}, u32[]{:S(2)}) collective-permute-start(bf16[288,512]{1,0:T(8,128)(2,1)S(1)} %constant_dynamic-update-slice_fusion.8), channel_id=1, source_target_pairs={{0,16},{4,20},{8,24},{12,28},{16,0},{20,4},{24,8},{28,12},{1,17},{... | collective-permute-start | bytes 884744 | tf_op jit(solution)/shard_map/ppermute | solution.py:76
  462.6 24.8 %collective-permute-start.71 = (bf16[288,512]{1,0:T(8,128)(2,1)S(1)}, bf16[288,512]{1,0:T(8,128)(2,1)S(1)}, u32[]{:S(2)}, u32[]{:S(2)}) collective-permute-start(bf16[288,512]{1,0:T(8,128)(2,1)S(1)} %constant_dynamic-update-slice_fusion.8), channel_id=1, source_target_pairs={{0,8},{4,12},{8,16},{12,20},{16,24},{20,28},{24,0},{28,4},{1,9},{5... | collective-permute-start | bytes 884744 | tf_op jit(solution)/shard_map/ppermute | solution.py:76
  494.0 18.3 %collective-permute-start.77 = (bf16[128,2048]{1,0:T(8,128)(2,1)S(1)}, bf16[128,2048]{1,0:T(8,128)(2,1)S(1)}, u32[]{:S(2)}, u32[]{:S(2)}) collective-permute-start(bf16[128,2048]{1,0:T(8,128)(2,1)S(1)} %copy-done.12), channel_id=1, source_target_pairs={{0,1},{1,0},{2,3},{3,2},{4,5},{5,4},{6,7},{7,6},{8,9},{9,8},{10,11... | collective-permute-start | bytes 1572872 | tf_op jit(solution)/shard_map/ppermute | solution.py:76
  494.2 18.2 %collective-permute-start.78 = (bf16[128,2048]{1,0:T(8,128)(2,1)S(1)}, bf16[128,2048]{1,0:T(8,128)(2,1)S(1)}, u32[]{:S(2)}, u32[]{:S(2)}) collective-permute-start(bf16[128,2048]{1,0:T(8,128)(2,1)S(1)} %collective-permute-done.69.refs_1_), channel_id=1, source_target_pairs={{0,1},{1,0},{2,3},{3,2},{4,5},{5,4},{6,7},{7,6},{8,9},{9,8},{10,11... | collective-permute-start | bytes 1572872 | tf_op jit(solution)/shard_map/ppermute | solution.py:76
  495.2 23.4 %collective-permute-start.80 = (bf16[512,512]{1,0:T(8,128)(2,1)}, bf16[512,512]{1,0:T(8,128)(2,1)}, u32[]{:S(2)}, u32[]{:S(2)}) collective-permute-start(bf16[512,512]{1,0:T(8,128)(2,1)} %bitcast.17), channel_id=1, source_target_pairs={{0,1},{1,0},{2,3},{3,2},{4,5},{5,4},{6,7},{7,6},{8,9},{9,8},{10,11... | collective-permute-start | bytes 1572872 | tf_op jit(solution)/shard_map/ppermute | solution.py:76
  (119 other events, 1228.2 us)

commit v6 on v5

--- a/solution.py
+++ b/solution.py
@@ -15,6 +15,7 @@
 ROPE_BASE = 10000.0
 MASKED_SCORE = -1e30
 VMEM_LIMIT = 56 * 2**20
+CHUNK = 128
 
 
 def ancestry(parents):
@@ -103,19 +104,23 @@
     return send_sum(pieces[:span], axes, "y"), send_sum(pieces[span:], axes, "x")
 
 
+def block(array, index, count):
+    size = array.shape[0] // count
+    return wide(array[index * size : (index + 1) * size])
+
+
 def scatter_second(pieces, came, axes):
-    span = axes["y"][1]
-    first = wide(pieces[0]) + wide(came[0])
-    second = wide(pieces[span]) + wide(came[1])
-    first = jnp.split(first, axes["x"][1], axis=0)
-    second = jnp.split(second, axes["y"][1], axis=0)
-    first_came = send_sum([low(part) for part in first], axes, "x")
-    second_came = send_sum([low(part) for part in second], axes, "y")
-    return (first[0], second[0]), (first_came, second_came)
-
-
-def scatter_last(kept, came):
-    return jnp.concatenate([kept[0] + wide(came[0]), kept[1] + wide(came[1])], axis=0)
+    near, span = axes["x"][1], axes["y"][1]
+    first = [low(block(pieces[0], k, near) + block(came[0], k, near)) for k in range(1, near)]
+    second = [low(block(pieces[span], k, span) + block(came[1], k, span)) for k in range(1, span)]
+    return send_sum([None] + first, axes, "x"), send_sum([None] + second, axes, "y")
+
+
+def scatter_last(pieces, came, last, axes):
+    near, span = axes["x"][1], axes["y"][1]
+    first = block(pieces[0], 0, near) + block(came[0], 0, near) + wide(last[0])
+    second = block(pieces[span], 0, span) + block(came[1], 0, span) + wide(last[1])
+    return jnp.concatenate([first, second], axis=0)
 
 
 def gather_tensor(rows, axes):
@@ -142,26 +147,20 @@
     return jnp.concatenate(ring(rows, axes, "x"), axis=0)
 
 
-def swap_columns(rows, axes):
+def place_columns(rows, axes):
     rank = lax.axis_index("tensor")
-    count = lax.axis_size("tensor")
-    size, width = rows.shape
     span = axes["y"][1]
-    share = width // count
+    size, share = rows.shape[0] // span, rows.shape[1] // 2
     level, core = rank // 2, rank % 2
-    whole = jnp.zeros((count * size, share), rows.dtype)
+    mine = lax.dynamic_slice_in_dim(rows, core * share, share, 1)
+    theirs = turn(lax.dynamic_slice_in_dim(rows, (1 - core) * share, share, 1), axes, "c", 1)
+    blocks = jnp.zeros((2 * span * size, share), rows.dtype)
     for step in range(span):
-        toward = (level + step) % span
-        piece = lax.dynamic_slice_in_dim(rows, toward * 2 * share, 2 * share, 1)
-        if step:
-            piece = turn(piece, axes, "y", step)
-        mine = lax.dynamic_slice_in_dim(piece, core * share, share, 1)
-        theirs = lax.dynamic_slice_in_dim(piece, (1 - core) * share, share, 1)
-        theirs = turn(theirs, axes, "c", 1)
-        source = (level + span - step) % span
-        whole = lax.dynamic_update_slice_in_dim(whole, mine, (source * 2 + core) * size, 0)
-        whole = lax.dynamic_update_slice_in_dim(whole, theirs, (source * 2 + 1 - core) * size, 0)
-    return whole
+        place = (level + span - step) % span * 2
+        for part, side in ((mine, core), (theirs, 1 - core)):
+            taken = part[step * size : (step + 1) * size]
+            blocks = lax.dynamic_update_slice_in_dim(blocks, taken, (place + side) * size, 0)
+    return blocks
 
 
 def sum_tensor(array, axes):
@@ -215,25 +214,51 @@
     )(*operands)
 
 
+def normalize_rows(source, gain, target):
+    step = 16
+
+    def some(index, carry):
+        rows = pl.ds(pl.multiple_of(index * step, step), step)
+        values = wide(source[rows, :])
+        inverse = lax.rsqrt(jnp.mean(values * values, axis=1, keepdims=True) + EPSILON)
+        target[rows, :] = low(values * inverse * gain)
+        return carry
+
+    lax.fori_loop(0, source.shape[0] // step, some, 0)
+
+
 def project_kernel(
     tokens, gain, query_weight, key_weight, value_weight, adapt_in, adapt_out, select,
     normed_out, lowrank_out, query_out, key_out, value_out, squares_out,
     weights, maps, sems,
 ):
-    copies = [pltpu.make_async_copy(adapt_in, maps, sems.at[3])]
+    step = pl.program_id(0)
+    rank = adapt_out.shape[1]
+    copies = [
+        pltpu.make_async_copy(
+            adapt_in.at[index], maps.at[:, pl.ds(index * rank, rank)], sems.at[3]
+        )
+        for index in range(3)
+    ]
     for index, source in enumerate((query_weight, key_weight, value_weight)):
         copies.append(pltpu.make_async_copy(source, weights.at[index], sems.at[index]))
-    for copy in copies:
-        copy.start()
-    inputs = wide(tokens[...])
-    inverse = lax.rsqrt(jnp.mean(inputs * inputs, axis=1, keepdims=True) + EPSILON)
-    normed_out[...] = low(inputs * inverse * wide(gain[...]))
-    copies[0].wait()
-    for index in range(3):
-        lowrank_out[index] = low(dot(normed_out[...], maps[index]) * select[...])
+
+    @pl.when(step == 0)
+    def _():
+        for copy in copies:
+            copy.start()
+
+    normalize_rows(tokens, wide(gain[...]), normed_out)
+
+    @pl.when(step == 0)
+    def _():
+        for copy in copies:
+            copy.wait()
+
+    lowrank = dot(normed_out[...], maps[...])
     squares = []
     for index, out in enumerate((query_out, key_out, value_out)):
-        copies[index + 1].wait()
+        lowrank_out[index] = low(lowrank[:, index * rank : (index + 1) * rank] * select[...])
         raw = dot(normed_out[...], weights[index]) + dot(lowrank_out[index], adapt_out[index])
         out[...] = raw
         squares.append(jnp.sum(raw * raw, axis=1, keepdims=True))
@@ -246,20 +271,25 @@
     rows, width = tokens.shape
     local = weights[0].shape[1]
     rank = adapt_in.shape[2]
+    tile = rows // 2
     out_shape = [((rows, width), jnp.bfloat16), ((3, rows, rank), jnp.bfloat16)]
     out_shape += [((rows, local), jnp.float32)] * 3 + [((8, rows), jnp.float32)]
     operands = [tokens, gain, *weights, adapt_in, adapt_out, select]
+    row_block = pl.BlockSpec((tile, width), lambda n: (n, 0))
+    local_block = pl.BlockSpec((tile, local), lambda n: (n, 0))
     return kernel_call(
         project_kernel,
-        (1,),
-        [whole(tokens), whole(gain), ANY, ANY, ANY, ANY, whole(adapt_out), whole(select)],
-        [pl.BlockSpec(shape, lambda *_, size=len(shape): (0,) * size) for shape, _ in out_shape],
+        (2,),
+        [row_block, whole(gain), ANY, ANY, ANY, ANY, whole(adapt_out), whole(select)],
+        [row_block, pl.BlockSpec((3, tile, rank), lambda n: (0, n, 0))]
+        + [local_block] * 3
+        + [pl.BlockSpec((8, tile), lambda n: (0, n))],
         out_shape,
         operands,
         6 * rows * width * local,
         [
             pltpu.VMEM((3, width, local), jnp.bfloat16),
-            pltpu.VMEM(adapt_in.shape, jnp.bfloat16),
+            pltpu.VMEM((width, 3 * rank), jnp.bfloat16),
             pltpu.SemaphoreType.DMA((4,)),
         ],
     )
@@ -276,7 +306,7 @@
 
 def attend_kernel(
     width, size, core, squares, query_raw, key_raw, value_raw, query_gain, key_gain, cosine, sine,
-    mask, output_weight, mix_in, queries, keys, values, attended, mine, theirs, held, weight, sem,
+    mask, output_weight, mix_in, queries, keys, values, attended, mine, theirs, held, weight, scales, sem,
 ):
     head = pl.program_id(0)
     last = pl.num_programs(0) - 1
@@ -285,8 +315,9 @@
     @pl.when(head == 0)
     def _():
         copy.start()
-
-    inverse = lax.rsqrt(spread_columns(squares[...]) / width + EPSILON)
+        scales[...] = lax.rsqrt(spread_columns(squares[...]) / width + EPSILON)
+
+    inverse = scales[:, :2]
     query = query_raw[...] * inverse[:, 0:1] * wide(query_gain[...])
     key = key_raw[...] * inverse[:, 1:2] * wide(key_gain[...])
     query = low(query * cosine[...] + turned(query) * sine[...])
@@ -297,7 +328,7 @@
     values[...] = value
     scores = dot_t(query, key) * HD ** (-0.5) + mask[...]
     raised = jnp.exp(scores - jnp.max(scores, axis=1, keepdims=True))
-    weights = low(raised / jnp.sum(raised, axis=1, keepdims=True))
+    weights = low(raised * (1.0 / jnp.sum(raised, axis=1, keepdims=True)))
     result = low(dot(weights, value))
     attended[...] = result
     held[head] = result
@@ -341,6 +372,7 @@
         [
             pltpu.VMEM((heads, rows, HD), jnp.bfloat16),
             pltpu.VMEM(output_weight.shape, jnp.bfloat16),
+            pltpu.VMEM((rows, 128), jnp.float32),
             pltpu.SemaphoreType.DMA,
         ],
         1,
@@ -348,33 +380,34 @@
 
 
 def resid_kernel(
-    width, kept, came, tokens, mix_out, select, gain, resid_out, norm_out, mixed_out
+    width, rank, kept, came, tokens, mix_out, select, gain, resid_out, norm_out, mixed_out
 ):
     mixed = low((kept[:, width:] + wide(came[:, width:])) * select[...])
     mixed_out[...] = mixed
-    resid = (
+    resid_out[...] = (
         wide(tokens[...])
         + (kept[:, :width] + wide(came[:, :width]))
         + dot(mixed, mix_out[...])
     )
-    resid_out[...] = resid
-    inverse = lax.rsqrt(jnp.mean(resid * resid, axis=1, keepdims=True) + EPSILON)
-    norm_out[...] = low(resid * inverse * wide(gain[...]))
-
-
-def resid_call(kept, came, tokens, mix_out, select, gain):
-    rows, width = tokens.shape
+    normalize_rows(resid_out, wide(gain[...]), norm_out)
+
+
+def resid_call(rank, kept, came, tokens, mix_out, select, gain):
+    rows, width = kept.shape[0], tokens.shape[1]
     out_shape = [((rows, width), jnp.float32), ((rows, width), jnp.bfloat16)]
     out_shape += [((rows, mix_out.shape[0]), jnp.bfloat16)]
-    operands = [kept, came, tokens, mix_out, select, gain]
+    operands = [rank, kept, came, tokens, mix_out, select, gain]
     return kernel_call(
         functools.partial(resid_kernel, width),
         (1,),
-        [whole(array) for array in operands],
+        [whole(kept), whole(came), pl.BlockSpec((rows, width), lambda n, rank: (rank[0], 0))]
+        + [whole(array) for array in operands[4:]],
         [pl.BlockSpec(shape, lambda *_: (0, 0)) for shape, _ in out_shape],
         out_shape,
         operands,
         2 * rows * width * mix_out.shape[0],
+        (),
+        1,
     )
 
 
@@ -484,6 +517,23 @@
     )
 
 
+def write_rows(total, outs, near, span):
+    rows = total.shape[0]
+    if not near:
+        for down in range(span):
+            size = rows // span
+            outs[down][...] = low(total[down * size : (down + 1) * size])
+        return
+    half = rows // (2 * near * span)
+    for down in range(span):
+        for across in range(near):
+            first = 2 * (down * near + across) * half
+            outs[down][across * half : (across + 1) * half] = low(total[first : first + half])
+            outs[span + across][down * half : (down + 1) * half] = low(
+                total[first + half : first + 2 * half]
+            )
+
+
 def expert_kernel(count, near, span, offset, *refs):
     pieces = refs[:count]
     gate_own, up_own, gate_other, up_other, spread, side, back = refs[count : count + 7]
@@ -560,18 +610,17 @@
                 first = (2 * half + index) * part
                 term = dot_t(grad[place], weights[expert, columns, first : first + part])
                 total = term if total is None else total + term
-    half = total_rows // (2 * near * span)
-    for down in range(span):
-        for across in range(near):
-            first = 2 * (down * near + across) * half
-            outs[down][across * half : (across + 1) * half] = low(total[first : first + half])
-            outs[span + across][down * half : (down + 1) * half] = low(
-                total[first + half : first + 2 * half]
-            )
+    write_rows(total, outs, near, span)
 
     @pl.when(step == pl.num_programs(0) - 1)
     def _():
         out_copy.wait()
+
+
+def block_sizes(rows, near, span):
+    if not near:
+        return [rows // span] * span
+    return [rows // (2 * span)] * span + [rows // (2 * near)] * near
 
 
 def expert_call(pieces, gates, ups, spread, side, back, offset, near, span):
@@ -582,17 +631,14 @@
     tile = min(width, 512)
     shape = (2 * experts, rows, part)
     slots = pltpu.VMEM(shape, jnp.bfloat16)
+    sizes = block_sizes(rows, near, span)
     side_block = pl.BlockSpec((rows, side.shape[1]), lambda n: (offset // rows, 0))
     return kernel_call(
         functools.partial(expert_kernel, count, near, span, offset),
         (width // tile,),
         [ANY] * (count + 4) + [whole(spread), side_block, ANY],
-        [pl.BlockSpec((rows // (2 * span), tile), lambda n: (0, n))] * span
-        + [pl.BlockSpec((rows // (2 * near), tile), lambda n: (0, n))] * near
-        + [ANY],
-        [((rows // (2 * span), width), jnp.bfloat16)] * span
-        + [((rows // (2 * near), width), jnp.bfloat16)] * near
-        + [(shape, jnp.bfloat16)],
+        [pl.BlockSpec((size, tile), lambda n: (0, n)) for size in sizes] + [ANY],
+        [((size, width), jnp.bfloat16) for size in sizes] + [(shape, jnp.bfloat16)],
         [*pieces, gates[0], ups[0], gates[1], ups[1], spread, side, back],
         16 * rows * experts * part * width,
         [
@@ -610,11 +656,188 @@
     )
 
 
+def whole_kernel(count, near, span, places, *refs):
+    pieces = refs[:count]
+    gate_own, up_own, gate_other, up_other, spread, down_own, down_other = refs[count : count + 7]
+    refs = refs[count + 7 :]
+    cot_pieces, refs = refs[: len(places)], refs[len(places) :]
+    outs, hidden_out = refs[: near + span], refs[near + span]
+    rows, weights, gate_grad, up_grad, hidden, grads, sems, row_sem, out_sem = refs[
+        near + span + 1 : near + span + 10
+    ]
+    cot_rows, side, downs, cot_sems, side_sems, down_sems = refs[near + span + 10 :]
+    step = pl.program_id(0)
+    size = pieces[0].shape[0]
+    experts, _, part = gate_own.shape
+    total_rows = rows.shape[0]
+    sources = (gate_own, up_own, gate_other, up_other)
+
+    def load(expert):
+        slot = weights.at[expert]
+        return [
+            pltpu.make_async_copy(
+                source.at[expert], slot.at[:, pl.ds(index * part, part)], sems.at[expert]
+            )
+            for index, source in enumerate(sources)
+        ]
+
+    row_copies = [
+        pltpu.make_async_copy(piece, rows.at[pl.ds(index * size, size)], row_sem.at[index])
+        for index, piece in enumerate(pieces)
+    ]
+    pairs = experts // 2
+
+    def load_down(chunk):
+        source = (down_own, down_other)[chunk // pairs]
+        taken = source.at[pl.ds(chunk % pairs * 2 * part, 2 * part)]
+        return pltpu.make_async_copy(taken, downs.at[chunk], down_sems.at[chunk])
+
+    out_copy = pltpu.make_async_copy(hidden, hidden_out, out_sem)
+
+    @pl.when(step == 0)
+    def _():
+        copies = copy_places(cot_pieces, places, cot_rows, side, cot_sems, side_sems)
+        for copy in copies + [load_down(0), load_down(1)] + row_copies:
+            copy.start()
+        for copy in copies:
+            copy.wait()
+
+        def back(chunk, carry):
+            for ahead in range(2 * pairs):
+
+                @pl.when(chunk == ahead)
+                def _():
+                    if ahead + 2 < 2 * pairs:
+                        load_down(ahead + 2).start()
+                    elif ahead + 2 - 2 * pairs < 2:
+                        for copy in load(ahead + 2 - 2 * pairs):
+                            copy.start()
+                    load_down(ahead).wait()
+
+            grad = dot_t(cot_rows[...], downs[chunk])
+            place = chunk // pairs * experts + lax.rem(chunk, pairs) * 2
+            for index in range(2):
+                weight = dot(side[...], spread[lax.rem(chunk, pairs) * 2 + index])
+                grads[place + index] = low(grad[:, index * part : (index + 1) * part] * weight)
+            return carry
+
+        lax.fori_loop(0, 2 * pairs, back, 0)
+        for copy in row_copies:
+            copy.wait()
+
+        def work(expert, carry):
+            for ahead in range(2, experts):
+
+                @pl.when(expert == ahead - 2)
+                def _():
+                    for copy in load(ahead):
+                        copy.start()
+
+            for copy in load(expert):
+                copy.wait()
+            values = dot(rows[...], weights[expert])
+            weight = dot(side[...], spread[expert])
+            for half in range(2):
+                gate_value = values[:, 2 * half * part : (2 * half + 1) * part]
+                up_value = values[:, (2 * half + 1) * part : (2 * half + 2) * part]
+                sigmoid = jax.nn.sigmoid(gate_value)
+                silu = gate_value * sigmoid
+                place = half * experts + expert
+                grad = wide(grads[place])
+                gate_grad[place] = low(grad * up_value * (sigmoid + silu * (1.0 - sigmoid)))
+                up_grad[place] = low(grad * silu)
+                hidden[place] = low(silu * up_value * weight)
+            return carry
+
+        lax.fori_loop(0, experts, work, 0)
+        out_copy.start()
+
+    tile = outs[0].shape[1]
+    columns = pl.ds(pl.multiple_of(step * tile, tile), tile)
+    total = None
+    for expert in range(experts):
+        for half in range(2):
+            place = half * experts + expert
+            for index, grad in enumerate((gate_grad, up_grad)):
+                first = (2 * half + index) * part
+                term = dot_t(grad[place], weights[expert, columns, first : first + part])
+                total = term if total is None else total + term
+    write_rows(total, outs, near, span)
+
+    @pl.when(step == pl.num_programs(0) - 1)
+    def _():
+        out_copy.wait()
+
+
+def copy_places(pieces, places, rows, side, row_sems, side_sems):
+    width, copies = rows.shape[1], []
+    for piece, targets in zip(pieces, places):
+        for source, target, size in targets:
+            taken, place = piece.at[pl.ds(source, size)], pl.ds(target, size)
+            slot = len(copies) // 2
+            copies.append(
+                pltpu.make_async_copy(
+                    taken.at[:, pl.ds(0, width)], rows.at[place], row_sems.at[slot]
+                )
+            )
+            copies.append(
+                pltpu.make_async_copy(
+                    taken.at[:, pl.ds(width, side.shape[1])], side.at[place], side_sems.at[slot]
+                )
+            )
+    return copies
+
+
+def whole_call(pieces, cot_plane, gates, ups, downs, spread, near, span, block_rows):
+    count = len(pieces)
+    experts, width, part = gates[0].shape
+    size = pieces[0].shape[0]
+    rows = size * count
+    tile = min(width, 512)
+    shape = (2 * experts, rows, part)
+    slots = pltpu.VMEM(shape, jnp.bfloat16)
+    places = [
+        [
+            (down * block_rows, (down * near + across) * block_rows, block_rows)
+            for down in range(piece.shape[0] // block_rows)
+        ]
+        for across, piece in enumerate(cot_plane)
+    ]
+    blocks = rows // block_rows
+    sizes = block_sizes(rows, near, span)
+    return kernel_call(
+        functools.partial(whole_kernel, count, near, span, places),
+        (width // tile,),
+        [ANY] * (count + 4) + [whole(spread)] + [ANY] * (2 + len(cot_plane)),
+        [pl.BlockSpec((size, tile), lambda n: (0, n)) for size in sizes] + [ANY],
+        [((size, width), jnp.bfloat16) for size in sizes] + [(shape, jnp.bfloat16)],
+        [*pieces, gates[0], ups[0], gates[1], ups[1], spread, *downs, *cot_plane],
+        20 * rows * experts * part * width,
+        [
+            pltpu.VMEM((rows, width), jnp.bfloat16),
+            pltpu.VMEM((experts, width, 4 * part), jnp.bfloat16),
+            slots,
+            slots,
+            slots,
+            slots,
+            pltpu.SemaphoreType.DMA((experts,)),
+            pltpu.SemaphoreType.DMA((count,)),
+            pltpu.SemaphoreType.DMA,
+            pltpu.VMEM((rows, width), jnp.bfloat16),
+            pltpu.VMEM((rows, spread.shape[1]), jnp.bfloat16),
+            pltpu.VMEM((experts // 2 * 2, 2 * part, width), jnp.bfloat16),
+            pltpu.SemaphoreType.DMA((blocks,)),
+            pltpu.SemaphoreType.DMA((blocks,)),
+            pltpu.SemaphoreType.DMA((experts // 2 * 2,)),
+        ],
+    )
+
+
 def down_kernel(count, span, *refs):
     hiddens, (down_own, down_other), outs = refs[:count], refs[count : count + 2], refs[count + 2 :]
     places, _, part = hiddens[0].shape
-    near = len(outs) // count
-    size = outs[0].shape[0] // span
+    near = len(outs) // (count * span)
+    size = outs[0].shape[0]
     for index, hidden in enumerate(hiddens):
         total = None
         for place in range(places):
@@ -623,7 +846,8 @@
             term = dot(hidden[place], down[first : first + part, :])
             total = term if total is None else total + term
         for across, target, first in plane_order(near, span, size):
-            outs[index * near + across][target : target + size] = low(total[first : first + size])
+            block = (index * near + across) * span + target // size
+            outs[block][...] = low(total[first : first + size])
 
 
 def down_call(hiddens, downs, near, span, size):
@@ -636,12 +860,13 @@
         functools.partial(down_kernel, count, span),
         (width // tile,),
         [whole(array) for array in hiddens] + [down_block] * 2,
-        [pl.BlockSpec((span * size, tile), lambda n: (0, n))] * (count * near),
-        [((span * size, width), jnp.bfloat16)] * (count * near),
+        [pl.BlockSpec((size, tile), lambda n: (0, n))] * (count * near * span),
+        [((size, width), jnp.bfloat16)] * (count * near * span),
         [*hiddens, *downs],
         4 * count * rows * hidden * width,
     )
-    return [outs[index * near : (index + 1) * near] for index in range(count)]
+    blocks = [outs[index * span : (index + 1) * span] for index in range(count * near)]
+    return [blocks[index * near : (index + 1) * near] for index in range(count)]
 
 
 def backward_kernel(width, share, count, scalars, *refs):
@@ -651,7 +876,7 @@
     (query_out, key_out, value_out, inner_out, mix_in_grad, mix_out_grad) = refs[
         count + 15 : count + 21
     ]
-    branch, mixed_grad, grads, inner, sems = refs[count + 21 :]
+    branch, mixed_grad, grads, inner, query_total, key_total, value_total, sems = refs[count + 21 :]
     head = pl.program_id(0)
     heads = grads.shape[0]
     size = pieces[0].shape[0]
@@ -670,12 +895,10 @@
         mixed_grad[...] = low(
             wide(low(dot_t(branch[:, :width], mix_out[...]))) * select[...]
         )
+        together = dot_t(branch[:, :width], output_weight[...])
+        together = low(together + dot_t(mixed_grad[...], mix_in[...]))
         for index in range(heads):
-            part = slice(index * HD, (index + 1) * HD)
-            grads[index] = low(
-                dot_t(branch[:, :width], output_weight[part, :])
-                + dot_t(mixed_grad[...], mix_in[part, :])
-            )
+            grads[index] = together[:, index * HD : (index + 1) * HD]
         columns = pl.ds(pl.multiple_of(scalars[count] * share, share), share)
         whole_grad = t_dot(branch[:, width:], branch[:, columns])
         mix_out_grad[...] = sliced(whole_grad)
@@ -684,15 +907,22 @@
     scale = HD ** (-0.5)
     query, key, value = queries[...], keys[...], values[...]
     grad = grads[head]
-    scores = dot_t(query, key) * scale + mask[...]
-    raised = jnp.exp(scores - jnp.max(scores, axis=1, keepdims=True))
-    weights = raised / jnp.sum(raised, axis=1, keepdims=True)
-    value_out[...] = low(t_dot(low(weights), grad))
-    weight_grad = dot_t(grad, value)
-    center = jnp.sum(weights * weight_grad, axis=1, keepdims=True)
-    score_grad = low(weights * (weight_grad - center))
-    query_grad = dot(score_grad, key) * scale
-    key_grad = t_dot(score_grad, query) * scale
+    key_total[...] = jnp.zeros_like(key_total)
+    value_total[...] = jnp.zeros_like(value_total)
+    for first in range(0, rows, CHUNK):
+        last = first + CHUNK
+        scores = dot_t(query[first:last], key[:last]) * scale + mask[first:last, :last]
+        raised = jnp.exp(scores - jnp.max(scores, axis=1, keepdims=True))
+        weights = raised * (1.0 / jnp.sum(raised, axis=1, keepdims=True))
+        value_total[:last, :] += t_dot(low(weights), grad[first:last])
+        weight_grad = dot_t(grad[first:last], value[:last])
+        center = jnp.sum(weights * weight_grad, axis=1, keepdims=True)
+        score_grad = low(weights * (weight_grad - center))
+        query_total[first:last, :] = dot(score_grad, key[:last]) * scale
+        key_total[:last, :] += t_dot(score_grad, query[first:last])
+    value_out[...] = low(value_total[...])
+    query_grad = query_total[...]
+    key_grad = key_total[...] * scale
     query_grad = (query_grad * cosine[...] - turned(query_grad) * sine[...]) * wide(query_gain[...])
     key_grad = (key_grad * cosine[...] - turned(key_grad) * sine[...]) * wide(key_gain[...])
     query_out[...] = query_grad
@@ -751,31 +981,36 @@
             pltpu.VMEM((rows, mix_out.shape[0]), jnp.bfloat16),
             pltpu.VMEM((heads, rows, HD), jnp.bfloat16),
             pltpu.VMEM((rows, 128), jnp.float32),
+            pltpu.VMEM((rows, HD), jnp.float32),
+            pltpu.VMEM((rows, HD), jnp.float32),
+            pltpu.VMEM((rows, HD), jnp.float32),
             pltpu.SemaphoreType.DMA((len(pieces),)),
         ],
         1,
     )
 
 
+def adapter_lanes(index, select):
+    row = lax.broadcasted_iota(jnp.int32, (128, 128), 0) - index * RANK
+    lane = lax.broadcasted_iota(jnp.int32, (128, 128), 1)
+    return low(jnp.where(lax.rem(lane, RANK) == row, select, 0.0))
+
+
 def raw_kernel(
-    width, scalars, inner, squares, query_grad, key_grad, value_grad, query_raw, key_raw, lowrank,
-    adapt_out, raw, lowrank_out, adapt_grad, maps,
+    width, inner, squares, query_grad, key_grad, value_grad, query_raw, key_raw, lowrank,
+    adapt_out, select, raw, lowrank_out, adapt_grad,
 ):
     inverse = lax.rsqrt(spread_columns(squares[...]) / width + EPSILON)
     totals = spread_columns(inner[...]) / width
     for index, (grad, value) in enumerate(((query_grad, query_raw), (key_grad, key_raw))):
         scale = inverse[:, index : index + 1]
-        raw[index] = low(
-            scale * grad[...]
-            - value[...] * scale**3 * totals[:, index : index + 1]
-        )
+        factor = scale**3 * totals[:, index : index + 1]
+        raw[index] = low(scale * grad[...] - value[...] * factor)
     raw[2] = value_grad[...]
-    picked = pl.ds(pl.multiple_of(scalars[0], RANK), RANK)
-    maps[...] = jnp.zeros_like(maps)
     lowrank_part = None
     for index in range(3):
-        maps[index, index * RANK : (index + 1) * RANK, :] = adapt_out[index, picked, :]
-        term = dot_t(raw[index], maps[index])
+        part = low(dot_t(raw[index], adapt_out[index]) * select[...])
+        term = dot_t(part, adapter_lanes(index, select[...]))
         lowrank_part = term if lowrank_part is None else lowrank_part + term
         adapt_grad[index * RANK : (index + 1) * RANK, :] = sliced(
             t_dot(lowrank[index], raw[index])
@@ -783,21 +1018,19 @@
     lowrank_out[...] = low(lowrank_part)
 
 
-def raw_call(scalars, width, inner, squares, grads, raws, lowrank, adapt_out):
+def raw_call(inner, squares, grads, raws, lowrank, adapt_out, select, width):
     rows, local = raws[0].shape
-    operands = [scalars, inner, squares, *grads, *raws, lowrank, adapt_out]
+    operands = [inner, squares, *grads, *raws, lowrank, adapt_out, select]
     out_shape = [((3, rows, local), jnp.bfloat16), ((rows, 128), jnp.bfloat16)]
     out_shape += [((3 * RANK, local), jnp.bfloat16)]
     return kernel_call(
         functools.partial(raw_kernel, width),
         (1,),
-        [whole(array) for array in operands[1:]],
+        [whole(array) for array in operands],
         [pl.BlockSpec(shape, lambda *_, size=len(shape): (0,) * size) for shape, _ in out_shape],
         out_shape,
         operands,
         6 * rows * local * 256,
-        [pltpu.VMEM((3, 128, local), jnp.bfloat16)],
-        1,
     )
 
 
@@ -843,9 +1076,12 @@
 
 
 def input_kernel(
-    kept, came, lowrank, maps, tokens, gain, resid_grad, out
+    rank, kept, came, lowrank, adapt_in, select, tokens, gain, resid_grad, out
 ):
-    grad = kept[...] + wide(came[...]) + dot_t(lowrank[...], maps[...])
+    grad = kept[...] + wide(came[...])
+    for index in range(3):
+        part = low(dot(lowrank[...], adapter_lanes(index, select[...])))
+        grad = grad + dot_t(part, adapt_in[index])
     scaled = grad * wide(gain[...])
     inputs = wide(tokens[...])
     width = inputs.shape[1]
@@ -856,17 +1092,28 @@
     )
 
 
-def input_call(kept, came, lowrank, maps, tokens, gain, resid_grad):
-    operands = [kept, came, lowrank, maps, tokens, gain, resid_grad]
-    rows, width = tokens.shape
+def input_call(rank, kept, came, lowrank, adapt_in, select, tokens, gain, resid_grad):
+    operands = [rank, kept, came, lowrank, adapt_in, select, tokens, gain, resid_grad]
+    rows, width = kept.shape
     return kernel_call(
         input_kernel,
         (1,),
-        [whole(array) for array in operands],
+        [
+            whole(kept),
+            whole(came),
+            pl.BlockSpec((rows, lowrank.shape[1]), lambda n, rank: (rank[0], 0)),
+            whole(adapt_in),
+            whole(select),
+            pl.BlockSpec((rows, width), lambda n, rank: (rank[0], 0)),
+            whole(gain),
+            whole(resid_grad),
+        ],
         [pl.BlockSpec((rows, width), lambda *_: (0, 0))],
         [((rows, width), jnp.bfloat16)],
         operands,
-        2 * rows * width * 128,
+        8 * rows * width * 128,
+        (),
+        1,
     )[0]
 
 
@@ -1020,6 +1267,7 @@
     row_share = rows_here // tensor_count
     hold = lax.optimization_barrier
     level, core = tensor_rank // 2, tensor_rank % 2
+    rank_list = jnp.reshape(tensor_rank, (1,)).astype(jnp.int32)
 
     def own_rows(array):
         return lax.dynamic_slice_in_dim(array, tensor_rank * row_share, row_share, 0)
@@ -1074,7 +1322,6 @@
     tables = (cosine_table, sine_table * signs)
     mask = jnp.where(token_mask(reached[0], rows_here), 0.0, MASKED_SCORE)
     select = jnp.repeat(wide(adapter_pick), RANK, axis=1)
-    picked = jnp.argmax(adapter_pick[0]).astype(jnp.int32) * RANK
     weights = (query_weight, key_weight, value_weight)
     normed_in, lowrank, *raws, squares = project_call(
         tokens, first_gain, weights, adapt_in, adapt_out, select
@@ -1084,10 +1331,8 @@
         return [rows[: rows.shape[0] // 2], rows[rows.shape[0] // 2 :]]
 
     squares = sum_tensor(squares, axes)
-    tokens_rows = own_rows(tokens)
-    held = (squares, cot_queue[1], cot_planes[0], expert_gate, expert_up, tables, mask, tokens_rows)
-    held = hold(held)
-    squares, cot_queue[1], cot_planes[0], expert_gate, expert_up, tables, mask, tokens_rows = held
+    held = (squares, cot_queue[1], cot_planes[0], expert_gate, expert_up, tables, mask)
+    squares, cot_queue[1], cot_planes[0], expert_gate, expert_up, tables, mask = hold(held)
     gates = (expert_gate, turn(expert_gate, axes, "c", 1))
     ups = (expert_up, turn(expert_up, axes, "c", 1))
     cot_queue[1] = halves(cot_queue[1])
@@ -1116,21 +1361,16 @@
     held = (branch_came, cot_later, cot_second, gates, ups, down_tall)
     branch_came, cot_later, cot_second, gates, ups, down_tall = hold(held)
     downs = (down_tall, turn(down_tall, axes, "c", 1))
-    cot_queue.append(cot_later)
+    cot_queue.append(jnp.concatenate(cot_later, axis=0))
     cot_planes[1] = [cot_queue[1]] + [list(pair) for pair in zip(cot_across, cot_second)]
     cot_planes[0] = [[piece] for piece in cot_planes[0]]
     resid_rows, norm_plane, mixed_rows = resid_call(
-        branch_kept, branch_came, tokens_rows, adapt_out_out, select, second_gain
+        rank_list, branch_kept, branch_came, tokens, adapt_out_out, select, second_gain
     )
 
     norm_queue = [norm_plane, turn(norm_plane, axes, "z", 1)]
     norm_pairs = [ring(norm_plane, axes, "x")]
     backs, sides = [None] * far, [None] * far
-    maps = jnp.swapaxes(lax.dynamic_slice_in_dim(adapt_in, picked, RANK, 2), 0, 1)
-    maps = maps.reshape(model_width, 3 * RANK)
-    maps = jnp.concatenate(
-        [maps, jnp.zeros((model_width, 128 - 3 * RANK), jnp.bfloat16)], axis=1
-    )
 
     def hidden_step(*indices):
         back, side = hidden_call(
@@ -1145,53 +1385,70 @@
             backs[index] = (back, backs[index][1])
 
     norm_planes = [None] * far
-    held = (norm_queue[1], norm_pairs[0], maps, downs)
-    norm_queue[1], norm_pairs[0], maps, downs = hold(held)
+    held = (norm_queue[1], norm_pairs[0], downs, cot_queue[2])
+    norm_queue[1], norm_pairs[0], downs, cot_queue[2] = hold(held)
     norm_planes[0] = ring(jnp.concatenate(norm_pairs[0], axis=0), axes, "y")
     norm_queue.append(turn(norm_queue[1], axes, "z", 1))
     norm_pairs.append(ring(norm_queue[1], axes, "x"))
-    cot_third = [turn(cot_queue[2][0], axes, "z", 1)]
-    cot_across = ring(cot_queue[2][0], axes, "x")[1:]
     back_first = hidden_step(0, 1)
-    held = (norm_planes[0], norm_queue[2], norm_pairs[1], cot_third, cot_across, cot_queue[2])
-    held, back_first = hold((held, back_first))
-    norm_planes[0], norm_queue[2], norm_pairs[1], cot_third, cot_across, cot_queue[2] = held
+    held = (norm_planes[0], norm_queue[2], norm_pairs[1], cot_queue[2], back_first)
+    norm_planes[0], norm_queue[2], norm_pairs[1], cot_queue[2], back_first = hold(held)
     set_back(back_first, 0, 1)
     parts, hiddens = [None] * far, [None] * far
 
     def expert_step(index):
         back, offset = backs[index]
         *parts[index], hiddens[index] = expert_call(
-            norm_planes[index], gates, ups, spread, sides[index], back, offset, near, span
+            norm_planes[index],
+            gates,
+            ups,
+            spread,
+            sides[index],
+            back,
+            offset,
+            near if index else 0,
+            span,
+        )
+
+    def whole_step(index):
+        *parts[index], hiddens[index] = whole_call(
+            norm_planes[index], cot_planes[index], gates, ups, downs, spread, near, span, row_share
         )
 
     norm_planes[1] = ring(jnp.concatenate(norm_pairs[1], axis=0), axes, "y")
     norm_queue.append(turn(norm_queue[2], axes, "z", 1))
     norm_pairs.append(ring(norm_queue[2], axes, "x"))
-    cot_third.append(turn(cot_queue[2][1], axes, "z", 1))
-    cot_second = ring(cot_queue[2][1], axes, "x")[1:]
+    cot_queue.append(turn(cot_queue[2], axes, "z", 1))
+    cot_planes[2] = ring(cot_queue[2], axes, "x")
     expert_step(0)
 
-    held = (norm_planes[1], norm_queue[3], norm_pairs[2], cot_third, cot_second, parts[0])
-    norm_planes[1], norm_queue[3], norm_pairs[2], cot_third, cot_second, parts[0] = hold(held)
-    cot_planes[2] = [cot_queue[2]] + [list(pair) for pair in zip(cot_across, cot_second)]
-    cot_queue.append(cot_third)
+    held = (norm_planes[1], norm_queue[3], norm_pairs[2], parts[0])
+    norm_planes[1], norm_queue[3], norm_pairs[2], parts[0] = hold(held)
     norm_planes[2] = ring(jnp.concatenate(norm_pairs[2], axis=0), axes, "y")
     norm_pairs.append(ring(norm_queue[3], axes, "x"))
-    cot_across = [ring(rows, axes, "x")[1:] for rows in cot_queue[3]]
     expert_step(1)
 
-    norm_planes[2], norm_pairs[3], parts[1] = hold((norm_planes[2], norm_pairs[3], parts[1]))
+    held = (norm_planes[2], norm_pairs[3], parts[1], cot_queue[3], cot_planes[2])
+    norm_planes[2], norm_pairs[3], parts[1], cot_queue[3], cot_planes[2] = hold(held)
     norm_planes[3] = ring(jnp.concatenate(norm_pairs[3], axis=0), axes, "y")
-    came = [None] * far
-    kept = [None] * far
+    came, last = [None] * far, [None] * far
     came[1] = scatter_first(parts[1], axes)
-    back_next = hidden_step(2)
-    cot_across, back_next, norm_planes[2] = hold((cot_across, back_next, norm_planes[2]))
-    set_back(back_next, 2)
-    came[0] = scatter_first(parts[0], axes)
-    cot_planes[3] = [cot_queue[3]] + [list(pair) for pair in zip(*cot_across)]
-    expert_step(2)
+    cot_across = [turn(piece, axes, "z", 1) for piece in cot_planes[2][1:]]
+    whole_step(2)
+
+    held = (norm_planes[3], came[1], parts[2], parts[0], cot_across)
+    norm_planes[3], came[1], parts[2], parts[0], cot_across = hold(held)
+    cot_planes[3] = [cot_queue[3]] + cot_across
+    last[1] = scatter_second(parts[1], came[1], axes)
+    came[2] = scatter_first(parts[2], axes)
+    came_y = send_sum(parts[0], axes, "y")
+    whole_step(3)
+
+    held = (last[1], came[2], came_y, parts[3], hiddens)
+    last[1], came[2], came_y, parts[3], hiddens = hold(held)
+    came[3] = scatter_first(parts[3], axes)
+    last[2] = scatter_second(parts[2], came[2], axes)
+    ring_sum = turn(low(scatter_last(parts[1], came[1], last[1], axes)), axes, "z", 1)
     mixes, mix_came = [None] * far, [None] * far
 
     def down_step(first, second):
@@ -1199,48 +1456,62 @@
             [hiddens[first], hiddens[second]], downs, near, span, row_share
         )
 
-    held = (norm_planes[3], came[1], came[0], parts[2], hiddens[1], hiddens[2])
-    norm_planes[3], came[1], came[0], parts[2], hiddens[1], hiddens[2] = hold(held)
-    kept[1], came[1] = scatter_second(parts[1], came[1], axes)
-    came[2] = scatter_first(parts[2], axes)
+    down_step(3, 0)
+
+    held = (ring_sum, came[3], last[2], mixes[3], mixes[0], hiddens)
+    ring_sum, came[3], last[2], mixes[3], mixes[0], hiddens = hold(held)
+    last[3] = scatter_second(parts[3], came[3], axes)
+    ring_sum = turn(
+        low(wide(ring_sum) + scatter_last(parts[2], came[2], last[2], axes)), axes, "z", 1
+    )
+
+    ring_sum, last[3], parts[0], hiddens = hold((ring_sum, last[3], parts[0], hiddens))
+    ring_sum = turn(
+        low(wide(ring_sum) + scatter_last(parts[3], came[3], last[3], axes)), axes, "z", 1
+    )
+    own_sums = [
+        [block(parts[0][0], k, near), block(came_y, k, near)] for k in range(near)
+    ]
+    came_x = send_sum([None] + [low(pair[0] + pair[1]) for pair in own_sums[1:]], axes, "x")
     down_step(1, 2)
-    held = (kept[1], came[1], came[2], mixes[1], mixes[2], cot_planes[3])
-    kept[1], came[1], came[2], mixes[1], mixes[2], cot_planes[3] = hold(held)
-    kept[2], came[2] = scatter_second(parts[2], came[2], axes)
-    ring_sum = turn(low(scatter_last(kept[1], came[1])), axes, "z", 1)
-    mix_came[1] = send_sum(mixes[1], axes, "x")
-    back_last = hidden_step(3)
-    kept[2], came[2], back_last, norm_planes[3] = hold(
-        (kept[2], came[2], back_last, norm_planes[3])
-    )
-    set_back(back_last, 3)
-    kept[0], came[0] = scatter_second(parts[0], came[0], axes)
-    expert_step(3)
-
-    held = (ring_sum, kept[0], came[0], parts[3], hiddens[3], mix_came[1])
-    ring_sum, kept[0], came[0], parts[3], hiddens[3], mix_came[1] = hold(held)
-    came[3] = scatter_first(parts[3], axes)
-    ring_sum = turn(low(wide(ring_sum) + scatter_last(kept[2], came[2])), axes, "z", 1)
-    down_step(3, 0)
-
-    ring_sum, came[3], mixes[3], mixes[0] = hold((ring_sum, came[3], mixes[3], mixes[0]))
-    kept[3], came[3] = scatter_second(parts[3], came[3], axes)
-
-    ring_sum, kept[3], came[3], mixes = hold((ring_sum, kept[3], came[3], mixes))
-    ring_sum = turn(low(wide(ring_sum) + scatter_last(kept[3], came[3])), axes, "z", 1)
-    mix_came[2] = send_sum(mixes[2], axes, "x")
+
+    half_width = model_width // span
+
+    def column_sum(arrays, owner):
+        first = owner * half_width
+        return sum(
+            wide(lax.dynamic_slice_in_dim(array, first, half_width, 1)) for array in arrays
+        )
+
+    def mix_columns(index, owner):
+        rows = [column_sum(arrays, owner) for arrays in mix_held[index]]
+        return jnp.concatenate(rows, axis=0)
 
     def mix_down(index):
-        total = wide(mixes[index][0]) + wide(mix_came[index])
-        total = jnp.split(total, span, axis=0)
-        return total[0], send_sum([low(part) for part in total], axes, "y")
-
+        came_rows = None
+        for step in range(span - 1, 0, -1):
+            total = mix_columns(index, (level + span - step) % span)
+            if came_rows is not None:
+                total = total + rolled(came_rows)
+            came_rows = turn(low(total), axes, "y", -1)
+        return came_rows
+
+    def rolled(rows):
+        size = rows.shape[0] // span
+        return wide(jnp.concatenate([rows[size:], rows[:size]], axis=0))
+
+    def mix_total(index):
+        return mix_columns(index, level) + rolled(mix_parts[index])
+
+    def mix_send(index, down):
+        return send_sum([blocks[down] for blocks in mixes[index]], axes, "x")
+
+    mix_held = [None] * far
     mix_parts = [None] * far
-    mix_parts[1] = mix_down(1)
-
-    ring_sum, mix_parts[1] = hold((ring_sum, mix_parts[1]))
-    mix_sum = turn(low(mix_parts[1][0] + wide(mix_parts[1][1])), axes, "z", 1)
-    ffn_rows_grad = wide(ring_sum) + scatter_last(kept[0], came[0])
+
+    ring_sum, came_x, mixes = hold((ring_sum, came_x, mixes))
+    mix_early = mix_send(3, 0)
+    ffn_rows_grad = wide(ring_sum) + (own_sums[0][0] + own_sums[0][1]) + wide(came_x)
     second_scaled = ffn_rows_grad * wide(second_gain)
     second_inverse = lax.rsqrt(
         jnp.mean(resid_rows * resid_rows, axis=1, keepdims=True) + EPSILON
@@ -1263,14 +1534,13 @@
         ]
     ).astype(jnp.int32)
 
-    branch_pieces = hold(branch_pieces)
+    branch_pieces, mix_early, mixes = hold((branch_pieces, mix_early, mixes))
     branch_others = [turn(piece, axes, "c", 1) for piece in branch_pieces[1:]]
-    held = (branch_others, branch_other, mix_sum, mix_came[2], mixes)
-    branch_others, branch_other, mix_sum, mix_came[2], mixes = hold(held)
+    branch_others, branch_other, mixes = hold((branch_others, branch_other, mixes))
     branch_pieces = branch_pieces + [branch_other] + branch_others
-    mix_parts[2] = mix_down(2)
-    mix_came[3] = send_sum(mixes[3], axes, "x")
-    rank_list = jnp.reshape(tensor_rank, (1,)).astype(jnp.int32)
+    mix_late = [mix_send(3, down) for down in range(1, span)]
+    mix_next = mix_send(2, 0)
+    mix_far = [[turn(part, axes, "z", -1) for part in blocks] for blocks in mixes[1][1:]]
     query_grad, key_grad, value_grad, inner, mix_in_grad, mix_out_grad = backward_call(
         jnp.concatenate([order, rank_list]),
         branch_pieces,
@@ -1287,74 +1557,88 @@
     )
 
     inner = sum_tensor(hold(inner), axes)
-    held = (inner, mix_sum, mix_parts[2], mix_came[3], mixes)
-    inner, mix_sum, mix_parts[2], mix_came[3], mixes = hold(held)
-    mix_came[0] = send_sum(mixes[0], axes, "x")
-    mix_sum = turn(
-        low(wide(mix_sum) + mix_parts[2][0] + wide(mix_parts[2][1])), axes, "z", 1
-    )
+    held = (inner, mix_late, mix_next, mix_far, mixes)
+    inner, mix_late, mix_next, mix_far, mixes = hold(held)
+    mix_held[3] = list(zip(mixes[3][0], [mix_early] + mix_late))
     mix_parts[3] = mix_down(3)
+    mix_last = [mix_send(2, down) for down in range(1, span)]
+    mix_near = [turn(mixes[1][0][0], axes, "z", -1)]
     raw_grads, lowrank_part, adapt_grad = raw_call(
-        jnp.reshape(picked, (1,)),
-        model_width,
         inner,
         squares,
         (query_grad, key_grad, value_grad),
         raws[:2],
         lowrank,
         adapt_out,
+        select,
+        model_width,
     )
     lowrank_came = turn(lowrank_part, axes, "c", 1)
+    lowrank_part, lowrank_came, raw_grads = hold((lowrank_part, lowrank_came, raw_grads))
+    lowrank_part = low(wide(lowrank_part) + wide(lowrank_came))
+    lowrank_parts = ring(lowrank_part, axes, "y")
     normed_mine, normed_theirs = weight_call(
         jnp.reshape(core, (1,)).astype(jnp.int32), raw_grads, weights, row_share
     )
 
-    lowrank_part, lowrank_came = hold((lowrank_part, lowrank_came))
-    lowrank_part = low(wide(lowrank_part) + wide(lowrank_came))
-    lowrank_parts = ring(lowrank_part, axes, "y")
-
-    held = (normed_mine, normed_theirs, lowrank_parts, mix_sum, mix_parts[3], mix_came[0])
-    normed_mine, normed_theirs, lowrank_parts, mix_sum, mix_parts[3], mix_came[0] = hold(held)
+    held = (normed_mine, normed_theirs, lowrank_parts, mix_parts[3], mix_last, mix_near, mixes)
+    held = hold(held)
+    normed_mine, normed_theirs, lowrank_parts, mix_parts[3], mix_last, mix_near, mixes = held
     normed_theirs = turn(normed_theirs, axes, "c", 1)
     lowrank_grad = low(sum(wide(part) for part in lowrank_parts))
+    mix_held[2] = list(zip(mixes[2][0], [mix_next] + mix_last))
+    mix_parts[2] = mix_down(2)
+    mix_beside = turn(low(mix_total(3)), axes, "z", 1)
     compact = compact_call(
         rank_list, lowrank_grad, normed_in, mix_out_grad, adapt_grad, mix_in_grad, select
     )
-    mix_parts[0] = mix_down(0)
-    normed_theirs, compact = hold((normed_theirs, compact))
-    trees = ring(compact, axes, "x")
+    normed_theirs, compact, mixes = hold((normed_theirs, compact, mixes))
+    mix_near = mix_near + [turn(part, axes, "z", -1) for part in mixes[1][0][1:]]
     normed_kept, normed_sent = scatter_core(normed_mine, normed_theirs, axes)
+    normed_sent, compact = hold((normed_sent, compact))
     normed_came = turn(normed_sent, axes, "y", -1)
-    mix_sum = turn(
-        low(wide(mix_sum) + mix_parts[3][0] + wide(mix_parts[3][1])), axes, "z", 1
-    )
-    trees = jnp.concatenate(hold(trees), axis=0)
+    trees, mix_near, mix_beside = hold((ring(compact, axes, "x"), mix_near, mix_beside))
+    trees = jnp.concatenate(trees, axis=0)
     tree_queue = [trees] + [turn(trees, axes, "z", step) for step in range(1, far)]
-    normed_came, mix_parts[0], mix_sum = hold((normed_came, mix_parts[0], mix_sum))
+    normed_came, mix_parts[2], mix_far, mixes = hold((normed_came, mix_parts[2], mix_far, mixes))
 
     input_rows = input_call(
+        rank_list,
         normed_kept,
         normed_came,
-        own_rows(lowrank_grad),
-        maps,
-        tokens_rows,
+        lowrank_grad,
+        adapt_in,
+        select,
+        tokens,
         first_gain,
         resid_grad_rows,
     )
     input_held = ring(input_rows, axes, "y")
-    layer_rows = low(resid_rows + wide(mix_sum) + mix_parts[0][0] + wide(mix_parts[0][1]))
-
-    input_held, layer_rows, tree_queue = hold((input_held, layer_rows, tree_queue))
-    input_pieces = input_held + [turn(piece, axes, "c", 1) for piece in input_held]
-    layer_out = swap_columns(layer_rows, axes)
+    for across in range(1, near):
+        pairs = zip(mixes[0][across], mix_far[across - 1])
+        mixes[0][across] = [low(wide(mine) + wide(other)) for mine, other in pairs]
+    mix_came[0] = [mix_send(0, down) for down in range(span)]
+    input_held, tree_queue = hold((input_held, tree_queue))
 
     trees = jnp.concatenate(tree_queue, axis=0)
     shared = trees.reshape(owners, -1, column_share)[:, : 4 * RANK]
-    shared = gather_tensor(shared.reshape(-1, column_share), axes)
-    input_grad = spread_call(order, input_pieces)
+    shared = ring(shared.reshape(-1, column_share), axes, "y")
+    mix_across = turn(low(mix_total(2)), axes, "z", -2)
+    input_pieces = input_held + [turn(piece, axes, "c", 1) for piece in input_held]
+    shared, mix_came[0] = hold((shared, mix_came[0]))
+    mix_held[0] = [list(arrays) for arrays in zip(mixes[0][0], mix_came[0], mix_near)]
+    mix_held[0][0].append(resid_rows)
+    mix_parts[0] = mix_down(0)
+    shared = shared + [turn(piece, axes, "c", 1) for piece in shared]
+    shared = hold(shared)
     grad_adapt_in, grad_adapt_out, grad_adapt_in_out, grad_adapt_out_out = assemble_call(
         order, trees, shared[1:], owners
     )
+    held = (mix_parts[0], mix_across, mix_beside, grad_adapt_in)
+    mix_parts[0], mix_across, mix_beside, grad_adapt_in = hold(held)
+    layer_columns = low(mix_total(0) + wide(mix_across) + wide(mix_beside))
+    layer_out = place_columns(layer_columns, axes)
+    input_grad = spread_call(order, input_pieces)
     return (
         layer_out,
         input_grad,

time: 532 us -> 484 us (0.910)
  the two profiles are of different devices: /device:TPU:0 before, /device:TPU:9 now
where the time goes in v6:
time: 484 us; the launch traced here: 477 us
  Pallas kernels  232 us (48%)
  waiting for transfers between devices  102 us (21%)
  starting transfers between devices  95.8 us (20%)
  other arithmetic  30.5 us (6%)
  local copies, waits for them, and re-layouts  13.9 us (3%)
    pallas_call x17, Pallas kernels, kernel_call(): pl.pallas_call(kernel, grid_spec=pltpu.PrefetchScalarGridSpec(num_scalar_...  232 us
    ppermute x79, waiting for transfers between devices, turn(): return lax.ppermute(array, axis, pairs)  102 us
    ppermute x79, starting transfers between devices, turn(): return lax.ppermute(array, axis, pairs)  95.8 us
    convert_element_type x22, other arithmetic, low(): return array.astype(jnp.bfloat16)  15.6 us
  transfers between devices with their start and end apart: 79, of which 24 were waited for; matrix products, arithmetic and copies ran while one was open for 7% of the time, Pallas kernels for 48%

profile of v6, /device:TPU:9, one launch (start us, length us, event | category | flops | bytes accessed | tf_op | source)
XLA Modules:
  0.0 476.9 jit_solution(2448156703807382710)
XLA Ops:
  7.4 13.1 %shard_map.244 = (bf16[512,2048]{1,0:T(8,128)(2,1)}, bf16[3,512,128]{2,1,0:T(8,128)(2,1)}, f32[512,512]{1,0:T(8,128)}, f32[512,512]{1,0:T(8,128)}, f32[512,512]{1,0:T(8,128)}, /*index=5*/f32[8,512]{1,0:T(8,128)}) custom-call(bf16[512,2048]{1,0:T(8,128)(2,1)} %tokens.5, bf16[1,2048]{1,0:T(2,128)(2,1)} %broadcast_in_dim.43.gain, ...), custom_call_target="tpu_custom_call" | custom-call | flops 3221225472 | bytes 10359296 | tf_op jit(solution)/shard_map/pallas_call | solution.py:202
  25.5 1.8 sine_multiply_fusion
  30.0 1.9 collective-permute-start.10
  36.6 10.5 %shard_map.245 = (bf16[512,512]{1,0:T(8,128)(2,1)}, bf16[512,512]{1,0:T(8,128)(2,1)}, bf16[512,512]{1,0:T(8,128)(2,1)}, bf16[512,512]{1,0:T(8,128)(2,1)}, f32[25...) custom-call(s32[1]{0:T(128)} %bitcast.core.scalars, f32[8,512]{1,0:T(8,128)} %add.407.squares, ...), custom_call_target="tpu_custom_call" | custom-call | flops 1610612736 | bytes 6965252 | tf_op jit(solution)/shard_map/pallas_call | solution.py:202
  49.3 2.6 collective-permute-done.6
  51.9 2.7 add_convert_fusion
  57.2 11.3 %collective-permute-done.7.came = bf16[128,2176]{1,0:T(8,128)(2,1)S(1)} collective-permute-done((bf16[128,2176]{1,0:T(8,128)(2,1)S(1)}, bf16[128,2176]{1,0:T(8,128)(2,1)S(1)}, u32[]{:S(2)}, u32[]{:S(2)}) %collective-permute-start.7) | collective-permute-done | bytes 557088 | tf_op jit(solution)/shard_map/ppermute | solution.py:77
  71.7 3.9 shard_map.246
  79.5 11.5 %collective-permute-done.12 = bf16[128,2048]{1,0:T(8,128)(2,1)S(1)} collective-permute-done((bf16[128,2048]{1,0:T(8,128)(2,1)}, bf16[128,2048]{1,0:T(8,128)(2,1)S(1)}, u32[]{:S(2)}, u32[]{:S(2)}) %collective-permute-start.12) | collective-permute-done | bytes 524320 | tf_op jit(solution)/shard_map/ppermute | solution.py:77
  92.3 1.9 collective-permute-start.16
  95.4 16.6 %shard_map.247 = (bf16[8,1024,256]{2,1,0:T(8,128)(2,1)}, bf16[1024,128]{1,0:T(8,128)(2,1)}) custom-call(bf16[256,2176]{1,0:T(8,128)(2,1)} %copy-done.5, bf16[256,2176]{1,0:T(8,128)(2,1)} %copy-done.53, bf16[128,2176]{1,0:T(8,128)(2,1)} %copy-done.10, bf16[128,2176]{1,0:T(8,128)(2,1)} %copy-done.9, bf16[128,2176]{1,0:T(8,128)(2,1)} %copy-done.59, ...), custom_call_target="tpu_custom_call" | custom-call | flops 8589934592 | bytes 13107200 | tf_op jit(solution)/shard_map/pallas_call | solution.py:202
  112.0 3.0 collective-permute-done.15.refs_1_
  117.2 1.8 collective-permute-start.23
  119.9 25.9 %shard_map.248 = (bf16[256,2048]{1,0:T(8,128)(2,1)}, bf16[256,2048]{1,0:T(8,128)(2,1)}, bf16[8,512,256]{2,1,0:T(8,128)(2,1)}) custom-call(bf16[256,2048]{1,0:T(8,128)(2,1)} %copy-done.42, bf16[256,2048]{1,0:T(8,128)(2,1)} %copy-done.57, bf16[4,2048,256]{2,1,0:T(8,128)(2,1)} %refs_2_.3, bf16[4,2048,256]{2,1,0:T(8,128)(2,1)} %refs_3_.3, ...), custom_call_target="tpu_custom_call" | custom-call | flops 17179869184 | bytes 23592960 | tf_op jit(solution)/shard_map/pallas_call | solution.py:202
  148.2 25.7 %shard_map.249 = (bf16[128,2048]{1,0:T(8,128)(2,1)}, bf16[128,2048]{1,0:T(8,128)(2,1)}, bf16[128,2048]{1,0:T(8,128)(2,1)}, bf16[128,2048]{1,0:T(8,128)(2,1)}, bf16[8,512,256]{2,1,0:T(8,128)(2,1)}) custom-call(bf16[256,2048]{1,0:T(8,128)(2,1)} %copy-done.43, bf16[256,2048]{1,0:T(8,128)(2,1)} %collective-permute-done.18.refs_1_, ...), custom_call_target="tpu_custom_call" | custom-call | flops 17179869184 | bytes 23592960 | tf_op jit(solution)/shard_map/pallas_call | solution.py:202
  175.6 2.6 collective-permute-start.28
  179.7 29.7 %shard_map.250 = (bf16[128,2048]{1,0:T(8,128)(2,1)}, bf16[128,2048]{1,0:T(8,128)(2,1)}, bf16[128,2048]{1,0:T(8,128)(2,1)}, bf16[128,2048]{1,0:T(8,128)(2,1)}, bf16[8,512,256]{2,1,0:T(8,128)(2,1)}) custom-call(bf16[256,2048]{1,0:T(8,128)(2,1)} %copy-done.44, bf16[256,2048]{1,0:T(8,128)(2,1)} %copy-done.58, bf16[4,2048,256]{2,1,0:T(8,128)(2,1)} %refs_2_.3, ...), custom_call_target="tpu_custom_call" | custom-call | flops 21474836480 | bytes 29753344 | tf_op jit(solution)/shard_map/pallas_call | solution.py:202
  213.0 29.7 %shard_map.251 = (bf16[128,2048]{1,0:T(8,128)(2,1)}, bf16[128,2048]{1,0:T(8,128)(2,1)}, bf16[128,2048]{1,0:T(8,128)(2,1)}, bf16[128,2048]{1,0:T(8,128)(2,1)}, bf16[8,512,256]{2,1,0:T(8,128)(2,1)}) custom-call(bf16[256,2048]{1,0:T(8,128)(2,1)} %copy-done.45, bf16[256,2048]{1,0:T(8,128)(2,1)} %collective-permute-done.25.refs_1_, ...), custom_call_target="tpu_custom_call" | custom-call | flops 21474836480 | bytes 29753344 | tf_op jit(solution)/shard_map/pallas_call | solution.py:202
  242.8 3.5 collective-permute-done.31
  248.4 2.0 collective-permute-start.34
  252.3 13.1 %shard_map.252 = (bf16[128,2048]{1,0:T(8,128)(2,1)}, bf16[128,2048]{1,0:T(8,128)(2,1)}, bf16[128,2048]{1,0:T(8,128)(2,1)}, bf16[128,2048]{1,0:T(8,128)(2,1)}, bf...) custom-call(bf16[8,512,256]{2,1,0:T(8,128)(2,1)} %get-tuple-element., ...), custom_call_target="tpu_custom_call" | custom-call | flops 8589934592 | bytes 12582912 | tf_op jit(solution)/shard_map/pallas_call | solution.py:202
  270.0 1.8 collective-permute-done.41
  271.8 2.6 collective-permute-done.40
  274.4 1.9 collective-permute-done.39
  280.1 13.2 %shard_map.253 = (bf16[128,2048]{1,0:T(8,128)(2,1)}, bf16[128,2048]{1,0:T(8,128)(2,1)}, bf16[128,2048]{1,0:T(8,128)(2,1)}, bf16[128,2048]{1,0:T(8,128)(2,1)}, bf...) custom-call(bf16[8,512,256]{2,1,0:T(8,128)(2,1)} %get-tuple-element., ...), custom_call_target="tpu_custom_call" | custom-call | flops 8589934592 | bytes 12582912 | tf_op jit(solution)/shard_map/pallas_call | solution.py:202
  293.9 2.6 fusion.23
  297.9 14.3 %collective-permute-start.47 = (bf16[128,2176]{1,0:T(8,128)(2,1)S(1)}, bf16[128,2176]{1,0:T(8,128)(2,1)S(1)}, u32[]{:S(2)}, u32[]{:S(2)}) collective-permute-start(bf16[128,2176]{1,0:T(8,128)(2,1)S(1)} %pad_maximum_fusion.1.refs_0_), channel_id=1, source_target_pairs={{0,1},{1,0},{2,3},{3,2},{4,5},{5,4},{6,7},{7,6},{8,9},{9,8},{10,11... | collective-permute-start | bytes 1671176 | tf_op jit(solution)/shard_map/ppermute | solution.py:77
  312.3 8.4 %collective-permute-start.46 = (bf16[128,2176]{1,0:T(8,128)(2,1)S(1)}, bf16[128,2176]{1,0:T(8,128)(2,1)S(1)}, u32[]{:S(2)}, u32[]{:S(2)}) collective-permute-start(bf16[128,2176]{1,0:T(8,128)(2,1)S(1)} %collective-permute-done.44.refs_1_), channel_id=1, source_target_pairs={{0,1},{1,0},{2,3},{3,2},{4,5},{5,4},{6,7},{7,6},{8,9},{9,8},{10,11... | collective-permute-start | bytes 1671176 | tf_op jit(solution)/shard_map/ppermute | solution.py:77
  323.7 1.8 collective-permute-start.52
  325.5 3.6 collective-permute-start.53
  329.7 18.9 %shard_map.254 = (f32[512,512]{1,0:T(8,128)}, f32[512,512]{1,0:T(8,128)}, bf16[512,512]{1,0:T(8,128)(2,1)}, f32[8,512]{1,0:T(8,128)}, bf16[16,512]{1,0:T(8,128)(2,1)}, /*index=5*/bf16[16,512]{1,0:T(8,128)(2,1)}) custom-call(s32[5]{0:T(128)} %concatenate.83.scalars, bf16[128,2176]{1,0:T(8,128)(2,1)} %copy-done.11, bf16[128,2176]{1,0:T(8,128)(2,1)} %copy-done.61, ...), custom_call_target="tpu_custom_call" | custom-call | flops 2952790016 | bytes 10750484 | tf_op jit(solution)/shard_map/pallas_call | solution.py:202
  352.2 2.3 collective-permute-done.49
  355.2 5.2 %shard_map.255 = (bf16[3,512,512]{2,1,0:T(8,128)(2,1)}, bf16[512,128]{1,0:T(8,128)(2,1)}, bf16[48,512]{1,0:T(8,128)(2,1)}) custom-call(f32[8,512]{1,0:T(8,128)} %add.452.inner, f32[8,512]{1,0:T(8,128)} %add.407.squares, f32[512,512]{1,0:T(8,128)} %get-tuple-element.502.query_grad, f32[512,512]{1,0:T(8,128)} %get-tuple-element.503.key_grad, ...), custom_call_target="tpu_custom_call" | custom-call | flops 402653184 | bytes 5538304 | tf_op jit(solution)/shard_map/pallas_call | solution.py:202
  365.5 9.1 %shard_map.256 = (f32[256,2048]{1,0:T(8,128)}, bf16[256,2048]{1,0:T(8,128)(2,1)}) custom-call(s32[1]{0:T(128)} %bitcast.core.scalars, bf16[3,512,512]{2,1,0:T(8,128)(2,1)} %get-tuple-element.508.raw, bf16[2048,512]{1,0:T(8,128)(2,1)} %query_weight.3, bf16[2048,512]{1,0:T(8,128)(2,1)} %key_weight.3, bf16[2048,512]{1,0:T(8,128)(2,1)} %value_weight.3), custom_call_target="tpu_custom_call" | custom-call | flops 3221225472 | bytes 7864324 | tf_op jit(solution)/shard_map/pallas_call | solution.py:202
  374.5 4.5 collective-permute-done.55
  384.9 3.0 shard_map.257
  391.0 4.7 collective-permute-done.65
  395.6 11.8 %collective-permute-done.64 = bf16[128,2048]{1,0:T(8,128)(2,1)S(1)} collective-permute-done((bf16[128,2048]{1,0:T(8,128)(2,1)}, bf16[128,2048]{1,0:T(8,128)(2,1)S(1)}, u32[]{:S(2)}, u32[]{:S(2)}) %collective-permute-start.64) | collective-permute-done | bytes 524320 | tf_op jit(solution)/shard_map/ppermute | solution.py:77
  407.6 3.2 collective-permute-start.67
  411.6 4.5 shard_map.258.refs_0_
  418.3 13.8 %collective-permute-done.67 = bf16[288,512]{1,0:T(8,128)(2,1)S(1)} collective-permute-done((bf16[288,512]{1,0:T(8,128)(2,1)S(1)}, bf16[288,512]{1,0:T(8,128)(2,1)S(1)}, u32[]{:S(2)}, u32[]{:S(2)}) %collective-permute-start.67) | collective-permute-done | bytes 294944 | tf_op jit(solution)/shard_map/ppermute | solution.py:77
  432.1 4.0 collective-permute-done.68
  440.1 10.2 %collective-permute-done.69.refs_1_ = bf16[512,512]{1,0:T(8,128)(2,1)} collective-permute-done((bf16[512,512]{1,0:T(8,128)(2,1)}, bf16[512,512]{1,0:T(8,128)(2,1)}, u32[]{:S(2)}, u32[]{:S(2)}) %collective-permute-start.69) | collective-permute-done | bytes 524320 | tf_op jit(solution)/shard_map/ppermute | solution.py:77
  450.3 2.0 collective-permute-start.74
  455.7 5.3 %shard_map.259 = (f32[3,2048,128]{2,1,0:T(8,128)}, f32[3,128,512]{2,1,0:T(8,128)}, f32[512,128]{1,0:T(8,128)}, f32[128,2048]{1,0:T(8,128)}) custom-call(s32[4]{0:T(128)} %pad_add_fusion.order, bf16[1152,512]{1,0:T(8,128)(2,1)} %copy-done.1, bf16[512,512]{1,0:T(8,128)(2,1)} %collective-permute-done.69.refs_1_, ...), custom_call_target="tpu_custom_call" | custom-call | flops 268435456 | bytes 2752528 | tf_op jit(solution)/shard_map/pallas_call | solution.py:202
  460.9 2.2 collective-permute-done.73
  463.1 3.9 collective-permute-done.72
  470.8 4.6 shard_map.260
  (378 shorter events, 96.4 us)
Async XLA Ops:
  3.5 25.5 %collective-permute-start.2 = (bf16[256,2176]{1,0:T(8,128)(2,1)S(1)}, bf16[256,2176]{1,0:T(8,128)(2,1)S(1)}, u32[]{:S(2)}, u32[]{:S(2)}) collective-permute-start(bf16[256,2176]{1,0:T(8,128)(2,1)S(1)} %maximum_maximum_fusion.refs_0_), channel_id=1, source_target_pairs={{0,8},{4,12},{8,16},{12,20},{16,24},{20,28},{24,0},{28,4},{1,9},{5... | collective-permute-start | bytes 3342344 | tf_op jit(solution)/shard_map/ppermute | solution.py:77
  4.8 25.1 %collective-permute-start.3 = (bf16[256,2176]{1,0:T(8,128)(2,1)S(1)}, bf16[256,2176]{1,0:T(8,128)(2,1)S(1)}, u32[]{:S(2)}, u32[]{:S(2)}) collective-permute-start(bf16[256,2176]{1,0:T(8,128)(2,1)S(1)} %maximum_maximum_fusion.refs_0_), channel_id=1, source_target_pairs={{0,4},{4,0},{8,12},{12,8},{16,20},{20,16},{24,28},{28,24},{1,5},{5... | collective-permute-start | bytes 3342344 | tf_op jit(solution)/shard_map/ppermute | solution.py:77
  30.0 39.4 %collective-permute-start.10 = (bf16[4,2048,256]{2,1,0:T(8,128)(2,1)}, bf16[4,2048,256]{2,1,0:T(8,128)(2,1)}, u32[]{:S(2)}, u32[]{:S(2)}) collective-permute-start(bf16[4,2048,256]{2,1,0:T(8,128)(2,1)} %refs_2_.3), channel_id=1, source_target_pairs={{0,1},{1,0},{2,3},{3,2},{4,5},{5,4},{6,7},{7,6},{8,9},{9,8},{10,11... | collective-permute-start | bytes 12582920 | tf_op jit(solution)/shard_map/ppermute | solution.py:77
  31.8 37.6 %collective-permute-start.11 = (bf16[4,2048,256]{2,1,0:T(8,128)(2,1)}, bf16[4,2048,256]{2,1,0:T(8,128)(2,1)}, u32[]{:S(2)}, u32[]{:S(2)}) collective-permute-start(bf16[4,2048,256]{2,1,0:T(8,128)(2,1)} %refs_3_.3), channel_id=1, source_target_pairs={{0,1},{1,0},{2,3},{3,2},{4,5},{5,4},{6,7},{7,6},{8,9},{9,8},{10,11... | collective-permute-start | bytes 12582920 | tf_op jit(solution)/shard_map/ppermute | solution.py:77
  69.4 21.6 %collective-permute-start.14 = (bf16[1024,2048]{1,0:T(8,128)(2,1)}, bf16[1024,2048]{1,0:T(8,128)(2,1)}, u32[]{:S(2)}, u32[]{:S(2)}) collective-permute-start(bf16[1024,2048]{1,0:T(8,128)(2,1)} %bitcast.11.refs_6_.refs_7_.refs_2_), channel_id=1, source_target_pairs={{0,1},{1,0},{2,3},{3,2},{4,5},{5,4},{6,7},{7,6},{8,9},{9,8},{10,11... | collective-permute-start | bytes 12582920 | tf_op jit(solution)/shard_map/ppermute | solution.py:77
  75.6 15.4 %collective-permute-start.12 = (bf16[128,2048]{1,0:T(8,128)(2,1)}, bf16[128,2048]{1,0:T(8,128)(2,1)S(1)}, u32[]{:S(2)}, u32[]{:S(2)}) collective-permute-start(bf16[128,2048]{1,0:T(8,128)(2,1)} %get-tuple-element.322), channel_id=1, source_target_pairs={{0,8},{4,12},{8,16},{12,20},{16,24},{20,28},{24,0},{28,4},{1,9},{5... | collective-permute-start | bytes 1572872 | tf_op jit(solution)/shard_map/ppermute | solution.py:77
  91.1 23.8 %collective-permute-start.15 = (bf16[256,2048]{1,0:T(8,128)(2,1)S(1)}, bf16[256,2048]{1,0:T(8,128)(2,1)S(1)}, u32[]{:S(2)}, u32[]{:S(2)}) collective-permute-start(bf16[256,2048]{1,0:T(8,128)(2,1)S(1)} %constant_dynamic-update-slice_fusion.refs_0_), channel_id=1, source_target_pairs={{0,2},{1,3},{2,0},{3,1},{4,6},{5,7},{6,4},{7,5},{8,10},{9,11},{10,... | collective-permute-start | bytes 3145736 | tf_op jit(solution)/shard_map/ppermute | solution.py:77
  92.3 19.7 %collective-permute-start.16 = (bf16[128,2048]{1,0:T(8,128)(2,1)S(1)}, bf16[128,2048]{1,0:T(8,128)(2,1)S(1)}, u32[]{:S(2)}, u32[]{:S(2)}) collective-permute-start(bf16[128,2048]{1,0:T(8,128)(2,1)S(1)} %collective-permute-done.12), channel_id=1, source_target_pairs={{0,8},{4,12},{8,16},{12,20},{16,24},{20,28},{24,0},{28,4},{1,9},{5... | collective-permute-start | bytes 1572872 | tf_op jit(solution)/shard_map/ppermute | solution.py:77
  94.2 17.8 %collective-permute-start.17 = (bf16[128,2048]{1,0:T(8,128)(2,1)S(1)}, bf16[128,2048]{1,0:T(8,128)(2,1)S(1)}, u32[]{:S(2)}, u32[]{:S(2)}) collective-permute-start(bf16[128,2048]{1,0:T(8,128)(2,1)S(1)} %collective-permute-done.12), channel_id=1, source_target_pairs={{0,4},{4,0},{8,12},{12,8},{16,20},{20,16},{24,28},{28,24},{1,5},{5... | collective-permute-start | bytes 1572872 | tf_op jit(solution)/shard_map/ppermute | solution.py:77
  115.0 30.8 %collective-permute-start.19 = (bf16[128,2048]{1,0:T(8,128)(2,1)S(1)}, bf16[128,2048]{1,0:T(8,128)(2,1)S(1)}, u32[]{:S(2)}, u32[]{:S(2)}) collective-permute-start(bf16[128,2048]{1,0:T(8,128)(2,1)S(1)} %collective-permute-done.16), channel_id=1, source_target_pairs={{0,8},{4,12},{8,16},{12,20},{16,24},{20,28},{24,0},{28,4},{1,9},{5... | collective-permute-start | bytes 1572872 | tf_op jit(solution)/shard_map/ppermute | solution.py:77
  116.0 29.8 %collective-permute-start.20 = (bf16[128,2048]{1,0:T(8,128)(2,1)S(1)}, bf16[128,2048]{1,0:T(8,128)(2,1)S(1)}, u32[]{:S(2)}, u32[]{:S(2)}) collective-permute-start(bf16[128,2048]{1,0:T(8,128)(2,1)S(1)} %collective-permute-done.16), channel_id=1, source_target_pairs={{0,4},{4,0},{8,12},{12,8},{16,20},{20,16},{24,28},{28,24},{1,5},{5... | collective-permute-start | bytes 1572872 | tf_op jit(solution)/shard_map/ppermute | solution.py:77
  117.2 56.7 %collective-permute-start.23 = (bf16[256,2176]{1,0:T(8,128)(2,1)S(1)}, bf16[256,2176]{1,0:T(8,128)(2,1)S(1)}, u32[]{:S(2)}, u32[]{:S(2)}) collective-permute-start(bf16[256,2176]{1,0:T(8,128)(2,1)S(1)} %pad_maximum_fusion.refs_9_), channel_id=1, source_target_pairs={{0,8},{4,12},{8,16},{12,20},{16,24},{20,28},{24,0},{28,4},{1,9},{5... | collective-permute-start | bytes 3342344 | tf_op jit(solution)/shard_map/ppermute | solution.py:77
  119.0 54.9 %collective-permute-start.24 = (bf16[256,2176]{1,0:T(8,128)(2,1)S(1)}, bf16[256,2176]{1,0:T(8,128)(2,1)S(1)}, u32[]{:S(2)}, u32[]{:S(2)}) collective-permute-start(bf16[256,2176]{1,0:T(8,128)(2,1)S(1)} %pad_maximum_fusion.refs_9_), channel_id=1, source_target_pairs={{0,4},{4,0},{8,12},{12,8},{16,20},{20,16},{24,28},{28,24},{1,5},{5... | collective-permute-start | bytes 3342344 | tf_op jit(solution)/shard_map/ppermute | solution.py:77
  119.6 26.2 %collective-permute-start.18 = (bf16[256,2048]{1,0:T(8,128)(2,1)S(1)}, bf16[256,2048]{1,0:T(8,128)(2,1)}, u32[]{:S(2)}, u32[]{:S(2)}) collective-permute-start(bf16[256,2048]{1,0:T(8,128)(2,1)S(1)} %constant_dynamic-update-slice_fusion.2.refs_0_), channel_id=1, source_target_pairs={{0,2},{1,3},{2,0},{3,1},{4,6},{5,7},{6,4},{7,5},{8,10},{9,11},{10,... | collective-permute-start | bytes 3145736 | tf_op jit(solution)/shard_map/ppermute | solution.py:77
  145.9 28.1 %collective-permute-start.21 = (bf16[256,2048]{1,0:T(8,128)(2,1)S(1)}, bf16[256,2048]{1,0:T(8,128)(2,1)S(1)}, u32[]{:S(2)}, u32[]{:S(2)}) collective-permute-start(bf16[256,2048]{1,0:T(8,128)(2,1)S(1)} %constant_dynamic-update-slice_fusion.4.refs_0_), channel_id=1, source_target_pairs={{0,2},{1,3},{2,0},{3,1},{4,6},{5,7},{6,4},{7,5},{8,10},{9,11},{10,... | collective-permute-start | bytes 3145736 | tf_op jit(solution)/shard_map/ppermute | solution.py:77
  147.2 26.8 %collective-permute-start.22 = (bf16[128,2048]{1,0:T(8,128)(2,1)S(1)}, bf16[128,2048]{1,0:T(8,128)(2,1)S(1)}, u32[]{:S(2)}, u32[]{:S(2)}) collective-permute-start(bf16[128,2048]{1,0:T(8,128)(2,1)S(1)} %collective-permute-done.19), channel_id=1, source_target_pairs={{0,4},{4,0},{8,12},{12,8},{16,20},{20,16},{24,28},{28,24},{1,5},{5... | collective-permute-start | bytes 1572872 | tf_op jit(solution)/shard_map/ppermute | solution.py:77
  175.1 34.4 %collective-permute-start.25 = (bf16[256,2048]{1,0:T(8,128)(2,1)S(1)}, bf16[256,2048]{1,0:T(8,128)(2,1)}, u32[]{:S(2)}, u32[]{:S(2)}) collective-permute-start(bf16[256,2048]{1,0:T(8,128)(2,1)S(1)} %constant_dynamic-update-slice_fusion.6.refs_0_), channel_id=1, source_target_pairs={{0,2},{1,3},{2,0},{3,1},{4,6},{5,7},{6,4},{7,5},{8,10},{9,11},{10,... | collective-permute-start | bytes 3145736 | tf_op jit(solution)/shard_map/ppermute | solution.py:77
  175.6 33.9 %collective-permute-start.28 = (bf16[256,2176]{1,0:T(8,128)(2,1)S(1)}, bf16[256,2176]{1,0:T(8,128)(2,1)S(1)}, u32[]{:S(2)}, u32[]{:S(2)}) collective-permute-start(bf16[256,2176]{1,0:T(8,128)(2,1)S(1)} %collective-permute-done.24.refs_10_), channel_id=1, source_target_pairs={{0,8},{4,12},{8,16},{12,20},{16,24},{20,28},{24,0},{28,4},{1,9},{5... | collective-permute-start | bytes 3342344 | tf_op jit(solution)/shard_map/ppermute | solution.py:77
  178.2 31.3 %collective-permute-start.26 = (bf16[128,2048]{1,0:T(8,128)(2,1)}, bf16[128,2048]{1,0:T(8,128)(2,1)S(1)}, u32[]{:S(2)}, u32[]{:S(2)}) collective-permute-start(bf16[128,2048]{1,0:T(8,128)(2,1)} %get-tuple-element.360), channel_id=1, source_target_pairs={{0,2},{1,3},{2,0},{3,1},{4,6},{5,7},{6,4},{7,5},{8,10},{9,11},{10,... | collective-permute-start | bytes 1572872 | tf_op jit(solution)/shard_map/ppermute | solution.py:77
  179.2 30.2 %collective-permute-start.27 = (bf16[128,2048]{1,0:T(8,128)(2,1)}, bf16[128,2048]{1,0:T(8,128)(2,1)S(1)}, u32[]{:S(2)}, u32[]{:S(2)}) collective-permute-start(bf16[128,2048]{1,0:T(8,128)(2,1)} %get-tuple-element.361), channel_id=1, source_target_pairs={{0,4},{4,0},{8,12},{12,8},{16,20},{20,16},{24,28},{28,24},{1,5},{5... | collective-permute-start | bytes 1572872 | tf_op jit(solution)/shard_map/ppermute | solution.py:77
  209.6 33.2 %collective-permute-start.30 = (bf16[64,2048]{1,0:T(8,128)(2,1)S(1)}, bf16[64,2048]{1,0:T(8,128)(2,1)S(1)}, u32[]{:S(2)}, u32[]{:S(2)}) collective-permute-start(bf16[64,2048]{1,0:T(8,128)(2,1)S(1)} %add_convert_fusion.17), channel_id=1, source_target_pairs={{0,2},{1,3},{2,0},{3,1},{4,6},{5,7},{6,4},{7,5},{8,10},{9,11},{10,... | collective-permute-start | bytes 786440 | tf_op jit(solution)/shard_map/ppermute | solution.py:77
  209.9 36.4 %collective-permute-start.33 = (bf16[256,2048]{1,0:T(8,128)(2,1)}, bf16[256,2048]{1,0:T(8,128)(2,1)S(1)}, u32[]{:S(2)}, u32[]{:S(2)}) collective-permute-start(bf16[256,2048]{1,0:T(8,128)(2,1)} %get-tuple-element.377), channel_id=1, source_target_pairs={{0,2},{1,3},{2,0},{3,1},{4,6},{5,7},{6,4},{7,5},{8,10},{9,11},{10,... | collective-permute-start | bytes 3145736 | tf_op jit(solution)/shard_map/ppermute | solution.py:77
  211.2 31.5 %collective-permute-start.29 = (bf16[64,2048]{1,0:T(8,128)(2,1)S(1)}, bf16[64,2048]{1,0:T(8,128)(2,1)S(1)}, u32[]{:S(2)}, u32[]{:S(2)}) collective-permute-start(bf16[64,2048]{1,0:T(8,128)(2,1)S(1)} %add_convert_fusion.18), channel_id=1, source_target_pairs={{0,4},{4,0},{8,12},{12,8},{16,20},{20,16},{24,28},{28,24},{1,5},{5... | collective-permute-start | bytes 786440 | tf_op jit(solution)/shard_map/ppermute | solution.py:77
  212.3 34.0 %collective-permute-start.31 = (bf16[128,2048]{1,0:T(8,128)(2,1)}, bf16[128,2048]{1,0:T(8,128)(2,1)S(1)}, u32[]{:S(2)}, u32[]{:S(2)}) collective-permute-start(bf16[128,2048]{1,0:T(8,128)(2,1)} %get-tuple-element.375), channel_id=1, source_target_pairs={{0,2},{1,3},{2,0},{3,1},{4,6},{5,7},{6,4},{7,5},{8,10},{9,11},{10,... | collective-permute-start | bytes 1572872 | tf_op jit(solution)/shard_map/ppermute | solution.py:77
  212.7 33.6 %collective-permute-start.32 = (bf16[128,2048]{1,0:T(8,128)(2,1)}, bf16[128,2048]{1,0:T(8,128)(2,1)S(1)}, u32[]{:S(2)}, u32[]{:S(2)}) collective-permute-start(bf16[128,2048]{1,0:T(8,128)(2,1)} %get-tuple-element.376), channel_id=1, source_target_pairs={{0,4},{4,0},{8,12},{12,8},{16,20},{20,16},{24,28},{28,24},{1,5},{5... | collective-permute-start | bytes 1572872 | tf_op jit(solution)/shard_map/ppermute | solution.py:77
  246.4 19.1 %collective-permute-start.38 = (bf16[64,2048]{1,0:T(8,128)(2,1)S(1)}, bf16[64,2048]{1,0:T(8,128)(2,1)S(1)}, u32[]{:S(2)}, u32[]{:S(2)}) collective-permute-start(bf16[64,2048]{1,0:T(8,128)(2,1)S(1)} %add_convert_fusion.13), channel_id=1, source_target_pairs={{0,2},{1,3},{2,0},{3,1},{4,6},{5,7},{6,4},{7,5},{8,10},{9,11},{10,... | collective-permute-start | bytes 786440 | tf_op jit(solution)/shard_map/ppermute | solution.py:77
  246.9 18.5 %collective-permute-start.37 = (bf16[64,2048]{1,0:T(8,128)(2,1)S(1)}, bf16[64,2048]{1,0:T(8,128)(2,1)S(1)}, u32[]{:S(2)}, u32[]{:S(2)}) collective-permute-start(bf16[64,2048]{1,0:T(8,128)(2,1)S(1)} %add_convert_fusion.14), channel_id=1, source_target_pairs={{0,4},{4,0},{8,12},{12,8},{16,20},{20,16},{24,28},{28,24},{1,5},{5... | collective-permute-start | bytes 786440 | tf_op jit(solution)/shard_map/ppermute | solution.py:77
  248.4 17.1 %collective-permute-start.34 = (bf16[128,2048]{1,0:T(8,128)(2,1)S(1)}, bf16[128,2048]{1,0:T(8,128)(2,1)S(1)}, u32[]{:S(2)}, u32[]{:S(2)}) collective-permute-start(bf16[128,2048]{1,0:T(8,128)(2,1)S(1)} %pad_maximum_fusion.2), channel_id=1, source_target_pairs={{0,8},{4,12},{8,16},{12,20},{16,24},{20,28},{24,0},{28,4},{1,9},{5... | collective-permute-start | bytes 1572872 | tf_op jit(solution)/shard_map/ppermute | solution.py:77
  276.4 16.9 %collective-permute-start.43 = (bf16[128,2048]{1,0:T(8,128)(2,1)S(1)}, bf16[128,2048]{1,0:T(8,128)(2,1)S(1)}, u32[]{:S(2)}, u32[]{:S(2)}) collective-permute-start(bf16[128,2048]{1,0:T(8,128)(2,1)S(1)} %add_convert_fusion.4), channel_id=1, source_target_pairs={{0,4},{4,0},{8,12},{12,8},{16,20},{20,16},{24,28},{28,24},{1,5},{5... | collective-permute-start | bytes 1572872 | tf_op jit(solution)/shard_map/ppermute | solution.py:77
  296.5 15.7 %collective-permute-start.44 = (bf16[128,2176]{1,0:T(8,128)(2,1)S(1)}, bf16[128,2176]{1,0:T(8,128)(2,1)S(1)}, u32[]{:S(2)}, u32[]{:S(2)}) collective-permute-start(bf16[128,2176]{1,0:T(8,128)(2,1)S(1)} %pad_maximum_fusion.1.refs_0_), channel_id=1, source_target_pairs={{0,2},{1,3},{2,0},{3,1},{4,6},{5,7},{6,4},{7,5},{8,10},{9,11},{10,... | collective-permute-start | bytes 1671176 | tf_op jit(solution)/shard_map/ppermute | solution.py:77
  297.9 22.7 %collective-permute-start.47 = (bf16[128,2176]{1,0:T(8,128)(2,1)S(1)}, bf16[128,2176]{1,0:T(8,128)(2,1)S(1)}, u32[]{:S(2)}, u32[]{:S(2)}) collective-permute-start(bf16[128,2176]{1,0:T(8,128)(2,1)S(1)} %pad_maximum_fusion.1.refs_0_), channel_id=1, source_target_pairs={{0,1},{1,0},{2,3},{3,2},{4,5},{5,4},{6,7},{7,6},{8,9},{9,8},{10,11... | collective-permute-start | bytes 1671176 | tf_op jit(solution)/shard_map/ppermute | solution.py:77
  322.2 32.9 %collective-permute-start.50 = (bf16[128,2048]{1,0:T(8,128)(2,1)}, bf16[128,2048]{1,0:T(8,128)(2,1)}, u32[]{:S(2)}, u32[]{:S(2)}) collective-permute-start(bf16[128,2048]{1,0:T(8,128)(2,1)} %get-tuple-element.486), channel_id=1, source_target_pairs={{0,4},{4,0},{8,12},{12,8},{16,20},{20,16},{24,28},{28,24},{1,5},{5... | collective-permute-start | bytes 1572872 | tf_op jit(solution)/shard_map/ppermute | solution.py:77
  322.8 32.3 %collective-permute-start.51 = (bf16[128,2048]{1,0:T(8,128)(2,1)}, bf16[128,2048]{1,0:T(8,128)(2,1)S(1)}, u32[]{:S(2)}, u32[]{:S(2)}) collective-permute-start(bf16[128,2048]{1,0:T(8,128)(2,1)} %get-tuple-element.487), channel_id=1, source_target_pairs={{0,4},{4,0},{8,12},{12,8},{16,20},{20,16},{24,28},{28,24},{1,5},{5... | collective-permute-start | bytes 1572872 | tf_op jit(solution)/shard_map/ppermute | solution.py:77
  323.7 31.4 %collective-permute-start.52 = (bf16[128,2048]{1,0:T(8,128)(2,1)}, bf16[128,2048]{1,0:T(8,128)(2,1)S(1)}, u32[]{:S(2)}, u32[]{:S(2)}) collective-permute-start(bf16[128,2048]{1,0:T(8,128)(2,1)} %get-tuple-element.488), channel_id=1, source_target_pairs={{0,24},{4,28},{8,0},{12,4},{16,8},{20,12},{24,16},{28,20},{1,25},{... | collective-permute-start | bytes 1572872 | tf_op jit(solution)/shard_map/ppermute | solution.py:77
  325.5 29.6 %collective-permute-start.53 = (bf16[128,2048]{1,0:T(8,128)(2,1)}, bf16[128,2048]{1,0:T(8,128)(2,1)S(1)}, u32[]{:S(2)}, u32[]{:S(2)}) collective-permute-start(bf16[128,2048]{1,0:T(8,128)(2,1)} %get-tuple-element.489), channel_id=1, source_target_pairs={{0,24},{4,28},{8,0},{12,4},{16,8},{20,12},{24,16},{28,20},{1,25},{... | collective-permute-start | bytes 1572872 | tf_op jit(solution)/shard_map/ppermute | solution.py:77
  363.5 15.6 %collective-permute-start.56 = (bf16[256,1024]{1,0:T(8,128)(2,1)S(1)}, bf16[256,1024]{1,0:T(8,128)(2,1)S(1)}, u32[]{:S(2)}, u32[]{:S(2)}) collective-permute-start(bf16[256,1024]{1,0:T(8,128)(2,1)S(1)} %pad_maximum_fusion.3), channel_id=1, source_target_pairs={{0,2},{1,3},{2,0},{3,1},{4,6},{5,7},{6,4},{7,5},{8,10},{9,11},{10,... | collective-permute-start | bytes 1572872 | tf_op jit(solution)/shard_map/ppermute | solution.py:77
  363.9 15.2 %collective-permute-start.57 = (bf16[128,2048]{1,0:T(8,128)(2,1)S(1)}, bf16[128,2048]{1,0:T(8,128)(2,1)S(1)}, u32[]{:S(2)}, u32[]{:S(2)}) collective-permute-start(bf16[128,2048]{1,0:T(8,128)(2,1)S(1)} %copy-done.65), channel_id=1, source_target_pairs={{0,4},{4,0},{8,12},{12,8},{16,20},{20,16},{24,28},{28,24},{1,5},{5... | collective-permute-start | bytes 1572872 | tf_op jit(solution)/shard_map/ppermute | solution.py:77
  363.9 15.2 %collective-permute-start.58 = (bf16[128,2048]{1,0:T(8,128)(2,1)S(1)}, bf16[128,2048]{1,0:T(8,128)(2,1)S(1)}, u32[]{:S(2)}, u32[]{:S(2)}) collective-permute-start(bf16[128,2048]{1,0:T(8,128)(2,1)S(1)} %copy-done.64), channel_id=1, source_target_pairs={{0,24},{4,28},{8,0},{12,4},{16,8},{20,12},{24,16},{28,20},{1,25},{... | collective-permute-start | bytes 1572872 | tf_op jit(solution)/shard_map/ppermute | solution.py:77
  383.9 26.9 %collective-permute-start.61 = (bf16[256,1024]{1,0:T(8,128)(2,1)}, bf16[256,1024]{1,0:T(8,128)(2,1)}, u32[]{:S(2)}, u32[]{:S(2)}) collective-permute-start(bf16[256,1024]{1,0:T(8,128)(2,1)} %pad_maximum_fusion.4), channel_id=1, source_target_pairs={{0,2},{1,3},{2,0},{3,1},{4,6},{5,7},{6,4},{7,5},{8,10},{9,11},{10,... | collective-permute-start | bytes 1572872 | tf_op jit(solution)/shard_map/ppermute | solution.py:77
  388.0 19.5 %collective-permute-start.64 = (bf16[128,2048]{1,0:T(8,128)(2,1)}, bf16[128,2048]{1,0:T(8,128)(2,1)S(1)}, u32[]{:S(2)}, u32[]{:S(2)}) collective-permute-start(bf16[128,2048]{1,0:T(8,128)(2,1)} %get-tuple-element.552), channel_id=1, source_target_pairs={{0,24},{4,28},{8,0},{12,4},{16,8},{20,12},{24,16},{28,20},{1,25},{... | collective-permute-start | bytes 1572872 | tf_op jit(solution)/shard_map/ppermute | solution.py:77
  389.8 21.0 %collective-permute-start.60 = (bf16[128,2048]{1,0:T(8,128)(2,1)S(1)}, bf16[128,2048]{1,0:T(8,128)(2,1)S(1)}, u32[]{:S(2)}, u32[]{:S(2)}) collective-permute-start(bf16[128,2048]{1,0:T(8,128)(2,1)S(1)} %get-tuple-element.543), channel_id=1, source_target_pairs={{0,2},{1,3},{2,0},{3,1},{4,6},{5,7},{6,4},{7,5},{8,10},{9,11},{10,... | collective-permute-start | bytes 1572872 | tf_op jit(solution)/shard_map/ppermute | solution.py:77
  407.6 24.5 %collective-permute-start.67 = (bf16[288,512]{1,0:T(8,128)(2,1)S(1)}, bf16[288,512]{1,0:T(8,128)(2,1)S(1)}, u32[]{:S(2)}, u32[]{:S(2)}) collective-permute-start(bf16[288,512]{1,0:T(8,128)(2,1)S(1)} %constant_dynamic-update-slice_fusion.8), channel_id=1, source_target_pairs={{0,16},{4,20},{8,24},{12,28},{16,0},{20,4},{24,8},{28,12},{1,17},{... | collective-permute-start | bytes 884744 | tf_op jit(solution)/shard_map/ppermute | solution.py:77
  410.8 25.3 %collective-permute-start.68 = (bf16[288,512]{1,0:T(8,128)(2,1)S(1)}, bf16[288,512]{1,0:T(8,128)(2,1)S(1)}, u32[]{:S(2)}, u32[]{:S(2)}) collective-permute-start(bf16[288,512]{1,0:T(8,128)(2,1)S(1)} %constant_dynamic-update-slice_fusion.8), channel_id=1, source_target_pairs={{0,24},{4,28},{8,0},{12,4},{16,8},{20,12},{24,16},{28,20},{1,25},{... | collective-permute-start | bytes 884744 | tf_op jit(solution)/shard_map/ppermute | solution.py:77
  416.1 20.0 %collective-permute-start.62 = (bf16[128,2048]{1,0:T(8,128)(2,1)}, bf16[128,2048]{1,0:T(8,128)(2,1)S(1)}, u32[]{:S(2)}, u32[]{:S(2)}) collective-permute-start(bf16[128,2048]{1,0:T(8,128)(2,1)} %shard_map.258.refs_0_), channel_id=1, source_target_pairs={{0,2},{1,3},{2,0},{3,1},{4,6},{5,7},{6,4},{7,5},{8,10},{9,11},{10,... | collective-permute-start | bytes 1572872 | tf_op jit(solution)/shard_map/ppermute | solution.py:77
  416.5 23.5 %collective-permute-start.71 = (bf16[128,2048]{1,0:T(8,128)(2,1)S(1)}, bf16[128,2048]{1,0:T(8,128)(2,1)S(1)}, u32[]{:S(2)}, u32[]{:S(2)}) collective-permute-start(bf16[128,2048]{1,0:T(8,128)(2,1)S(1)} %add_convert_fusion.1), channel_id=1, source_target_pairs={{0,4},{4,0},{8,12},{12,8},{16,20},{20,16},{24,28},{28,24},{1,5},{5... | collective-permute-start | bytes 1572872 | tf_op jit(solution)/shard_map/ppermute | solution.py:77
  417.2 22.8 %collective-permute-start.70 = (bf16[128,2048]{1,0:T(8,128)(2,1)S(1)}, bf16[128,2048]{1,0:T(8,128)(2,1)S(1)}, u32[]{:S(2)}, u32[]{:S(2)}) collective-permute-start(bf16[128,2048]{1,0:T(8,128)(2,1)S(1)} %add_convert_fusion.2), channel_id=1, source_target_pairs={{0,4},{4,0},{8,12},{12,8},{16,20},{20,16},{24,28},{28,24},{1,5},{5... | collective-permute-start | bytes 1572872 | tf_op jit(solution)/shard_map/ppermute | solution.py:77
  440.1 23.0 %collective-permute-start.73 = (bf16[256,1024]{1,0:T(8,128)(2,1)}, bf16[256,1024]{1,0:T(8,128)(2,1)}, u32[]{:S(2)}, u32[]{:S(2)}) collective-permute-start(bf16[256,1024]{1,0:T(8,128)(2,1)} %fusion.6), channel_id=1, source_target_pairs={{0,16},{4,20},{8,24},{12,28},{16,0},{20,4},{24,8},{28,12},{1,17},{... | collective-permute-start | bytes 1572872 | tf_op jit(solution)/shard_map/ppermute | solution.py:77
  454.8 15.2 %collective-permute-start.77 = (bf16[128,2048]{1,0:T(8,128)(2,1)S(1)}, bf16[128,2048]{1,0:T(8,128)(2,1)S(1)}, u32[]{:S(2)}, u32[]{:S(2)}) collective-permute-start(bf16[128,2048]{1,0:T(8,128)(2,1)S(1)} %copy-done.3), channel_id=1, source_target_pairs={{0,1},{1,0},{2,3},{3,2},{4,5},{5,4},{6,7},{7,6},{8,9},{9,8},{10,11... | collective-permute-start | bytes 1572872 | tf_op jit(solution)/shard_map/ppermute | solution.py:77
  (102 other events, 1011.5 us)

commit v7 on v6

--- a/solution.py
+++ b/solution.py
@@ -517,12 +517,14 @@
     )
 
 
-def write_rows(total, outs, near, span):
+def write_rows(total, outs, near, span, levels):
     rows = total.shape[0]
-    if not near:
-        for down in range(span):
-            size = rows // span
-            outs[down][...] = low(total[down * size : (down + 1) * size])
+    if not span:
+        block = rows // (near * levels)
+        for across in range(near):
+            for down in range(levels):
+                first = (down * near + across) * block
+                outs[across][down * block : (down + 1) * block] = low(total[first : first + block])
         return
     half = rows // (2 * near * span)
     for down in range(span):
@@ -534,7 +536,7 @@
             )
 
 
-def expert_kernel(count, near, span, offset, *refs):
+def expert_kernel(count, near, span, levels, offset, *refs):
     pieces = refs[:count]
     gate_own, up_own, gate_other, up_other, spread, side, back = refs[count : count + 7]
     outs, hidden_out = refs[count + 7 : count + 7 + near + span], refs[count + 7 + near + span]
@@ -610,7 +612,7 @@
                 first = (2 * half + index) * part
                 term = dot_t(grad[place], weights[expert, columns, first : first + part])
                 total = term if total is None else total + term
-    write_rows(total, outs, near, span)
+    write_rows(total, outs, near, span, levels)
 
     @pl.when(step == pl.num_programs(0) - 1)
     def _():
@@ -618,12 +620,12 @@
 
 
 def block_sizes(rows, near, span):
-    if not near:
-        return [rows // span] * span
+    if not span:
+        return [rows // near] * near
     return [rows // (2 * span)] * span + [rows // (2 * near)] * near
 
 
-def expert_call(pieces, gates, ups, spread, side, back, offset, near, span):
+def expert_call(pieces, gates, ups, spread, side, back, offset, near, span, levels):
     count = len(pieces)
     experts, width, part = gates[0].shape
     size = pieces[0].shape[0]
@@ -634,7 +636,7 @@
     sizes = block_sizes(rows, near, span)
     side_block = pl.BlockSpec((rows, side.shape[1]), lambda n: (offset // rows, 0))
     return kernel_call(
-        functools.partial(expert_kernel, count, near, span, offset),
+        functools.partial(expert_kernel, count, near, span, levels, offset),
         (width // tile,),
         [ANY] * (count + 4) + [whole(spread), side_block, ANY],
         [pl.BlockSpec((size, tile), lambda n: (0, n)) for size in sizes] + [ANY],
@@ -656,7 +658,7 @@
     )
 
 
-def whole_kernel(count, near, span, places, *refs):
+def whole_kernel(count, near, span, levels, places, *refs):
     pieces = refs[:count]
     gate_own, up_own, gate_other, up_other, spread, down_own, down_other = refs[count : count + 7]
     refs = refs[count + 7 :]
@@ -762,7 +764,7 @@
                 first = (2 * half + index) * part
                 term = dot_t(grad[place], weights[expert, columns, first : first + part])
                 total = term if total is None else total + term
-    write_rows(total, outs, near, span)
+    write_rows(total, outs, near, span, levels)
 
     @pl.when(step == pl.num_programs(0) - 1)
     def _():
@@ -796,22 +798,25 @@
     tile = min(width, 512)
     shape = (2 * experts, rows, part)
     slots = pltpu.VMEM(shape, jnp.bfloat16)
-    places = [
-        [
-            (down * block_rows, (down * near + across) * block_rows, block_rows)
-            for down in range(piece.shape[0] // block_rows)
-        ]
-        for across, piece in enumerate(cot_plane)
-    ]
+    cot_pieces, places = [], []
+    for across, column in enumerate(cot_plane):
+        down = 0
+        for piece in column:
+            targets = []
+            for source in range(0, piece.shape[0], block_rows):
+                targets.append((source, (down * near + across) * block_rows, block_rows))
+                down += 1
+            cot_pieces.append(piece)
+            places.append(targets)
     blocks = rows // block_rows
     sizes = block_sizes(rows, near, span)
     return kernel_call(
-        functools.partial(whole_kernel, count, near, span, places),
+        functools.partial(whole_kernel, count, near, span, span, places),
         (width // tile,),
-        [ANY] * (count + 4) + [whole(spread)] + [ANY] * (2 + len(cot_plane)),
+        [ANY] * (count + 4) + [whole(spread)] + [ANY] * (2 + len(cot_pieces)),
         [pl.BlockSpec((size, tile), lambda n: (0, n)) for size in sizes] + [ANY],
         [((size, width), jnp.bfloat16) for size in sizes] + [(shape, jnp.bfloat16)],
-        [*pieces, gates[0], ups[0], gates[1], ups[1], spread, *downs, *cot_plane],
+        [*pieces, gates[0], ups[0], gates[1], ups[1], spread, *downs, *cot_pieces],
         20 * rows * experts * part * width,
         [
             pltpu.VMEM((rows, width), jnp.bfloat16),
@@ -865,7 +870,7 @@
         [*hiddens, *downs],
         4 * count * rows * hidden * width,
     )
-    blocks = [outs[index * span : (index + 1) * span] for index in range(count * near)]
+    blocks = [list(outs[index * span : (index + 1) * span]) for index in range(count * near)]
     return [blocks[index * near : (index + 1) * near] for index in range(count)]
 
 
@@ -876,66 +881,51 @@
     (query_out, key_out, value_out, inner_out, mix_in_grad, mix_out_grad) = refs[
         count + 15 : count + 21
     ]
-    branch, mixed_grad, grads, inner, query_total, key_total, value_total, sems = refs[count + 21 :]
-    head = pl.program_id(0)
-    heads = grads.shape[0]
+    branch, mixed_grad, grads, sems = refs[count + 21 :]
     size = pieces[0].shape[0]
-    rows = branch.shape[0]
-
-    @pl.when(head == 0)
-    def _():
-        copies = []
-        for index, piece in enumerate(pieces):
-            place = pl.ds(pl.multiple_of(scalars[index] * size, size), size)
-            copies.append(pltpu.make_async_copy(piece, branch.at[place], sems.at[index]))
-        for copy in copies:
-            copy.start()
-        for copy in copies:
-            copy.wait()
-        mixed_grad[...] = low(
-            wide(low(dot_t(branch[:, :width], mix_out[...]))) * select[...]
-        )
-        together = dot_t(branch[:, :width], output_weight[...])
-        together = low(together + dot_t(mixed_grad[...], mix_in[...]))
-        for index in range(heads):
-            grads[index] = together[:, index * HD : (index + 1) * HD]
-        columns = pl.ds(pl.multiple_of(scalars[count] * share, share), share)
-        whole_grad = t_dot(branch[:, width:], branch[:, columns])
-        mix_out_grad[...] = sliced(whole_grad)
-        inner[...] = jnp.zeros_like(inner)
-
+    rows, local = grads.shape
+    heads = local // HD
+    copies = []
+    for index, piece in enumerate(pieces):
+        place = pl.ds(pl.multiple_of(scalars[index] * size, size), size)
+        copies.append(pltpu.make_async_copy(piece, branch.at[place], sems.at[index]))
+    for copy in copies:
+        copy.start()
+    for copy in copies:
+        copy.wait()
+    mixed_grad[...] = low(wide(low(dot_t(branch[:, :width], mix_out[...]))) * select[...])
+    grads[...] = low(
+        dot_t(branch[:, :width], output_weight[...]) + dot_t(mixed_grad[...], mix_in[...])
+    )
+    columns = pl.ds(pl.multiple_of(scalars[count] * share, share), share)
+    mix_out_grad[...] = sliced(t_dot(branch[:, width:], branch[:, columns]))
     scale = HD ** (-0.5)
-    query, key, value = queries[...], keys[...], values[...]
-    grad = grads[head]
-    key_total[...] = jnp.zeros_like(key_total)
-    value_total[...] = jnp.zeros_like(value_total)
-    for first in range(0, rows, CHUNK):
-        last = first + CHUNK
-        scores = dot_t(query[first:last], key[:last]) * scale + mask[first:last, :last]
+    lane = lax.broadcasted_iota(jnp.int32, (rows, 128), 1)
+    sums = jnp.zeros((rows, 128), jnp.float32)
+    for head in range(heads):
+        part = slice(head * HD, (head + 1) * HD)
+        query, key, value = queries[:, part], keys[:, part], values[:, part]
+        grad = grads[:, part]
+        scores = dot_t(query, key) * scale + mask[...]
         raised = jnp.exp(scores - jnp.max(scores, axis=1, keepdims=True))
         weights = raised * (1.0 / jnp.sum(raised, axis=1, keepdims=True))
-        value_total[:last, :] += t_dot(low(weights), grad[first:last])
-        weight_grad = dot_t(grad[first:last], value[:last])
+        weight_grad = dot_t(grad, value)
         center = jnp.sum(weights * weight_grad, axis=1, keepdims=True)
         score_grad = low(weights * (weight_grad - center))
-        query_total[first:last, :] = dot(score_grad, key[:last]) * scale
-        key_total[:last, :] += t_dot(score_grad, query[first:last])
-    value_out[...] = low(value_total[...])
-    query_grad = query_total[...]
-    key_grad = key_total[...] * scale
-    query_grad = (query_grad * cosine[...] - turned(query_grad) * sine[...]) * wide(query_gain[...])
-    key_grad = (key_grad * cosine[...] - turned(key_grad) * sine[...]) * wide(key_gain[...])
-    query_out[...] = query_grad
-    key_out[...] = key_grad
-    query_inner = jnp.sum(query_grad * query_raw[...], axis=1, keepdims=True)
-    key_inner = jnp.sum(key_grad * key_raw[...], axis=1, keepdims=True)
-    lane = lax.broadcasted_iota(jnp.int32, (rows, 128), 1)
-    inner[...] += jnp.where(lane == 0, query_inner, jnp.where(lane == 1, key_inner, 0.0))
+        value_out[:, part] = low(t_dot(low(weights), grad))
+        query_grad = dot(score_grad, key) * scale
+        key_grad = t_dot(score_grad, query) * scale
+        query_grad = query_grad * cosine[...] - turned(query_grad) * sine[...]
+        key_grad = key_grad * cosine[...] - turned(key_grad) * sine[...]
+        query_grad = query_grad * wide(query_gain[:, part])
+        key_grad = key_grad * wide(key_gain[:, part])
+        query_out[:, part] = query_grad
+        key_out[:, part] = key_grad
+        query_inner = jnp.sum(query_grad * query_raw[:, part], axis=1, keepdims=True)
+        key_inner = jnp.sum(key_grad * key_raw[:, part], axis=1, keepdims=True)
+        sums = sums + jnp.where(lane == 0, query_inner, jnp.where(lane == 1, key_inner, 0.0))
     mix_in_grad[...] = sliced(t_dot(mixed_grad[...], attended[...]))
-
-    @pl.when(head == heads - 1)
-    def _():
-        inner_out[...] = jnp.transpose(inner[...])[:8]
+    inner_out[...] = jnp.transpose(sums)[:8]
 
 
 def sliced(values):
@@ -949,41 +939,25 @@
     scalars, pieces, output_weight, mix_in, mix_out, select, states, raws, gains, tables, mask, share
 ):
     rows, local = raws[0].shape
-    heads = local // HD
     width = output_weight.shape[1]
-    block = pl.BlockSpec((rows, HD), lambda head, *_: (0, head))
-    gain_block = pl.BlockSpec((1, HD), lambda head, *_: (0, head))
-    adapter_block = pl.BlockSpec((RANK, HD), lambda head, *_: (0, head))
     operands = [
         scalars, *pieces, output_weight, mix_in, mix_out, select, *states, *raws, *gains, *tables, mask,
     ]
-    wide_out = ((rows, local), jnp.float32)
+    out_shape = [((rows, local), jnp.float32)] * 2 + [((rows, local), jnp.bfloat16)]
+    out_shape += [((8, rows), jnp.float32), ((RANK, local), jnp.bfloat16)]
+    out_shape += [((RANK, share), jnp.bfloat16)]
     return kernel_call(
         functools.partial(backward_kernel, width, share, len(pieces)),
-        (heads,),
-        [ANY] * len(pieces)
-        + [whole(output_weight), whole(mix_in), whole(mix_out), whole(select)]
-        + [block] * 6
-        + [gain_block] * 2
-        + [whole(tables[0]), whole(tables[1]), whole(mask)],
-        [block] * 3
-        + [
-            pl.BlockSpec((8, rows), lambda *_: (0, 0)),
-            adapter_block,
-            pl.BlockSpec((RANK, share), lambda *_: (0, 0)),
-        ],
-        [wide_out, wide_out, ((rows, local), jnp.bfloat16), ((8, rows), jnp.float32)]
-        + [((RANK, local), jnp.bfloat16), ((RANK, share), jnp.bfloat16)],
+        (1,),
+        [ANY] * len(pieces) + [whole(array) for array in operands[len(pieces) + 1 :]],
+        [pl.BlockSpec(shape, lambda *_: (0, 0)) for shape, _ in out_shape],
+        out_shape,
         operands,
         14 * rows * rows * local + 2 * rows * local * width,
         [
             pltpu.VMEM((rows, pieces[0].shape[1]), jnp.bfloat16),
             pltpu.VMEM((rows, mix_out.shape[0]), jnp.bfloat16),
-            pltpu.VMEM((heads, rows, HD), jnp.bfloat16),
-            pltpu.VMEM((rows, 128), jnp.float32),
-            pltpu.VMEM((rows, HD), jnp.float32),
-            pltpu.VMEM((rows, HD), jnp.float32),
-            pltpu.VMEM((rows, HD), jnp.float32),
+            pltpu.VMEM((rows, local), jnp.bfloat16),
             pltpu.SemaphoreType.DMA((len(pieces),)),
         ],
         1,
@@ -1034,25 +1008,16 @@
     )
 
 
-def weight_kernel(
-    size, scalars, raw, query_weight, key_weight, value_weight, mine, theirs, weights, sems
-):
-    copies = []
-    for index, source in enumerate((query_weight, key_weight, value_weight)):
-        copies.append(pltpu.make_async_copy(source, weights.at[index], sems.at[index]))
-    for copy in copies:
-        copy.start()
-    for copy in copies:
-        copy.wait()
+def weight_kernel(size, scalars, raw, query_weight, key_weight, value_weight, mine, theirs):
     levels = mine.shape[0] // size
     for out, offset in ((theirs, 1 - scalars[0]), (mine, scalars[0])):
         total = None
-        for index in range(3):
+        for index, weight in enumerate((query_weight, key_weight, value_weight)):
             taken = [
                 raw[index, pl.ds(pl.multiple_of((2 * level + offset) * size, size), size), :]
                 for level in range(levels)
             ]
-            term = dot_t(jnp.concatenate(taken, axis=0), weights[index])
+            term = dot_t(jnp.concatenate(taken, axis=0), weight[...])
             total = term if total is None else total + term
         out[...] = total.astype(out.dtype)
 
@@ -1060,17 +1025,18 @@
 def weight_call(scalars, raw, weights, size):
     _, rows, local = raw.shape
     width = weights[0].shape[0]
+    tile = min(width, 512)
     operands = [scalars, raw, *weights]
     out_shape = [((rows // 2, width), jnp.float32), ((rows // 2, width), jnp.bfloat16)]
     return kernel_call(
         functools.partial(weight_kernel, size),
-        (1,),
-        [whole(raw)] + [ANY] * 3,
-        [pl.BlockSpec(shape, lambda *_: (0, 0)) for shape, _ in out_shape],
+        (width // tile,),
+        [whole(raw)] + [pl.BlockSpec((tile, local), lambda n, *_: (n, 0))] * 3,
+        [pl.BlockSpec((rows // 2, tile), lambda n, *_: (0, n))] * 2,
         out_shape,
         operands,
         6 * rows * local * width,
-        [pltpu.VMEM((3, width, local), jnp.bfloat16), pltpu.SemaphoreType.DMA((3,))],
+        (),
         1,
     )
 
@@ -1406,7 +1372,8 @@
             sides[index],
             back,
             offset,
-            near if index else 0,
+            near,
+            span if index else 0,
             span,
         )
 
@@ -1433,15 +1400,20 @@
     norm_planes[3] = ring(jnp.concatenate(norm_pairs[3], axis=0), axes, "y")
     came, last = [None] * far, [None] * far
     came[1] = scatter_first(parts[1], axes)
+    came_x = send_sum(parts[0], axes, "x")
     cot_across = [turn(piece, axes, "z", 1) for piece in cot_planes[2][1:]]
+    cot_planes[2] = [[piece] for piece in cot_planes[2]]
     whole_step(2)
 
-    held = (norm_planes[3], came[1], parts[2], parts[0], cot_across)
-    norm_planes[3], came[1], parts[2], parts[0], cot_across = hold(held)
-    cot_planes[3] = [cot_queue[3]] + cot_across
+    held = (norm_planes[3], came[1], parts[2], came_x, cot_across)
+    norm_planes[3], came[1], parts[2], came_x, cot_across = hold(held)
+    cot_planes[3] = [[piece] for piece in [cot_queue[3]] + cot_across]
+    came[2] = scatter_first(parts[2], axes)
     last[1] = scatter_second(parts[1], came[1], axes)
-    came[2] = scatter_first(parts[2], axes)
-    came_y = send_sum(parts[0], axes, "y")
+    own_sums = [
+        [block(parts[0][0], k, span), block(came_x, k, span)] for k in range(span)
+    ]
+    came_y = send_sum([None] + [low(pair[0] + pair[1]) for pair in own_sums[1:]], axes, "y")
     whole_step(3)
 
     held = (last[1], came[2], came_y, parts[3], hiddens)
@@ -1451,10 +1423,10 @@
     ring_sum = turn(low(scatter_last(parts[1], came[1], last[1], axes)), axes, "z", 1)
     mixes, mix_came = [None] * far, [None] * far
 
-    def down_step(first, second):
-        mixes[first], mixes[second] = down_call(
-            [hiddens[first], hiddens[second]], downs, near, span, row_share
-        )
+    def down_step(*indices):
+        done = down_call([hiddens[index] for index in indices], downs, near, span, row_share)
+        for index, blocks in zip(indices, done):
+            mixes[index] = blocks
 
     down_step(3, 0)
 
@@ -1464,17 +1436,13 @@
     ring_sum = turn(
         low(wide(ring_sum) + scatter_last(parts[2], came[2], last[2], axes)), axes, "z", 1
     )
-
-    ring_sum, last[3], parts[0], hiddens = hold((ring_sum, last[3], parts[0], hiddens))
+    down_step(2)
+
+    ring_sum, last[3], hiddens, mixes[2] = hold((ring_sum, last[3], hiddens, mixes[2]))
     ring_sum = turn(
         low(wide(ring_sum) + scatter_last(parts[3], came[3], last[3], axes)), axes, "z", 1
     )
-    own_sums = [
-        [block(parts[0][0], k, near), block(came_y, k, near)] for k in range(near)
-    ]
-    came_x = send_sum([None] + [low(pair[0] + pair[1]) for pair in own_sums[1:]], axes, "x")
-    down_step(1, 2)
-
+    down_step(1)
     half_width = model_width // span
 
     def column_sum(arrays, owner):
@@ -1487,12 +1455,13 @@
         rows = [column_sum(arrays, owner) for arrays in mix_held[index]]
         return jnp.concatenate(rows, axis=0)
 
-    def mix_down(index):
-        came_rows = None
-        for step in range(span - 1, 0, -1):
-            total = mix_columns(index, (level + span - step) % span)
-            if came_rows is not None:
-                total = total + rolled(came_rows)
+    def mix_sent(index):
+        return low(mix_columns(index, (level + 1) % span))
+
+    def mix_down(index, came_rows):
+        came_rows = turn(came_rows, axes, "y", -1)
+        for step in range(span - 2, 0, -1):
+            total = mix_columns(index, (level + span - step) % span) + rolled(came_rows)
             came_rows = turn(low(total), axes, "y", -1)
         return came_rows
 
@@ -1509,9 +1478,9 @@
     mix_held = [None] * far
     mix_parts = [None] * far
 
-    ring_sum, came_x, mixes = hold((ring_sum, came_x, mixes))
+    ring_sum, mixes = hold((ring_sum, mixes))
     mix_early = mix_send(3, 0)
-    ffn_rows_grad = wide(ring_sum) + (own_sums[0][0] + own_sums[0][1]) + wide(came_x)
+    ffn_rows_grad = wide(ring_sum) + (own_sums[0][0] + own_sums[0][1]) + wide(came_y)
     second_scaled = ffn_rows_grad * wide(second_gain)
     second_inverse = lax.rsqrt(
         jnp.mean(resid_rows * resid_rows, axis=1, keepdims=True) + EPSILON
@@ -1556,11 +1525,13 @@
         column_share,
     )
 
-    inner = sum_tensor(hold(inner), axes)
     held = (inner, mix_late, mix_next, mix_far, mixes)
     inner, mix_late, mix_next, mix_far, mixes = hold(held)
     mix_held[3] = list(zip(mixes[3][0], [mix_early] + mix_late))
-    mix_parts[3] = mix_down(3)
+    mix_ready = mix_sent(3)
+    inner = sum_tensor(inner, axes)
+    inner, mix_ready, mixes = hold((inner, mix_ready, mixes))
+    mix_parts[3] = mix_down(3, mix_ready)
     mix_last = [mix_send(2, down) for down in range(1, span)]
     mix_near = [turn(mixes[1][0][0], axes, "z", -1)]
     raw_grads, lowrank_part, adapt_grad = raw_call(
@@ -1584,24 +1555,23 @@
     held = (normed_mine, normed_theirs, lowrank_parts, mix_parts[3], mix_last, mix_near, mixes)
     held = hold(held)
     normed_mine, normed_theirs, lowrank_parts, mix_parts[3], mix_last, mix_near, mixes = held
-    normed_theirs = turn(normed_theirs, axes, "c", 1)
+    normed_theirs = hold(turn(normed_theirs, axes, "c", 1))
+    normed_kept, normed_sent = scatter_core(normed_mine, normed_theirs, axes)
+    held = (normed_sent, lowrank_parts, mixes, mix_last)
+    normed_sent, lowrank_parts, mixes, mix_last = hold(held)
+    normed_came = turn(normed_sent, axes, "y", -1)
     lowrank_grad = low(sum(wide(part) for part in lowrank_parts))
-    mix_held[2] = list(zip(mixes[2][0], [mix_next] + mix_last))
-    mix_parts[2] = mix_down(2)
-    mix_beside = turn(low(mix_total(3)), axes, "z", 1)
+    mix_near = mix_near + [turn(part, axes, "z", -1) for part in mixes[1][0][1:]]
     compact = compact_call(
         rank_list, lowrank_grad, normed_in, mix_out_grad, adapt_grad, mix_in_grad, select
     )
-    normed_theirs, compact, mixes = hold((normed_theirs, compact, mixes))
-    mix_near = mix_near + [turn(part, axes, "z", -1) for part in mixes[1][0][1:]]
-    normed_kept, normed_sent = scatter_core(normed_mine, normed_theirs, axes)
-    normed_sent, compact = hold((normed_sent, compact))
-    normed_came = turn(normed_sent, axes, "y", -1)
-    trees, mix_near, mix_beside = hold((ring(compact, axes, "x"), mix_near, mix_beside))
-    trees = jnp.concatenate(trees, axis=0)
-    tree_queue = [trees] + [turn(trees, axes, "z", step) for step in range(1, far)]
-    normed_came, mix_parts[2], mix_far, mixes = hold((normed_came, mix_parts[2], mix_far, mixes))
-
+    trees = ring(compact, axes, "x")
+    mix_held[2] = list(zip(mixes[2][0], [mix_next] + mix_last))
+    mix_ready = mix_sent(2)
+    trees, mix_near, mix_ready, normed_came = hold((trees, mix_near, mix_ready, normed_came))
+
+    tree_queue = [jnp.concatenate(trees, axis=0)]
+    tree_queue.append(turn(tree_queue[-1], axes, "z", 1))
     input_rows = input_call(
         rank_list,
         normed_kept,
@@ -1613,32 +1583,40 @@
         first_gain,
         resid_grad_rows,
     )
+    input_rows, tree_queue = hold((input_rows, tree_queue))
     input_held = ring(input_rows, axes, "y")
+    tree_queue.append(turn(tree_queue[-1], axes, "z", 1))
     for across in range(1, near):
         pairs = zip(mixes[0][across], mix_far[across - 1])
         mixes[0][across] = [low(wide(mine) + wide(other)) for mine, other in pairs]
-    mix_came[0] = [mix_send(0, down) for down in range(span)]
-    input_held, tree_queue = hold((input_held, tree_queue))
+    whole_blocks = [jnp.concatenate(blocks, axis=0) for blocks in mixes[0][1:]]
+    mix_came[0] = send_sum([None] + whole_blocks, axes, "x")
+    mix_parts[2] = mix_down(2, mix_ready)
+    tree_queue, mixes, input_held = hold((tree_queue, mixes, input_held))
+    tree_queue.append(turn(tree_queue[-1], axes, "z", 1))
+    input_pieces = input_held + [turn(piece, axes, "c", 1) for piece in input_held]
+    mix_parts[2], tree_queue = hold((mix_parts[2], tree_queue))
 
     trees = jnp.concatenate(tree_queue, axis=0)
     shared = trees.reshape(owners, -1, column_share)[:, : 4 * RANK]
     shared = ring(shared.reshape(-1, column_share), axes, "y")
-    mix_across = turn(low(mix_total(2)), axes, "z", -2)
-    input_pieces = input_held + [turn(piece, axes, "c", 1) for piece in input_held]
+    mix_sum = turn(low(mix_total(2)), axes, "z", 1)
     shared, mix_came[0] = hold((shared, mix_came[0]))
-    mix_held[0] = [list(arrays) for arrays in zip(mixes[0][0], mix_came[0], mix_near)]
+    arrived = [mix_came[0][down * row_share : (down + 1) * row_share] for down in range(span)]
+    mix_held[0] = [list(arrays) for arrays in zip(mixes[0][0], arrived, mix_near)]
     mix_held[0][0].append(resid_rows)
-    mix_parts[0] = mix_down(0)
     shared = shared + [turn(piece, axes, "c", 1) for piece in shared]
-    shared = hold(shared)
+    mix_parts[0] = mix_down(0, mix_sent(0))
+    shared, mix_sum = hold((shared, mix_sum))
+    mix_sum = turn(low(wide(mix_sum) + mix_total(3)), axes, "z", 1)
     grad_adapt_in, grad_adapt_out, grad_adapt_in_out, grad_adapt_out_out = assemble_call(
         order, trees, shared[1:], owners
     )
-    held = (mix_parts[0], mix_across, mix_beside, grad_adapt_in)
-    mix_parts[0], mix_across, mix_beside, grad_adapt_in = hold(held)
-    layer_columns = low(mix_total(0) + wide(mix_across) + wide(mix_beside))
+    input_grad = spread_call(order, input_pieces)
+    held = (mix_parts[0], mix_sum, grad_adapt_in, input_grad)
+    mix_parts[0], mix_sum, grad_adapt_in, input_grad = hold(held)
+    layer_columns = low(mix_total(0) + wide(mix_sum))
     layer_out = place_columns(layer_columns, axes)
-    input_grad = spread_call(order, input_pieces)
     return (
         layer_out,
         input_grad,

time: 484 us -> 476 us (0.983)
  the two profiles are of different devices: /device:TPU:9 before, /device:TPU:0 now
where the time goes in v7:
time: 476 us; the launch traced here: 468 us
  Pallas kernels  233 us (49%)
  waiting for transfers between devices  121 us (25%)
  starting transfers between devices  67.5 us (14%)
  other arithmetic  30 us (6%)
  local copies, waits for them, and re-layouts  14.2 us (3%)
    pallas_call x18, Pallas kernels, kernel_call(): pl.pallas_call(kernel, grid_spec=pltpu.PrefetchScalarGridSpec(num_scalar_...  233 us
    ppermute x78, waiting for transfers between devices, turn(): return lax.ppermute(array, axis, pairs)  121 us
    ppermute x78, starting transfers between devices, turn(): return lax.ppermute(array, axis, pairs)  67.5 us
    convert_element_type x22, other arithmetic, low(): return array.astype(jnp.bfloat16)  12.8 us
  transfers between devices with their start and end apart: 78, of which 30 were waited for; matrix products, arithmetic and copies ran while one was open for 5% of the time, Pallas kernels for 49%

profile of v7, /device:TPU:0, one launch (start us, length us, event | category | flops | bytes accessed | tf_op | source)
XLA Modules:
  0.0 468.0 jit_solution(7663885495434516800)
XLA Ops:
  3.5 3.1 collective-permute-start.2
  9.4 13.1 %shard_map.244 = (bf16[512,2048]{1,0:T(8,128)(2,1)}, bf16[3,512,128]{2,1,0:T(8,128)(2,1)}, f32[512,512]{1,0:T(8,128)}, f32[512,512]{1,0:T(8,128)}, f32[512,512]{1,0:T(8,128)}, /*index=5*/f32[8,512]{1,0:T(8,128)}) custom-call(bf16[512,2048]{1,0:T(8,128)(2,1)} %tokens.5, bf16[1,2048]{1,0:T(2,128)(2,1)} %broadcast_in_dim.43.gain, ...), custom_call_target="tpu_custom_call" | custom-call | flops 3221225472 | bytes 10359296 | tf_op jit(solution)/shard_map/pallas_call | solution.py:202
  29.4 3.7 collective-permute-done.2
  37.8 10.5 %shard_map.245 = (bf16[512,512]{1,0:T(8,128)(2,1)}, bf16[512,512]{1,0:T(8,128)(2,1)}, bf16[512,512]{1,0:T(8,128)(2,1)}, bf16[512,512]{1,0:T(8,128)(2,1)}, f32[25...) custom-call(s32[1]{0:T(128)} %bitcast.1.core.scalars, f32[8,512]{1,0:T(8,128)} %add.407.squares, ...), custom_call_target="tpu_custom_call" | custom-call | flops 1610612736 | bytes 6965252 | tf_op jit(solution)/shard_map/pallas_call | solution.py:202
  50.3 2.9 collective-permute-done.6
  53.2 2.7 add_convert_fusion
  59.4 11.2 %collective-permute-done.7.came = bf16[128,2176]{1,0:T(8,128)(2,1)S(1)} collective-permute-done((bf16[128,2176]{1,0:T(8,128)(2,1)S(1)}, bf16[128,2176]{1,0:T(8,128)(2,1)S(1)}, u32[]{:S(2)}, u32[]{:S(2)}) %collective-permute-start.7) | collective-permute-done | bytes 557088 | tf_op jit(solution)/shard_map/ppermute | solution.py:77
  70.6 3.0 collective-permute-done.8
  74.5 3.9 shard_map.246
  81.0 13.8 %collective-permute-done.12 = bf16[128,2048]{1,0:T(8,128)(2,1)S(1)} collective-permute-done((bf16[128,2048]{1,0:T(8,128)(2,1)}, bf16[128,2048]{1,0:T(8,128)(2,1)S(1)}, u32[]{:S(2)}, u32[]{:S(2)}) %collective-permute-start.12) | collective-permute-done | bytes 524320 | tf_op jit(solution)/shard_map/ppermute | solution.py:77
  98.0 16.6 %shard_map.247 = (bf16[8,1024,256]{2,1,0:T(8,128)(2,1)}, bf16[1024,128]{1,0:T(8,128)(2,1)}) custom-call(bf16[256,2176]{1,0:T(8,128)(2,1)} %copy-done.6, bf16[256,2176]{1,0:T(8,128)(2,1)} %copy-done.53, bf16[128,2176]{1,0:T(8,128)(2,1)} %copy-done.11, bf16[128,2176]{1,0:T(8,128)(2,1)} %copy-done.10, bf16[128,2176]{1,0:T(8,128)(2,1)} %copy-done.59, ...), custom_call_target="tpu_custom_call" | custom-call | flops 8589934592 | bytes 13107200 | tf_op jit(solution)/shard_map/pallas_call | solution.py:202
  114.6 5.0 %collective-permute-done.15.refs_1_ = bf16[256,2048]{1,0:T(8,128)(2,1)S(1)} collective-permute-done((bf16[256,2048]{1,0:T(8,128)(2,1)S(1)}, bf16[256,2048]{1,0:T(8,128)(2,1)S(1)}, u32[]{:S(2)}, u32[]{:S(2)}) %collective-permute-start.15) | collective-permute-done | bytes 1048608 | tf_op jit(solution)/shard_map/ppermute | solution.py:77
  122.8 25.8 %shard_map.248 = (bf16[256,2048]{1,0:T(8,128)(2,1)}, bf16[256,2048]{1,0:T(8,128)(2,1)}, bf16[8,512,256]{2,1,0:T(8,128)(2,1)}) custom-call(bf16[256,2048]{1,0:T(8,128)(2,1)} %copy-done.40, bf16[256,2048]{1,0:T(8,128)(2,1)} %copy-done.56, bf16[4,2048,256]{2,1,0:T(8,128)(2,1)} %refs_2_.3, bf16[4,2048,256]{2,1,0:T(8,128)(2,1)} %refs_3_.3, ...), custom_call_target="tpu_custom_call" | custom-call | flops 17179869184 | bytes 23592960 | tf_op jit(solution)/shard_map/pallas_call | solution.py:202
  152.3 25.7 %shard_map.249 = (bf16[128,2048]{1,0:T(8,128)(2,1)}, bf16[128,2048]{1,0:T(8,128)(2,1)}, bf16[128,2048]{1,0:T(8,128)(2,1)}, bf16[128,2048]{1,0:T(8,128)(2,1)}, bf16[8,512,256]{2,1,0:T(8,128)(2,1)}) custom-call(bf16[256,2048]{1,0:T(8,128)(2,1)} %copy-done.41, bf16[256,2048]{1,0:T(8,128)(2,1)} %copy-done.58, bf16[4,2048,256]{2,1,0:T(8,128)(2,1)} %refs_2_.3, ...), custom_call_target="tpu_custom_call" | custom-call | flops 17179869184 | bytes 23592960 | tf_op jit(solution)/shard_map/pallas_call | solution.py:202
  180.0 2.4 collective-permute-start.29
  185.2 29.7 %shard_map.250 = (bf16[128,2048]{1,0:T(8,128)(2,1)}, bf16[128,2048]{1,0:T(8,128)(2,1)}, bf16[128,2048]{1,0:T(8,128)(2,1)}, bf16[128,2048]{1,0:T(8,128)(2,1)}, bf16[8,512,256]{2,1,0:T(8,128)(2,1)}) custom-call(bf16[256,2048]{1,0:T(8,128)(2,1)} %copy-done.42, bf16[256,2048]{1,0:T(8,128)(2,1)} %copy-done.57, bf16[4,2048,256]{2,1,0:T(8,128)(2,1)} %refs_2_.3, ...), custom_call_target="tpu_custom_call" | custom-call | flops 21474836480 | bytes 29753344 | tf_op jit(solution)/shard_map/pallas_call | solution.py:202
  220.5 29.7 %shard_map.251 = (bf16[128,2048]{1,0:T(8,128)(2,1)}, bf16[128,2048]{1,0:T(8,128)(2,1)}, bf16[128,2048]{1,0:T(8,128)(2,1)}, bf16[128,2048]{1,0:T(8,128)(2,1)}, bf16[8,512,256]{2,1,0:T(8,128)(2,1)}) custom-call(bf16[256,2048]{1,0:T(8,128)(2,1)} %copy-done.43, bf16[256,2048]{1,0:T(8,128)(2,1)} %collective-permute-done.25.refs_1_, ...), custom_call_target="tpu_custom_call" | custom-call | flops 21474836480 | bytes 29753344 | tf_op jit(solution)/shard_map/pallas_call | solution.py:202
  254.7 2.6 collective-permute-start.35
  259.7 13.1 %shard_map.252 = (bf16[128,2048]{1,0:T(8,128)(2,1)}, bf16[128,2048]{1,0:T(8,128)(2,1)}, bf16[128,2048]{1,0:T(8,128)(2,1)}, bf16[128,2048]{1,0:T(8,128)(2,1)}, bf...) custom-call(bf16[8,512,256]{2,1,0:T(8,128)(2,1)} %get-tuple-element., ...), custom_call_target="tpu_custom_call" | custom-call | flops 8589934592 | bytes 12582912 | tf_op jit(solution)/shard_map/pallas_call | solution.py:202
  277.3 8.5 %shard_map.253 = (bf16[128,2048]{1,0:T(8,128)(2,1)}, bf16[128,2048]{1,0:T(8,128)(2,1)}, bf16[128,2048]{1,0:T(8,128)(2,1)}, bf16[128,2048]{1,0:T(8,128)(2,1)}) custom-call(bf16[8,512,256]{2,1,0:T(8,128)(2,1)} %get-tuple-element.433.refs_0_, bf16[1024,2048]{1,0:T(8,128)(2,1)} %bitcast.11.refs_6_.refs_7_.refs_2_.refs_1_, ...), custom_call_target="tpu_custom_call" | custom-call | flops 4294967296 | bytes 10485760 | tf_op jit(solution)/shard_map/pallas_call | solution.py:202
  285.9 3.1 collective-permute-done.40
  290.1 8.7 %shard_map.254 = (bf16[128,2048]{1,0:T(8,128)(2,1)}, bf16[128,2048]{1,0:T(8,128)(2,1)}, bf16[128,2048]{1,0:T(8,128)(2,1)}, bf16[128,2048]{1,0:T(8,128)(2,1)}) custom-call(bf16[8,512,256]{2,1,0:T(8,128)(2,1)} %get-tuple-element.445.refs_0_, bf16[1024,2048]{1,0:T(8,128)(2,1)} %bitcast.11.refs_6_.refs_7_.refs_2_.refs_1_, ...), custom_call_target="tpu_custom_call" | custom-call | flops 4294967296 | bytes 10485760 | tf_op jit(solution)/shard_map/pallas_call | solution.py:202
  298.7 2.6 collective-permute-done.43
  302.9 2.8 fusion.23
  306.8 9.2 %collective-permute-done.45 = bf16[128,2048]{1,0:T(8,128)(2,1)S(1)} collective-permute-done((bf16[128,2048]{1,0:T(8,128)(2,1)S(1)}, bf16[128,2048]{1,0:T(8,128)(2,1)S(1)}, u32[]{:S(2)}, u32[]{:S(2)}) %collective-permute-start.45) | collective-permute-done | bytes 524320 | tf_op jit(solution)/shard_map/ppermute | solution.py:77
  321.9 17.5 %shard_map.255 = (f32[512,512]{1,0:T(8,128)}, f32[512,512]{1,0:T(8,128)}, bf16[512,512]{1,0:T(8,128)(2,1)}, f32[8,512]{1,0:T(8,128)}, bf16[16,512]{1,0:T(8,128)(2,1)}, /*index=5*/bf16[16,512]{1,0:T(8,128)(2,1)}) custom-call(s32[5]{0:T(128)} %concatenate.86.scalars, bf16[128,2176]{1,0:T(8,128)(2,1)} %copy-done.12, bf16[128,2176]{1,0:T(8,128)(2,1)} %copy-done.61, ...), custom_call_target="tpu_custom_call" | custom-call | flops 2952790016 | bytes 10750484 | tf_op jit(solution)/shard_map/pallas_call | solution.py:202
  339.5 3.9 collective-permute-done.49
  347.5 2.6 collective-permute-done.53
  350.7 5.1 %shard_map.256 = (bf16[3,512,512]{2,1,0:T(8,128)(2,1)}, bf16[512,128]{1,0:T(8,128)(2,1)}, bf16[48,512]{1,0:T(8,128)(2,1)}) custom-call(f32[8,512]{1,0:T(8,128)} %add.452.inner, f32[8,512]{1,0:T(8,128)} %add.407.squares, f32[512,512]{1,0:T(8,128)} %get-tuple-element.531.query_grad, f32[512,512]{1,0:T(8,128)} %get-tuple-element.532.key_grad, ...), custom_call_target="tpu_custom_call" | custom-call | flops 402653184 | bytes 5538304 | tf_op jit(solution)/shard_map/pallas_call | solution.py:202
  357.3 3.0 collective-permute-start.58
  362.2 7.7 %shard_map.257 = (f32[256,2048]{1,0:T(8,128)}, bf16[256,2048]{1,0:T(8,128)(2,1)}) custom-call(s32[1]{0:T(128)} %bitcast.1.core.scalars, bf16[3,512,512]{2,1,0:T(8,128)(2,1)} %get-tuple-element.537.raw, bf16[2048,512]{1,0:T(8,128)(2,1)} %query_weight.3, bf16[2048,512]{1,0:T(8,128)(2,1)} %key_weight.3, bf16[2048,512]{1,0:T(8,128)(2,1)} %value_weight.3), custom_call_target="tpu_custom_call" | custom-call | flops 3221225472 | bytes 7864324 | tf_op jit(solution)/shard_map/pallas_call | solution.py:202
  369.9 3.0 collective-permute-done.55
  373.1 2.9 collective-permute-done.59
  375.9 3.0 convert_add_fusion.1
  378.9 3.3 collective-permute-start.61
  384.0 2.9 shard_map.258
  388.7 3.8 collective-permute-done.60
  393.9 2.1 collective-permute-done.62.came
  396.8 4.4 shard_map.259.refs_0_
  401.3 4.5 collective-permute-done.63
  408.2 8.4 %collective-permute-done.64 = bf16[288,512]{1,0:T(8,128)(2,1)S(1)} collective-permute-done((bf16[288,512]{1,0:T(8,128)(2,1)S(1)}, bf16[288,512]{1,0:T(8,128)(2,1)S(1)}, u32[]{:S(2)}, u32[]{:S(2)}) %collective-permute-start.64) | collective-permute-done | bytes 294944 | tf_op jit(solution)/shard_map/ppermute | solution.py:77
  416.6 4.4 collective-permute-done.65.refs_1_
  422.7 6.5 %collective-permute-done.66 = bf16[256,1024]{1,0:T(8,128)(2,1)S(1)} collective-permute-done((bf16[256,1024]{1,0:T(8,128)(2,1)S(1)}, bf16[256,1024]{1,0:T(8,128)(2,1)S(1)}, u32[]{:S(2)}, u32[]{:S(2)}) %collective-permute-start.66) | collective-permute-done | bytes 524320 | tf_op jit(solution)/shard_map/ppermute | solution.py:77
  431.8 8.6 %collective-permute-done.69 = bf16[256,2048]{1,0:T(8,128)(2,1)S(1)} collective-permute-done((bf16[256,2048]{1,0:T(8,128)(2,1)S(1)}, bf16[256,2048]{1,0:T(8,128)(2,1)S(1)}, u32[]{:S(2)}, u32[]{:S(2)}) %collective-permute-start.69) | collective-permute-done | bytes 1048608 | tf_op jit(solution)/shard_map/ppermute | solution.py:77
  444.2 3.3 collective-permute-done.73
  450.8 4.6 shard_map.261
  455.5 5.3 %shard_map.260 = (f32[3,2048,128]{2,1,0:T(8,128)}, f32[3,128,512]{2,1,0:T(8,128)}, f32[512,128]{1,0:T(8,128)}, f32[128,2048]{1,0:T(8,128)}) custom-call(s32[4]{0:T(128)} %pad_add_fusion.order, bf16[1152,512]{1,0:T(8,128)(2,1)} %copy-done.1, bf16[512,512]{1,0:T(8,128)(2,1)} %copy-done.37, bf16[512,512]{1,0:T(8,128)(2,1)} %copy-done.38, ...), custom_call_target="tpu_custom_call" | custom-call | flops 268435456 | bytes 2752528 | tf_op jit(solution)/shard_map/pallas_call | solution.py:202
  460.9 3.0 collective-permute-done.74
  (377 shorter events, 98.1 us)
Async XLA Ops:
  3.5 29.7 %collective-permute-start.2 = (bf16[256,2176]{1,0:T(8,128)(2,1)S(1)}, bf16[256,2176]{1,0:T(8,128)(2,1)S(1)}, u32[]{:S(2)}, u32[]{:S(2)}) collective-permute-start(bf16[256,2176]{1,0:T(8,128)(2,1)S(1)} %maximum_maximum_fusion.refs_0_), channel_id=1, source_target_pairs={{0,8},{4,12},{8,16},{12,20},{16,24},{20,28},{24,0},{28,4},{1,9},{5... | collective-permute-start | bytes 3342344 | tf_op jit(solution)/shard_map/ppermute | solution.py:77
  6.6 26.6 %collective-permute-start.3 = (bf16[256,2176]{1,0:T(8,128)(2,1)S(1)}, bf16[256,2176]{1,0:T(8,128)(2,1)S(1)}, u32[]{:S(2)}, u32[]{:S(2)}) collective-permute-start(bf16[256,2176]{1,0:T(8,128)(2,1)S(1)} %maximum_maximum_fusion.refs_0_), channel_id=1, source_target_pairs={{0,4},{4,0},{8,12},{12,8},{16,20},{20,16},{24,28},{28,24},{1,5},{5... | collective-permute-start | bytes 3342344 | tf_op jit(solution)/shard_map/ppermute | solution.py:77
  33.2 40.5 %collective-permute-start.10 = (bf16[4,2048,256]{2,1,0:T(8,128)(2,1)}, bf16[4,2048,256]{2,1,0:T(8,128)(2,1)}, u32[]{:S(2)}, u32[]{:S(2)}) collective-permute-start(bf16[4,2048,256]{2,1,0:T(8,128)(2,1)} %refs_2_.3), channel_id=1, source_target_pairs={{0,1},{1,0},{2,3},{3,2},{4,5},{5,4},{6,7},{7,6},{8,9},{9,8},{10,11... | collective-permute-start | bytes 12582920 | tf_op jit(solution)/shard_map/ppermute | solution.py:77
  33.2 40.5 %collective-permute-start.11 = (bf16[4,2048,256]{2,1,0:T(8,128)(2,1)}, bf16[4,2048,256]{2,1,0:T(8,128)(2,1)}, u32[]{:S(2)}, u32[]{:S(2)}) collective-permute-start(bf16[4,2048,256]{2,1,0:T(8,128)(2,1)} %refs_3_.3), channel_id=1, source_target_pairs={{0,1},{1,0},{2,3},{3,2},{4,5},{5,4},{6,7},{7,6},{8,9},{9,8},{10,11... | collective-permute-start | bytes 12582920 | tf_op jit(solution)/shard_map/ppermute | solution.py:77
  34.2 16.1 %collective-permute-start.4 = (bf16[128,2176]{1,0:T(8,128)(2,1)S(1)}, bf16[128,2176]{1,0:T(8,128)(2,1)S(1)}, u32[]{:S(2)}, u32[]{:S(2)}) collective-permute-start(bf16[128,2176]{1,0:T(8,128)(2,1)S(1)} %get-tuple-element.343.refs_2_), channel_id=1, source_target_pairs={{0,8},{4,12},{8,16},{12,20},{16,24},{20,28},{24,0},{28,4},{1,9},{5... | collective-permute-start | bytes 1671176 | tf_op jit(solution)/shard_map/ppermute | solution.py:77
  35.2 15.1 %collective-permute-start.5 = (bf16[128,2176]{1,0:T(8,128)(2,1)S(1)}, bf16[128,2176]{1,0:T(8,128)(2,1)S(1)}, u32[]{:S(2)}, u32[]{:S(2)}) collective-permute-start(bf16[128,2176]{1,0:T(8,128)(2,1)S(1)} %get-tuple-element.343.refs_2_), channel_id=1, source_target_pairs={{0,4},{4,0},{8,12},{12,8},{16,20},{20,16},{24,28},{28,24},{1,5},{5... | collective-permute-start | bytes 1671176 | tf_op jit(solution)/shard_map/ppermute | solution.py:77
  57.5 16.2 %collective-permute-start.8 = (bf16[128,2176]{1,0:T(8,128)(2,1)S(1)}, bf16[128,2176]{1,0:T(8,128)(2,1)S(1)}, u32[]{:S(2)}, u32[]{:S(2)}) collective-permute-start(bf16[128,2176]{1,0:T(8,128)(2,1)S(1)} %get-tuple-element.328.refs_3_), channel_id=1, source_target_pairs={{0,8},{4,12},{8,16},{12,20},{16,24},{20,28},{24,0},{28,4},{1,9},{5... | collective-permute-start | bytes 1671176 | tf_op jit(solution)/shard_map/ppermute | solution.py:77
  57.9 15.7 %collective-permute-start.9 = (bf16[128,2176]{1,0:T(8,128)(2,1)S(1)}, bf16[128,2176]{1,0:T(8,128)(2,1)S(1)}, u32[]{:S(2)}, u32[]{:S(2)}) collective-permute-start(bf16[128,2176]{1,0:T(8,128)(2,1)S(1)} %get-tuple-element.328.refs_3_), channel_id=1, source_target_pairs={{0,4},{4,0},{8,12},{12,8},{16,20},{20,16},{24,28},{28,24},{1,5},{5... | collective-permute-start | bytes 1671176 | tf_op jit(solution)/shard_map/ppermute | solution.py:77
  73.7 21.0 %collective-permute-start.14 = (bf16[1024,2048]{1,0:T(8,128)(2,1)}, bf16[1024,2048]{1,0:T(8,128)(2,1)}, u32[]{:S(2)}, u32[]{:S(2)}) collective-permute-start(bf16[1024,2048]{1,0:T(8,128)(2,1)} %bitcast.11.refs_6_.refs_7_.refs_2_.refs_1_), channel_id=1, source_target_pairs={{0,1},{1,0},{2,3},{3,2},{4,5},{5,4},{6,7},{7,6},{8,9},{9,8},{10,11... | collective-permute-start | bytes 12582920 | tf_op jit(solution)/shard_map/ppermute | solution.py:77
  78.4 16.3 %collective-permute-start.12 = (bf16[128,2048]{1,0:T(8,128)(2,1)}, bf16[128,2048]{1,0:T(8,128)(2,1)S(1)}, u32[]{:S(2)}, u32[]{:S(2)}) collective-permute-start(bf16[128,2048]{1,0:T(8,128)(2,1)} %get-tuple-element.337), channel_id=1, source_target_pairs={{0,8},{4,12},{8,16},{12,20},{16,24},{20,28},{24,0},{28,4},{1,9},{5... | collective-permute-start | bytes 1572872 | tf_op jit(solution)/shard_map/ppermute | solution.py:77
  78.5 16.3 %collective-permute-start.13 = (bf16[128,2048]{1,0:T(8,128)(2,1)}, bf16[128,2048]{1,0:T(8,128)(2,1)S(1)}, u32[]{:S(2)}, u32[]{:S(2)}) collective-permute-start(bf16[128,2048]{1,0:T(8,128)(2,1)} %get-tuple-element.337), channel_id=1, source_target_pairs={{0,4},{4,0},{8,12},{12,8},{16,20},{20,16},{24,28},{28,24},{1,5},{5... | collective-permute-start | bytes 1572872 | tf_op jit(solution)/shard_map/ppermute | solution.py:77
  94.8 24.8 %collective-permute-start.15 = (bf16[256,2048]{1,0:T(8,128)(2,1)S(1)}, bf16[256,2048]{1,0:T(8,128)(2,1)S(1)}, u32[]{:S(2)}, u32[]{:S(2)}) collective-permute-start(bf16[256,2048]{1,0:T(8,128)(2,1)S(1)} %constant_dynamic-update-slice_fusion.refs_0_), channel_id=1, source_target_pairs={{0,2},{1,3},{2,0},{3,1},{4,6},{5,7},{6,4},{7,5},{8,10},{9,11},{10,... | collective-permute-start | bytes 3145736 | tf_op jit(solution)/shard_map/ppermute | solution.py:77
  96.3 18.3 %collective-permute-start.16 = (bf16[128,2048]{1,0:T(8,128)(2,1)S(1)}, bf16[128,2048]{1,0:T(8,128)(2,1)S(1)}, u32[]{:S(2)}, u32[]{:S(2)}) collective-permute-start(bf16[128,2048]{1,0:T(8,128)(2,1)S(1)} %collective-permute-done.12), channel_id=1, source_target_pairs={{0,8},{4,12},{8,16},{12,20},{16,24},{20,28},{24,0},{28,4},{1,9},{5... | collective-permute-start | bytes 1572872 | tf_op jit(solution)/shard_map/ppermute | solution.py:77
  96.4 18.2 %collective-permute-start.17 = (bf16[128,2048]{1,0:T(8,128)(2,1)S(1)}, bf16[128,2048]{1,0:T(8,128)(2,1)S(1)}, u32[]{:S(2)}, u32[]{:S(2)}) collective-permute-start(bf16[128,2048]{1,0:T(8,128)(2,1)S(1)} %collective-permute-done.12), channel_id=1, source_target_pairs={{0,4},{4,0},{8,12},{12,8},{16,20},{20,16},{24,28},{28,24},{1,5},{5... | collective-permute-start | bytes 1572872 | tf_op jit(solution)/shard_map/ppermute | solution.py:77
  119.6 28.9 %collective-permute-start.19 = (bf16[128,2048]{1,0:T(8,128)(2,1)S(1)}, bf16[128,2048]{1,0:T(8,128)(2,1)S(1)}, u32[]{:S(2)}, u32[]{:S(2)}) collective-permute-start(bf16[128,2048]{1,0:T(8,128)(2,1)S(1)} %collective-permute-done.16), channel_id=1, source_target_pairs={{0,8},{4,12},{8,16},{12,20},{16,24},{20,28},{24,0},{28,4},{1,9},{5... | collective-permute-start | bytes 1572872 | tf_op jit(solution)/shard_map/ppermute | solution.py:77
  119.6 29.0 %collective-permute-start.20 = (bf16[128,2048]{1,0:T(8,128)(2,1)S(1)}, bf16[128,2048]{1,0:T(8,128)(2,1)S(1)}, u32[]{:S(2)}, u32[]{:S(2)}) collective-permute-start(bf16[128,2048]{1,0:T(8,128)(2,1)S(1)} %collective-permute-done.16), channel_id=1, source_target_pairs={{0,4},{4,0},{8,12},{12,8},{16,20},{20,16},{24,28},{28,24},{1,5},{5... | collective-permute-start | bytes 1572872 | tf_op jit(solution)/shard_map/ppermute | solution.py:77
  121.1 57.0 %collective-permute-start.23 = (bf16[256,2176]{1,0:T(8,128)(2,1)S(1)}, bf16[256,2176]{1,0:T(8,128)(2,1)S(1)}, u32[]{:S(2)}, u32[]{:S(2)}) collective-permute-start(bf16[256,2176]{1,0:T(8,128)(2,1)S(1)} %pad_maximum_fusion.refs_9_), channel_id=1, source_target_pairs={{0,8},{4,12},{8,16},{12,20},{16,24},{20,28},{24,0},{28,4},{1,9},{5... | collective-permute-start | bytes 3342344 | tf_op jit(solution)/shard_map/ppermute | solution.py:77
  121.6 56.5 %collective-permute-start.24 = (bf16[256,2176]{1,0:T(8,128)(2,1)S(1)}, bf16[256,2176]{1,0:T(8,128)(2,1)}, u32[]{:S(2)}, u32[]{:S(2)}) collective-permute-start(bf16[256,2176]{1,0:T(8,128)(2,1)S(1)} %pad_maximum_fusion.refs_9_), channel_id=1, source_target_pairs={{0,4},{4,0},{8,12},{12,8},{16,20},{20,16},{24,28},{28,24},{1,5},{5... | collective-permute-start | bytes 3342344 | tf_op jit(solution)/shard_map/ppermute | solution.py:77
  122.2 26.4 %collective-permute-start.18 = (bf16[256,2048]{1,0:T(8,128)(2,1)S(1)}, bf16[256,2048]{1,0:T(8,128)(2,1)S(1)}, u32[]{:S(2)}, u32[]{:S(2)}) collective-permute-start(bf16[256,2048]{1,0:T(8,128)(2,1)S(1)} %constant_dynamic-update-slice_fusion.2.refs_0_), channel_id=1, source_target_pairs={{0,2},{1,3},{2,0},{3,1},{4,6},{5,7},{6,4},{7,5},{8,10},{9,11},{10,... | collective-permute-start | bytes 3145736 | tf_op jit(solution)/shard_map/ppermute | solution.py:77
  148.7 29.4 %collective-permute-start.21 = (bf16[256,2048]{1,0:T(8,128)(2,1)S(1)}, bf16[256,2048]{1,0:T(8,128)(2,1)S(1)}, u32[]{:S(2)}, u32[]{:S(2)}) collective-permute-start(bf16[256,2048]{1,0:T(8,128)(2,1)S(1)} %constant_dynamic-update-slice_fusion.4.refs_0_), channel_id=1, source_target_pairs={{0,2},{1,3},{2,0},{3,1},{4,6},{5,7},{6,4},{7,5},{8,10},{9,11},{10,... | collective-permute-start | bytes 3145736 | tf_op jit(solution)/shard_map/ppermute | solution.py:77
  150.3 27.8 %collective-permute-start.22 = (bf16[128,2048]{1,0:T(8,128)(2,1)S(1)}, bf16[128,2048]{1,0:T(8,128)(2,1)S(1)}, u32[]{:S(2)}, u32[]{:S(2)}) collective-permute-start(bf16[128,2048]{1,0:T(8,128)(2,1)S(1)} %collective-permute-done.19), channel_id=1, source_target_pairs={{0,4},{4,0},{8,12},{12,8},{16,20},{20,16},{24,28},{28,24},{1,5},{5... | collective-permute-start | bytes 1572872 | tf_op jit(solution)/shard_map/ppermute | solution.py:77
  151.8 63.2 %collective-permute-start.28 = (bf16[256,2048]{1,0:T(8,128)(2,1)}, bf16[256,2048]{1,0:T(8,128)(2,1)S(1)}, u32[]{:S(2)}, u32[]{:S(2)}) collective-permute-start(bf16[256,2048]{1,0:T(8,128)(2,1)} %get-tuple-element.385), channel_id=1, source_target_pairs={{0,4},{4,0},{8,12},{12,8},{16,20},{20,16},{24,28},{28,24},{1,5},{5... | collective-permute-start | bytes 3145736 | tf_op jit(solution)/shard_map/ppermute | solution.py:77
  179.2 35.8 %collective-permute-start.25 = (bf16[256,2048]{1,0:T(8,128)(2,1)S(1)}, bf16[256,2048]{1,0:T(8,128)(2,1)}, u32[]{:S(2)}, u32[]{:S(2)}) collective-permute-start(bf16[256,2048]{1,0:T(8,128)(2,1)S(1)} %constant_dynamic-update-slice_fusion.6.refs_0_), channel_id=1, source_target_pairs={{0,2},{1,3},{2,0},{3,1},{4,6},{5,7},{6,4},{7,5},{8,10},{9,11},{10,... | collective-permute-start | bytes 3145736 | tf_op jit(solution)/shard_map/ppermute | solution.py:77
  180.0 35.0 %collective-permute-start.29 = (bf16[256,2176]{1,0:T(8,128)(2,1)}, bf16[256,2176]{1,0:T(8,128)(2,1)S(1)}, u32[]{:S(2)}, u32[]{:S(2)}) collective-permute-start(bf16[256,2176]{1,0:T(8,128)(2,1)} %collective-permute-done.24.refs_10_), channel_id=1, source_target_pairs={{0,8},{4,12},{8,16},{12,20},{16,24},{20,28},{24,0},{28,4},{1,9},{5... | collective-permute-start | bytes 3342344 | tf_op jit(solution)/shard_map/ppermute | solution.py:77
  182.5 32.5 %collective-permute-start.26 = (bf16[128,2048]{1,0:T(8,128)(2,1)}, bf16[128,2048]{1,0:T(8,128)(2,1)S(1)}, u32[]{:S(2)}, u32[]{:S(2)}) collective-permute-start(bf16[128,2048]{1,0:T(8,128)(2,1)} %get-tuple-element.375), channel_id=1, source_target_pairs={{0,2},{1,3},{2,0},{3,1},{4,6},{5,7},{6,4},{7,5},{8,10},{9,11},{10,... | collective-permute-start | bytes 1572872 | tf_op jit(solution)/shard_map/ppermute | solution.py:77
  183.7 31.3 %collective-permute-start.27 = (bf16[128,2048]{1,0:T(8,128)(2,1)S(1)}, bf16[128,2048]{1,0:T(8,128)(2,1)S(1)}, u32[]{:S(2)}, u32[]{:S(2)}) collective-permute-start(bf16[128,2048]{1,0:T(8,128)(2,1)S(1)} %copy-done.67), channel_id=1, source_target_pairs={{0,4},{4,0},{8,12},{12,8},{16,20},{20,16},{24,28},{28,24},{1,5},{5... | collective-permute-start | bytes 1572872 | tf_op jit(solution)/shard_map/ppermute | solution.py:77
  215.2 35.0 %collective-permute-start.34 = (bf16[128,2048]{1,0:T(8,128)(2,1)S(1)}, bf16[128,2048]{1,0:T(8,128)(2,1)S(1)}, u32[]{:S(2)}, u32[]{:S(2)}) collective-permute-start(bf16[128,2048]{1,0:T(8,128)(2,1)S(1)} %add_convert_fusion.4), channel_id=1, source_target_pairs={{0,2},{1,3},{2,0},{3,1},{4,6},{5,7},{6,4},{7,5},{8,10},{9,11},{10,... | collective-permute-start | bytes 1572872 | tf_op jit(solution)/shard_map/ppermute | solution.py:77
  216.2 34.0 %collective-permute-start.31 = (bf16[64,2048]{1,0:T(8,128)(2,1)S(1)}, bf16[64,2048]{1,0:T(8,128)(2,1)S(1)}, u32[]{:S(2)}, u32[]{:S(2)}) collective-permute-start(bf16[64,2048]{1,0:T(8,128)(2,1)S(1)} %add_convert_fusion.17), channel_id=1, source_target_pairs={{0,2},{1,3},{2,0},{3,1},{4,6},{5,7},{6,4},{7,5},{8,10},{9,11},{10,... | collective-permute-start | bytes 786440 | tf_op jit(solution)/shard_map/ppermute | solution.py:77
  217.5 32.7 %collective-permute-start.30 = (bf16[64,2048]{1,0:T(8,128)(2,1)S(1)}, bf16[64,2048]{1,0:T(8,128)(2,1)}, u32[]{:S(2)}, u32[]{:S(2)}) collective-permute-start(bf16[64,2048]{1,0:T(8,128)(2,1)S(1)} %add_convert_fusion.18), channel_id=1, source_target_pairs={{0,4},{4,0},{8,12},{12,8},{16,20},{20,16},{24,28},{28,24},{1,5},{5... | collective-permute-start | bytes 786440 | tf_op jit(solution)/shard_map/ppermute | solution.py:77
  218.1 32.1 %collective-permute-start.32 = (bf16[128,2048]{1,0:T(8,128)(2,1)}, bf16[128,2048]{1,0:T(8,128)(2,1)S(1)}, u32[]{:S(2)}, u32[]{:S(2)}) collective-permute-start(bf16[128,2048]{1,0:T(8,128)(2,1)} %get-tuple-element.389), channel_id=1, source_target_pairs={{0,2},{1,3},{2,0},{3,1},{4,6},{5,7},{6,4},{7,5},{8,10},{9,11},{10,... | collective-permute-start | bytes 1572872 | tf_op jit(solution)/shard_map/ppermute | solution.py:77
  219.0 31.2 %collective-permute-start.33 = (bf16[128,2048]{1,0:T(8,128)(2,1)}, bf16[128,2048]{1,0:T(8,128)(2,1)S(1)}, u32[]{:S(2)}, u32[]{:S(2)}) collective-permute-start(bf16[128,2048]{1,0:T(8,128)(2,1)} %get-tuple-element.390), channel_id=1, source_target_pairs={{0,4},{4,0},{8,12},{12,8},{16,20},{20,16},{24,28},{28,24},{1,5},{5... | collective-permute-start | bytes 1572872 | tf_op jit(solution)/shard_map/ppermute | solution.py:77
  250.9 21.9 %collective-permute-start.39 = (bf16[64,2048]{1,0:T(8,128)(2,1)S(1)}, bf16[64,2048]{1,0:T(8,128)(2,1)S(1)}, u32[]{:S(2)}, u32[]{:S(2)}) collective-permute-start(bf16[64,2048]{1,0:T(8,128)(2,1)S(1)} %add_convert_fusion.13), channel_id=1, source_target_pairs={{0,2},{1,3},{2,0},{3,1},{4,6},{5,7},{6,4},{7,5},{8,10},{9,11},{10,... | collective-permute-start | bytes 786440 | tf_op jit(solution)/shard_map/ppermute | solution.py:77
  252.9 19.9 %collective-permute-start.38 = (bf16[64,2048]{1,0:T(8,128)(2,1)}, bf16[64,2048]{1,0:T(8,128)(2,1)S(1)}, u32[]{:S(2)}, u32[]{:S(2)}) collective-permute-start(bf16[64,2048]{1,0:T(8,128)(2,1)} %add_convert_fusion.14), channel_id=1, source_target_pairs={{0,4},{4,0},{8,12},{12,8},{16,20},{20,16},{24,28},{28,24},{1,5},{5... | collective-permute-start | bytes 786440 | tf_op jit(solution)/shard_map/ppermute | solution.py:77
  254.7 18.2 %collective-permute-start.35 = (bf16[128,2048]{1,0:T(8,128)(2,1)S(1)}, bf16[128,2048]{1,0:T(8,128)(2,1)S(1)}, u32[]{:S(2)}, u32[]{:S(2)}) collective-permute-start(bf16[128,2048]{1,0:T(8,128)(2,1)S(1)} %pad_maximum_fusion.3), channel_id=1, source_target_pairs={{0,8},{4,12},{8,16},{12,20},{16,24},{20,28},{24,0},{28,4},{1,9},{5... | collective-permute-start | bytes 1572872 | tf_op jit(solution)/shard_map/ppermute | solution.py:77
  257.3 15.5 %collective-permute-start.36 = (bf16[128,2048]{1,0:T(8,128)(2,1)}, bf16[128,2048]{1,0:T(8,128)(2,1)S(1)}, u32[]{:S(2)}, u32[]{:S(2)}) collective-permute-start(bf16[128,2048]{1,0:T(8,128)(2,1)} %get-tuple-element.407), channel_id=1, source_target_pairs={{0,2},{1,3},{2,0},{3,1},{4,6},{5,7},{6,4},{7,5},{8,10},{9,11},{10,... | collective-permute-start | bytes 1572872 | tf_op jit(solution)/shard_map/ppermute | solution.py:77
  318.0 21.5 %collective-permute-start.48 = (bf16[128,2048]{1,0:T(8,128)(2,1)}, bf16[128,2048]{1,0:T(8,128)(2,1)}, u32[]{:S(2)}, u32[]{:S(2)}) collective-permute-start(bf16[128,2048]{1,0:T(8,128)(2,1)} %get-tuple-element.501), channel_id=1, source_target_pairs={{0,4},{4,0},{8,12},{12,8},{16,20},{20,16},{24,28},{28,24},{1,5},{5... | collective-permute-start | bytes 1572872 | tf_op jit(solution)/shard_map/ppermute | solution.py:77
  318.0 25.4 %collective-permute-start.49 = (bf16[128,2048]{1,0:T(8,128)(2,1)}, bf16[128,2048]{1,0:T(8,128)(2,1)S(1)}, u32[]{:S(2)}, u32[]{:S(2)}) collective-permute-start(bf16[128,2048]{1,0:T(8,128)(2,1)} %get-tuple-element.502), channel_id=1, source_target_pairs={{0,4},{4,0},{8,12},{12,8},{16,20},{20,16},{24,28},{28,24},{1,5},{5... | collective-permute-start | bytes 1572872 | tf_op jit(solution)/shard_map/ppermute | solution.py:77
  320.0 23.4 %collective-permute-start.50 = (bf16[128,2048]{1,0:T(8,128)(2,1)}, bf16[128,2048]{1,0:T(8,128)(2,1)S(1)}, u32[]{:S(2)}, u32[]{:S(2)}) collective-permute-start(bf16[128,2048]{1,0:T(8,128)(2,1)} %get-tuple-element.503), channel_id=1, source_target_pairs={{0,24},{4,28},{8,0},{12,4},{16,8},{20,12},{24,16},{28,20},{1,25},{... | collective-permute-start | bytes 1572872 | tf_op jit(solution)/shard_map/ppermute | solution.py:77
  321.2 23.6 %collective-permute-start.51 = (bf16[128,2048]{1,0:T(8,128)(2,1)}, bf16[128,2048]{1,0:T(8,128)(2,1)S(1)}, u32[]{:S(2)}, u32[]{:S(2)}) collective-permute-start(bf16[128,2048]{1,0:T(8,128)(2,1)} %get-tuple-element.504), channel_id=1, source_target_pairs={{0,24},{4,28},{8,0},{12,4},{16,8},{20,12},{24,16},{28,20},{1,25},{... | collective-permute-start | bytes 1572872 | tf_op jit(solution)/shard_map/ppermute | solution.py:77
  355.8 17.1 %collective-permute-start.56 = (bf16[256,1024]{1,0:T(8,128)(2,1)S(1)}, bf16[256,1024]{1,0:T(8,128)(2,1)S(1)}, u32[]{:S(2)}, u32[]{:S(2)}) collective-permute-start(bf16[256,1024]{1,0:T(8,128)(2,1)S(1)} %pad_maximum_fusion.4), channel_id=1, source_target_pairs={{0,2},{1,3},{2,0},{3,1},{4,6},{5,7},{6,4},{7,5},{8,10},{9,11},{10,... | collective-permute-start | bytes 1572872 | tf_op jit(solution)/shard_map/ppermute | solution.py:77
  357.0 16.0 %collective-permute-start.57 = (bf16[128,2048]{1,0:T(8,128)(2,1)S(1)}, bf16[128,2048]{1,0:T(8,128)(2,1)S(1)}, u32[]{:S(2)}, u32[]{:S(2)}) collective-permute-start(bf16[128,2048]{1,0:T(8,128)(2,1)S(1)} %copy-done.64), channel_id=1, source_target_pairs={{0,4},{4,0},{8,12},{12,8},{16,20},{20,16},{24,28},{28,24},{1,5},{5... | collective-permute-start | bytes 1572872 | tf_op jit(solution)/shard_map/ppermute | solution.py:77
  357.3 15.7 %collective-permute-start.58 = (bf16[128,2048]{1,0:T(8,128)(2,1)S(1)}, bf16[128,2048]{1,0:T(8,128)(2,1)S(1)}, u32[]{:S(2)}, u32[]{:S(2)}) collective-permute-start(bf16[128,2048]{1,0:T(8,128)(2,1)S(1)} %copy-done.65), channel_id=1, source_target_pairs={{0,24},{4,28},{8,0},{12,4},{16,8},{20,12},{24,16},{28,20},{1,25},{... | collective-permute-start | bytes 1572872 | tf_op jit(solution)/shard_map/ppermute | solution.py:77
  405.8 15.2 %collective-permute-start.65 = (bf16[128,2048]{1,0:T(8,128)(2,1)}, bf16[128,2048]{1,0:T(8,128)(2,1)}, u32[]{:S(2)}, u32[]{:S(2)}) collective-permute-start(bf16[128,2048]{1,0:T(8,128)(2,1)} %shard_map.259.refs_0_), channel_id=1, source_target_pairs={{0,2},{1,3},{2,0},{3,1},{4,6},{5,7},{6,4},{7,5},{8,10},{9,11},{10,... | collective-permute-start | bytes 1572872 | tf_op jit(solution)/shard_map/ppermute | solution.py:77
  407.1 22.1 %collective-permute-start.66 = (bf16[256,1024]{1,0:T(8,128)(2,1)S(1)}, bf16[256,1024]{1,0:T(8,128)(2,1)S(1)}, u32[]{:S(2)}, u32[]{:S(2)}) collective-permute-start(bf16[256,1024]{1,0:T(8,128)(2,1)S(1)} %pad_maximum_fusion.5), channel_id=1, source_target_pairs={{0,2},{1,3},{2,0},{3,1},{4,6},{5,7},{6,4},{7,5},{8,10},{9,11},{10,... | collective-permute-start | bytes 1572872 | tf_op jit(solution)/shard_map/ppermute | solution.py:77
  421.1 19.3 %collective-permute-start.69 = (bf16[256,2048]{1,0:T(8,128)(2,1)S(1)}, bf16[256,2048]{1,0:T(8,128)(2,1)S(1)}, u32[]{:S(2)}, u32[]{:S(2)}) collective-permute-start(bf16[256,2048]{1,0:T(8,128)(2,1)S(1)} %pad_maximum_fusion.1), channel_id=1, source_target_pairs={{0,4},{4,0},{8,12},{12,8},{16,20},{20,16},{24,28},{28,24},{1,5},{5... | collective-permute-start | bytes 3145736 | tf_op jit(solution)/shard_map/ppermute | solution.py:77
  431.0 19.1 %collective-permute-start.75 = (bf16[128,2048]{1,0:T(8,128)(2,1)S(1)}, bf16[128,2048]{1,0:T(8,128)(2,1)S(1)}, u32[]{:S(2)}, u32[]{:S(2)}) collective-permute-start(bf16[128,2048]{1,0:T(8,128)(2,1)S(1)} %copy-done.3), channel_id=1, source_target_pairs={{0,1},{1,0},{2,3},{3,2},{4,5},{5,4},{6,7},{7,6},{8,9},{9,8},{10,11... | collective-permute-start | bytes 1572872 | tf_op jit(solution)/shard_map/ppermute | solution.py:77
  431.0 19.0 %collective-permute-start.76 = (bf16[128,2048]{1,0:T(8,128)(2,1)}, bf16[128,2048]{1,0:T(8,128)(2,1)}, u32[]{:S(2)}, u32[]{:S(2)}) collective-permute-start(bf16[128,2048]{1,0:T(8,128)(2,1)} %collective-permute-done.65.refs_1_), channel_id=1, source_target_pairs={{0,1},{1,0},{2,3},{3,2},{4,5},{5,4},{6,7},{7,6},{8,9},{9,8},{10,11... | collective-permute-start | bytes 1572872 | tf_op jit(solution)/shard_map/ppermute | solution.py:77
  431.8 15.8 %collective-permute-start.73 = (bf16[256,1024]{1,0:T(8,128)(2,1)S(1)}, bf16[256,1024]{1,0:T(8,128)(2,1)S(1)}, u32[]{:S(2)}, u32[]{:S(2)}) collective-permute-start(bf16[256,1024]{1,0:T(8,128)(2,1)S(1)} %fusion.4), channel_id=1, source_target_pairs={{0,8},{4,12},{8,16},{12,20},{16,24},{20,28},{24,0},{28,4},{1,9},{5... | collective-permute-start | bytes 1572872 | tf_op jit(solution)/shard_map/ppermute | solution.py:77
  (100 other events, 941.4 us)

commit v8 on v7

--- a/solution.py
+++ b/solution.py
@@ -198,7 +198,7 @@
 
 
 def kernel_call(kernel, grid, in_specs, out_specs, out_shape, operands, flops, scratch=(), scalars=0):
-    moved = sum(array.size * array.dtype.itemsize for array in operands)
+    moved = sum(array.size * array.dtype.itemsize for array in operands) if flops else 0
     return pl.pallas_call(
         kernel,
         grid_spec=pltpu.PrefetchScalarGridSpec(
@@ -306,73 +306,58 @@
 
 def attend_kernel(
     width, size, core, squares, query_raw, key_raw, value_raw, query_gain, key_gain, cosine, sine,
-    mask, output_weight, mix_in, queries, keys, values, attended, mine, theirs, held, weight, scales, sem,
+    mask, output_weight, mix_in, queries, keys, values, attended, mine, theirs, held, weight, sem,
 ):
-    head = pl.program_id(0)
-    last = pl.num_programs(0) - 1
     copy = pltpu.make_async_copy(output_weight, weight, sem)
-
-    @pl.when(head == 0)
-    def _():
-        copy.start()
-        scales[...] = lax.rsqrt(spread_columns(squares[...]) / width + EPSILON)
-
-    inverse = scales[:, :2]
-    query = query_raw[...] * inverse[:, 0:1] * wide(query_gain[...])
-    key = key_raw[...] * inverse[:, 1:2] * wide(key_gain[...])
-    query = low(query * cosine[...] + turned(query) * sine[...])
-    key = low(key * cosine[...] + turned(key) * sine[...])
-    value = low(value_raw[...])
-    queries[...] = query
-    keys[...] = key
-    values[...] = value
-    scores = dot_t(query, key) * HD ** (-0.5) + mask[...]
-    raised = jnp.exp(scores - jnp.max(scores, axis=1, keepdims=True))
-    weights = low(raised * (1.0 / jnp.sum(raised, axis=1, keepdims=True)))
-    result = low(dot(weights, value))
-    attended[...] = result
-    held[head] = result
-
-    @pl.when(head == last)
-    def _():
-        copy.wait()
-        heads = held.shape[0]
-        levels = mine.shape[0] // size
-        for out, offset in ((mine, core[0]), (theirs, 1 - core[0])):
-            taken = []
-            for level in range(levels):
-                rows = pl.ds(pl.multiple_of((2 * level + offset) * size, size), size)
-                taken.append(
-                    jnp.concatenate([held[index, rows, :] for index in range(heads)], axis=1)
-                )
-            taken = jnp.concatenate(taken, axis=0)
-            out[:, :width] = dot(taken, weight[...]).astype(out.dtype)
-            out[:, width:] = dot(taken, mix_in[...]).astype(out.dtype)
+    copy.start()
+    inverse = lax.rsqrt(spread_columns(squares[...]) / width + EPSILON)
+    heads = query_raw.shape[1] // HD
+    for head in range(heads):
+        part = slice(head * HD, (head + 1) * HD)
+        query = query_raw[:, part] * inverse[:, 0:1] * wide(query_gain[:, part])
+        key = key_raw[:, part] * inverse[:, 1:2] * wide(key_gain[:, part])
+        query = low(query * cosine[...] + turned(query) * sine[...])
+        key = low(key * cosine[...] + turned(key) * sine[...])
+        value = low(value_raw[:, part])
+        queries[:, part] = query
+        keys[:, part] = key
+        values[:, part] = value
+        scores = dot_t(query, key) * HD ** (-0.5) + mask[...]
+        raised = jnp.exp(scores - jnp.max(scores, axis=1, keepdims=True))
+        weights = low(raised * (1.0 / jnp.sum(raised, axis=1, keepdims=True)))
+        result = low(dot(weights, value))
+        attended[:, part] = result
+        held[:, part] = result
+    copy.wait()
+    levels = mine.shape[0] // size
+    for out, offset in ((theirs, 1 - core[0]), (mine, core[0])):
+        taken = [
+            held[pl.ds(pl.multiple_of((2 * level + offset) * size, size), size), :]
+            for level in range(levels)
+        ]
+        taken = jnp.concatenate(taken, axis=0)
+        out[:, :width] = dot(taken, weight[...]).astype(out.dtype)
+        out[:, width:] = dot(taken, mix_in[...]).astype(out.dtype)
 
 
 def attend_call(core, squares, raws, gains, tables, mask, output_weight, mix_in, size):
     rows, local = raws[0].shape
-    heads = local // HD
     width = output_weight.shape[1]
     wide_width = width + mix_in.shape[1]
-    block = pl.BlockSpec((rows, HD), lambda head, *_: (0, head))
-    gain_block = pl.BlockSpec((1, HD), lambda head, *_: (0, head))
-    fixed = pl.BlockSpec((rows // 2, wide_width), lambda *_: (0, 0))
     operands = [core, squares, *raws, *gains, *tables, mask, output_weight, mix_in]
+    out_shape = [((rows, local), jnp.bfloat16)] * 4
+    out_shape += [((rows // 2, wide_width), jnp.float32), ((rows // 2, wide_width), jnp.bfloat16)]
     return kernel_call(
         functools.partial(attend_kernel, width, size),
-        (heads,),
-        [whole(squares)] + [block] * 3 + [gain_block] * 2
-        + [whole(tables[0]), whole(tables[1]), whole(mask), ANY, whole(mix_in)],
-        [block] * 4 + [fixed] * 2,
-        [((rows, local), jnp.bfloat16)] * 4
-        + [((rows // 2, wide_width), jnp.float32), ((rows // 2, wide_width), jnp.bfloat16)],
+        (1,),
+        [whole(array) for array in operands[1:-2]] + [ANY, whole(mix_in)],
+        [pl.BlockSpec(shape, lambda *_: (0, 0)) for shape, _ in out_shape],
+        out_shape,
         operands,
         4 * rows * rows * local + 2 * rows * local * width,
         [
-            pltpu.VMEM((heads, rows, HD), jnp.bfloat16),
+            pltpu.VMEM((rows, local), jnp.bfloat16),
             pltpu.VMEM(output_weight.shape, jnp.bfloat16),
-            pltpu.VMEM((rows, 128), jnp.float32),
             pltpu.SemaphoreType.DMA,
         ],
         1,
@@ -405,7 +390,7 @@
         [pl.BlockSpec(shape, lambda *_: (0, 0)) for shape, _ in out_shape],
         out_shape,
         operands,
-        2 * rows * width * mix_out.shape[0],
+        0,
         (),
         1,
     )
@@ -868,7 +853,7 @@
         [pl.BlockSpec((size, tile), lambda n: (0, n))] * (count * near * span),
         [((size, width), jnp.bfloat16)] * (count * near * span),
         [*hiddens, *downs],
-        4 * count * rows * hidden * width,
+        0,
     )
     blocks = [list(outs[index * span : (index + 1) * span]) for index in range(count * near)]
     return [blocks[index * near : (index + 1) * near] for index in range(count)]
@@ -1004,7 +989,7 @@
         [pl.BlockSpec(shape, lambda *_, size=len(shape): (0,) * size) for shape, _ in out_shape],
         out_shape,
         operands,
-        6 * rows * local * 256,
+        0,
     )
 
 
@@ -1035,7 +1020,7 @@
         [pl.BlockSpec((rows // 2, tile), lambda n, *_: (0, n))] * 2,
         out_shape,
         operands,
-        6 * rows * local * width,
+        0,
         (),
         1,
     )
@@ -1077,7 +1062,7 @@
         [pl.BlockSpec((rows, width), lambda *_: (0, 0))],
         [((rows, width), jnp.bfloat16)],
         operands,
-        8 * rows * width * 128,
+        0,
         (),
         1,
     )[0]
@@ -1111,7 +1096,7 @@
         [pl.BlockSpec((9 * RANK, share), lambda *_: (0, 0))],
         [((9 * RANK, share), jnp.bfloat16)],
         operands,
-        2 * rows * share * 128,
+        0,
         [pltpu.VMEM((rows, share), jnp.bfloat16), pltpu.SemaphoreType.DMA],
         1,
     )[0]
@@ -1137,7 +1122,7 @@
         [pl.BlockSpec((size, width), lambda step, order: (order[step], 0))],
         [((count * size, width), jnp.float32)],
         [order, *pieces],
-        size * width,
+        0,
         (),
         1,
     )[0]
@@ -1191,7 +1176,7 @@
         [pl.BlockSpec(shape, lambda *_, size=len(shape): (0,) * size) for shape, _ in out_shape],
         out_shape,
         operands,
-        2 * trees * RANK * 128 * width * 4,
+        0,
         [pltpu.VMEM((trees * RANK, 128), jnp.bfloat16)],
         1,
     )
@@ -1555,23 +1540,29 @@
     held = (normed_mine, normed_theirs, lowrank_parts, mix_parts[3], mix_last, mix_near, mixes)
     held = hold(held)
     normed_mine, normed_theirs, lowrank_parts, mix_parts[3], mix_last, mix_near, mixes = held
-    normed_theirs = hold(turn(normed_theirs, axes, "c", 1))
+    for across in range(1, near):
+        pairs = zip(mixes[0][across], mix_far[across - 1])
+        mixes[0][across] = [low(wide(mine) + wide(other)) for mine, other in pairs]
+    normed_theirs, mixes = hold((turn(normed_theirs, axes, "c", 1), mixes))
     normed_kept, normed_sent = scatter_core(normed_mine, normed_theirs, axes)
     held = (normed_sent, lowrank_parts, mixes, mix_last)
     normed_sent, lowrank_parts, mixes, mix_last = hold(held)
     normed_came = turn(normed_sent, axes, "y", -1)
     lowrank_grad = low(sum(wide(part) for part in lowrank_parts))
-    mix_near = mix_near + [turn(part, axes, "z", -1) for part in mixes[1][0][1:]]
+    mix_came[0] = [mix_send(0, 0)]
     compact = compact_call(
         rank_list, lowrank_grad, normed_in, mix_out_grad, adapt_grad, mix_in_grad, select
     )
-    trees = ring(compact, axes, "x")
+    tree_queue = [compact, turn(compact, axes, "z", 1)]
+    mix_near = mix_near + [turn(part, axes, "z", -1) for part in mixes[1][0][1:]]
     mix_held[2] = list(zip(mixes[2][0], [mix_next] + mix_last))
     mix_ready = mix_sent(2)
-    trees, mix_near, mix_ready, normed_came = hold((trees, mix_near, mix_ready, normed_came))
-
-    tree_queue = [jnp.concatenate(trees, axis=0)]
+    held = (tree_queue, mix_ready, normed_came, mix_came[0], mix_near, mixes)
+    tree_queue, mix_ready, normed_came, mix_came[0], mix_near, mixes = hold(held)
+
     tree_queue.append(turn(tree_queue[-1], axes, "z", 1))
+    mix_parts[2] = mix_down(2, mix_ready)
+    mix_came[0] = mix_came[0] + [mix_send(0, down) for down in range(1, span)]
     input_rows = input_call(
         rank_list,
         normed_kept,
@@ -1586,37 +1577,29 @@
     input_rows, tree_queue = hold((input_rows, tree_queue))
     input_held = ring(input_rows, axes, "y")
     tree_queue.append(turn(tree_queue[-1], axes, "z", 1))
-    for across in range(1, near):
-        pairs = zip(mixes[0][across], mix_far[across - 1])
-        mixes[0][across] = [low(wide(mine) + wide(other)) for mine, other in pairs]
-    whole_blocks = [jnp.concatenate(blocks, axis=0) for blocks in mixes[0][1:]]
-    mix_came[0] = send_sum([None] + whole_blocks, axes, "x")
-    mix_parts[2] = mix_down(2, mix_ready)
-    tree_queue, mixes, input_held = hold((tree_queue, mixes, input_held))
-    tree_queue.append(turn(tree_queue[-1], axes, "z", 1))
+    held = (tree_queue, mix_came[0], mix_parts[2])
+    tree_queue, mix_came[0], mix_parts[2] = hold(held)
+
+    trees = ring(jnp.concatenate(tree_queue, axis=0), axes, "x")
+    mix_sum = turn(low(mix_total(2)), axes, "z", 1)
+    mix_held[0] = [list(arrays) for arrays in zip(mixes[0][0], mix_came[0], mix_near)]
+    mix_held[0][0].append(resid_rows)
+    mix_parts[0] = mix_down(0, mix_sent(0))
+    held = (trees, mix_sum, mix_parts[0], input_held)
+    trees, mix_sum, mix_parts[0], input_held = hold(held)
     input_pieces = input_held + [turn(piece, axes, "c", 1) for piece in input_held]
-    mix_parts[2], tree_queue = hold((mix_parts[2], tree_queue))
-
-    trees = jnp.concatenate(tree_queue, axis=0)
+    trees = jnp.concatenate(trees, axis=0)
     shared = trees.reshape(owners, -1, column_share)[:, : 4 * RANK]
     shared = ring(shared.reshape(-1, column_share), axes, "y")
-    mix_sum = turn(low(mix_total(2)), axes, "z", 1)
-    shared, mix_came[0] = hold((shared, mix_came[0]))
-    arrived = [mix_came[0][down * row_share : (down + 1) * row_share] for down in range(span)]
-    mix_held[0] = [list(arrays) for arrays in zip(mixes[0][0], arrived, mix_near)]
-    mix_held[0][0].append(resid_rows)
+    mix_sum = turn(low(wide(mix_sum) + mix_total(3)), axes, "z", 1)
+    input_grad = spread_call(order, input_pieces)
+    shared, mix_sum, input_grad = hold((shared, mix_sum, input_grad))
     shared = shared + [turn(piece, axes, "c", 1) for piece in shared]
-    mix_parts[0] = mix_down(0, mix_sent(0))
-    shared, mix_sum = hold((shared, mix_sum))
-    mix_sum = turn(low(wide(mix_sum) + mix_total(3)), axes, "z", 1)
+    layer_columns = low(mix_total(0) + wide(mix_sum))
+    layer_out = place_columns(layer_columns, axes)
     grad_adapt_in, grad_adapt_out, grad_adapt_in_out, grad_adapt_out_out = assemble_call(
         order, trees, shared[1:], owners
     )
-    input_grad = spread_call(order, input_pieces)
-    held = (mix_parts[0], mix_sum, grad_adapt_in, input_grad)
-    mix_parts[0], mix_sum, grad_adapt_in, input_grad = hold(held)
-    layer_columns = low(mix_total(0) + wide(mix_sum))
-    layer_out = place_columns(layer_columns, axes)
     return (
         layer_out,
         input_grad,

time: 476 us -> 469 us (0.985)
  waiting for transfers between devices: 121 us -> 115 us
    ppermute x78 -> x79, waiting for transfers between devices: 121 us -> 115 us  [turn(): return lax.ppermute(array, axis, pairs)]
    ppermute x78 -> x79, starting transfers between devices: 67.5 us -> 67.9 us  [turn(): return lax.ppermute(array, axis, pairs)]
  transfers between devices with their start and end apart: 78 -> 79, of which waited for: 30 -> 28; matrix products, arithmetic and copies ran while one was open for 5% -> 6% of each run, Pallas kernels for 49% -> 49%
where the time goes in v8:
time: 469 us; the launch traced here: 460 us
  Pallas kernels  232 us (49%)
  waiting for transfers between devices  115 us (25%)
  starting transfers between devices  67.9 us (14%)
  other arithmetic  28.9 us (6%)
  local copies, waits for them, and re-layouts  12.9 us (3%)
    pallas_call x18, Pallas kernels, kernel_call(): pl.pallas_call(kernel, grid_spec=pltpu.PrefetchScalarGridSpec(num_scalar_...  232 us
    ppermute x79, waiting for transfers between devices, turn(): return lax.ppermute(array, axis, pairs)  115 us
    ppermute x79, starting transfers between devices, turn(): return lax.ppermute(array, axis, pairs)  67.9 us
    convert_element_type x22, other arithmetic, low(): return array.astype(jnp.bfloat16)  13.9 us
  transfers between devices with their start and end apart: 79, of which 28 were waited for; matrix products, arithmetic and copies ran while one was open for 6% of the time, Pallas kernels for 49%

profile of v8, /device:TPU:0, one launch (start us, length us, event | category | flops | bytes accessed | tf_op | source)
XLA Modules:
  0.0 459.6 jit_solution(12113434778085129361)
XLA Ops:
  3.5 3.1 collective-permute-start.2
  9.3 13.1 %shard_map.244 = (bf16[512,2048]{1,0:T(8,128)(2,1)}, bf16[3,512,128]{2,1,0:T(8,128)(2,1)}, f32[512,512]{1,0:T(8,128)}, f32[512,512]{1,0:T(8,128)}, f32[512,512]{1,0:T(8,128)}, /*index=5*/f32[8,512]{1,0:T(8,128)}) custom-call(bf16[512,2048]{1,0:T(8,128)(2,1)} %tokens.5, bf16[1,2048]{1,0:T(2,128)(2,1)} %broadcast_in_dim.43.gain, ...), custom_call_target="tpu_custom_call" | custom-call | flops 3221225472 | bytes 10359296 | tf_op jit(solution)/shard_map/pallas_call | solution.py:202
  26.5 1.8 sine_multiply_fusion
  29.4 3.8 collective-permute-done.2
  37.5 9.8 %shard_map.245 = (bf16[512,512]{1,0:T(8,128)(2,1)}, bf16[512,512]{1,0:T(8,128)(2,1)}, bf16[512,512]{1,0:T(8,128)(2,1)}, bf16[512,512]{1,0:T(8,128)(2,1)}, f32[25...) custom-call(s32[1]{0:T(128)} %bitcast.1.core.scalars, f32[8,512]{1,0:T(8,128)} %add.407.squares, ...), custom_call_target="tpu_custom_call" | custom-call | flops 1610612736 | bytes 6965252 | tf_op jit(solution)/shard_map/pallas_call | solution.py:202
  47.3 2.9 collective-permute-done.4
  50.3 2.9 collective-permute-done.6
  53.2 2.7 add_convert_fusion
  59.4 11.2 %collective-permute-done.7.came = bf16[128,2176]{1,0:T(8,128)(2,1)S(1)} collective-permute-done((bf16[128,2176]{1,0:T(8,128)(2,1)S(1)}, bf16[128,2176]{1,0:T(8,128)(2,1)S(1)}, u32[]{:S(2)}, u32[]{:S(2)}) %collective-permute-start.7) | collective-permute-done | bytes 557088 | tf_op jit(solution)/shard_map/ppermute | solution.py:77
  70.6 3.0 collective-permute-done.8
  74.5 3.9 shard_map.246
  80.9 13.7 %collective-permute-done.12 = bf16[128,2048]{1,0:T(8,128)(2,1)S(1)} collective-permute-done((bf16[128,2048]{1,0:T(8,128)(2,1)}, bf16[128,2048]{1,0:T(8,128)(2,1)S(1)}, u32[]{:S(2)}, u32[]{:S(2)}) %collective-permute-start.12) | collective-permute-done | bytes 524320 | tf_op jit(solution)/shard_map/ppermute | solution.py:77
  98.0 16.6 %shard_map.247 = (bf16[8,1024,256]{2,1,0:T(8,128)(2,1)}, bf16[1024,128]{1,0:T(8,128)(2,1)}) custom-call(bf16[256,2176]{1,0:T(8,128)(2,1)} %copy-done.7, bf16[256,2176]{1,0:T(8,128)(2,1)} %copy-done.51, bf16[128,2176]{1,0:T(8,128)(2,1)} %copy-done.12, bf16[128,2176]{1,0:T(8,128)(2,1)} %copy-done.11, bf16[128,2176]{1,0:T(8,128)(2,1)} %copy-done.56, ...), custom_call_target="tpu_custom_call" | custom-call | flops 8589934592 | bytes 13107200 | tf_op jit(solution)/shard_map/pallas_call | solution.py:202
  114.6 5.0 %collective-permute-done.15.refs_1_ = bf16[256,2048]{1,0:T(8,128)(2,1)S(1)} collective-permute-done((bf16[256,2048]{1,0:T(8,128)(2,1)S(1)}, bf16[256,2048]{1,0:T(8,128)(2,1)S(1)}, u32[]{:S(2)}, u32[]{:S(2)}) %collective-permute-start.15) | collective-permute-done | bytes 1048608 | tf_op jit(solution)/shard_map/ppermute | solution.py:77
  122.8 25.8 %shard_map.248 = (bf16[256,2048]{1,0:T(8,128)(2,1)}, bf16[256,2048]{1,0:T(8,128)(2,1)}, bf16[8,512,256]{2,1,0:T(8,128)(2,1)}) custom-call(bf16[256,2048]{1,0:T(8,128)(2,1)} %copy-done.40, bf16[256,2048]{1,0:T(8,128)(2,1)} %copy-done.54, bf16[4,2048,256]{2,1,0:T(8,128)(2,1)} %refs_2_.3, bf16[4,2048,256]{2,1,0:T(8,128)(2,1)} %refs_3_.3, ...), custom_call_target="tpu_custom_call" | custom-call | flops 17179869184 | bytes 23592960 | tf_op jit(solution)/shard_map/pallas_call | solution.py:202
  152.3 25.7 %shard_map.249 = (bf16[128,2048]{1,0:T(8,128)(2,1)}, bf16[128,2048]{1,0:T(8,128)(2,1)}, bf16[128,2048]{1,0:T(8,128)(2,1)}, bf16[128,2048]{1,0:T(8,128)(2,1)}, bf16[8,512,256]{2,1,0:T(8,128)(2,1)}) custom-call(bf16[256,2048]{1,0:T(8,128)(2,1)} %copy-done.41, bf16[256,2048]{1,0:T(8,128)(2,1)} %collective-permute-done.18.refs_1_, ...), custom_call_target="tpu_custom_call" | custom-call | flops 17179869184 | bytes 23592960 | tf_op jit(solution)/shard_map/pallas_call | solution.py:202
  179.7 2.5 collective-permute-start.29
  185.2 29.8 %shard_map.250 = (bf16[128,2048]{1,0:T(8,128)(2,1)}, bf16[128,2048]{1,0:T(8,128)(2,1)}, bf16[128,2048]{1,0:T(8,128)(2,1)}, bf16[128,2048]{1,0:T(8,128)(2,1)}, bf16[8,512,256]{2,1,0:T(8,128)(2,1)}) custom-call(bf16[256,2048]{1,0:T(8,128)(2,1)} %copy-done.42, bf16[256,2048]{1,0:T(8,128)(2,1)} %copy-done.55, bf16[4,2048,256]{2,1,0:T(8,128)(2,1)} %refs_2_.3, ...), custom_call_target="tpu_custom_call" | custom-call | flops 21474836480 | bytes 29753344 | tf_op jit(solution)/shard_map/pallas_call | solution.py:202
  221.1 29.7 %shard_map.251 = (bf16[128,2048]{1,0:T(8,128)(2,1)}, bf16[128,2048]{1,0:T(8,128)(2,1)}, bf16[128,2048]{1,0:T(8,128)(2,1)}, bf16[128,2048]{1,0:T(8,128)(2,1)}, bf16[8,512,256]{2,1,0:T(8,128)(2,1)}) custom-call(bf16[256,2048]{1,0:T(8,128)(2,1)} %copy-done.43, bf16[256,2048]{1,0:T(8,128)(2,1)} %collective-permute-done.25.refs_1_, ...), custom_call_target="tpu_custom_call" | custom-call | flops 21474836480 | bytes 29753344 | tf_op jit(solution)/shard_map/pallas_call | solution.py:202
  253.8 2.6 collective-permute-start.35
  259.1 13.1 %shard_map.252 = (bf16[128,2048]{1,0:T(8,128)(2,1)}, bf16[128,2048]{1,0:T(8,128)(2,1)}, bf16[128,2048]{1,0:T(8,128)(2,1)}, bf16[128,2048]{1,0:T(8,128)(2,1)}, bf...) custom-call(bf16[8,512,256]{2,1,0:T(8,128)(2,1)} %get-tuple-element., ...), custom_call_target="tpu_custom_call" | custom-call | tf_op jit(solution)/shard_map/pallas_call | solution.py:202
  275.8 8.5 %shard_map.253 = (bf16[128,2048]{1,0:T(8,128)(2,1)}, bf16[128,2048]{1,0:T(8,128)(2,1)}, bf16[128,2048]{1,0:T(8,128)(2,1)}, bf16[128,2048]{1,0:T(8,128)(2,1)}) custom-call(bf16[8,512,256]{2,1,0:T(8,128)(2,1)} %get-tuple-element.440.refs_0_, bf16[1024,2048]{1,0:T(8,128)(2,1)} %bitcast.11.refs_6_.refs_7_.refs_2_.refs_1_, ...), custom_call_target="tpu_custom_call" | custom-call | tf_op jit(solution)/shard_map/pallas_call | solution.py:202
  284.3 4.1 collective-permute-done.40
  289.6 8.7 %shard_map.254 = (bf16[128,2048]{1,0:T(8,128)(2,1)}, bf16[128,2048]{1,0:T(8,128)(2,1)}, bf16[128,2048]{1,0:T(8,128)(2,1)}, bf16[128,2048]{1,0:T(8,128)(2,1)}) custom-call(bf16[8,512,256]{2,1,0:T(8,128)(2,1)} %get-tuple-element.452.refs_0_, bf16[1024,2048]{1,0:T(8,128)(2,1)} %bitcast.11.refs_6_.refs_7_.refs_2_.refs_1_, ...), custom_call_target="tpu_custom_call" | custom-call | tf_op jit(solution)/shard_map/pallas_call | solution.py:202
  298.2 2.6 collective-permute-done.43
  302.4 2.8 fusion.23
  305.7 9.2 %collective-permute-done.45 = bf16[128,2048]{1,0:T(8,128)(2,1)S(1)} collective-permute-done((bf16[128,2048]{1,0:T(8,128)(2,1)S(1)}, bf16[128,2048]{1,0:T(8,128)(2,1)S(1)}, u32[]{:S(2)}, u32[]{:S(2)}) %collective-permute-start.45) | collective-permute-done | bytes 524320 | tf_op jit(solution)/shard_map/ppermute | solution.py:77
  315.0 1.9 collective-permute-done.46.refs_3_
  317.0 2.0 collective-permute-start.49
  320.9 17.5 %shard_map.255 = (f32[512,512]{1,0:T(8,128)}, f32[512,512]{1,0:T(8,128)}, bf16[512,512]{1,0:T(8,128)(2,1)}, f32[8,512]{1,0:T(8,128)}, bf16[16,512]{1,0:T(8,128)(2,1)}, /*index=5*/bf16[16,512]{1,0:T(8,128)(2,1)}) custom-call(s32[5]{0:T(128)} %concatenate.83.scalars, bf16[128,2176]{1,0:T(8,128)(2,1)} %copy-done.13, bf16[128,2176]{1,0:T(8,128)(2,1)} %copy-done.58, ...), custom_call_target="tpu_custom_call" | custom-call | flops 2952790016 | bytes 10750484 | tf_op jit(solution)/shard_map/pallas_call | solution.py:202
  338.4 3.9 collective-permute-done.49
  347.1 2.1 collective-permute-done.53
  351.7 3.2 collective-permute-start.58
  354.9 5.0 %shard_map.256 = (bf16[3,512,512]{2,1,0:T(8,128)(2,1)}, bf16[512,128]{1,0:T(8,128)(2,1)}, bf16[48,512]{1,0:T(8,128)(2,1)}) custom-call(f32[8,512]{1,0:T(8,128)} %add.452.inner, f32[8,512]{1,0:T(8,128)} %add.407.squares, f32[512,512]{1,0:T(8,128)} %get-tuple-element.538.query_grad, f32[512,512]{1,0:T(8,128)} %get-tuple-element.539.key_grad, ...), custom_call_target="tpu_custom_call" | custom-call | tf_op jit(solution)/shard_map/pallas_call | solution.py:202
  362.9 7.7 %shard_map.257 = (f32[256,2048]{1,0:T(8,128)}, bf16[256,2048]{1,0:T(8,128)(2,1)}) custom-call(s32[1]{0:T(128)} %bitcast.1.core.scalars, bf16[3,512,512]{2,1,0:T(8,128)(2,1)} %get-tuple-element.544.raw, bf16[2048,512]{1,0:T(8,128)(2,1)} %query_weight.3, bf16[2048,512]{1,0:T(8,128)(2,1)} %key_weight.3, bf16[2048,512]{1,0:T(8,128)(2,1)} %value_weight.3), custom_call_target="tpu_custom_call" | custom-call | tf_op jit(solution)/shard_map/pallas_call | solution.py:202
  372.5 1.8 collective-permute-done.59
  379.7 2.9 shard_map.258
  382.7 2.1 collective-permute-start.60
  385.2 9.1 %collective-permute-done.60 = bf16[144,512]{1,0:T(8,128)(2,1)S(1)} collective-permute-done((bf16[144,512]{1,0:T(8,128)(2,1)}, bf16[144,512]{1,0:T(8,128)(2,1)S(1)}, u32[]{:S(2)}, u32[]{:S(2)}) %collective-permute-start.60) | collective-permute-done | bytes 147488 | tf_op jit(solution)/shard_map/ppermute | solution.py:77
  397.0 4.5 shard_map.259.refs_0_
  401.5 2.1 collective-permute-done.64
  405.2 5.3 %collective-permute-done.65 = bf16[144,512]{1,0:T(8,128)(2,1)S(1)} collective-permute-done((bf16[144,512]{1,0:T(8,128)(2,1)S(1)}, bf16[144,512]{1,0:T(8,128)(2,1)S(1)}, u32[]{:S(2)}, u32[]{:S(2)}) %collective-permute-start.65) | collective-permute-done | bytes 147488 | tf_op jit(solution)/shard_map/ppermute | solution.py:77
  414.2 1.7 collective-permute-start.68
  416.2 6.1 %collective-permute-done.71.refs_1_ = bf16[128,2048]{1,0:T(8,128)(2,1)S(1)} collective-permute-done((bf16[128,2048]{1,0:T(8,128)(2,1)}, bf16[128,2048]{1,0:T(8,128)(2,1)S(1)}, u32[]{:S(2)}, u32[]{:S(2)}) %collective-permute-start.71) | collective-permute-done | bytes 524320 | tf_op jit(solution)/shard_map/ppermute | solution.py:77
  422.3 8.6 %collective-permute-done.70 = bf16[256,1024]{1,0:T(8,128)(2,1)S(1)} collective-permute-done((bf16[256,1024]{1,0:T(8,128)(2,1)S(1)}, bf16[256,1024]{1,0:T(8,128)(2,1)S(1)}, u32[]{:S(2)}, u32[]{:S(2)}) %collective-permute-start.70) | collective-permute-done | bytes 524320 | tf_op jit(solution)/shard_map/ppermute | solution.py:77
  436.5 4.6 %shard_map.260 = f32[512,2048]{1,0:T(8,128)} custom-call(s32[4]{0:T(128)} %pad_add_fusion.order, bf16[128,2048]{1,0:T(8,128)(2,1)} %shard_map.259.refs_0_, bf16[128,2048]{1,0:T(8,128)(2,1)} %copy-done.25, bf16[128,2048]{1,0:T(8,128)(2,1)} %collective-permute-done.74.refs_2_, bf16[128,2048]{1,0:T(8,128)(2,1)} %collective-permute-done.75.refs_3_), custom_call_target="tpu_custom_call" | custom-call | tf_op jit(solution)/shard_map/pallas_call | solution.py:202
  441.1 7.5 %collective-permute-done.73 = bf16[256,1024]{1,0:T(8,128)(2,1)} collective-permute-done((bf16[256,1024]{1,0:T(8,128)(2,1)}, bf16[256,1024]{1,0:T(8,128)(2,1)}, u32[]{:S(2)}, u32[]{:S(2)}) %collective-permute-start.73) | collective-permute-done | bytes 524320 | tf_op jit(solution)/shard_map/ppermute | solution.py:77
  454.1 5.3 %shard_map.261 = (f32[3,2048,128]{2,1,0:T(8,128)}, f32[3,128,512]{2,1,0:T(8,128)}, f32[512,128]{1,0:T(8,128)}, f32[128,2048]{1,0:T(8,128)}) custom-call(s32[4]{0:T(128)} %pad_add_fusion.order, bf16[1152,512]{1,0:T(8,128)(2,1)} %copy-done.1, bf16[512,512]{1,0:T(8,128)(2,1)} %collective-permute-done.72.refs_1_, bf16[512,512]{1,0:T(8,128)(2,1)} %copy-done.38, ...), custom_call_target="tpu_custom_call" | custom-call | tf_op jit(solution)/shard_map/pallas_call | solution.py:202
  (371 shorter events, 93.5 us)
Async XLA Ops:
  3.5 29.7 %collective-permute-start.2 = (bf16[256,2176]{1,0:T(8,128)(2,1)S(1)}, bf16[256,2176]{1,0:T(8,128)(2,1)S(1)}, u32[]{:S(2)}, u32[]{:S(2)}) collective-permute-start(bf16[256,2176]{1,0:T(8,128)(2,1)S(1)} %maximum_maximum_fusion.refs_0_), channel_id=1, source_target_pairs={{0,8},{4,12},{8,16},{12,20},{16,24},{20,28},{24,0},{28,4},{1,9},{5... | collective-permute-start | bytes 3342344 | tf_op jit(solution)/shard_map/ppermute | solution.py:77
  6.6 26.6 %collective-permute-start.3 = (bf16[256,2176]{1,0:T(8,128)(2,1)S(1)}, bf16[256,2176]{1,0:T(8,128)(2,1)S(1)}, u32[]{:S(2)}, u32[]{:S(2)}) collective-permute-start(bf16[256,2176]{1,0:T(8,128)(2,1)S(1)} %maximum_maximum_fusion.refs_0_), channel_id=1, source_target_pairs={{0,4},{4,0},{8,12},{12,8},{16,20},{20,16},{24,28},{28,24},{1,5},{5... | collective-permute-start | bytes 3342344 | tf_op jit(solution)/shard_map/ppermute | solution.py:77
  33.2 40.5 %collective-permute-start.10 = (bf16[4,2048,256]{2,1,0:T(8,128)(2,1)}, bf16[4,2048,256]{2,1,0:T(8,128)(2,1)}, u32[]{:S(2)}, u32[]{:S(2)}) collective-permute-start(bf16[4,2048,256]{2,1,0:T(8,128)(2,1)} %refs_2_.3), channel_id=1, source_target_pairs={{0,1},{1,0},{2,3},{3,2},{4,5},{5,4},{6,7},{7,6},{8,9},{9,8},{10,11... | collective-permute-start | bytes 12582920 | tf_op jit(solution)/shard_map/ppermute | solution.py:77
  33.2 40.5 %collective-permute-start.11 = (bf16[4,2048,256]{2,1,0:T(8,128)(2,1)}, bf16[4,2048,256]{2,1,0:T(8,128)(2,1)}, u32[]{:S(2)}, u32[]{:S(2)}) collective-permute-start(bf16[4,2048,256]{2,1,0:T(8,128)(2,1)} %refs_3_.3), channel_id=1, source_target_pairs={{0,1},{1,0},{2,3},{3,2},{4,5},{5,4},{6,7},{7,6},{8,9},{9,8},{10,11... | collective-permute-start | bytes 12582920 | tf_op jit(solution)/shard_map/ppermute | solution.py:77
  33.8 16.5 %collective-permute-start.4 = (bf16[128,2176]{1,0:T(8,128)(2,1)S(1)}, bf16[128,2176]{1,0:T(8,128)(2,1)S(1)}, u32[]{:S(2)}, u32[]{:S(2)}) collective-permute-start(bf16[128,2176]{1,0:T(8,128)(2,1)S(1)} %get-tuple-element.350.refs_2_), channel_id=1, source_target_pairs={{0,8},{4,12},{8,16},{12,20},{16,24},{20,28},{24,0},{28,4},{1,9},{5... | collective-permute-start | bytes 1671176 | tf_op jit(solution)/shard_map/ppermute | solution.py:77
  34.8 15.4 %collective-permute-start.5 = (bf16[128,2176]{1,0:T(8,128)(2,1)S(1)}, bf16[128,2176]{1,0:T(8,128)(2,1)S(1)}, u32[]{:S(2)}, u32[]{:S(2)}) collective-permute-start(bf16[128,2176]{1,0:T(8,128)(2,1)S(1)} %get-tuple-element.350.refs_2_), channel_id=1, source_target_pairs={{0,4},{4,0},{8,12},{12,8},{16,20},{20,16},{24,28},{28,24},{1,5},{5... | collective-permute-start | bytes 1671176 | tf_op jit(solution)/shard_map/ppermute | solution.py:77
  57.5 16.2 %collective-permute-start.8 = (bf16[128,2176]{1,0:T(8,128)(2,1)S(1)}, bf16[128,2176]{1,0:T(8,128)(2,1)S(1)}, u32[]{:S(2)}, u32[]{:S(2)}) collective-permute-start(bf16[128,2176]{1,0:T(8,128)(2,1)S(1)} %get-tuple-element.335.refs_3_), channel_id=1, source_target_pairs={{0,8},{4,12},{8,16},{12,20},{16,24},{20,28},{24,0},{28,4},{1,9},{5... | collective-permute-start | bytes 1671176 | tf_op jit(solution)/shard_map/ppermute | solution.py:77
  57.9 15.7 %collective-permute-start.9 = (bf16[128,2176]{1,0:T(8,128)(2,1)S(1)}, bf16[128,2176]{1,0:T(8,128)(2,1)S(1)}, u32[]{:S(2)}, u32[]{:S(2)}) collective-permute-start(bf16[128,2176]{1,0:T(8,128)(2,1)S(1)} %get-tuple-element.335.refs_3_), channel_id=1, source_target_pairs={{0,4},{4,0},{8,12},{12,8},{16,20},{20,16},{24,28},{28,24},{1,5},{5... | collective-permute-start | bytes 1671176 | tf_op jit(solution)/shard_map/ppermute | solution.py:77
  73.7 21.0 %collective-permute-start.14 = (bf16[1024,2048]{1,0:T(8,128)(2,1)}, bf16[1024,2048]{1,0:T(8,128)(2,1)}, u32[]{:S(2)}, u32[]{:S(2)}) collective-permute-start(bf16[1024,2048]{1,0:T(8,128)(2,1)} %bitcast.11.refs_6_.refs_7_.refs_2_.refs_1_), channel_id=1, source_target_pairs={{0,1},{1,0},{2,3},{3,2},{4,5},{5,4},{6,7},{7,6},{8,9},{9,8},{10,11... | collective-permute-start | bytes 12582920 | tf_op jit(solution)/shard_map/ppermute | solution.py:77
  78.4 16.3 %collective-permute-start.12 = (bf16[128,2048]{1,0:T(8,128)(2,1)}, bf16[128,2048]{1,0:T(8,128)(2,1)S(1)}, u32[]{:S(2)}, u32[]{:S(2)}) collective-permute-start(bf16[128,2048]{1,0:T(8,128)(2,1)} %get-tuple-element.344), channel_id=1, source_target_pairs={{0,8},{4,12},{8,16},{12,20},{16,24},{20,28},{24,0},{28,4},{1,9},{5... | collective-permute-start | bytes 1572872 | tf_op jit(solution)/shard_map/ppermute | solution.py:77
  78.4 16.3 %collective-permute-start.13 = (bf16[128,2048]{1,0:T(8,128)(2,1)}, bf16[128,2048]{1,0:T(8,128)(2,1)S(1)}, u32[]{:S(2)}, u32[]{:S(2)}) collective-permute-start(bf16[128,2048]{1,0:T(8,128)(2,1)} %get-tuple-element.344), channel_id=1, source_target_pairs={{0,4},{4,0},{8,12},{12,8},{16,20},{20,16},{24,28},{28,24},{1,5},{5... | collective-permute-start | bytes 1572872 | tf_op jit(solution)/shard_map/ppermute | solution.py:77
  94.8 24.8 %collective-permute-start.15 = (bf16[256,2048]{1,0:T(8,128)(2,1)S(1)}, bf16[256,2048]{1,0:T(8,128)(2,1)S(1)}, u32[]{:S(2)}, u32[]{:S(2)}) collective-permute-start(bf16[256,2048]{1,0:T(8,128)(2,1)S(1)} %constant_dynamic-update-slice_fusion.refs_0_), channel_id=1, source_target_pairs={{0,2},{1,3},{2,0},{3,1},{4,6},{5,7},{6,4},{7,5},{8,10},{9,11},{10,... | collective-permute-start | bytes 3145736 | tf_op jit(solution)/shard_map/ppermute | solution.py:77
  96.2 18.3 %collective-permute-start.16 = (bf16[128,2048]{1,0:T(8,128)(2,1)S(1)}, bf16[128,2048]{1,0:T(8,128)(2,1)S(1)}, u32[]{:S(2)}, u32[]{:S(2)}) collective-permute-start(bf16[128,2048]{1,0:T(8,128)(2,1)S(1)} %collective-permute-done.12), channel_id=1, source_target_pairs={{0,8},{4,12},{8,16},{12,20},{16,24},{20,28},{24,0},{28,4},{1,9},{5... | collective-permute-start | bytes 1572872 | tf_op jit(solution)/shard_map/ppermute | solution.py:77
  96.4 18.2 %collective-permute-start.17 = (bf16[128,2048]{1,0:T(8,128)(2,1)S(1)}, bf16[128,2048]{1,0:T(8,128)(2,1)S(1)}, u32[]{:S(2)}, u32[]{:S(2)}) collective-permute-start(bf16[128,2048]{1,0:T(8,128)(2,1)S(1)} %collective-permute-done.12), channel_id=1, source_target_pairs={{0,4},{4,0},{8,12},{12,8},{16,20},{20,16},{24,28},{28,24},{1,5},{5... | collective-permute-start | bytes 1572872 | tf_op jit(solution)/shard_map/ppermute | solution.py:77
  119.6 29.0 %collective-permute-start.19 = (bf16[128,2048]{1,0:T(8,128)(2,1)S(1)}, bf16[128,2048]{1,0:T(8,128)(2,1)S(1)}, u32[]{:S(2)}, u32[]{:S(2)}) collective-permute-start(bf16[128,2048]{1,0:T(8,128)(2,1)S(1)} %collective-permute-done.16), channel_id=1, source_target_pairs={{0,8},{4,12},{8,16},{12,20},{16,24},{20,28},{24,0},{28,4},{1,9},{5... | collective-permute-start | bytes 1572872 | tf_op jit(solution)/shard_map/ppermute | solution.py:77
  119.6 29.0 %collective-permute-start.20 = (bf16[128,2048]{1,0:T(8,128)(2,1)S(1)}, bf16[128,2048]{1,0:T(8,128)(2,1)S(1)}, u32[]{:S(2)}, u32[]{:S(2)}) collective-permute-start(bf16[128,2048]{1,0:T(8,128)(2,1)S(1)} %collective-permute-done.16), channel_id=1, source_target_pairs={{0,4},{4,0},{8,12},{12,8},{16,20},{20,16},{24,28},{28,24},{1,5},{5... | collective-permute-start | bytes 1572872 | tf_op jit(solution)/shard_map/ppermute | solution.py:77
  121.1 57.0 %collective-permute-start.23 = (bf16[256,2176]{1,0:T(8,128)(2,1)S(1)}, bf16[256,2176]{1,0:T(8,128)(2,1)S(1)}, u32[]{:S(2)}, u32[]{:S(2)}) collective-permute-start(bf16[256,2176]{1,0:T(8,128)(2,1)S(1)} %pad_maximum_fusion.refs_9_), channel_id=1, source_target_pairs={{0,8},{4,12},{8,16},{12,20},{16,24},{20,28},{24,0},{28,4},{1,9},{5... | collective-permute-start | bytes 3342344 | tf_op jit(solution)/shard_map/ppermute | solution.py:77
  121.5 56.6 %collective-permute-start.24 = (bf16[256,2176]{1,0:T(8,128)(2,1)S(1)}, bf16[256,2176]{1,0:T(8,128)(2,1)}, u32[]{:S(2)}, u32[]{:S(2)}) collective-permute-start(bf16[256,2176]{1,0:T(8,128)(2,1)S(1)} %pad_maximum_fusion.refs_9_), channel_id=1, source_target_pairs={{0,4},{4,0},{8,12},{12,8},{16,20},{20,16},{24,28},{28,24},{1,5},{5... | collective-permute-start | bytes 3342344 | tf_op jit(solution)/shard_map/ppermute | solution.py:77
  122.2 26.4 %collective-permute-start.18 = (bf16[256,2048]{1,0:T(8,128)(2,1)S(1)}, bf16[256,2048]{1,0:T(8,128)(2,1)}, u32[]{:S(2)}, u32[]{:S(2)}) collective-permute-start(bf16[256,2048]{1,0:T(8,128)(2,1)S(1)} %constant_dynamic-update-slice_fusion.2.refs_0_), channel_id=1, source_target_pairs={{0,2},{1,3},{2,0},{3,1},{4,6},{5,7},{6,4},{7,5},{8,10},{9,11},{10,... | collective-permute-start | bytes 3145736 | tf_op jit(solution)/shard_map/ppermute | solution.py:77
  148.7 29.4 %collective-permute-start.21 = (bf16[256,2048]{1,0:T(8,128)(2,1)S(1)}, bf16[256,2048]{1,0:T(8,128)(2,1)S(1)}, u32[]{:S(2)}, u32[]{:S(2)}) collective-permute-start(bf16[256,2048]{1,0:T(8,128)(2,1)S(1)} %constant_dynamic-update-slice_fusion.4.refs_0_), channel_id=1, source_target_pairs={{0,2},{1,3},{2,0},{3,1},{4,6},{5,7},{6,4},{7,5},{8,10},{9,11},{10,... | collective-permute-start | bytes 3145736 | tf_op jit(solution)/shard_map/ppermute | solution.py:77
  150.3 27.8 %collective-permute-start.22 = (bf16[128,2048]{1,0:T(8,128)(2,1)S(1)}, bf16[128,2048]{1,0:T(8,128)(2,1)S(1)}, u32[]{:S(2)}, u32[]{:S(2)}) collective-permute-start(bf16[128,2048]{1,0:T(8,128)(2,1)S(1)} %collective-permute-done.19), channel_id=1, source_target_pairs={{0,4},{4,0},{8,12},{12,8},{16,20},{20,16},{24,28},{28,24},{1,5},{5... | collective-permute-start | bytes 1572872 | tf_op jit(solution)/shard_map/ppermute | solution.py:77
  151.8 63.2 %collective-permute-start.28 = (bf16[256,2048]{1,0:T(8,128)(2,1)}, bf16[256,2048]{1,0:T(8,128)(2,1)S(1)}, u32[]{:S(2)}, u32[]{:S(2)}) collective-permute-start(bf16[256,2048]{1,0:T(8,128)(2,1)} %get-tuple-element.392), channel_id=1, source_target_pairs={{0,4},{4,0},{8,12},{12,8},{16,20},{20,16},{24,28},{28,24},{1,5},{5... | collective-permute-start | bytes 3145736 | tf_op jit(solution)/shard_map/ppermute | solution.py:77
  179.2 35.9 %collective-permute-start.25 = (bf16[256,2048]{1,0:T(8,128)(2,1)S(1)}, bf16[256,2048]{1,0:T(8,128)(2,1)}, u32[]{:S(2)}, u32[]{:S(2)}) collective-permute-start(bf16[256,2048]{1,0:T(8,128)(2,1)S(1)} %constant_dynamic-update-slice_fusion.6.refs_0_), channel_id=1, source_target_pairs={{0,2},{1,3},{2,0},{3,1},{4,6},{5,7},{6,4},{7,5},{8,10},{9,11},{10,... | collective-permute-start | bytes 3145736 | tf_op jit(solution)/shard_map/ppermute | solution.py:77
  179.7 35.3 %collective-permute-start.29 = (bf16[256,2176]{1,0:T(8,128)(2,1)}, bf16[256,2176]{1,0:T(8,128)(2,1)S(1)}, u32[]{:S(2)}, u32[]{:S(2)}) collective-permute-start(bf16[256,2176]{1,0:T(8,128)(2,1)} %collective-permute-done.24.refs_10_), channel_id=1, source_target_pairs={{0,8},{4,12},{8,16},{12,20},{16,24},{20,28},{24,0},{28,4},{1,9},{5... | collective-permute-start | bytes 3342344 | tf_op jit(solution)/shard_map/ppermute | solution.py:77
  182.2 32.8 %collective-permute-start.26 = (bf16[128,2048]{1,0:T(8,128)(2,1)}, bf16[128,2048]{1,0:T(8,128)(2,1)S(1)}, u32[]{:S(2)}, u32[]{:S(2)}) collective-permute-start(bf16[128,2048]{1,0:T(8,128)(2,1)} %get-tuple-element.382), channel_id=1, source_target_pairs={{0,2},{1,3},{2,0},{3,1},{4,6},{5,7},{6,4},{7,5},{8,10},{9,11},{10,... | collective-permute-start | bytes 1572872 | tf_op jit(solution)/shard_map/ppermute | solution.py:77
  183.7 31.3 %collective-permute-start.27 = (bf16[128,2048]{1,0:T(8,128)(2,1)S(1)}, bf16[128,2048]{1,0:T(8,128)(2,1)S(1)}, u32[]{:S(2)}, u32[]{:S(2)}) collective-permute-start(bf16[128,2048]{1,0:T(8,128)(2,1)S(1)} %copy-done.64), channel_id=1, source_target_pairs={{0,4},{4,0},{8,12},{12,8},{16,20},{20,16},{24,28},{28,24},{1,5},{5... | collective-permute-start | bytes 1572872 | tf_op jit(solution)/shard_map/ppermute | solution.py:77
  216.3 34.6 %collective-permute-start.34 = (bf16[128,2048]{1,0:T(8,128)(2,1)S(1)}, bf16[128,2048]{1,0:T(8,128)(2,1)S(1)}, u32[]{:S(2)}, u32[]{:S(2)}) collective-permute-start(bf16[128,2048]{1,0:T(8,128)(2,1)S(1)} %add_convert_fusion.4), channel_id=1, source_target_pairs={{0,2},{1,3},{2,0},{3,1},{4,6},{5,7},{6,4},{7,5},{8,10},{9,11},{10,... | collective-permute-start | bytes 1572872 | tf_op jit(solution)/shard_map/ppermute | solution.py:77
  216.9 34.0 %collective-permute-start.31 = (bf16[64,2048]{1,0:T(8,128)(2,1)S(1)}, bf16[64,2048]{1,0:T(8,128)(2,1)S(1)}, u32[]{:S(2)}, u32[]{:S(2)}) collective-permute-start(bf16[64,2048]{1,0:T(8,128)(2,1)S(1)} %add_convert_fusion.17), channel_id=1, source_target_pairs={{0,2},{1,3},{2,0},{3,1},{4,6},{5,7},{6,4},{7,5},{8,10},{9,11},{10,... | collective-permute-start | bytes 786440 | tf_op jit(solution)/shard_map/ppermute | solution.py:77
  218.6 32.3 %collective-permute-start.30 = (bf16[64,2048]{1,0:T(8,128)(2,1)S(1)}, bf16[64,2048]{1,0:T(8,128)(2,1)}, u32[]{:S(2)}, u32[]{:S(2)}) collective-permute-start(bf16[64,2048]{1,0:T(8,128)(2,1)S(1)} %add_convert_fusion.18), channel_id=1, source_target_pairs={{0,4},{4,0},{8,12},{12,8},{16,20},{20,16},{24,28},{28,24},{1,5},{5... | collective-permute-start | bytes 786440 | tf_op jit(solution)/shard_map/ppermute | solution.py:77
  219.2 31.7 %collective-permute-start.32 = (bf16[128,2048]{1,0:T(8,128)(2,1)}, bf16[128,2048]{1,0:T(8,128)(2,1)S(1)}, u32[]{:S(2)}, u32[]{:S(2)}) collective-permute-start(bf16[128,2048]{1,0:T(8,128)(2,1)} %get-tuple-element.396), channel_id=1, source_target_pairs={{0,2},{1,3},{2,0},{3,1},{4,6},{5,7},{6,4},{7,5},{8,10},{9,11},{10,... | collective-permute-start | bytes 1572872 | tf_op jit(solution)/shard_map/ppermute | solution.py:77
  219.7 31.2 %collective-permute-start.33 = (bf16[128,2048]{1,0:T(8,128)(2,1)S(1)}, bf16[128,2048]{1,0:T(8,128)(2,1)S(1)}, u32[]{:S(2)}, u32[]{:S(2)}) collective-permute-start(bf16[128,2048]{1,0:T(8,128)(2,1)S(1)} %copy-done.63), channel_id=1, source_target_pairs={{0,4},{4,0},{8,12},{12,8},{16,20},{20,16},{24,28},{28,24},{1,5},{5... | collective-permute-start | bytes 1572872 | tf_op jit(solution)/shard_map/ppermute | solution.py:77
  251.0 21.3 %collective-permute-start.39 = (bf16[64,2048]{1,0:T(8,128)(2,1)S(1)}, bf16[64,2048]{1,0:T(8,128)(2,1)S(1)}, u32[]{:S(2)}, u32[]{:S(2)}) collective-permute-start(bf16[64,2048]{1,0:T(8,128)(2,1)S(1)} %add_convert_fusion.13), channel_id=1, source_target_pairs={{0,2},{1,3},{2,0},{3,1},{4,6},{5,7},{6,4},{7,5},{8,10},{9,11},{10,... | collective-permute-start | bytes 786440 | tf_op jit(solution)/shard_map/ppermute | solution.py:77
  253.8 18.4 %collective-permute-start.35 = (bf16[128,2048]{1,0:T(8,128)(2,1)S(1)}, bf16[128,2048]{1,0:T(8,128)(2,1)S(1)}, u32[]{:S(2)}, u32[]{:S(2)}) collective-permute-start(bf16[128,2048]{1,0:T(8,128)(2,1)S(1)} %pad_maximum_fusion.2), channel_id=1, source_target_pairs={{0,8},{4,12},{8,16},{12,20},{16,24},{20,28},{24,0},{28,4},{1,9},{5... | collective-permute-start | bytes 1572872 | tf_op jit(solution)/shard_map/ppermute | solution.py:77
  256.5 15.8 %collective-permute-start.36 = (bf16[128,2048]{1,0:T(8,128)(2,1)}, bf16[128,2048]{1,0:T(8,128)(2,1)S(1)}, u32[]{:S(2)}, u32[]{:S(2)}) collective-permute-start(bf16[128,2048]{1,0:T(8,128)(2,1)} %get-tuple-element.414), channel_id=1, source_target_pairs={{0,2},{1,3},{2,0},{3,1},{4,6},{5,7},{6,4},{7,5},{8,10},{9,11},{10,... | collective-permute-start | bytes 1572872 | tf_op jit(solution)/shard_map/ppermute | solution.py:77
  316.9 21.5 %collective-permute-start.48 = (bf16[128,2048]{1,0:T(8,128)(2,1)}, bf16[128,2048]{1,0:T(8,128)(2,1)}, u32[]{:S(2)}, u32[]{:S(2)}) collective-permute-start(bf16[128,2048]{1,0:T(8,128)(2,1)} %get-tuple-element.508), channel_id=1, source_target_pairs={{0,4},{4,0},{8,12},{12,8},{16,20},{20,16},{24,28},{28,24},{1,5},{5... | collective-permute-start | bytes 1572872 | tf_op jit(solution)/shard_map/ppermute | solution.py:77
  317.0 25.4 %collective-permute-start.49 = (bf16[128,2048]{1,0:T(8,128)(2,1)}, bf16[128,2048]{1,0:T(8,128)(2,1)S(1)}, u32[]{:S(2)}, u32[]{:S(2)}) collective-permute-start(bf16[128,2048]{1,0:T(8,128)(2,1)} %get-tuple-element.509), channel_id=1, source_target_pairs={{0,4},{4,0},{8,12},{12,8},{16,20},{20,16},{24,28},{28,24},{1,5},{5... | collective-permute-start | bytes 1572872 | tf_op jit(solution)/shard_map/ppermute | solution.py:77
  319.0 23.4 %collective-permute-start.50 = (bf16[128,2048]{1,0:T(8,128)(2,1)}, bf16[128,2048]{1,0:T(8,128)(2,1)S(1)}, u32[]{:S(2)}, u32[]{:S(2)}) collective-permute-start(bf16[128,2048]{1,0:T(8,128)(2,1)} %get-tuple-element.510), channel_id=1, source_target_pairs={{0,24},{4,28},{8,0},{12,4},{16,8},{20,12},{24,16},{28,20},{1,25},{... | collective-permute-start | bytes 1572872 | tf_op jit(solution)/shard_map/ppermute | solution.py:77
  320.2 23.6 %collective-permute-start.51 = (bf16[128,2048]{1,0:T(8,128)(2,1)}, bf16[128,2048]{1,0:T(8,128)(2,1)S(1)}, u32[]{:S(2)}, u32[]{:S(2)}) collective-permute-start(bf16[128,2048]{1,0:T(8,128)(2,1)} %get-tuple-element.511), channel_id=1, source_target_pairs={{0,24},{4,28},{8,0},{12,4},{16,8},{20,12},{24,16},{28,20},{1,25},{... | collective-permute-start | bytes 1572872 | tf_op jit(solution)/shard_map/ppermute | solution.py:77
  349.8 20.9 %collective-permute-start.56 = (bf16[256,1024]{1,0:T(8,128)(2,1)S(1)}, bf16[256,1024]{1,0:T(8,128)(2,1)S(1)}, u32[]{:S(2)}, u32[]{:S(2)}) collective-permute-start(bf16[256,1024]{1,0:T(8,128)(2,1)S(1)} %pad_maximum_fusion.3), channel_id=1, source_target_pairs={{0,2},{1,3},{2,0},{3,1},{4,6},{5,7},{6,4},{7,5},{8,10},{9,11},{10,... | collective-permute-start | bytes 1572872 | tf_op jit(solution)/shard_map/ppermute | solution.py:77
  351.4 19.3 %collective-permute-start.57 = (bf16[128,2048]{1,0:T(8,128)(2,1)S(1)}, bf16[128,2048]{1,0:T(8,128)(2,1)S(1)}, u32[]{:S(2)}, u32[]{:S(2)}) collective-permute-start(bf16[128,2048]{1,0:T(8,128)(2,1)S(1)} %copy-done.61), channel_id=1, source_target_pairs={{0,4},{4,0},{8,12},{12,8},{16,20},{20,16},{24,28},{28,24},{1,5},{5... | collective-permute-start | bytes 1572872 | tf_op jit(solution)/shard_map/ppermute | solution.py:77
  351.7 18.9 %collective-permute-start.58 = (bf16[128,2048]{1,0:T(8,128)(2,1)}, bf16[128,2048]{1,0:T(8,128)(2,1)S(1)}, u32[]{:S(2)}, u32[]{:S(2)}) collective-permute-start(bf16[128,2048]{1,0:T(8,128)(2,1)} %get-tuple-element.551), channel_id=1, source_target_pairs={{0,24},{4,28},{8,0},{12,4},{16,8},{20,12},{24,16},{28,20},{1,25},{... | collective-permute-start | bytes 1572872 | tf_op jit(solution)/shard_map/ppermute | solution.py:77
  375.7 18.5 %collective-permute-start.61 = (bf16[128,2048]{1,0:T(8,128)(2,1)}, bf16[128,2048]{1,0:T(8,128)(2,1)S(1)}, u32[]{:S(2)}, u32[]{:S(2)}) collective-permute-start(bf16[128,2048]{1,0:T(8,128)(2,1)} %get-tuple-element.591), channel_id=1, source_target_pairs={{0,2},{1,3},{2,0},{3,1},{4,6},{5,7},{6,4},{7,5},{8,10},{9,11},{10,... | collective-permute-start | bytes 1572872 | tf_op jit(solution)/shard_map/ppermute | solution.py:77
  377.3 16.9 %collective-permute-start.62 = (bf16[128,2048]{1,0:T(8,128)(2,1)S(1)}, bf16[128,2048]{1,0:T(8,128)(2,1)S(1)}, u32[]{:S(2)}, u32[]{:S(2)}) collective-permute-start(bf16[128,2048]{1,0:T(8,128)(2,1)S(1)} %add_convert_fusion.3), channel_id=1, source_target_pairs={{0,4},{4,0},{8,12},{12,8},{16,20},{20,16},{24,28},{28,24},{1,5},{5... | collective-permute-start | bytes 1572872 | tf_op jit(solution)/shard_map/ppermute | solution.py:77
  379.0 16.9 %collective-permute-start.63 = (bf16[128,2048]{1,0:T(8,128)(2,1)}, bf16[128,2048]{1,0:T(8,128)(2,1)}, u32[]{:S(2)}, u32[]{:S(2)}) collective-permute-start(bf16[128,2048]{1,0:T(8,128)(2,1)} %get-tuple-element.594), channel_id=1, source_target_pairs={{0,24},{4,28},{8,0},{12,4},{16,8},{20,12},{24,16},{28,20},{1,25},{... | collective-permute-start | bytes 1572872 | tf_op jit(solution)/shard_map/ppermute | solution.py:77
  403.6 18.8 %collective-permute-start.71 = (bf16[128,2048]{1,0:T(8,128)(2,1)}, bf16[128,2048]{1,0:T(8,128)(2,1)S(1)}, u32[]{:S(2)}, u32[]{:S(2)}) collective-permute-start(bf16[128,2048]{1,0:T(8,128)(2,1)} %shard_map.259.refs_0_), channel_id=1, source_target_pairs={{0,2},{1,3},{2,0},{3,1},{4,6},{5,7},{6,4},{7,5},{8,10},{9,11},{10,... | collective-permute-start | bytes 1572872 | tf_op jit(solution)/shard_map/ppermute | solution.py:77
  412.9 18.0 %collective-permute-start.70 = (bf16[256,1024]{1,0:T(8,128)(2,1)S(1)}, bf16[256,1024]{1,0:T(8,128)(2,1)S(1)}, u32[]{:S(2)}, u32[]{:S(2)}) collective-permute-start(bf16[256,1024]{1,0:T(8,128)(2,1)S(1)} %pad_maximum_fusion.5), channel_id=1, source_target_pairs={{0,2},{1,3},{2,0},{3,1},{4,6},{5,7},{6,4},{7,5},{8,10},{9,11},{10,... | collective-permute-start | bytes 1572872 | tf_op jit(solution)/shard_map/ppermute | solution.py:77
  414.2 16.7 %collective-permute-start.68 = (bf16[576,512]{1,0:T(8,128)(2,1)S(1)}, bf16[576,512]{1,0:T(8,128)(2,1)S(1)}, u32[]{:S(2)}, u32[]{:S(2)}) collective-permute-start(bf16[576,512]{1,0:T(8,128)(2,1)S(1)} %constant_dynamic-update-slice_fusion.8), channel_id=1, source_target_pairs={{0,4},{4,0},{8,12},{12,8},{16,20},{20,16},{24,28},{28,24},{1,5},{5... | collective-permute-start | bytes 1769480 | tf_op jit(solution)/shard_map/ppermute | solution.py:77
  432.6 16.0 %collective-permute-start.73 = (bf16[256,1024]{1,0:T(8,128)(2,1)}, bf16[256,1024]{1,0:T(8,128)(2,1)}, u32[]{:S(2)}, u32[]{:S(2)}) collective-permute-start(bf16[256,1024]{1,0:T(8,128)(2,1)} %fusion.6), channel_id=1, source_target_pairs={{0,8},{4,12},{8,16},{12,20},{16,24},{20,28},{24,0},{28,4},{1,9},{5... | collective-permute-start | bytes 1572872 | tf_op jit(solution)/shard_map/ppermute | solution.py:77
  (98 other events, 928.8 us)

commit v9 on v8

--- a/solution.py
+++ b/solution.py
@@ -218,13 +218,14 @@
     step = 16
 
     def some(index, carry):
-        rows = pl.ds(pl.multiple_of(index * step, step), step)
-        values = wide(source[rows, :])
-        inverse = lax.rsqrt(jnp.mean(values * values, axis=1, keepdims=True) + EPSILON)
-        target[rows, :] = low(values * inverse * gain)
+        for part in range(4):
+            rows = pl.ds(pl.multiple_of((index * 4 + part) * step, step), step)
+            values = wide(source[rows, :])
+            inverse = lax.rsqrt(jnp.mean(values * values, axis=1, keepdims=True) + EPSILON)
+            target[rows, :] = low(values * inverse * gain)
         return carry
 
-    lax.fori_loop(0, source.shape[0] // step, some, 0)
+    lax.fori_loop(0, source.shape[0] // (4 * step), some, 0)
 
 
 def project_kernel(
@@ -492,7 +493,7 @@
         ],
         [((2 * experts, rows, part), jnp.bfloat16), ((rows, side), jnp.bfloat16)],
         [*pieces, *downs, spread],
-        4 * rows * hidden * width,
+        0,
         [
             pltpu.VMEM((rows, width), jnp.bfloat16),
             pltpu.VMEM((rows, side), jnp.bfloat16),
@@ -615,7 +616,7 @@
     experts, width, part = gates[0].shape
     size = pieces[0].shape[0]
     rows = size * count
-    tile = min(width, 512)
+    tile = min(width, 1024)
     shape = (2 * experts, rows, part)
     slots = pltpu.VMEM(shape, jnp.bfloat16)
     sizes = block_sizes(rows, near, span)
@@ -780,7 +781,7 @@
     experts, width, part = gates[0].shape
     size = pieces[0].shape[0]
     rows = size * count
-    tile = min(width, 512)
+    tile = min(width, 1024)
     shape = (2 * experts, rows, part)
     slots = pltpu.VMEM(shape, jnp.bfloat16)
     cot_pieces, places = [], []
@@ -955,6 +956,45 @@
     return low(jnp.where(lax.rem(lane, RANK) == row, select, 0.0))
 
 
+def resid_grad_kernel(
+    rank, arrived, own, own_x, own_y, cotangent, resid, mixed, gain, grad_out, sent_out
+):
+    width = resid.shape[1]
+    step = 16
+
+    for first in range(0, resid.shape[0], step):
+        rows = pl.ds(first, step)
+        total = wide(arrived[rows, :]) + wide(own_y[rows, :])
+        total = total + wide(own[rows, :]) + wide(own_x[rows, :])
+        scaled = total * wide(gain[...])
+        values = resid[rows, :]
+        inverse = lax.rsqrt(jnp.mean(values * values, axis=1, keepdims=True) + EPSILON)
+        inner = jnp.sum(scaled * values, axis=1, keepdims=True)
+        grad = wide(cotangent[rows, :]) + norm_back(scaled, values, inverse, width, inner)
+        grad_out[rows, :] = grad
+        sent_out[rows, pl.ds(0, width)] = low(grad)
+    sent_out[:, width:] = mixed[...]
+
+
+def resid_grad_call(rank, arrived, own, own_x, own_y, cotangent, resid, mixed, gain):
+    rows, width = resid.shape
+    wide_width = width + mixed.shape[1]
+    first = pl.BlockSpec((rows, width), lambda n, rank: (0, 0))
+    return kernel_call(
+        resid_grad_kernel,
+        (1,),
+        [first] * 4
+        + [pl.BlockSpec((rows, width), lambda n, rank: (rank[0], 0))]
+        + [whole(resid), whole(mixed), whole(gain)],
+        [first, pl.BlockSpec((rows, wide_width), lambda n, rank: (0, 0))],
+        [((rows, width), jnp.float32), ((rows, wide_width), jnp.bfloat16)],
+        [rank, arrived, own, own_x, own_y, cotangent, resid, mixed, gain],
+        0,
+        (),
+        1,
+    )
+
+
 def raw_kernel(
     width, inner, squares, query_grad, key_grad, value_grad, query_raw, key_raw, lowrank,
     adapt_out, select, raw, lowrank_out, adapt_grad,
@@ -1465,19 +1505,17 @@
 
     ring_sum, mixes = hold((ring_sum, mixes))
     mix_early = mix_send(3, 0)
-    ffn_rows_grad = wide(ring_sum) + (own_sums[0][0] + own_sums[0][1]) + wide(came_y)
-    second_scaled = ffn_rows_grad * wide(second_gain)
-    second_inverse = lax.rsqrt(
-        jnp.mean(resid_rows * resid_rows, axis=1, keepdims=True) + EPSILON
-    )
-    resid_grad_rows = wide(own_rows(cotangent)) + norm_back(
-        second_scaled,
+    resid_grad_rows, branch_sent = resid_grad_call(
+        rank_list,
+        ring_sum,
+        parts[0][0],
+        came_x,
+        came_y,
+        cotangent,
         resid_rows,
-        second_inverse,
-        model_width,
-        jnp.sum(second_scaled * resid_rows, axis=1, keepdims=True),
-    )
-    branch_sent = jnp.concatenate([low(resid_grad_rows), mixed_rows], axis=1)
+        mixed_rows,
+        second_gain,
+    )
     branch_pieces = ring(branch_sent, axes, "y")
     branch_other = turn(branch_pieces[0], axes, "c", 1)
     order = jnp.stack(

time: 469 us -> 466 us (level)
  other arithmetic: 28.9 us -> 20.3 us
    convert_element_type x22 -> x21, other arithmetic: 13.9 us -> 9.57 us  [low(): return array.astype(jnp.bfloat16)]
    pallas_call x18 -> x19, Pallas kernels: 232 us -> 233 us  [kernel_call(): pl.pallas_call(kernel, grid_spec=pltpu.PrefetchScalarGridSpec(num_scalar_...]
  transfers between devices with their start and end apart: 79 -> 79, of which waited for: 28 -> 30; matrix products, arithmetic and copies ran while one was open for 6% -> 5% of each run, Pallas kernels for 49% -> 49%
where the time goes in v9:
time: 466 us; the launch traced here: 457 us
  Pallas kernels  233 us (50%)
  waiting for transfers between devices  118 us (25%)
  starting transfers between devices  69.7 us (15%)
  other arithmetic  20.3 us (4%)
  local copies, waits for them, and re-layouts  13.1 us (3%)
    pallas_call x19, Pallas kernels, kernel_call(): pl.pallas_call(kernel, grid_spec=pltpu.PrefetchScalarGridSpec(num_scalar_...  233 us
    ppermute x79, waiting for transfers between devices, turn(): return lax.ppermute(array, axis, pairs)  118 us
    ppermute x79, starting transfers between devices, turn(): return lax.ppermute(array, axis, pairs)  69.7 us
    convert_element_type x21, other arithmetic, low(): return array.astype(jnp.bfloat16)  9.57 us
  transfers between devices with their start and end apart: 79, of which 30 were waited for; matrix products, arithmetic and copies ran while one was open for 5% of the time, Pallas kernels for 49%

profile of v9, /device:TPU:0, one launch (start us, length us, event | category | flops | bytes accessed | tf_op | source)
XLA Modules:
  0.0 457.1 jit_solution(15007779173999579686)
XLA Ops:
  3.5 3.1 collective-permute-start.2
  9.4 11.9 %shard_map.244 = (bf16[512,2048]{1,0:T(8,128)(2,1)}, bf16[3,512,128]{2,1,0:T(8,128)(2,1)}, f32[512,512]{1,0:T(8,128)}, f32[512,512]{1,0:T(8,128)}, f32[512,512]{1,0:T(8,128)}, /*index=5*/f32[8,512]{1,0:T(8,128)}) custom-call(bf16[512,2048]{1,0:T(8,128)(2,1)} %tokens.5, bf16[1,2048]{1,0:T(2,128)(2,1)} %broadcast_in_dim.43.gain, ...), custom_call_target="tpu_custom_call" | custom-call | flops 3221225472 | bytes 10359296 | tf_op jit(solution)/shard_map/pallas_call | solution.py:202
  26.0 1.8 sine_multiply_fusion
  28.8 4.3 collective-permute-done.2
  37.5 9.8 %shard_map.245 = (bf16[512,512]{1,0:T(8,128)(2,1)}, bf16[512,512]{1,0:T(8,128)(2,1)}, bf16[512,512]{1,0:T(8,128)(2,1)}, bf16[512,512]{1,0:T(8,128)(2,1)}, f32[25...) custom-call(s32[1]{0:T(128)} %bitcast.1.core.scalars, f32[8,512]{1,0:T(8,128)} %add.377.squares, ...), custom_call_target="tpu_custom_call" | custom-call | flops 1610612736 | bytes 6965252 | tf_op jit(solution)/shard_map/pallas_call | solution.py:202
  47.3 2.9 collective-permute-done.4
  50.3 2.9 collective-permute-done.6
  53.2 2.7 add_convert_fusion
  59.4 11.2 %collective-permute-done.7.came = bf16[128,2176]{1,0:T(8,128)(2,1)S(1)} collective-permute-done((bf16[128,2176]{1,0:T(8,128)(2,1)S(1)}, bf16[128,2176]{1,0:T(8,128)(2,1)S(1)}, u32[]{:S(2)}, u32[]{:S(2)}) %collective-permute-start.7) | collective-permute-done | bytes 557088 | tf_op jit(solution)/shard_map/ppermute | solution.py:77
  70.6 3.0 collective-permute-done.8
  74.5 3.3 shard_map.246
  79.5 14.5 %collective-permute-done.12 = bf16[128,2048]{1,0:T(8,128)(2,1)S(1)} collective-permute-done((bf16[128,2048]{1,0:T(8,128)(2,1)}, bf16[128,2048]{1,0:T(8,128)(2,1)S(1)}, u32[]{:S(2)}, u32[]{:S(2)}) %collective-permute-start.12) | collective-permute-done | bytes 524320 | tf_op jit(solution)/shard_map/ppermute | solution.py:77
  98.3 16.6 %shard_map.247 = (bf16[8,1024,256]{2,1,0:T(8,128)(2,1)}, bf16[1024,128]{1,0:T(8,128)(2,1)}) custom-call(bf16[256,2176]{1,0:T(8,128)(2,1)} %copy-done.2, bf16[256,2176]{1,0:T(8,128)(2,1)} %copy-done.10, bf16[128,2176]{1,0:T(8,128)(2,1)} %copy-done.7, bf16[128,2176]{1,0:T(8,128)(2,1)} %copy-done.6, bf16[128,2176]{1,0:T(8,128)(2,1)} %copy-done.13, ...), custom_call_target="tpu_custom_call" | custom-call | tf_op jit(solution)/shard_map/pallas_call | solution.py:202
  114.9 4.0 collective-permute-done.15.refs_1_
  122.1 25.5 %shard_map.248 = (bf16[256,2048]{1,0:T(8,128)(2,1)}, bf16[256,2048]{1,0:T(8,128)(2,1)}, bf16[8,512,256]{2,1,0:T(8,128)(2,1)}) custom-call(bf16[256,2048]{1,0:T(8,128)(2,1)} %copy-done.43, bf16[256,2048]{1,0:T(8,128)(2,1)} %collective-permute-done.15.refs_1_, bf16[4,2048,256]{2,1,0:T(8,128)(2,1)} %refs_2_.3, bf16[4,2048,256]{2,1,0:T(8,128)(2,1)} %refs_3_.3, ...), custom_call_target="tpu_custom_call" | custom-call | flops 17179869184 | bytes 23592960 | tf_op jit(solution)/shard_map/pallas_call | solution.py:202
  151.4 25.4 %shard_map.249 = (bf16[128,2048]{1,0:T(8,128)(2,1)}, bf16[128,2048]{1,0:T(8,128)(2,1)}, bf16[128,2048]{1,0:T(8,128)(2,1)}, bf16[128,2048]{1,0:T(8,128)(2,1)}, bf16[8,512,256]{2,1,0:T(8,128)(2,1)}) custom-call(bf16[256,2048]{1,0:T(8,128)(2,1)} %copy-done.44, bf16[256,2048]{1,0:T(8,128)(2,1)} %copy-done.55, bf16[4,2048,256]{2,1,0:T(8,128)(2,1)} %refs_2_.3, ...), custom_call_target="tpu_custom_call" | custom-call | flops 17179869184 | bytes 23592960 | tf_op jit(solution)/shard_map/pallas_call | solution.py:202
  178.8 2.4 collective-permute-start.29
  183.9 29.4 %shard_map.250 = (bf16[128,2048]{1,0:T(8,128)(2,1)}, bf16[128,2048]{1,0:T(8,128)(2,1)}, bf16[128,2048]{1,0:T(8,128)(2,1)}, bf16[128,2048]{1,0:T(8,128)(2,1)}, bf16[8,512,256]{2,1,0:T(8,128)(2,1)}) custom-call(bf16[256,2048]{1,0:T(8,128)(2,1)} %copy-done.45, bf16[256,2048]{1,0:T(8,128)(2,1)} %copy-done.54, bf16[4,2048,256]{2,1,0:T(8,128)(2,1)} %refs_2_.3, ...), custom_call_target="tpu_custom_call" | custom-call | flops 21474836480 | bytes 29753344 | tf_op jit(solution)/shard_map/pallas_call | solution.py:202
  219.8 29.6 %shard_map.251 = (bf16[128,2048]{1,0:T(8,128)(2,1)}, bf16[128,2048]{1,0:T(8,128)(2,1)}, bf16[128,2048]{1,0:T(8,128)(2,1)}, bf16[128,2048]{1,0:T(8,128)(2,1)}, bf16[8,512,256]{2,1,0:T(8,128)(2,1)}) custom-call(bf16[256,2048]{1,0:T(8,128)(2,1)} %copy-done.46, bf16[256,2048]{1,0:T(8,128)(2,1)} %copy-done.53, bf16[4,2048,256]{2,1,0:T(8,128)(2,1)} %refs_2_.3, ...), custom_call_target="tpu_custom_call" | custom-call | flops 21474836480 | bytes 29753344 | tf_op jit(solution)/shard_map/pallas_call | solution.py:202
  251.2 2.5 collective-permute-start.35
  256.7 13.1 %shard_map.252 = (bf16[128,2048]{1,0:T(8,128)(2,1)}, bf16[128,2048]{1,0:T(8,128)(2,1)}, bf16[128,2048]{1,0:T(8,128)(2,1)}, bf16[128,2048]{1,0:T(8,128)(2,1)}, bf...) custom-call(bf16[8,512,256]{2,1,0:T(8,128)(2,1)} %get-tuple-element., ...), custom_call_target="tpu_custom_call" | custom-call | tf_op jit(solution)/shard_map/pallas_call | solution.py:202
  273.1 8.6 %shard_map.253 = (bf16[128,2048]{1,0:T(8,128)(2,1)}, bf16[128,2048]{1,0:T(8,128)(2,1)}, bf16[128,2048]{1,0:T(8,128)(2,1)}, bf16[128,2048]{1,0:T(8,128)(2,1)}) custom-call(bf16[8,512,256]{2,1,0:T(8,128)(2,1)} %get-tuple-element.441.refs_0_, bf16[1024,2048]{1,0:T(8,128)(2,1)} %bitcast.26, bf16[1024,2048]{1,0:T(8,128)(2,1)} %collective-permute-done.14.refs_7_.refs_8_.refs_3_.refs_2_), custom_call_target="tpu_custom_call" | custom-call | tf_op jit(solution)/shard_map/pallas_call | solution.py:202
  281.7 5.0 %collective-permute-done.40 = bf16[128,2048]{1,0:T(8,128)(2,1)S(1)} collective-permute-done((bf16[128,2048]{1,0:T(8,128)(2,1)S(1)}, bf16[128,2048]{1,0:T(8,128)(2,1)S(1)}, u32[]{:S(2)}, u32[]{:S(2)}) %collective-permute-start.40) | collective-permute-done | bytes 524320 | tf_op jit(solution)/shard_map/ppermute | solution.py:77
  287.0 8.6 %shard_map.254 = (bf16[128,2048]{1,0:T(8,128)(2,1)}, bf16[128,2048]{1,0:T(8,128)(2,1)}, bf16[128,2048]{1,0:T(8,128)(2,1)}, bf16[128,2048]{1,0:T(8,128)(2,1)}) custom-call(bf16[8,512,256]{2,1,0:T(8,128)(2,1)} %get-tuple-element.453.refs_0_, bf16[1024,2048]{1,0:T(8,128)(2,1)} %bitcast.27, bf16[1024,2048]{1,0:T(8,128)(2,1)} %collective-permute-done.14.refs_7_.refs_8_.refs_3_.refs_2_), custom_call_target="tpu_custom_call" | custom-call | tf_op jit(solution)/shard_map/pallas_call | solution.py:202
  295.6 2.4 collective-permute-done.43.arrived
  298.8 3.9 shard_map.255
  303.6 8.9 %collective-permute-done.45 = bf16[128,2048]{1,0:T(8,128)(2,1)S(1)} collective-permute-done((bf16[128,2048]{1,0:T(8,128)(2,1)S(1)}, bf16[128,2048]{1,0:T(8,128)(2,1)S(1)}, u32[]{:S(2)}, u32[]{:S(2)}) %collective-permute-start.45) | collective-permute-done | bytes 524320 | tf_op jit(solution)/shard_map/ppermute | solution.py:77
  312.5 1.9 collective-permute-done.46.refs_3_
  314.7 1.8 collective-permute-start.49
  318.9 17.5 %shard_map.256 = (f32[512,512]{1,0:T(8,128)}, f32[512,512]{1,0:T(8,128)}, bf16[512,512]{1,0:T(8,128)(2,1)}, f32[8,512]{1,0:T(8,128)}, bf16[16,512]{1,0:T(8,128)(2,1)}, /*index=5*/bf16[16,512]{1,0:T(8,128)(2,1)}) custom-call(s32[5]{0:T(128)} %concatenate.80.scalars, bf16[128,2176]{1,0:T(8,128)(2,1)} %get-tuple-element.487.refs_0_, ...), custom_call_target="tpu_custom_call" | custom-call | flops 2952790016 | bytes 10750484 | tf_op jit(solution)/shard_map/pallas_call | solution.py:202
  336.4 3.4 collective-permute-done.49
  344.3 2.2 collective-permute-done.53
  348.9 3.5 collective-permute-start.58
  352.4 5.0 %shard_map.257 = (bf16[3,512,512]{2,1,0:T(8,128)(2,1)}, bf16[512,128]{1,0:T(8,128)(2,1)}, bf16[48,512]{1,0:T(8,128)(2,1)}) custom-call(f32[8,512]{1,0:T(8,128)} %add.416.inner, f32[8,512]{1,0:T(8,128)} %add.377.squares, f32[512,512]{1,0:T(8,128)} %get-tuple-element.541.query_grad, f32[512,512]{1,0:T(8,128)} %get-tuple-element.542.key_grad, ...), custom_call_target="tpu_custom_call" | custom-call | tf_op jit(solution)/shard_map/pallas_call | solution.py:202
  360.5 7.7 %shard_map.258 = (f32[256,2048]{1,0:T(8,128)}, bf16[256,2048]{1,0:T(8,128)(2,1)}) custom-call(s32[1]{0:T(128)} %bitcast.1.core.scalars, bf16[3,512,512]{2,1,0:T(8,128)(2,1)} %get-tuple-element.547.raw, bf16[2048,512]{1,0:T(8,128)(2,1)} %query_weight.3, bf16[2048,512]{1,0:T(8,128)(2,1)} %key_weight.3, bf16[2048,512]{1,0:T(8,128)(2,1)} %value_weight.3), custom_call_target="tpu_custom_call" | custom-call | tf_op jit(solution)/shard_map/pallas_call | solution.py:202
  368.7 2.6 collective-permute-done.59
  376.4 2.9 shard_map.259
  379.3 2.1 collective-permute-start.60
  381.8 9.0 %collective-permute-done.60 = bf16[144,512]{1,0:T(8,128)(2,1)S(1)} collective-permute-done((bf16[144,512]{1,0:T(8,128)(2,1)}, bf16[144,512]{1,0:T(8,128)(2,1)S(1)}, u32[]{:S(2)}, u32[]{:S(2)}) %collective-permute-start.60) | collective-permute-done | bytes 147488 | tf_op jit(solution)/shard_map/ppermute | solution.py:77
  394.6 4.5 shard_map.260.refs_0_
  399.1 2.0 collective-permute-done.64
  402.5 5.5 %collective-permute-done.65 = bf16[144,512]{1,0:T(8,128)(2,1)S(1)} collective-permute-done((bf16[144,512]{1,0:T(8,128)(2,1)S(1)}, bf16[144,512]{1,0:T(8,128)(2,1)S(1)}, u32[]{:S(2)}, u32[]{:S(2)}) %collective-permute-start.65) | collective-permute-done | bytes 147488 | tf_op jit(solution)/shard_map/ppermute | solution.py:77
  410.4 1.8 collective-permute-start.68
  412.4 7.2 %collective-permute-done.71.refs_1_ = bf16[128,2048]{1,0:T(8,128)(2,1)S(1)} collective-permute-done((bf16[128,2048]{1,0:T(8,128)(2,1)}, bf16[128,2048]{1,0:T(8,128)(2,1)S(1)}, u32[]{:S(2)}, u32[]{:S(2)}) %collective-permute-start.71) | collective-permute-done | bytes 524320 | tf_op jit(solution)/shard_map/ppermute | solution.py:77
  419.7 8.6 %collective-permute-done.70 = bf16[256,1024]{1,0:T(8,128)(2,1)S(1)} collective-permute-done((bf16[256,1024]{1,0:T(8,128)(2,1)S(1)}, bf16[256,1024]{1,0:T(8,128)(2,1)S(1)}, u32[]{:S(2)}, u32[]{:S(2)}) %collective-permute-start.70) | collective-permute-done | bytes 524320 | tf_op jit(solution)/shard_map/ppermute | solution.py:77
  434.0 4.6 %shard_map.261 = f32[512,2048]{1,0:T(8,128)} custom-call(s32[4]{0:T(128)} %pad_add_fusion.order, bf16[128,2048]{1,0:T(8,128)(2,1)} %shard_map.260.refs_0_, bf16[128,2048]{1,0:T(8,128)(2,1)} %copy-done.28, bf16[128,2048]{1,0:T(8,128)(2,1)} %collective-permute-done.74.refs_2_, bf16[128,2048]{1,0:T(8,128)(2,1)} %collective-permute-done.75.refs_3_), custom_call_target="tpu_custom_call" | custom-call | tf_op jit(solution)/shard_map/pallas_call | solution.py:202
  438.6 7.3 %collective-permute-done.73 = bf16[256,1024]{1,0:T(8,128)(2,1)} collective-permute-done((bf16[256,1024]{1,0:T(8,128)(2,1)}, bf16[256,1024]{1,0:T(8,128)(2,1)}, u32[]{:S(2)}, u32[]{:S(2)}) %collective-permute-start.73) | collective-permute-done | bytes 524320 | tf_op jit(solution)/shard_map/ppermute | solution.py:77
  451.4 5.3 %shard_map.262 = (f32[3,2048,128]{2,1,0:T(8,128)}, f32[3,128,512]{2,1,0:T(8,128)}, f32[512,128]{1,0:T(8,128)}, f32[128,2048]{1,0:T(8,128)}) custom-call(s32[4]{0:T(128)} %pad_add_fusion.order, bf16[1152,512]{1,0:T(8,128)(2,1)} %copy-done.1, bf16[512,512]{1,0:T(8,128)(2,1)} %collective-permute-done.72.refs_1_, bf16[512,512]{1,0:T(8,128)(2,1)} %copy-done.41, ...), custom_call_target="tpu_custom_call" | custom-call | tf_op jit(solution)/shard_map/pallas_call | solution.py:202
  (360 shorter events, 90.6 us)
Async XLA Ops:
  3.5 29.7 %collective-permute-start.2 = (bf16[256,2176]{1,0:T(8,128)(2,1)S(1)}, bf16[256,2176]{1,0:T(8,128)(2,1)S(1)}, u32[]{:S(2)}, u32[]{:S(2)}) collective-permute-start(bf16[256,2176]{1,0:T(8,128)(2,1)S(1)} %maximum_maximum_fusion.refs_0_), channel_id=1, source_target_pairs={{0,8},{4,12},{8,16},{12,20},{16,24},{20,28},{24,0},{28,4},{1,9},{5... | collective-permute-start | bytes 3342344 | tf_op jit(solution)/shard_map/ppermute | solution.py:77
  6.6 26.6 %collective-permute-start.3 = (bf16[256,2176]{1,0:T(8,128)(2,1)S(1)}, bf16[256,2176]{1,0:T(8,128)(2,1)S(1)}, u32[]{:S(2)}, u32[]{:S(2)}) collective-permute-start(bf16[256,2176]{1,0:T(8,128)(2,1)S(1)} %maximum_maximum_fusion.refs_0_), channel_id=1, source_target_pairs={{0,4},{4,0},{8,12},{12,8},{16,20},{20,16},{24,28},{28,24},{1,5},{5... | collective-permute-start | bytes 3342344 | tf_op jit(solution)/shard_map/ppermute | solution.py:77
  33.2 40.5 %collective-permute-start.10 = (bf16[4,2048,256]{2,1,0:T(8,128)(2,1)}, bf16[4,2048,256]{2,1,0:T(8,128)(2,1)}, u32[]{:S(2)}, u32[]{:S(2)}) collective-permute-start(bf16[4,2048,256]{2,1,0:T(8,128)(2,1)} %refs_2_.3), channel_id=1, source_target_pairs={{0,1},{1,0},{2,3},{3,2},{4,5},{5,4},{6,7},{7,6},{8,9},{9,8},{10,11... | collective-permute-start | bytes 12582920 | tf_op jit(solution)/shard_map/ppermute | solution.py:77
  33.2 40.5 %collective-permute-start.11 = (bf16[4,2048,256]{2,1,0:T(8,128)(2,1)}, bf16[4,2048,256]{2,1,0:T(8,128)(2,1)}, u32[]{:S(2)}, u32[]{:S(2)}) collective-permute-start(bf16[4,2048,256]{2,1,0:T(8,128)(2,1)} %refs_3_.3), channel_id=1, source_target_pairs={{0,1},{1,0},{2,3},{3,2},{4,5},{5,4},{6,7},{7,6},{8,9},{9,8},{10,11... | collective-permute-start | bytes 12582920 | tf_op jit(solution)/shard_map/ppermute | solution.py:77
  33.8 16.5 %collective-permute-start.4 = (bf16[128,2176]{1,0:T(8,128)(2,1)S(1)}, bf16[128,2176]{1,0:T(8,128)(2,1)S(1)}, u32[]{:S(2)}, u32[]{:S(2)}) collective-permute-start(bf16[128,2176]{1,0:T(8,128)(2,1)S(1)} %get-tuple-element.351.refs_2_), channel_id=1, source_target_pairs={{0,8},{4,12},{8,16},{12,20},{16,24},{20,28},{24,0},{28,4},{1,9},{5... | collective-permute-start | bytes 1671176 | tf_op jit(solution)/shard_map/ppermute | solution.py:77
  57.5 16.2 %collective-permute-start.8 = (bf16[128,2176]{1,0:T(8,128)(2,1)S(1)}, bf16[128,2176]{1,0:T(8,128)(2,1)S(1)}, u32[]{:S(2)}, u32[]{:S(2)}) collective-permute-start(bf16[128,2176]{1,0:T(8,128)(2,1)S(1)} %get-tuple-element.337.refs_3_), channel_id=1, source_target_pairs={{0,8},{4,12},{8,16},{12,20},{16,24},{20,28},{24,0},{28,4},{1,9},{5... | collective-permute-start | bytes 1671176 | tf_op jit(solution)/shard_map/ppermute | solution.py:77
  57.9 15.7 %collective-permute-start.9 = (bf16[128,2176]{1,0:T(8,128)(2,1)S(1)}, bf16[128,2176]{1,0:T(8,128)(2,1)S(1)}, u32[]{:S(2)}, u32[]{:S(2)}) collective-permute-start(bf16[128,2176]{1,0:T(8,128)(2,1)S(1)} %get-tuple-element.337.refs_3_), channel_id=1, source_target_pairs={{0,4},{4,0},{8,12},{12,8},{16,20},{20,16},{24,28},{28,24},{1,5},{5... | collective-permute-start | bytes 1671176 | tf_op jit(solution)/shard_map/ppermute | solution.py:77
  73.7 20.3 %collective-permute-start.14 = (bf16[1024,2048]{1,0:T(8,128)(2,1)S(1)}, bf16[1024,2048]{1,0:T(8,128)(2,1)}, u32[]{:S(2)}, u32[]{:S(2)}) collective-permute-start(bf16[1024,2048]{1,0:T(8,128)(2,1)S(1)} %bitcast.28), channel_id=1, source_target_pairs={{0,1},{1,0},{2,3},{3,2},{4,5},{5,4},{6,7},{7,6},{8,9},{9,8},{10,11... | collective-permute-start | bytes 12582920 | tf_op jit(solution)/shard_map/ppermute | solution.py:77
  77.8 16.2 %collective-permute-start.12 = (bf16[128,2048]{1,0:T(8,128)(2,1)}, bf16[128,2048]{1,0:T(8,128)(2,1)S(1)}, u32[]{:S(2)}, u32[]{:S(2)}) collective-permute-start(bf16[128,2048]{1,0:T(8,128)(2,1)} %get-tuple-element.345), channel_id=1, source_target_pairs={{0,8},{4,12},{8,16},{12,20},{16,24},{20,28},{24,0},{28,4},{1,9},{5... | collective-permute-start | bytes 1572872 | tf_op jit(solution)/shard_map/ppermute | solution.py:77
  77.8 16.2 %collective-permute-start.13 = (bf16[128,2048]{1,0:T(8,128)(2,1)}, bf16[128,2048]{1,0:T(8,128)(2,1)S(1)}, u32[]{:S(2)}, u32[]{:S(2)}) collective-permute-start(bf16[128,2048]{1,0:T(8,128)(2,1)} %get-tuple-element.345), channel_id=1, source_target_pairs={{0,4},{4,0},{8,12},{12,8},{16,20},{20,16},{24,28},{28,24},{1,5},{5... | collective-permute-start | bytes 1572872 | tf_op jit(solution)/shard_map/ppermute | solution.py:77
  94.1 24.8 %collective-permute-start.15 = (bf16[256,2048]{1,0:T(8,128)(2,1)S(1)}, bf16[256,2048]{1,0:T(8,128)(2,1)}, u32[]{:S(2)}, u32[]{:S(2)}) collective-permute-start(bf16[256,2048]{1,0:T(8,128)(2,1)S(1)} %constant_dynamic-update-slice_fusion.refs_0_), channel_id=1, source_target_pairs={{0,2},{1,3},{2,0},{3,1},{4,6},{5,7},{6,4},{7,5},{8,10},{9,11},{10,... | collective-permute-start | bytes 3145736 | tf_op jit(solution)/shard_map/ppermute | solution.py:77
  94.7 20.1 %collective-permute-start.16 = (bf16[128,2048]{1,0:T(8,128)(2,1)S(1)}, bf16[128,2048]{1,0:T(8,128)(2,1)S(1)}, u32[]{:S(2)}, u32[]{:S(2)}) collective-permute-start(bf16[128,2048]{1,0:T(8,128)(2,1)S(1)} %collective-permute-done.12), channel_id=1, source_target_pairs={{0,8},{4,12},{8,16},{12,20},{16,24},{20,28},{24,0},{28,4},{1,9},{5... | collective-permute-start | bytes 1572872 | tf_op jit(solution)/shard_map/ppermute | solution.py:77
  95.0 19.9 %collective-permute-start.17 = (bf16[128,2048]{1,0:T(8,128)(2,1)S(1)}, bf16[128,2048]{1,0:T(8,128)(2,1)S(1)}, u32[]{:S(2)}, u32[]{:S(2)}) collective-permute-start(bf16[128,2048]{1,0:T(8,128)(2,1)S(1)} %collective-permute-done.12), channel_id=1, source_target_pairs={{0,4},{4,0},{8,12},{12,8},{16,20},{20,16},{24,28},{28,24},{1,5},{5... | collective-permute-start | bytes 1572872 | tf_op jit(solution)/shard_map/ppermute | solution.py:77
  118.9 28.7 %collective-permute-start.19 = (bf16[128,2048]{1,0:T(8,128)(2,1)S(1)}, bf16[128,2048]{1,0:T(8,128)(2,1)S(1)}, u32[]{:S(2)}, u32[]{:S(2)}) collective-permute-start(bf16[128,2048]{1,0:T(8,128)(2,1)S(1)} %collective-permute-done.16), channel_id=1, source_target_pairs={{0,8},{4,12},{8,16},{12,20},{16,24},{20,28},{24,0},{28,4},{1,9},{5... | collective-permute-start | bytes 1572872 | tf_op jit(solution)/shard_map/ppermute | solution.py:77
  118.9 28.7 %collective-permute-start.20 = (bf16[128,2048]{1,0:T(8,128)(2,1)S(1)}, bf16[128,2048]{1,0:T(8,128)(2,1)S(1)}, u32[]{:S(2)}, u32[]{:S(2)}) collective-permute-start(bf16[128,2048]{1,0:T(8,128)(2,1)S(1)} %collective-permute-done.16), channel_id=1, source_target_pairs={{0,4},{4,0},{8,12},{12,8},{16,20},{20,16},{24,28},{28,24},{1,5},{5... | collective-permute-start | bytes 1572872 | tf_op jit(solution)/shard_map/ppermute | solution.py:77
  120.4 56.4 %collective-permute-start.23 = (bf16[256,2176]{1,0:T(8,128)(2,1)S(1)}, bf16[256,2176]{1,0:T(8,128)(2,1)}, u32[]{:S(2)}, u32[]{:S(2)}) collective-permute-start(bf16[256,2176]{1,0:T(8,128)(2,1)S(1)} %pad_maximum_fusion.refs_9_), channel_id=1, source_target_pairs={{0,8},{4,12},{8,16},{12,20},{16,24},{20,28},{24,0},{28,4},{1,9},{5... | collective-permute-start | bytes 3342344 | tf_op jit(solution)/shard_map/ppermute | solution.py:77
  120.9 55.9 %collective-permute-start.24 = (bf16[256,2176]{1,0:T(8,128)(2,1)S(1)}, bf16[256,2176]{1,0:T(8,128)(2,1)}, u32[]{:S(2)}, u32[]{:S(2)}) collective-permute-start(bf16[256,2176]{1,0:T(8,128)(2,1)S(1)} %pad_maximum_fusion.refs_9_), channel_id=1, source_target_pairs={{0,4},{4,0},{8,12},{12,8},{16,20},{20,16},{24,28},{28,24},{1,5},{5... | collective-permute-start | bytes 3342344 | tf_op jit(solution)/shard_map/ppermute | solution.py:77
  121.5 26.1 %collective-permute-start.18 = (bf16[256,2048]{1,0:T(8,128)(2,1)S(1)}, bf16[256,2048]{1,0:T(8,128)(2,1)S(1)}, u32[]{:S(2)}, u32[]{:S(2)}) collective-permute-start(bf16[256,2048]{1,0:T(8,128)(2,1)S(1)} %constant_dynamic-update-slice_fusion.2.refs_0_), channel_id=1, source_target_pairs={{0,2},{1,3},{2,0},{3,1},{4,6},{5,7},{6,4},{7,5},{8,10},{9,11},{10,... | collective-permute-start | bytes 3145736 | tf_op jit(solution)/shard_map/ppermute | solution.py:77
  147.7 29.1 %collective-permute-start.21 = (bf16[256,2048]{1,0:T(8,128)(2,1)S(1)}, bf16[256,2048]{1,0:T(8,128)(2,1)S(1)}, u32[]{:S(2)}, u32[]{:S(2)}) collective-permute-start(bf16[256,2048]{1,0:T(8,128)(2,1)S(1)} %constant_dynamic-update-slice_fusion.4.refs_0_), channel_id=1, source_target_pairs={{0,2},{1,3},{2,0},{3,1},{4,6},{5,7},{6,4},{7,5},{8,10},{9,11},{10,... | collective-permute-start | bytes 3145736 | tf_op jit(solution)/shard_map/ppermute | solution.py:77
  149.3 27.5 %collective-permute-start.22 = (bf16[128,2048]{1,0:T(8,128)(2,1)S(1)}, bf16[128,2048]{1,0:T(8,128)(2,1)S(1)}, u32[]{:S(2)}, u32[]{:S(2)}) collective-permute-start(bf16[128,2048]{1,0:T(8,128)(2,1)S(1)} %collective-permute-done.19), channel_id=1, source_target_pairs={{0,4},{4,0},{8,12},{12,8},{16,20},{20,16},{24,28},{28,24},{1,5},{5... | collective-permute-start | bytes 1572872 | tf_op jit(solution)/shard_map/ppermute | solution.py:77
  150.8 62.5 %collective-permute-start.28 = (bf16[256,2048]{1,0:T(8,128)(2,1)}, bf16[256,2048]{1,0:T(8,128)(2,1)S(1)}, u32[]{:S(2)}, u32[]{:S(2)}) collective-permute-start(bf16[256,2048]{1,0:T(8,128)(2,1)} %get-tuple-element.393), channel_id=1, source_target_pairs={{0,4},{4,0},{8,12},{12,8},{16,20},{20,16},{24,28},{28,24},{1,5},{5... | collective-permute-start | bytes 3145736 | tf_op jit(solution)/shard_map/ppermute | solution.py:77
  177.9 35.5 %collective-permute-start.25 = (bf16[256,2048]{1,0:T(8,128)(2,1)S(1)}, bf16[256,2048]{1,0:T(8,128)(2,1)S(1)}, u32[]{:S(2)}, u32[]{:S(2)}) collective-permute-start(bf16[256,2048]{1,0:T(8,128)(2,1)S(1)} %constant_dynamic-update-slice_fusion.6.refs_0_), channel_id=1, source_target_pairs={{0,2},{1,3},{2,0},{3,1},{4,6},{5,7},{6,4},{7,5},{8,10},{9,11},{10,... | collective-permute-start | bytes 3145736 | tf_op jit(solution)/shard_map/ppermute | solution.py:77
  178.8 34.7 %collective-permute-start.29 = (bf16[256,2176]{1,0:T(8,128)(2,1)}, bf16[256,2176]{1,0:T(8,128)(2,1)S(1)}, u32[]{:S(2)}, u32[]{:S(2)}) collective-permute-start(bf16[256,2176]{1,0:T(8,128)(2,1)} %collective-permute-done.24.refs_10_), channel_id=1, source_target_pairs={{0,8},{4,12},{8,16},{12,20},{16,24},{20,28},{24,0},{28,4},{1,9},{5... | collective-permute-start | bytes 3342344 | tf_op jit(solution)/shard_map/ppermute | solution.py:77
  181.2 32.2 %collective-permute-start.26 = (bf16[128,2048]{1,0:T(8,128)(2,1)}, bf16[128,2048]{1,0:T(8,128)(2,1)S(1)}, u32[]{:S(2)}, u32[]{:S(2)}) collective-permute-start(bf16[128,2048]{1,0:T(8,128)(2,1)} %get-tuple-element.383), channel_id=1, source_target_pairs={{0,2},{1,3},{2,0},{3,1},{4,6},{5,7},{6,4},{7,5},{8,10},{9,11},{10,... | collective-permute-start | bytes 1572872 | tf_op jit(solution)/shard_map/ppermute | solution.py:77
  182.4 31.0 %collective-permute-start.27 = (bf16[128,2048]{1,0:T(8,128)(2,1)}, bf16[128,2048]{1,0:T(8,128)(2,1)S(1)}, u32[]{:S(2)}, u32[]{:S(2)}) collective-permute-start(bf16[128,2048]{1,0:T(8,128)(2,1)} %get-tuple-element.384), channel_id=1, source_target_pairs={{0,4},{4,0},{8,12},{12,8},{16,20},{20,16},{24,28},{28,24},{1,5},{5... | collective-permute-start | bytes 1572872 | tf_op jit(solution)/shard_map/ppermute | solution.py:77
  214.6 34.9 %collective-permute-start.34 = (bf16[128,2048]{1,0:T(8,128)(2,1)S(1)}, bf16[128,2048]{1,0:T(8,128)(2,1)S(1)}, u32[]{:S(2)}, u32[]{:S(2)}) collective-permute-start(bf16[128,2048]{1,0:T(8,128)(2,1)S(1)} %add_convert_fusion.4), channel_id=1, source_target_pairs={{0,2},{1,3},{2,0},{3,1},{4,6},{5,7},{6,4},{7,5},{8,10},{9,11},{10,... | collective-permute-start | bytes 1572872 | tf_op jit(solution)/shard_map/ppermute | solution.py:77
  215.6 33.9 %collective-permute-start.31 = (bf16[64,2048]{1,0:T(8,128)(2,1)S(1)}, bf16[64,2048]{1,0:T(8,128)(2,1)S(1)}, u32[]{:S(2)}, u32[]{:S(2)}) collective-permute-start(bf16[64,2048]{1,0:T(8,128)(2,1)S(1)} %add_convert_fusion.17), channel_id=1, source_target_pairs={{0,2},{1,3},{2,0},{3,1},{4,6},{5,7},{6,4},{7,5},{8,10},{9,11},{10,... | collective-permute-start | bytes 786440 | tf_op jit(solution)/shard_map/ppermute | solution.py:77
  216.9 32.6 %collective-permute-start.30 = (bf16[64,2048]{1,0:T(8,128)(2,1)S(1)}, bf16[64,2048]{1,0:T(8,128)(2,1)S(1)}, u32[]{:S(2)}, u32[]{:S(2)}) collective-permute-start(bf16[64,2048]{1,0:T(8,128)(2,1)S(1)} %add_convert_fusion.18), channel_id=1, source_target_pairs={{0,4},{4,0},{8,12},{12,8},{16,20},{20,16},{24,28},{28,24},{1,5},{5... | collective-permute-start | bytes 786440 | tf_op jit(solution)/shard_map/ppermute | solution.py:77
  217.5 32.0 %collective-permute-start.32 = (bf16[128,2048]{1,0:T(8,128)(2,1)}, bf16[128,2048]{1,0:T(8,128)(2,1)S(1)}, u32[]{:S(2)}, u32[]{:S(2)}) collective-permute-start(bf16[128,2048]{1,0:T(8,128)(2,1)} %get-tuple-element.397), channel_id=1, source_target_pairs={{0,2},{1,3},{2,0},{3,1},{4,6},{5,7},{6,4},{7,5},{8,10},{9,11},{10,... | collective-permute-start | bytes 1572872 | tf_op jit(solution)/shard_map/ppermute | solution.py:77
  218.3 31.2 %collective-permute-start.33 = (bf16[128,2048]{1,0:T(8,128)(2,1)}, bf16[128,2048]{1,0:T(8,128)(2,1)S(1)}, u32[]{:S(2)}, u32[]{:S(2)}) collective-permute-start(bf16[128,2048]{1,0:T(8,128)(2,1)} %get-tuple-element.398), channel_id=1, source_target_pairs={{0,4},{4,0},{8,12},{12,8},{16,20},{20,16},{24,28},{28,24},{1,5},{5... | collective-permute-start | bytes 1572872 | tf_op jit(solution)/shard_map/ppermute | solution.py:77
  249.6 20.2 %collective-permute-start.39 = (bf16[64,2048]{1,0:T(8,128)(2,1)S(1)}, bf16[64,2048]{1,0:T(8,128)(2,1)S(1)}, u32[]{:S(2)}, u32[]{:S(2)}) collective-permute-start(bf16[64,2048]{1,0:T(8,128)(2,1)S(1)} %add_convert_fusion.13), channel_id=1, source_target_pairs={{0,2},{1,3},{2,0},{3,1},{4,6},{5,7},{6,4},{7,5},{8,10},{9,11},{10,... | collective-permute-start | bytes 786440 | tf_op jit(solution)/shard_map/ppermute | solution.py:77
  251.2 18.6 %collective-permute-start.35 = (bf16[128,2048]{1,0:T(8,128)(2,1)S(1)}, bf16[128,2048]{1,0:T(8,128)(2,1)S(1)}, u32[]{:S(2)}, u32[]{:S(2)}) collective-permute-start(bf16[128,2048]{1,0:T(8,128)(2,1)S(1)} %pad_maximum_fusion.1), channel_id=1, source_target_pairs={{0,8},{4,12},{8,16},{12,20},{16,24},{20,28},{24,0},{28,4},{1,9},{5... | collective-permute-start | bytes 1572872 | tf_op jit(solution)/shard_map/ppermute | solution.py:77
  253.7 16.1 %collective-permute-start.36 = (bf16[128,2048]{1,0:T(8,128)(2,1)}, bf16[128,2048]{1,0:T(8,128)(2,1)S(1)}, u32[]{:S(2)}, u32[]{:S(2)}) collective-permute-start(bf16[128,2048]{1,0:T(8,128)(2,1)} %get-tuple-element.415), channel_id=1, source_target_pairs={{0,2},{1,3},{2,0},{3,1},{4,6},{5,7},{6,4},{7,5},{8,10},{9,11},{10,... | collective-permute-start | bytes 1572872 | tf_op jit(solution)/shard_map/ppermute | solution.py:77
  314.4 22.0 %collective-permute-start.48 = (bf16[128,2048]{1,0:T(8,128)(2,1)}, bf16[128,2048]{1,0:T(8,128)(2,1)S(1)}, u32[]{:S(2)}, u32[]{:S(2)}) collective-permute-start(bf16[128,2048]{1,0:T(8,128)(2,1)} %get-tuple-element.511), channel_id=1, source_target_pairs={{0,4},{4,0},{8,12},{12,8},{16,20},{20,16},{24,28},{28,24},{1,5},{5... | collective-permute-start | bytes 1572872 | tf_op jit(solution)/shard_map/ppermute | solution.py:77
  314.7 25.1 %collective-permute-start.49 = (bf16[128,2048]{1,0:T(8,128)(2,1)}, bf16[128,2048]{1,0:T(8,128)(2,1)S(1)}, u32[]{:S(2)}, u32[]{:S(2)}) collective-permute-start(bf16[128,2048]{1,0:T(8,128)(2,1)} %get-tuple-element.512), channel_id=1, source_target_pairs={{0,4},{4,0},{8,12},{12,8},{16,20},{20,16},{24,28},{28,24},{1,5},{5... | collective-permute-start | bytes 1572872 | tf_op jit(solution)/shard_map/ppermute | solution.py:77
  316.5 23.4 %collective-permute-start.50 = (bf16[128,2048]{1,0:T(8,128)(2,1)}, bf16[128,2048]{1,0:T(8,128)(2,1)S(1)}, u32[]{:S(2)}, u32[]{:S(2)}) collective-permute-start(bf16[128,2048]{1,0:T(8,128)(2,1)} %get-tuple-element.513), channel_id=1, source_target_pairs={{0,24},{4,28},{8,0},{12,4},{16,8},{20,12},{24,16},{28,20},{1,25},{... | collective-permute-start | bytes 1572872 | tf_op jit(solution)/shard_map/ppermute | solution.py:77
  317.9 23.4 %collective-permute-start.51 = (bf16[128,2048]{1,0:T(8,128)(2,1)}, bf16[128,2048]{1,0:T(8,128)(2,1)S(1)}, u32[]{:S(2)}, u32[]{:S(2)}) collective-permute-start(bf16[128,2048]{1,0:T(8,128)(2,1)} %get-tuple-element.514), channel_id=1, source_target_pairs={{0,24},{4,28},{8,0},{12,4},{16,8},{20,12},{24,16},{28,20},{1,25},{... | collective-permute-start | bytes 1572872 | tf_op jit(solution)/shard_map/ppermute | solution.py:77
  347.1 21.1 %collective-permute-start.56 = (bf16[256,1024]{1,0:T(8,128)(2,1)S(1)}, bf16[256,1024]{1,0:T(8,128)(2,1)S(1)}, u32[]{:S(2)}, u32[]{:S(2)}) collective-permute-start(bf16[256,1024]{1,0:T(8,128)(2,1)S(1)} %pad_maximum_fusion.2), channel_id=1, source_target_pairs={{0,2},{1,3},{2,0},{3,1},{4,6},{5,7},{6,4},{7,5},{8,10},{9,11},{10,... | collective-permute-start | bytes 1572872 | tf_op jit(solution)/shard_map/ppermute | solution.py:77
  348.6 19.7 %collective-permute-start.57 = (bf16[128,2048]{1,0:T(8,128)(2,1)S(1)}, bf16[128,2048]{1,0:T(8,128)(2,1)S(1)}, u32[]{:S(2)}, u32[]{:S(2)}) collective-permute-start(bf16[128,2048]{1,0:T(8,128)(2,1)S(1)} %copy-done.59), channel_id=1, source_target_pairs={{0,4},{4,0},{8,12},{12,8},{16,20},{20,16},{24,28},{28,24},{1,5},{5... | collective-permute-start | bytes 1572872 | tf_op jit(solution)/shard_map/ppermute | solution.py:77
  348.9 19.4 %collective-permute-start.58 = (bf16[128,2048]{1,0:T(8,128)(2,1)}, bf16[128,2048]{1,0:T(8,128)(2,1)S(1)}, u32[]{:S(2)}, u32[]{:S(2)}) collective-permute-start(bf16[128,2048]{1,0:T(8,128)(2,1)} %get-tuple-element.554), channel_id=1, source_target_pairs={{0,24},{4,28},{8,0},{12,4},{16,8},{20,12},{24,16},{28,20},{1,25},{... | collective-permute-start | bytes 1572872 | tf_op jit(solution)/shard_map/ppermute | solution.py:77
  372.5 18.3 %collective-permute-start.61 = (bf16[128,2048]{1,0:T(8,128)(2,1)S(1)}, bf16[128,2048]{1,0:T(8,128)(2,1)S(1)}, u32[]{:S(2)}, u32[]{:S(2)}) collective-permute-start(bf16[128,2048]{1,0:T(8,128)(2,1)S(1)} %get-tuple-element.594), channel_id=1, source_target_pairs={{0,2},{1,3},{2,0},{3,1},{4,6},{5,7},{6,4},{7,5},{8,10},{9,11},{10,... | collective-permute-start | bytes 1572872 | tf_op jit(solution)/shard_map/ppermute | solution.py:77
  374.0 16.9 %collective-permute-start.62 = (bf16[128,2048]{1,0:T(8,128)(2,1)S(1)}, bf16[128,2048]{1,0:T(8,128)(2,1)S(1)}, u32[]{:S(2)}, u32[]{:S(2)}) collective-permute-start(bf16[128,2048]{1,0:T(8,128)(2,1)S(1)} %add_convert_fusion.3), channel_id=1, source_target_pairs={{0,4},{4,0},{8,12},{12,8},{16,20},{20,16},{24,28},{28,24},{1,5},{5... | collective-permute-start | bytes 1572872 | tf_op jit(solution)/shard_map/ppermute | solution.py:77
  375.7 16.8 %collective-permute-start.63 = (bf16[128,2048]{1,0:T(8,128)(2,1)}, bf16[128,2048]{1,0:T(8,128)(2,1)S(1)}, u32[]{:S(2)}, u32[]{:S(2)}) collective-permute-start(bf16[128,2048]{1,0:T(8,128)(2,1)} %get-tuple-element.597), channel_id=1, source_target_pairs={{0,24},{4,28},{8,0},{12,4},{16,8},{20,12},{24,16},{28,20},{1,25},{... | collective-permute-start | bytes 1572872 | tf_op jit(solution)/shard_map/ppermute | solution.py:77
  401.1 18.6 %collective-permute-start.71 = (bf16[128,2048]{1,0:T(8,128)(2,1)}, bf16[128,2048]{1,0:T(8,128)(2,1)S(1)}, u32[]{:S(2)}, u32[]{:S(2)}) collective-permute-start(bf16[128,2048]{1,0:T(8,128)(2,1)} %shard_map.260.refs_0_), channel_id=1, source_target_pairs={{0,2},{1,3},{2,0},{3,1},{4,6},{5,7},{6,4},{7,5},{8,10},{9,11},{10,... | collective-permute-start | bytes 1572872 | tf_op jit(solution)/shard_map/ppermute | solution.py:77
  409.1 19.2 %collective-permute-start.70 = (bf16[256,1024]{1,0:T(8,128)(2,1)S(1)}, bf16[256,1024]{1,0:T(8,128)(2,1)S(1)}, u32[]{:S(2)}, u32[]{:S(2)}) collective-permute-start(bf16[256,1024]{1,0:T(8,128)(2,1)S(1)} %pad_maximum_fusion.4), channel_id=1, source_target_pairs={{0,2},{1,3},{2,0},{3,1},{4,6},{5,7},{6,4},{7,5},{8,10},{9,11},{10,... | collective-permute-start | bytes 1572872 | tf_op jit(solution)/shard_map/ppermute | solution.py:77
  410.4 17.9 %collective-permute-start.68 = (bf16[576,512]{1,0:T(8,128)(2,1)S(1)}, bf16[576,512]{1,0:T(8,128)(2,1)S(1)}, u32[]{:S(2)}, u32[]{:S(2)}) collective-permute-start(bf16[576,512]{1,0:T(8,128)(2,1)S(1)} %constant_dynamic-update-slice_fusion.8), channel_id=1, source_target_pairs={{0,4},{4,0},{8,12},{12,8},{16,20},{20,16},{24,28},{28,24},{1,5},{5... | collective-permute-start | bytes 1769480 | tf_op jit(solution)/shard_map/ppermute | solution.py:77
  412.3 15.9 %collective-permute-start.69 = (bf16[256,1024]{1,0:T(8,128)(2,1)S(1)}, bf16[256,1024]{1,0:T(8,128)(2,1)S(1)}, u32[]{:S(2)}, u32[]{:S(2)}) collective-permute-start(bf16[256,1024]{1,0:T(8,128)(2,1)S(1)} %fusion.4), channel_id=1, source_target_pairs={{0,8},{4,12},{8,16},{12,20},{16,24},{20,28},{24,0},{28,4},{1,9},{5... | collective-permute-start | bytes 1572872 | tf_op jit(solution)/shard_map/ppermute | solution.py:77
  429.9 16.0 %collective-permute-start.73 = (bf16[256,1024]{1,0:T(8,128)(2,1)}, bf16[256,1024]{1,0:T(8,128)(2,1)}, u32[]{:S(2)}, u32[]{:S(2)}) collective-permute-start(bf16[256,1024]{1,0:T(8,128)(2,1)} %fusion.6), channel_id=1, source_target_pairs={{0,8},{4,12},{8,16},{12,20},{16,24},{20,28},{24,0},{28,4},{1,9},{5... | collective-permute-start | bytes 1572872 | tf_op jit(solution)/shard_map/ppermute | solution.py:77
  (95 other events, 995.3 us)
